TPU v7x, 32 devices: a whole 2x2x4 slice. The times are simulated.
32 devices in a mesh: gx: 4 (over z), gy: 8 (over y, x, core).
Axes of the slice: x: 2, y: 2, z: 4, core: 2. Of those that a mesh axis runs over, the one named last changes fastest.
Arguments:
- tokens: bfloat16 [8, 2560, 1536], P('gx', 'gy'), may hold values from -6 to 6
- cotangent: bfloat16 [8, 2560, 1536], P('gx', 'gy'), may hold values from -6 to 6
- segment: int32 [8, 2560], P('gx'), may hold values from -1 to 12, as said below
- parent: int32 [8, 13], P('gx'), may hold values from 0 to 12, as said below
- w_qkv: bfloat16 [1536, 2048], P(('gx', 'gy')), may hold values from -0.21875 to 0.21875
- qkv_bias: bfloat16 [2048], P(('gx', 'gy')), may hold values from -3 to 3
- w_out: bfloat16 [1536, 1536], P(None, ('gx', 'gy')), may hold values from -1.75 to 1.75
- gain_attn: bfloat16 [1536], P(('gx', 'gy')), may hold values from 0.5 to 1.5
- gain_ffn: bfloat16 [1536], P(('gx', 'gy')), may hold values from 0.5 to 1.5
- w_gate: bfloat16 [1536, 8960], P('gx', 'gy'), may hold values from -0.15625 to 0.15625
- w_up: bfloat16 [1536, 8960], P('gx', 'gy'), may hold values from -0.15625 to 0.15625
- w_down: bfloat16 [8960, 1536], P('gy', 'gx'), may hold values from -0.1875 to 0.1875
Outputs:
- layer_out: bfloat16 [8, 2560, 1536], P('gx', 'gy')
- grad_tokens: bfloat16 [8, 2560, 1536], P('gx', 'gy')
- grad_w_qkv: float32 [1536, 2048], P(('gx', 'gy'))
- grad_qkv_bias: float32 [2048], P(('gx', 'gy'))
- grad_w_out: float32 [1536, 1536], P(None, ('gx', 'gy'))
- grad_gain_attn: float32 [1536], P(('gx', 'gy'))
- grad_gain_ffn: float32 [1536], P(('gx', 'gy'))
- grad_w_gate: float32 [1536, 8960], P('gx', 'gy')
- grad_w_up: float32 [1536, 8960], P('gx', 'gy')
- grad_w_down: float32 [8960, 1536], P('gy', 'gx')
Inputs may be any that keep to these rules, and one draw needn't show every extreme that they name: In each tree, the segment labels 0 to 12 each cover one run of slots, the runs in the order of a depth-first walk: a trunk of 1024 slots, then for each of four branches a run of 128 slots followed by its two leaves of 64 slots; -1 marks padding slots between runs; the trunk starts at slot 0 and the last leaf ends at slot 2559. Which label takes which run varies from tree to tree. The label of each segment's parent: the trunk is its own parent, each branch's parent is the trunk, each leaf's parent is a branch; consistent with segment of the same tree.
All inputs are finite; a program needn't handle non-finite values.
Results may differ from a plain program's by a relative error of at most 0.013.
Values may be sent and summed in bfloat16 or wider, within the bound.
A program may use at most 272 MiB of HBM per device.

v0:
```python
from functools import reduce
import math

import jax
import jax.numpy as jnp
from jax import lax
from jax.sharding import PartitionSpec as P

HEADS = 12
KV_HEADS = 2
HEAD = 128


EPS = 1e-06
THETA = 1000000.0
NEGATIVE = -1e30


def tree_tables(segment, parent):
    slot_len = segment.shape[0]
    seg_count = parent.shape[0]
    places = jnp.arange(slot_len, dtype=jnp.int32)
    labels = jnp.arange(seg_count, dtype=jnp.int32)
    member = segment[:, None] == labels[None, :]
    valid = segment >= 0
    first = jnp.min(jnp.where(member, places[:, None], slot_len), axis=0)
    length = jnp.sum(member.astype(jnp.int32), axis=0)
    parent_hit = parent[:, None] == labels[None, :]
    grand = jnp.sum(jnp.where(parent_hit, parent[None, :], 0), axis=1)
    grand_hit = grand[:, None] == labels[None, :]
    parent_len = jnp.sum(jnp.where(parent_hit, length[None, :], 0), axis=1)
    grand_len = jnp.sum(jnp.where(grand_hit, length[None, :], 0), axis=1)
    base = jnp.where(parent != labels, parent_len, 0) + jnp.where(grand != parent, grand_len, 0)

    def lookup(table):
        return jnp.sum(jnp.where(member, table[None, :], 0), axis=1)

    upper_one = jnp.where(valid, lookup(parent), -2)
    upper_two = jnp.where(valid, lookup(grand), -2)
    depth_pos = jnp.where(valid, places - lookup(first) + lookup(base), 0)
    return (valid, upper_one, upper_two, depth_pos)


def allowed(seg_query, upper_one, upper_two, place_query, seg_keys, valid_keys, place_keys):
    related = (seg_keys[None, :] == seg_query[:, None]) | (seg_keys[None, :] == upper_one[:, None])
    related = related | (seg_keys[None, :] == upper_two[:, None])
    earlier = place_keys[None, :] <= place_query[:, None]
    return related & earlier & valid_keys[None, :] | (place_keys[None, :] == place_query[:, None])


def rotation(depth_pos, width):
    half = width // 2
    freqs = jnp.exp(jnp.arange(half, dtype=jnp.float32) * (-2.0 * math.log(THETA) / width))
    angle = depth_pos.astype(jnp.float32)[:, None] * freqs[None, :]
    cosine = jnp.concatenate([jnp.cos(angle), jnp.cos(angle)], axis=1)
    sine = jnp.concatenate([jnp.sin(angle), jnp.sin(angle)], axis=1)
    return (cosine, sine)


def turn(heads, cosine, sine):
    half = heads.shape[-1] // 2
    swapped = jnp.concatenate([-heads[..., half:], heads[..., :half]], axis=-1)
    return heads * cosine[:, None, :] + swapped * sine[:, None, :]


def norm_parts(values, gain):
    inverse = lax.rsqrt(jnp.mean(values * values, axis=-1, keepdims=True) + EPS)
    unit = values * inverse
    return (unit, inverse, (unit * gain).astype(jnp.bfloat16))


def norm_back(grad_normed, unit, inverse, gain):
    scaled = grad_normed * gain
    back = inverse * (scaled - unit * jnp.mean(scaled * unit, axis=-1, keepdims=True))
    return (back, jnp.sum(grad_normed * unit, axis=0))


def masked_scores(group_query, group_keys, mask, scale):
    scores = (
        jnp.einsum("rhd,kd->hrk", group_query, group_keys, preferred_element_type=jnp.float32)
        * scale
    )
    return jnp.where(mask[None], scores, NEGATIVE)


def attend(query_low, keys_all, values_all, mask, scale):
    group = HEADS // KV_HEADS
    pieces = []
    totals = []
    for head_group in range(KV_HEADS):
        group_query = query_low[:, head_group * group : (head_group + 1) * group, :]
        columns = slice(head_group * HEAD, (head_group + 1) * HEAD)
        scores = masked_scores(group_query, keys_all[:, columns], mask, scale)
        top_score = jnp.max(scores, axis=-1, keepdims=True)
        expo = jnp.exp(scores - top_score)
        denom = jnp.sum(expo, axis=-1, keepdims=True)
        probs_low = (expo / denom).astype(jnp.bfloat16)
        pieces.append(
            jnp.einsum(
                "hrk,kd->rhd", probs_low, values_all[:, columns], preferred_element_type=jnp.float32
            )
        )
        totals.append(top_score + jnp.log(denom))
    return (jnp.concatenate(pieces, axis=1), totals)


def attend_back(query_low, keys_all, values_all, mask, totals, grad_heads, scale):
    group = HEADS // KV_HEADS
    grad_query, grad_keys, grad_values = ([], [], [])
    for head_group in range(KV_HEADS):
        heads_sel = slice(head_group * group, (head_group + 1) * group)
        columns = slice(head_group * HEAD, (head_group + 1) * HEAD)
        group_query = query_low[:, heads_sel, :]
        group_keys = keys_all[:, columns]
        group_grad = grad_heads[:, heads_sel, :]
        scores = masked_scores(group_query, group_keys, mask, scale)
        probs = jnp.exp(scores - totals[head_group])
        probs_low = probs.astype(jnp.bfloat16)
        grad_values.append(
            jnp.einsum("hrk,rhd->kd", probs_low, group_grad, preferred_element_type=jnp.float32)
        )
        grad_probs = jnp.einsum(
            "rhd,kd->hrk", group_grad, values_all[:, columns], preferred_element_type=jnp.float32
        )
        grad_scores = (
            probs * (grad_probs - jnp.sum(probs * grad_probs, axis=-1, keepdims=True))
        ).astype(jnp.bfloat16)
        grad_query.append(
            jnp.einsum("hrk,kd->rhd", grad_scores, group_keys, preferred_element_type=jnp.float32)
            * scale
        )
        grad_keys.append(
            jnp.einsum("hrk,rhd->kd", grad_scores, group_query, preferred_element_type=jnp.float32)
            * scale
        )
    return (
        jnp.concatenate(grad_query, axis=1),
        jnp.concatenate(grad_keys, axis=1),
        jnp.concatenate(grad_values, axis=1),
    )


def add_trees(left, right):
    return jax.tree.map(jnp.add, left, right)


def on_device(
    tokens,
    cotangent,
    segment,
    parent,
    w_qkv,
    qkv_bias,
    w_out,
    gain_attn,
    gain_ffn,
    w_gate,
    w_up,
    w_down,
):
    micro = tokens.shape[0]
    row_count = tokens.shape[1]
    slot_len = segment.shape[1]
    qwidth = HEADS * HEAD
    kwidth = KV_HEADS * HEAD
    scale = 1.0 / math.sqrt(HEAD)
    offset = lax.axis_index("gy") * row_count
    place_all = jnp.arange(slot_len, dtype=jnp.int32)
    place_own = offset + jnp.arange(row_count, dtype=jnp.int32)
    outputs, input_grads, attn_list, ffn_list = ([], [], [], [])
    for micro_index in range(micro):
        attn_full = (
            lax.all_gather(w_qkv, ("gx", "gy"), axis=0, tiled=True),
            lax.all_gather(qkv_bias, ("gx", "gy"), axis=0, tiled=True),
            lax.all_gather(w_out, ("gx", "gy"), axis=1, tiled=True),
            lax.all_gather(gain_attn, ("gx", "gy"), axis=0, tiled=True),
            lax.all_gather(gain_ffn, ("gx", "gy"), axis=0, tiled=True),
        )
        ffn_full = (
            lax.all_gather(w_gate, "gx", axis=0, tiled=True),
            lax.all_gather(w_up, "gx", axis=0, tiled=True),
            lax.all_gather(w_down, "gx", axis=1, tiled=True),
        )
        qkv_full, bias_full, out_full, gain_one_full, gain_two_full = attn_full
        gate_full, up_full, down_full = ffn_full
        gain_one = gain_one_full.astype(jnp.float32)
        gain_two = gain_two_full.astype(jnp.float32)
        seg_tree = segment[micro_index]
        valid, upper_one, upper_two, depth_pos = tree_tables(seg_tree, parent[micro_index])

        def take_own(array):
            return lax.dynamic_slice_in_dim(array, offset, row_count, 0)

        mask = allowed(
            take_own(seg_tree),
            take_own(upper_one),
            take_own(upper_two),
            place_own,
            seg_tree,
            valid,
            place_all,
        )
        cosine, sine = rotation(take_own(depth_pos), HEAD)
        inputs = tokens[micro_index].astype(jnp.float32)
        unit_one, inverse_one, normed_one = norm_parts(inputs, gain_one)
        linear = jnp.dot(
            normed_one, qkv_full, preferred_element_type=jnp.float32
        ) + bias_full.astype(jnp.float32)
        query_low = turn(linear[:, :qwidth].reshape(row_count, HEADS, HEAD), cosine, sine).astype(
            jnp.bfloat16
        )
        keys_low = turn(
            linear[:, qwidth : qwidth + kwidth].reshape(row_count, KV_HEADS, HEAD), cosine, sine
        )
        keys_low = keys_low.reshape(row_count, kwidth).astype(jnp.bfloat16)
        values_low = linear[:, qwidth + kwidth :].astype(jnp.bfloat16)
        keys_all, values_all = (
            lax.all_gather(keys_low, "gy", axis=0, tiled=True),
            lax.all_gather(values_low, "gy", axis=0, tiled=True),
        )
        heads_raw, totals = attend(query_low, keys_all, values_all, mask, scale)
        heads_out = heads_raw.reshape(row_count, qwidth).astype(jnp.bfloat16)
        resid = inputs + jnp.dot(heads_out, out_full, preferred_element_type=jnp.float32)
        unit_two, inverse_two, normed_two = norm_parts(resid, gain_two)
        normed_all = lax.all_gather(normed_two, "gy", axis=0, tiled=True)
        gate = jnp.dot(normed_all, gate_full, preferred_element_type=jnp.float32)
        upward = jnp.dot(normed_all, up_full, preferred_element_type=jnp.float32)
        sigma = jax.nn.sigmoid(gate)
        swish = gate * sigma
        hidden = (swish * upward).astype(jnp.bfloat16)
        ffn_own = lax.psum_scatter(
            jnp.dot(hidden, down_full, preferred_element_type=jnp.float32),
            "gy",
            scatter_dimension=0,
            tiled=True,
        )
        outputs.append((resid + ffn_own).astype(jnp.bfloat16))
        grad_low = cotangent[micro_index]
        grad_all = lax.all_gather(grad_low, "gy", axis=0, tiled=True)
        grad_hidden = jnp.dot(grad_all, down_full.T, preferred_element_type=jnp.float32)
        grad_down = jnp.dot(hidden.T, grad_all, preferred_element_type=jnp.float32)
        grad_gate = (grad_hidden * upward * sigma * (1.0 + gate * (1.0 - sigma))).astype(
            jnp.bfloat16
        )
        grad_up = (grad_hidden * swish).astype(jnp.bfloat16)
        grad_wgate = jnp.dot(normed_all.T, grad_gate, preferred_element_type=jnp.float32)
        grad_wup = jnp.dot(normed_all.T, grad_up, preferred_element_type=jnp.float32)
        grad_normed_two = lax.psum_scatter(
            jnp.dot(grad_gate, gate_full.T, preferred_element_type=jnp.float32)
            + jnp.dot(grad_up, up_full.T, preferred_element_type=jnp.float32),
            "gy",
            scatter_dimension=0,
            tiled=True,
        )
        back_two, grad_gain_two = norm_back(grad_normed_two, unit_two, inverse_two, gain_two)
        grad_resid = grad_low.astype(jnp.float32) + back_two
        grad_branch = grad_resid.astype(jnp.bfloat16)
        grad_wout = jnp.dot(heads_out.T, grad_branch, preferred_element_type=jnp.float32)
        grad_heads = jnp.dot(grad_branch, out_full.T, preferred_element_type=jnp.float32).astype(
            jnp.bfloat16
        )
        grad_heads = grad_heads.reshape(row_count, HEADS, HEAD)
        grad_query, keys_part, values_part = attend_back(
            query_low, keys_all, values_all, mask, totals, grad_heads, scale
        )
        grad_keys, grad_values = (
            lax.psum_scatter(keys_part, "gy", scatter_dimension=0, tiled=True),
            lax.psum_scatter(values_part, "gy", scatter_dimension=0, tiled=True),
        )
        query_lin = turn(grad_query, cosine, -sine).reshape(row_count, qwidth)
        keys_lin = turn(grad_keys.reshape(row_count, KV_HEADS, HEAD), cosine, -sine).reshape(
            row_count, kwidth
        )
        grad_linear = jnp.concatenate([query_lin, keys_lin, grad_values], axis=1).astype(
            jnp.bfloat16
        )
        grad_wqkv = jnp.dot(normed_one.T, grad_linear, preferred_element_type=jnp.float32)
        grad_bias = jnp.sum(grad_linear.astype(jnp.float32), axis=0)
        grad_normed_one = jnp.dot(grad_linear, qkv_full.T, preferred_element_type=jnp.float32)
        back_one, grad_gain_one = norm_back(grad_normed_one, unit_one, inverse_one, gain_one)
        input_grads.append((grad_resid + back_one).astype(jnp.bfloat16))
        attn_list.append((grad_wqkv, grad_bias, grad_wout, grad_gain_one, grad_gain_two))
        ffn_list.append((grad_wgate, grad_wup, grad_down))
    attn_total = reduce(add_trees, attn_list)
    ffn_total = reduce(add_trees, ffn_list)
    attn_total = (
        lax.psum_scatter(attn_total[0], ("gx", "gy"), scatter_dimension=0, tiled=True),
        lax.psum_scatter(attn_total[1], ("gx", "gy"), scatter_dimension=0, tiled=True),
        lax.psum_scatter(attn_total[2], ("gx", "gy"), scatter_dimension=1, tiled=True),
        lax.psum_scatter(attn_total[3], ("gx", "gy"), scatter_dimension=0, tiled=True),
        lax.psum_scatter(attn_total[4], ("gx", "gy"), scatter_dimension=0, tiled=True),
    )
    ffn_total = (
        lax.psum_scatter(ffn_total[0], "gx", scatter_dimension=0, tiled=True),
        lax.psum_scatter(ffn_total[1], "gx", scatter_dimension=0, tiled=True),
        lax.psum_scatter(ffn_total[2], "gx", scatter_dimension=1, tiled=True),
    )
    layer_out = jnp.stack(outputs, axis=0)
    grad_tokens = jnp.stack(input_grads, axis=0)
    return (
        layer_out,
        grad_tokens,
        attn_total[0],
        attn_total[1],
        attn_total[2],
        attn_total[3],
        attn_total[4],
        ffn_total[0],
        ffn_total[1],
        ffn_total[2],
    )


def solution(mesh):
    in_specs = (
        P("gx", "gy", None),
        P("gx", "gy", None),
        P("gx", None),
        P("gx", None),
        P(("gx", "gy"), None),
        P(("gx", "gy")),
        P(None, ("gx", "gy")),
        P(("gx", "gy")),
        P(("gx", "gy")),
        P("gx", "gy"),
        P("gx", "gy"),
        P("gy", "gx"),
    )
    out_specs = (
        P("gx", "gy", None),
        P("gx", "gy", None),
        P(("gx", "gy"), None),
        P(("gx", "gy")),
        P(None, ("gx", "gy")),
        P(("gx", "gy")),
        P(("gx", "gy")),
        P("gx", "gy"),
        P("gx", "gy"),
        P("gy", "gx"),
    )
    return jax.shard_map(
        on_device, mesh=mesh, in_specs=in_specs, out_specs=out_specs, check_vma=False
    )
```

profile of v0, /device:TPU:9, one launch (start us, length us, event | category | flops | bytes accessed | tf_op | source)
XLA Modules:
  0.0 2162.3 jit_solution(3158315480112552710)
XLA Ops:
  10.5 40.7 %all-reduce.7 = (bf16[2048]{0:T(1024)(128)(2,1)S(1)}, bf16[1536]{0:T(1024)(128)(2,1)S(1)}, bf16[1536]{0:T(1024)(128)(2,1)S(1)}) all-reduce(bf16[2048]{0:T(1024)(128)(2,1)S(1)} %dynamic-update-slice.1, bf16[1536]{0:T(1024)(128)(2,1)S(1)} %dynamic-update-slice, ...), channel_id=1, replica_groups=mesh['gx'=4,'gy'=8] {'gx','gy'}, use_global_device_ids=true, to_apply=%add.1 | all-reduce | flops 5120 | bytes 20480
  58.3 23.8 %all-gather.16.cloned.1.call-done = bf16[1536,2048]{1,0:T(8,128)(2,1)} async-done(((bf16[48,2048]{1,0:T(8,128)(2,1)}), bf16[1536,2048]{1,0:T(8,128)(2,1)}) %all-gather.16.cloned.1.call-update) | async-done | bytes 6291472 | tf_op jit(solution)/shard_map/all_gather | solution.py:173
  115.5 10.2 fusion.170
  181.5 28.0 %all-gather.22.cloned.1.call-done = bf16[1536,1536]{0,1:T(8,128)(2,1)} async-done(((bf16[1536,48]{0,1:T(8,128)(2,1)}), bf16[1536,1536]{0,1:T(8,128)(2,1)}) %all-gather.22.cloned.1.call-update) | async-done | bytes 4718608 | tf_op jit(solution)/shard_map/all_gather | solution.py:175
  234.3 41.0 %all-gather.28.cloned.1.call-done = bf16[1536,1120]{0,1:T(8,128)(2,1)} async-done(((bf16[384,1120]{0,1:T(8,128)(2,1)}), bf16[1536,1120]{0,1:T(8,128)(2,1)}) %all-gather.28.cloned.1.call-update) | async-done | bytes 3440656 | tf_op jit(solution)/shard_map/all_gather | solution.py:181
  275.3 55.5 %all-gather.24.cloned.1.call-done = bf16[2560,1536]{1,0:T(8,128)(2,1)} async-done(((bf16[320,1536]{1,0:T(8,128)(2,1)}), bf16[2560,1536]{1,0:T(8,128)(2,1)}) %all-gather.24.cloned.1.call-update) | async-done | bytes 7864336 | tf_op jit(solution)/shard_map/all_gather | solution.py:225
  330.9 15.0 fusion.175
  345.9 52.6 %all-gather.26.cloned.1.call-done = bf16[1536,1120]{0,1:T(8,128)(2,1)} async-done(((bf16[384,1120]{0,1:T(8,128)(2,1)}), bf16[1536,1120]{0,1:T(8,128)(2,1)}) %all-gather.26.cloned.1.call-update) | async-done | bytes 3440656 | tf_op jit(solution)/shard_map/all_gather | solution.py:180
  398.5 15.0 fusion.174
  413.5 53.6 %all-gather.30.cloned.1.call-done = bf16[1120,1536]{1,0:T(8,128)(2,1)} async-done(((bf16[1120,384]{1,0:T(8,128)(2,1)}), bf16[1120,1536]{1,0:T(8,128)(2,1)}) %all-gather.30.cloned.1.call-update) | async-done | bytes 3440656 | tf_op jit(solution)/shard_map/all_gather | solution.py:182
  467.1 55.7 %all-gather.38.cloned.1.call-done = bf16[1,2560,1536]{2,1,0:T(8,128)(2,1)} async-done(((bf16[1,320,1536]{2,1,0:T(8,128)(2,1)}), bf16[1,2560,1536]{2,1,0:T(8,128)(2,1)}) %all-gather.38.cloned.1.call-update) | async-done | bytes 7864336 | tf_op jit(solution)/shard_map/all_gather | solution.py:239
  522.8 24.4 %multiply_convert_fusion.2 = (bf16[2560,1120]{0,1:T(8,128)(2,1)}, bf16[2560,1120]{0,1:T(8,128)(2,1)}, bf16[2560,1120]{0,1:T(8,128)(2,1)}) fusion(f32[2560,1120]{0,1:T(8,128)} %fusion.174, f32[2560,1120]{0,1:T(8,128)} %fusion.175, bf16[1120,1536]{1,0:T(8,128)(2,1)} %all-gather.30.cloned.1.call-done, bf16[1,2560,1536]{2,1,0:T(8,128)(2,1)} %all-gather.38.cloned.1.call-done), kind=kOutput, calls=%fused_computation.48 | convolution fusion | flops 8851046400 | bytes 51445760 | tf_op jit(solution)/shard_map/dot_general | solution.py:240
  547.2 17.1 fusion.180
  564.2 16.6 convolution_add_fusion.1
  588.4 14.7 fusion.172
  611.8 10.6 fusion.15
  659.1 30.6 %reduce-scatter.22.cloned.1.call-done = f32[320,1536]{1,0:T(8,128)} async-done(((f32[2560,1536]{1,0:T(8,128)}), f32[320,1536]{1,0:T(8,128)}) %reduce-scatter.22.cloned.1.call-update) | async-done | bytes 1966096 | tf_op jit(solution)/shard_map/reduce_scatter | solution.py:248
  695.3 52.1 %all-gather.36.cloned.1.call-done = bf16[2560,1536]{1,0:T(8,128)(2,1)} async-done(((bf16[320,1536]{1,0:T(8,128)(2,1)}), bf16[2560,1536]{1,0:T(8,128)(2,1)}) %all-gather.36.cloned.1.call-update) | async-done | bytes 7864336 | tf_op jit(solution)/shard_map/all_gather | solution.py:225
  747.4 15.4 fusion.178
  762.8 13.5 fusion.177
  776.3 25.7 %all-gather.40.cloned.1.call-done = bf16[1,2560,1536]{2,1,0:T(8,128)(2,1)} async-done(((bf16[1,320,1536]{2,1,0:T(8,128)(2,1)}), bf16[1,2560,1536]{2,1,0:T(8,128)(2,1)}) %all-gather.40.cloned.1.call-update) | async-done | bytes 7864336 | tf_op jit(solution)/shard_map/all_gather | solution.py:239
  802.0 21.9 %multiply_convert_fusion = (bf16[2560,1120]{0,1:T(8,128)(2,1)}, bf16[2560,1120]{0,1:T(8,128)(2,1)}, bf16[2560,1120]{0,1:T(8,128)(2,1)}) fusion(f32[2560,1120]{0,1:T(8,128)} %fusion.177, f32[2560,1120]{0,1:T(8,128)} %fusion.178, bf16[1120,1536]{1,0:T(8,128)(2,1)S(1)} %copy-done.87, bf16[1,2560,1536]{2,1,0:T(8,128)(2,1)} %all-gather.40.cloned.1.call-done), kind=kOutput, calls=%fused_computation.46 | convolution fusion | flops 8851046400 | bytes 51445760 | tf_op jit(solution)/shard_map/dot_general | solution.py:240
  823.9 17.0 fusion.181
  840.9 16.5 convolution_add_fusion
  857.5 17.6 fusion.176
  875.1 17.0 fusion.179
  893.0 73.4 %reduce-scatter.26.cloned.1.call-done = f32[320,1536]{1,0:T(8,128)} async-done(((f32[2560,1536]{1,0:T(8,128)}), f32[320,1536]{1,0:T(8,128)}) %reduce-scatter.26.cloned.1.call-update) | async-done | bytes 1966096 | tf_op jit(solution)/shard_map/reduce_scatter | solution.py:248
  969.1 109.9 %reduce-scatter.18.cloned.1.call-done = f32[320,1536]{1,0:T(8,128)} async-done(((f32[2560,1536]{1,0:T(8,128)}), f32[320,1536]{1,0:T(8,128)}) %reduce-scatter.18.cloned.1.call-update) | async-done | bytes 1966096 | tf_op jit(solution)/shard_map/reduce_scatter | solution.py:231
  1078.9 112.6 %reduce-scatter.20.cloned.1.call-done = f32[320,1536]{1,0:T(8,128)} async-done(((f32[2560,1536]{1,0:T(8,128)}), f32[320,1536]{1,0:T(8,128)}) %reduce-scatter.20.cloned.1.call-update) | async-done | bytes 1966096 | tf_op jit(solution)/shard_map/reduce_scatter | solution.py:231
  1213.2 12.6 fusion.9
  1225.8 13.5 fusion.11
  1245.7 12.5 fusion.6
  1258.3 13.4 fusion.8
  1277.1 13.5 fusion.3
  1290.7 13.8 fusion.5
  1304.5 16.3 fusion
  1324.6 13.5 fusion.2
  1386.2 13.3 fusion.182
  1399.6 15.6 convolution_add_fusion.4
  1415.3 13.4 fusion.183
  1428.7 15.2 convolution_add_fusion.3
  1444.0 14.0 fusion.41
  1458.0 15.5 convolution_add_fusion.5
  1553.5 46.0 %all-reduce.6 = (f32[2048]{0:T(1024)S(1)}, f32[1536]{0:T(1024)S(1)}, f32[1536]{0:T(1024)S(1)}) all-reduce(f32[2048]{0:T(1024)} %add.289, f32[1536]{0:T(1024)S(1)} %add.291, f32[1536]{0:T(1024)} %add.292), channel_id=13, replica_groups=mesh['gx'=4,'gy'=8] {'gx','gy'}, use_global_device_ids=true, to_apply=%region_49.50.clone | all-reduce | flops 5120 | bytes 40960
  1608.5 120.9 %reduce-scatter.36.cloned.1.call-done = f32[384,1120]{0,1:T(8,128)} async-done(((f32[1536,1120]{0,1:T(8,128)}), f32[384,1120]{0,1:T(8,128)}) %reduce-scatter.36.cloned.1.call-update) | async-done | bytes 1720336 | tf_op jit(solution)/shard_map/reduce_scatter | solution.py:295
  1729.4 123.6 %reduce-scatter.38.cloned.1.call-done = f32[1120,384]{1,0:T(8,128)} async-done(((f32[1120,1536]{1,0:T(8,128)}), f32[1120,384]{1,0:T(8,128)}) %reduce-scatter.38.cloned.1.call-update) | async-done | bytes 1720336 | tf_op jit(solution)/shard_map/reduce_scatter | solution.py:296
  1853.0 141.5 %reduce-scatter.32.cloned.1.call-done = f32[1536,48]{0,1:T(8,128)} async-done(((f32[1536,1536]{0,1:T(8,128)}), f32[1536,48]{0,1:T(8,128)}) %reduce-scatter.32.cloned.1.call-update) | async-done | bytes 294928 | tf_op jit(solution)/shard_map/reduce_scatter | solution.py:289
  1994.5 161.0 %reduce-scatter.30.cloned.1.call-done = f32[48,2048]{1,0:T(8,128)} async-done(((f32[1536,2048]{1,0:T(8,128)}), f32[48,2048]{1,0:T(8,128)}) %reduce-scatter.30.cloned.1.call-update) | async-done | bytes 393232 | tf_op jit(solution)/shard_map/reduce_scatter | solution.py:287
  (394 shorter events, 359.7 us)
Async XLA Ops:
  7.2 50.7 %copy-start.4 = (bf16[2,320,1536]{2,1,0:T(8,128)(2,1)S(1)}, bf16[2,320,1536]{2,1,0:T(8,128)(2,1)}, u32[]{:S(2)}) copy-start(bf16[2,320,1536]{2,1,0:T(8,128)(2,1)} %param.12) | copy-start | bytes 5898244
  7.2 74.9 %all-gather.16.cloned.1.call-start = ((), (), s32[]{:S(2)}) async-start(), calls=%async_computation.13 | async-start | bytes 6488064 | tf_op jit(solution)/shard_map/all_gather | solution.py:173
  7.9 107.6 %all-gather.20.cloned.1.call-start = ((), (), s32[]{:S(2)}) async-start(), calls=%async_computation.15 | async-start | bytes 1474560 | tf_op jit(solution)/shard_map/all_gather | solution.py:218
  51.2 170.8 %copy-start.52 = (f32[1536]{0:T(1024)}, f32[1536]{0:T(1024)S(1)}, u32[]{:S(2)}) copy-start(f32[1536]{0:T(1024)S(1)} %convert_element_type.164) | copy-start | bytes 18436
  57.1 50.3 %copy-start.24 = (f32[320,128]{1,0:T(8,128)}, f32[320,128]{1,0:T(8,128)S(1)}, u32[]{:S(2)}) copy-start(f32[320,128]{1,0:T(8,128)S(1)} %pad_maximum_fusion.12) | copy-start | bytes 491524
  58.3 28.8 %copy-start.58 = (f32[320]{0:T(512)}, f32[320]{0:T(512)S(1)}, u32[]{:S(2)}) copy-start(f32[320]{0:T(512)S(1)} %add_rsqrt_fusion.3) | copy-start | bytes 3844
  92.3 50.4 %all-gather.18.cloned.1.call-start = ((), (), s32[]{:S(2)}) async-start(), calls=%async_computation.14 | async-start | bytes 1474560 | tf_op jit(solution)/shard_map/all_gather | solution.py:219
  94.0 115.5 %all-gather.22.cloned.1.call-start = ((), (), s32[]{:S(2)}) async-start(), calls=%async_computation.16 | async-start | bytes 4866048 | tf_op jit(solution)/shard_map/all_gather | solution.py:175
  94.6 180.7 %all-gather.28.cloned.1.call-start = ((), (), s32[]{:S(2)}) async-start(), calls=%async_computation.19 | async-start | bytes 4300800 | tf_op jit(solution)/shard_map/all_gather | solution.py:181
  95.2 235.7 %all-gather.24.cloned.1.call-start = ((), (), s32[]{:S(2)}) async-start(), calls=%async_computation.17 | async-start | bytes 8847360 | tf_op jit(solution)/shard_map/all_gather | solution.py:225
  95.5 118.5 %copy-start.54 = (f32[1536]{0:T(1024)}, f32[1536]{0:T(1024)S(1)}, u32[]{:S(2)}) copy-start(f32[1536]{0:T(1024)S(1)} %convert_element_type.174) | copy-start | bytes 18436
  108.0 43.8 %copy-start.44 = (bf16[320,12,128]{2,0,1:T(8,128)(2,1)}, bf16[320,12,128]{2,0,1:T(8,128)(2,1)S(1)}, u32[]{:S(2)}) copy-start(bf16[320,12,128]{2,0,1:T(8,128)(2,1)S(1)} %fusion.104) | copy-start | bytes 2949124
  178.7 30.8 %copy-start.5 = (bf16[2,320,1536]{2,1,0:T(8,128)(2,1)S(1)}, bf16[2,320,1536]{2,1,0:T(8,128)(2,1)}, u32[]{:S(2)}) copy-start(bf16[2,320,1536]{2,1,0:T(8,128)(2,1)} %param.12) | copy-start | bytes 5898244
  181.5 32.5 %copy-start.18 = (bf16[320,12,128]{0,2,1:T(8,128)(2,1)}, bf16[320,12,128]{0,2,1:T(8,128)(2,1)S(1)}, u32[]{:S(2)}) copy-start(bf16[320,12,128]{0,2,1:T(8,128)(2,1)S(1)} %copy.90) | copy-start | bytes 2949124
  216.5 182.0 %all-gather.26.cloned.1.call-start = ((), (), s32[]{:S(2)}) async-start(), calls=%async_computation.18 | async-start | bytes 4300800 | tf_op jit(solution)/shard_map/all_gather | solution.py:180
  217.2 249.8 %all-gather.30.cloned.1.call-start = ((), (), s32[]{:S(2)}) async-start(), calls=%async_computation.20 | async-start | bytes 4300800 | tf_op jit(solution)/shard_map/all_gather | solution.py:182
  218.0 304.8 %all-gather.38.cloned.1.call-start = ((), (), s32[]{:S(2)}) async-start(), calls=%async_computation.35 | async-start | bytes 8847360 | tf_op jit(solution)/shard_map/all_gather | solution.py:239
  221.1 367.3 %all-gather.34.cloned.1.call-start = ((), (), s32[]{:S(2)}) async-start(), calls=%async_computation.23 | async-start | bytes 1474560 | tf_op jit(solution)/shard_map/all_gather | solution.py:218
  221.3 366.5 %copy-start.26 = (f32[320,128]{1,0:T(8,128)}, f32[320,128]{1,0:T(8,128)S(1)}, u32[]{:S(2)}) copy-start(f32[320,128]{1,0:T(8,128)S(1)} %pad_maximum_fusion.14) | copy-start | bytes 491524
  232.4 399.9 %all-gather.32.cloned.1.call-start = ((), (), s32[]{:S(2)}) async-start(), calls=%async_computation.22 | async-start | bytes 1474560 | tf_op jit(solution)/shard_map/all_gather | solution.py:219
  234.1 455.7 %reduce-scatter.22.cloned.1.call-start = ((), (), s32[]{:S(2)}) async-start(), calls=%async_computation.26 | async-start | bytes 17694720 | tf_op jit(solution)/shard_map/reduce_scatter | solution.py:248
  547.2 17.1 copy-start.85
  547.2 17.1 copy-start.88
  580.8 166.6 %all-gather.36.cloned.1.call-start = ((), (), s32[]{:S(2)}) async-start(), calls=%async_computation.24 | async-start | bytes 8847360 | tf_op jit(solution)/shard_map/all_gather | solution.py:225
  603.1 29.1 %copy-start.68 = (f32[6,320]{1,0:T(8,128)}, f32[6,320]{1,0:T(8,128)S(1)}, u32[]{:S(2)}) copy-start(f32[6,320]{1,0:T(8,128)S(1)} %get-tuple-element.109) | copy-start | bytes 23044
  611.8 30.0 %copy-start.70 = (f32[6,320]{1,0:T(8,128)}, f32[6,320]{1,0:T(8,128)S(1)}, u32[]{:S(2)}) copy-start(f32[6,320]{1,0:T(8,128)S(1)} %get-tuple-element.111) | copy-start | bytes 23044
  653.0 36.8 %copy-start.55 = (f32[1536]{0:T(1024)S(1)}, f32[1536]{0:T(1024)}, u32[]{:S(2)}) copy-start(f32[1536]{0:T(1024)} %copy-done.54) | copy-start | bytes 18436
  653.0 36.8 %copy-start.79 = (f32[320]{0:T(512)S(1)}, f32[320]{0:T(512)}, u32[]{:S(2)}) copy-start(f32[320]{0:T(512)} %copy-done.78) | copy-start | bytes 3844
  659.1 35.5 %copy-start.81 = (f32[320]{0:T(512)}, f32[320]{0:T(512)S(1)}, u32[]{:S(2)}) copy-start(f32[320]{0:T(512)S(1)} %add_rsqrt_fusion) | copy-start | bytes 3844
  694.7 107.3 %all-gather.40.cloned.1.call-start = ((), (), s32[]{:S(2)}) async-start(), calls=%async_computation.36 | async-start | bytes 8847360 | tf_op jit(solution)/shard_map/all_gather | solution.py:239
  695.3 271.1 %reduce-scatter.26.cloned.1.call-start = ((), (), s32[]{:S(2)}) async-start(), calls=%async_computation.28 | async-start | bytes 17694720 | tf_op jit(solution)/shard_map/reduce_scatter | solution.py:248
  762.8 39.2 %copy-start.87 = (bf16[1120,1536]{1,0:T(8,128)(2,1)S(1)}, bf16[1120,1536]{1,0:T(8,128)(2,1)}, u32[]{:S(2)}) copy-start(bf16[1120,1536]{1,0:T(8,128)(2,1)} %all-gather.30.cloned.1.call-done) | copy-start | bytes 10321924
  857.4 221.5 %reduce-scatter.18.cloned.1.call-start = ((), (), s32[]{:S(2)}) async-start(), calls=%async_computation.21 | async-start | bytes 17694720 | tf_op jit(solution)/shard_map/reduce_scatter | solution.py:231
  875.1 316.4 %reduce-scatter.20.cloned.1.call-start = ((), (), s32[]{:S(2)}) async-start(), calls=%async_computation.25 | async-start | bytes 17694720 | tf_op jit(solution)/shard_map/reduce_scatter | solution.py:231
  892.2 74.2 %copy-start.13 = (f32[320,1536]{1,0:T(8,128)S(1)}, f32[320,1536]{1,0:T(8,128)}, u32[]{:S(2)}) copy-start(f32[320,1536]{1,0:T(8,128)} %get-tuple-element.114) | copy-start | bytes 5898244
  892.2 74.2 %copy-start.56 = (f32[1536]{0:T(1024)S(1)}, f32[1536]{0:T(1024)}, u32[]{:S(2)}) copy-start(f32[1536]{0:T(1024)} %copy-done.54) | copy-start | bytes 18436
  892.2 74.2 %copy-start.82 = (f32[320]{0:T(512)S(1)}, f32[320]{0:T(512)}, u32[]{:S(2)}) copy-start(f32[320]{0:T(512)} %copy-done.81) | copy-start | bytes 3844
  892.2 299.2 %copy-start.80 = (f32[320]{0:T(512)S(1)}, f32[320]{0:T(512)}, u32[]{:S(2)}) copy-start(f32[320]{0:T(512)} %copy-done.78) | copy-start | bytes 3844
  892.3 621.9 %reduce-scatter.24.cloned.1.call-start = ((), (), s32[]{:S(2)}) async-start(), calls=%async_computation.27 | async-start | bytes 2949120 | tf_op jit(solution)/shard_map/reduce_scatter | solution.py:267
  1225.8 17.1 copy-start.45
  1277.1 240.1 %reduce-scatter.28.cloned.1.call-start = ((), (), s32[]{:S(2)}) async-start(), calls=%async_computation.29 | async-start | bytes 2949120 | tf_op jit(solution)/shard_map/reduce_scatter | solution.py:267
  1343.5 178.6 %reduce-scatter.40.cloned.1.call-start = ((), (), s32[]{:S(2)}) async-start(), calls=%async_computation.37 | async-start | bytes 2949120
  1366.6 156.6 %reduce-scatter.42.cloned.1.call-start = ((), (), s32[]{:S(2)}) async-start(), calls=%async_computation.38 | async-start | bytes 2949120
  1386.2 222.3 %reduce-scatter.34.cloned.1.call-start = ((), (), s32[]{:S(2)}) async-start(), calls=%async_computation.32 | async-start | bytes 8601600 | tf_op jit(solution)/shard_map/reduce_scatter | solution.py:294
  1415.2 314.2 %reduce-scatter.36.cloned.1.call-start = ((), (), s32[]{:S(2)}) async-start(), calls=%async_computation.33 | async-start | bytes 8601600 | tf_op jit(solution)/shard_map/reduce_scatter | solution.py:295
  1444.0 409.0 %reduce-scatter.38.cloned.1.call-start = ((), (), s32[]{:S(2)}) async-start(), calls=%async_computation.34 | async-start | bytes 8601600 | tf_op jit(solution)/shard_map/reduce_scatter | solution.py:296
  1473.5 521.0 %reduce-scatter.32.cloned.1.call-start = ((), (), s32[]{:S(2)}) async-start(), calls=%async_computation.31 | async-start | bytes 9732096 | tf_op jit(solution)/shard_map/reduce_scatter | solution.py:289
  1484.6 670.9 %reduce-scatter.30.cloned.1.call-start = ((), (), s32[]{:S(2)}) async-start(), calls=%async_computation.30 | async-start | bytes 12976128 | tf_op jit(solution)/shard_map/reduce_scatter | solution.py:287
  (70 other events, 434.0 us)
Sparse Core Ops, SparseCore 0:
  10.9 71.1 all-gather.15
  92.4 23.0 all-gather.19
  118.0 24.5 all-gather.17
  145.4 64.0 all-gather.21
  210.9 64.3 all-gather.27
  277.6 53.1 all-gather.23
  332.5 65.9 all-gather.25
  400.1 66.9 all-gather.29
  469.5 53.1 all-gather.37
  525.1 24.6 all-gather.33
  551.6 24.5 all-gather.31
  581.0 108.7 reduce-scatter.21
  694.8 52.5 all-gather.35
  749.8 52.1 all-gather.39
  857.6 108.7 reduce-scatter.25
  969.7 109.1 reduce-scatter.17
  1082.3 109.1 reduce-scatter.19
  1277.2 43.6 reduce-scatter.23
  1343.6 43.7 reduce-scatter.27
  1390.6 43.6 reduce-scatter.39
  1437.6 43.6 reduce-scatter.41
  1484.1 121.4 reduce-scatter.33
  1608.6 120.7 reduce-scatter.35
  1732.2 120.8 reduce-scatter.37
  1860.5 134.0 reduce-scatter.31
  2001.0 154.4 reduce-scatter.29
where the time goes:
time: 2170 us; the launch traced here: 2160 us
  waiting for transfers between devices  1280 us (59%)
  matrix products  560 us (26%)
  other arithmetic  155 us (7%)
  blocking collectives  86.7 us (4%)
  local copies, waits for them, and re-layouts  62.6 us (3%)
    reduce_scatter x2, waiting for transfers between devices, on_device(): lax.psum_scatter(jnp.dot(hidden, down_full, preferred_element_type=jnp.fl...  222 us
    reduce_scatter x1, waiting for transfers between devices, on_device(): lax.psum_scatter(attn_total[0], ('gx', 'gy'), scatter_dimension=0, tiled=...  161 us
    reduce_scatter x1, waiting for transfers between devices, on_device(): lax.psum_scatter(attn_total[2], ('gx', 'gy'), scatter_dimension=1, tiled=...  142 us
    reduce_scatter x1, waiting for transfers between devices, on_device(): lax.psum_scatter(ffn_total[2], 'gx', scatter_dimension=1, tiled=True)  124 us
    reduce_scatter x1, waiting for transfers between devices, on_device(): lax.psum_scatter(ffn_total[1], 'gx', scatter_dimension=0, tiled=True)  121 us
    all_gather x2, waiting for transfers between devices, on_device(): normed_all = lax.all_gather(normed_two, 'gy', axis=0, tiled=True)  108 us
    reduce_scatter x2, waiting for transfers between devices, on_device(): lax.psum_scatter(jnp.dot(grad_gate, gate_full.T, preferred_element_type=j...  104 us
    unnamed x2, blocking collectives  86.7 us
  transfers between devices with their start and end apart: 26, of which 19 were waited for; matrix products, arithmetic and copies ran while one was open for 28% of the time, Pallas kernels for 0%

commit v1 on v0

--- a/solution.py
+++ b/solution.py
@@ -4,11 +4,21 @@
 import jax
 import jax.numpy as jnp
 from jax import lax
+from jax.experimental import pallas as pl
+from jax.experimental.pallas import tpu as pltpu
 from jax.sharding import PartitionSpec as P
 
 HEADS = 12
 KV_HEADS = 2
 HEAD = 128
+
+QUERY_TILE = 128
+KEY_TILE = 256
+ROW_TILE = 128
+FFN_CHUNK = 768
+FFN_PARTS = 2
+WG_TILE = 384
+LOG2E = 1.0 / math.log(2.0)
 
 
 EPS = 1e-06
@@ -311,6 +321,588 @@
     )
 
 
+def dot_nn(left, right):
+    return lax.dot_general(left, right, (((1,), (0,)), ((), ())), preferred_element_type=jnp.float32)
+
+
+def dot_nt(left, right):
+    return lax.dot_general(left, right, (((1,), (1,)), ((), ())), preferred_element_type=jnp.float32)
+
+
+def dot_tn(left, right):
+    return lax.dot_general(left, right, (((0,), (0,)), ((), ())), preferred_element_type=jnp.float32)
+
+
+def cost(flops, moved, trans=0):
+    return pl.CostEstimate(flops=int(flops), bytes_accessed=int(moved), transcendentals=int(trans))
+
+
+def params(mib):
+    return pltpu.CompilerParams(vmem_limit_bytes=mib * 1024 * 1024)
+
+
+def sigmoid(v):
+    return 0.5 * jnp.tanh(0.5 * v) + 0.5
+
+
+def ffn_body(n_ref, c_ref, wg_ref, wu_ref, wd_ref, hid_ref, dg_ref, du_ref, f_ref, dn_ref, f_acc, dn_acc):
+    step = pl.program_id(0)
+
+    @pl.when(step == 0)
+    def _():
+        f_acc[...] = jnp.zeros_like(f_acc)
+        dn_acc[...] = jnp.zeros_like(dn_acc)
+
+    rows = n_ref.shape[0]
+    part = rows // FFN_PARTS
+    for index in range(FFN_PARTS):
+        take = pl.ds(index * part, part)
+        gate = dot_nn(n_ref[take, :], wg_ref[...])
+        upward = dot_nn(n_ref[take, :], wu_ref[...])
+        sigma = sigmoid(gate)
+        swish = gate * sigma
+        hidden = (swish * upward).astype(jnp.bfloat16)
+        hid_ref[take, :] = hidden
+        grad_hidden = dot_nt(c_ref[take, :], wd_ref[...])
+        grad_gate = (grad_hidden * upward * sigma * (1.0 + gate * (1.0 - sigma))).astype(jnp.bfloat16)
+        grad_up = (grad_hidden * swish).astype(jnp.bfloat16)
+        dg_ref[take, :] = grad_gate
+        du_ref[take, :] = grad_up
+        f_acc[take, :] += dot_nn(hidden, wd_ref[...])
+        dn_acc[take, :] += dot_nt(grad_gate, wg_ref[...]) + dot_nt(grad_up, wu_ref[...])
+
+    @pl.when(step == pl.num_programs(0) - 1)
+    def _():
+        f_ref[...] = f_acc[...].astype(f_ref.dtype)
+        dn_ref[...] = dn_acc[...].astype(dn_ref.dtype)
+
+
+def ffn_block(normed, cotan, w_gate, w_up, w_down):
+    rows, width = normed.shape
+    units = w_gate.shape[1]
+    chunk = FFN_CHUNK
+    steps = units // chunk
+    whole = pl.BlockSpec((rows, width), lambda j: (0, 0))
+    tall = pl.BlockSpec((rows, chunk), lambda j: (0, j))
+    low = jnp.bfloat16
+    return pl.pallas_call(
+        ffn_body,
+        grid=(steps,),
+        in_specs=[
+            whole,
+            whole,
+            pl.BlockSpec((width, chunk), lambda j: (0, j)),
+            pl.BlockSpec((width, chunk), lambda j: (0, j)),
+            pl.BlockSpec((chunk, width), lambda j: (j, 0)),
+        ],
+        out_specs=[tall, tall, tall, whole, whole],
+        out_shape=[jax.ShapeDtypeStruct((rows, units), low)] * 3
+        + [jax.ShapeDtypeStruct((rows, width), low)] * 2,
+        scratch_shapes=[pltpu.VMEM((rows, width), jnp.float32)] * 2,
+        compiler_params=params(60),
+        cost_estimate=cost(12 * rows * width * units, 6 * width * units + 6 * rows * (width + units)),
+        name="ffn_block",
+    )(normed, cotan, w_gate, w_up, w_down)
+
+
+def wgrad_body(*refs):
+    count = (len(refs) - 1) // 2
+    out_ref = refs[-1]
+    slots, wide = out_ref.shape[1], out_ref.shape[3]
+    total = dot_tn(refs[0][...], refs[count][...])
+    for index in range(1, count):
+        total = total + dot_tn(refs[index][...], refs[count + index][...])
+    for slot in range(slots):
+        out_ref[0, slot] = total[:, slot * wide : (slot + 1) * wide].astype(out_ref.dtype)
+
+
+def wgrad(lefts, rights, slots):
+    rows, units = lefts[0].shape
+    width = rights[0].shape[1]
+    tile = WG_TILE
+    per_half = units // 2 // tile
+    wide = width // slots
+    count = len(lefts)
+    return pl.pallas_call(
+        wgrad_body,
+        grid=(units // tile,),
+        in_specs=[pl.BlockSpec((rows, tile), lambda j: (0, j))] * count
+        + [pl.BlockSpec((rows, width), lambda j: (0, 0))] * count,
+        out_specs=pl.BlockSpec((1, slots, tile, wide), lambda j: (j // per_half, 0, j % per_half, 0)),
+        out_shape=jax.ShapeDtypeStruct((2, slots, units // 2, wide), jnp.bfloat16),
+        compiler_params=params(60),
+        cost_estimate=cost(2 * count * rows * width * units, 2 * count * rows * (width + units)),
+        name="ffn_wgrad",
+    )(*lefts, *rights)
+
+
+def group_rows(source_ref, group, per_group):
+    return jnp.concatenate(
+        [source_ref[:, (group * per_group + h) * HEAD : (group * per_group + h + 1) * HEAD] for h in range(per_group)],
+        axis=0,
+    )
+
+
+def attend_body(list_ref, count_ref, q_ref, kv_ref, bias_ref, o_ref, lse_ref, qs, acc, top, den):
+    block = pl.program_id(0)
+    per_group = HEADS // KV_HEADS
+    for group in range(KV_HEADS):
+        qs[group] = group_rows(q_ref, group, per_group)
+    acc[...] = jnp.zeros_like(acc)
+    den[...] = jnp.zeros_like(den)
+    top[...] = jnp.full_like(top, 2 * NEGATIVE)
+    factor = LOG2E / math.sqrt(HEAD)
+
+    def body(n, carry):
+        rows = pl.ds(pl.multiple_of(list_ref[block, n] * KEY_TILE, KEY_TILE), KEY_TILE)
+        bias = jnp.concatenate([bias_ref[rows, :].astype(jnp.float32)] * per_group, axis=1)
+        for group in range(KV_HEADS):
+            keys = kv_ref[rows, group * HEAD : (group + 1) * HEAD]
+            values = kv_ref[rows, (KV_HEADS + group) * HEAD : (KV_HEADS + group + 1) * HEAD]
+            scores = dot_nt(keys, qs[group]) * factor + bias
+            old = top[group]
+            new = jnp.maximum(old, jnp.max(scores, axis=0, keepdims=True))
+            probs = jnp.exp2(scores - new)
+            shrink = jnp.exp2(old - new)
+            den[group] = den[group] * shrink + jnp.sum(probs, axis=0, keepdims=True)
+            acc[group] = acc[group] * shrink + dot_tn(values, probs.astype(jnp.bfloat16))
+            top[group] = new
+        return carry
+
+    lax.fori_loop(0, count_ref[block], body, 0)
+    for group in range(KV_HEADS):
+        out = acc[group] / den[group]
+        lse_ref[0, group] = top[group] + jnp.log(den[group]) * LOG2E
+        for h in range(per_group):
+            head = group * per_group + h
+            o_ref[:, head * HEAD : (head + 1) * HEAD] = out[:, h * HEAD : (h + 1) * HEAD].T.astype(o_ref.dtype)
+
+
+def attend_fast(block_list, block_count, query, keyval, bias):
+    rows, qwidth = query.shape
+    slots = keyval.shape[0]
+    blocks = rows // QUERY_TILE
+    per_group = HEADS // KV_HEADS
+    lanes = per_group * QUERY_TILE
+    whole = pl.BlockSpec(keyval.shape, lambda i, a, b: (0, 0))
+    tile = pl.BlockSpec((QUERY_TILE, qwidth), lambda i, a, b: (i, 0))
+    return pl.pallas_call(
+        attend_body,
+        grid_spec=pltpu.PrefetchScalarGridSpec(
+            num_scalar_prefetch=2,
+            grid=(blocks,),
+            in_specs=[tile, whole, pl.BlockSpec((slots, QUERY_TILE), lambda i, a, b: (0, i))],
+            out_specs=[tile, pl.BlockSpec((1, KV_HEADS, 1, lanes), lambda i, a, b: (i, 0, 0, 0))],
+            scratch_shapes=[
+                pltpu.VMEM((KV_HEADS, lanes, HEAD), jnp.bfloat16),
+                pltpu.VMEM((KV_HEADS, HEAD, lanes), jnp.float32),
+                pltpu.VMEM((KV_HEADS, 1, lanes), jnp.float32),
+                pltpu.VMEM((KV_HEADS, 1, lanes), jnp.float32),
+            ],
+        ),
+        out_shape=[
+            jax.ShapeDtypeStruct((rows, qwidth), jnp.bfloat16),
+            jax.ShapeDtypeStruct((blocks, KV_HEADS, 1, lanes), jnp.float32),
+        ],
+        compiler_params=params(48),
+        cost_estimate=cost(2 * rows * slots * qwidth * 2, 4 * slots * rows, HEADS * rows * slots // 2),
+        name="tree_attention",
+    )(block_list, block_count, query, keyval, bias)
+
+
+def attend_back_body(
+    list_ref, count_ref, q_ref, kv_ref, bias_ref, lse_ref, o_ref, do_ref, cos_ref, sin_ref,
+    dq_ref, dkv_ref, qs, dos, delta, dqt, dkv,
+):
+    block = pl.program_id(0)
+    per_group = HEADS // KV_HEADS
+    scale = 1.0 / math.sqrt(HEAD)
+    factor = LOG2E * scale
+    lanes = qs.shape[1]
+
+    @pl.when(block == 0)
+    def _():
+        dkv[...] = jnp.zeros_like(dkv)
+
+    for group in range(KV_HEADS):
+        qs[group] = group_rows(q_ref, group, per_group)
+        grads = group_rows(do_ref, group, per_group)
+        dos[group] = grads
+        both = grads.astype(jnp.float32) * group_rows(o_ref, group, per_group).astype(jnp.float32)
+        delta[group] = lax.dot_general(
+            jnp.ones((8, HEAD), jnp.float32), both, (((1,), (1,)), ((), ())),
+            precision=lax.Precision.HIGHEST, preferred_element_type=jnp.float32,
+        )[0:1]
+    dqt[...] = jnp.zeros_like(dqt)
+
+    def body(n, carry):
+        rows = pl.ds(pl.multiple_of(list_ref[block, n] * KEY_TILE, KEY_TILE), KEY_TILE)
+        bias = jnp.concatenate([bias_ref[rows, :].astype(jnp.float32)] * per_group, axis=1)
+        for group in range(KV_HEADS):
+            kcols = slice(group * HEAD, (group + 1) * HEAD)
+            vcols = slice((KV_HEADS + group) * HEAD, (KV_HEADS + group + 1) * HEAD)
+            keys = kv_ref[rows, kcols]
+            values = kv_ref[rows, vcols]
+            scores = dot_nt(keys, qs[group]) * factor + bias
+            probs = jnp.exp2(scores - lse_ref[0, group])
+            grad_probs = dot_nt(values, dos[group])
+            grad_scores = (probs * (grad_probs - delta[group])).astype(jnp.bfloat16)
+            dkv[rows, vcols] += dot_nn(probs.astype(jnp.bfloat16), dos[group])
+            dkv[rows, kcols] += dot_nn(grad_scores, qs[group])
+            dqt[group] += dot_tn(keys, grad_scores)
+        return carry
+
+    lax.fori_loop(0, count_ref[block], body, 0)
+    cosine, sine = cos_ref[...], sin_ref[...]
+    for group in range(KV_HEADS):
+        for h in range(per_group):
+            head = group * per_group + h
+            grad = dqt[group, :, h * HEAD : (h + 1) * HEAD].T * scale
+            grad = grad * cosine - pltpu.roll(grad, HEAD // 2, 1) * sine
+            dq_ref[:, head * HEAD : (head + 1) * HEAD] = grad.astype(dq_ref.dtype)
+
+    @pl.when(block == pl.num_programs(0) - 1)
+    def _():
+        kwidth = KV_HEADS * HEAD
+        dkv_ref[:, :kwidth] = (dkv[:, :kwidth] * scale).astype(dkv_ref.dtype)
+        dkv_ref[:, kwidth:] = dkv[:, kwidth:].astype(dkv_ref.dtype)
+
+
+def attend_back_fast(block_list, block_count, query, keyval, bias, lse, heads_out, grad_heads, cosine, sine):
+    rows, qwidth = query.shape
+    slots = keyval.shape[0]
+    blocks = rows // QUERY_TILE
+    per_group = HEADS // KV_HEADS
+    lanes = per_group * QUERY_TILE
+    whole = pl.BlockSpec(keyval.shape, lambda i, a, b: (0, 0))
+    tile = pl.BlockSpec((QUERY_TILE, qwidth), lambda i, a, b: (i, 0))
+    turned = pl.BlockSpec((QUERY_TILE, HEAD), lambda i, a, b: (i, 0))
+    return pl.pallas_call(
+        attend_back_body,
+        grid_spec=pltpu.PrefetchScalarGridSpec(
+            num_scalar_prefetch=2,
+            grid=(blocks,),
+            in_specs=[
+                tile,
+                whole,
+                pl.BlockSpec((slots, QUERY_TILE), lambda i, a, b: (0, i)),
+                pl.BlockSpec((1, KV_HEADS, 1, lanes), lambda i, a, b: (i, 0, 0, 0)),
+                tile,
+                tile,
+                turned,
+                turned,
+            ],
+            out_specs=[tile, whole],
+            scratch_shapes=[
+                pltpu.VMEM((KV_HEADS, lanes, HEAD), jnp.bfloat16),
+                pltpu.VMEM((KV_HEADS, lanes, HEAD), jnp.bfloat16),
+                pltpu.VMEM((KV_HEADS, 1, lanes), jnp.float32),
+                pltpu.VMEM((KV_HEADS, HEAD, lanes), jnp.float32),
+                pltpu.VMEM(keyval.shape, jnp.float32),
+            ],
+        ),
+        out_shape=[
+            jax.ShapeDtypeStruct((rows, qwidth), jnp.bfloat16),
+            jax.ShapeDtypeStruct(keyval.shape, jnp.bfloat16),
+        ],
+        compiler_params=params(56),
+        cost_estimate=cost(5 * rows * slots * qwidth * 2, 8 * slots * rows, HEADS * rows * slots // 2),
+        name="tree_attention_back",
+    )(block_list, block_count, query, keyval, bias, lse, heads_out, grad_heads, cosine, sine)
+
+
+def project_body(x_ref, gain_ref, w_ref, b_ref, cos_ref, sin_ref, n_ref, q_ref, kv_ref):
+    values = x_ref[...].astype(jnp.float32)
+    inverse = lax.rsqrt(jnp.mean(values * values, axis=-1, keepdims=True) + EPS)
+    normed = (values * inverse * gain_ref[...]).astype(jnp.bfloat16)
+    n_ref[...] = normed
+    linear = dot_nn(normed, w_ref[...]) + b_ref[...]
+    cosine, sine = cos_ref[...], sin_ref[...]
+    for head in range(HEADS + KV_HEADS):
+        lane = linear[:, head * HEAD : (head + 1) * HEAD]
+        lane = (lane * cosine + pltpu.roll(lane, HEAD // 2, 1) * sine).astype(jnp.bfloat16)
+        if head < HEADS:
+            q_ref[:, head * HEAD : (head + 1) * HEAD] = lane
+        else:
+            kv_ref[:, (head - HEADS) * HEAD : (head - HEADS + 1) * HEAD] = lane
+    kv_ref[:, KV_HEADS * HEAD :] = linear[:, (HEADS + KV_HEADS) * HEAD :].astype(jnp.bfloat16)
+
+
+def project(inputs, gain, w_qkv, bias, cosine, sine):
+    rows, width = inputs.shape
+    qwidth, kwidth = HEADS * HEAD, 2 * KV_HEADS * HEAD
+    tile = ROW_TILE
+    fixed = lambda i: (0, 0)
+    moving = lambda i: (i, 0)
+    return pl.pallas_call(
+        project_body,
+        grid=(rows // tile,),
+        in_specs=[
+            pl.BlockSpec((tile, width), moving),
+            pl.BlockSpec((1, width), fixed),
+            pl.BlockSpec(w_qkv.shape, fixed),
+            pl.BlockSpec((1, qwidth + kwidth), fixed),
+            pl.BlockSpec((tile, HEAD), moving),
+            pl.BlockSpec((tile, HEAD), moving),
+        ],
+        out_specs=[
+            pl.BlockSpec((tile, width), moving),
+            pl.BlockSpec((tile, qwidth), moving),
+            pl.BlockSpec((tile, kwidth), moving),
+        ],
+        out_shape=[
+            jax.ShapeDtypeStruct((rows, width), jnp.bfloat16),
+            jax.ShapeDtypeStruct((rows, qwidth), jnp.bfloat16),
+            jax.ShapeDtypeStruct((rows, kwidth), jnp.bfloat16),
+        ],
+        compiler_params=params(48),
+        cost_estimate=cost(2 * rows * width * (qwidth + kwidth), 2 * width * (qwidth + kwidth) + 8 * rows * width),
+        name="project",
+    )(inputs, gain, w_qkv, bias, cosine, sine)
+
+
+CORE, ALONG_X, ALONG_Y, ACROSS = 1, 2, 4, 6
+OTHERS = (ALONG_X, ALONG_Y, ACROSS)
+
+
+def swap(array, bits):
+    return lax.ppermute(array, "gy", [(i, i ^ bits) for i in range(8)])
+
+
+def ring(array):
+    return lax.ppermute(array, "gx", [(i, (i + 1) % 4) for i in range(4)])
+
+
+def pick(array, index):
+    return lax.dynamic_index_in_dim(array, index, 0, keepdims=False)
+
+
+def after(array, *earlier):
+    return lax.optimization_barrier((array, *earlier))[0]
+
+
+def slot_columns(array, plane):
+    wide = array.shape[-1] // 4
+    return jnp.concatenate(
+        [lax.dynamic_slice_in_dim(array, lax.rem(plane + 4 - s, 4) * wide, wide, array.ndim - 1) for s in range(4)],
+        axis=array.ndim - 1,
+    )
+
+
+def pair_rows(pair, core):
+    kept, got = pick(pair, core), swap(pick(pair, 1 - core), CORE)
+    return jnp.where(core == 0, jnp.concatenate([kept, got]), jnp.concatenate([got, kept]))
+
+
+def unpair_rows(rows, core):
+    half = rows.shape[0] // 2
+    kept = lax.dynamic_slice_in_dim(rows, core * half, half, 0)
+    got = swap(lax.dynamic_slice_in_dim(rows, (1 - core) * half, half, 0), CORE)
+    return jnp.where(core == 0, jnp.stack([kept, got]), jnp.stack([got, kept]))
+
+
+def ring_slots(own):
+    slots = [own]
+    for _ in range(3):
+        slots.append(ring(slots[-1]))
+    return slots
+
+
+def ring_sums(slots):
+    moving = ring(slots[1])
+    for s in (2, 3):
+        moving = ring((slots[s].astype(jnp.float32) + moving.astype(jnp.float32)).astype(jnp.bfloat16))
+    return slots[0].astype(jnp.float32) + moving.astype(jnp.float32)
+
+
+def plane_order(blocks, chip):
+    rows = blocks[0].shape[0]
+    whole = jnp.zeros((4 * rows,) + blocks[0].shape[1:], blocks[0].dtype)
+    for index, block in enumerate(blocks):
+        whole = lax.dynamic_update_slice_in_dim(whole, block, (chip ^ index) * rows, 0)
+    return whole
+
+
+def gather_small(row, plane, me):
+    slots = ring_slots(row)
+    rows = jnp.concatenate(slots)
+    rows = jnp.concatenate([pick(rows, lax.rem(plane + 4 - s, 4))[None] for s in range(4)])[:, None]
+    for level, bits in enumerate((CORE, ALONG_X, ALONG_Y)):
+        other = swap(rows, bits)
+        rows = jnp.where(
+            (me >> level) % 2 == 0,
+            jnp.concatenate([rows, other], axis=1),
+            jnp.concatenate([other, rows], axis=1),
+        )
+    return rows.reshape(32, row.shape[1])
+
+
+def sum_small(rows, plane, me):
+    rows = rows.reshape(4, 8, rows.shape[1])
+    for level, bits in ((2, ALONG_Y), (1, ALONG_X), (0, CORE)):
+        half = rows.shape[1] // 2
+        bit = (me >> level) % 2
+        kept = lax.dynamic_slice_in_dim(rows, bit * half, half, 1)
+        rows = kept + swap(lax.dynamic_slice_in_dim(rows, (1 - bit) * half, half, 1), bits)
+    slots = [pick(rows, lax.rem(plane + 4 - s, 4)) for s in range(4)]
+    moving = ring(slots[1])
+    for s in (2, 3):
+        moving = ring(slots[s] + moving)
+    return (slots[0] + moving)[0]
+
+
+def on_core(
+    tokens,
+    cotangent,
+    segment,
+    parent,
+    w_qkv,
+    qkv_bias,
+    w_out,
+    gain_attn,
+    gain_ffn,
+    w_gate,
+    w_up,
+    w_down,
+):
+    low, full = jnp.bfloat16, jnp.float32
+    me = lax.axis_index("gy")
+    plane = lax.axis_index("gx")
+    core, chip = me % 2, me // 2
+    rows, width = 2 * tokens.shape[1], tokens.shape[2]
+    slot_len = segment.shape[1]
+    own_units = w_gate.shape[1]
+    pad_units = -(-own_units // 384) * 384
+    qwidth, kwidth = HEADS * HEAD, KV_HEADS * HEAD
+    offset = chip * rows
+
+    nb, ng = qkv_bias.shape[0], gain_attn.shape[0]
+    packed = jnp.zeros((1, 256), low)
+    packed = packed.at[0, :nb].set(qkv_bias).at[0, nb : nb + ng].set(gain_attn)
+    packed = packed.at[0, nb + ng : nb + 2 * ng].set(gain_ffn)
+    small = gather_small(packed, plane, me).astype(full)
+    bias_full = small[:, :nb].reshape(1, -1)
+    gain_one = small[:, nb : nb + ng].reshape(1, -1)
+    gain_two = small[:, nb + ng : nb + 2 * ng].reshape(1, -1)
+    qkv_full = lax.all_gather(w_qkv, ("gx", "gy"), axis=0, tiled=True)
+    out_full = lax.all_gather(after(w_out, qkv_full), ("gx", "gy"), axis=1, tiled=True)
+
+    inputs_low = pair_rows(tokens, core)
+    grad_low = pair_rows(cotangent, core)
+
+    more = pad_units - own_units
+    gate_slots = ring_slots(jnp.pad(w_gate, ((0, 0), (0, more))))
+    up_slots = ring_slots(jnp.pad(w_up, ((0, 0), (0, more))))
+    down_slots = ring_slots(jnp.pad(w_down, ((0, more), (0, 0))))
+
+    def both_cores(slots, axis):
+        mine = jnp.concatenate(slots, axis=axis)
+        return jnp.concatenate([mine] + [jnp.concatenate([swap(s, CORE) for s in slots], axis=axis)], axis=1 - axis)
+
+    gate_full, up_full = both_cores(gate_slots, 0), both_cores(up_slots, 0)
+    down_full = both_cores(down_slots, 1)
+
+    seg_tree = pick(segment, core)
+    valid, upper_one, upper_two, depth_pos = tree_tables(seg_tree, pick(parent, core))
+    places = jnp.arange(slot_len, dtype=jnp.int32)
+
+    def take_own(array):
+        return lax.dynamic_slice_in_dim(array, offset, rows, 0)
+
+    mask = allowed(
+        take_own(seg_tree), take_own(upper_one), take_own(upper_two), take_own(places), seg_tree, valid, places
+    )
+    qblocks, kblocks = rows // QUERY_TILE, slot_len // KEY_TILE
+    active = mask.reshape(qblocks, QUERY_TILE, kblocks, KEY_TILE).any(axis=(1, 3))
+    block_count = active.sum(axis=1).astype(jnp.int32)
+    rank = jnp.cumsum(active.astype(jnp.int32), axis=1) - 1
+    numbers = jnp.arange(kblocks, dtype=jnp.int32)
+    hit = active[:, :, None] & (rank[:, :, None] == numbers[None, None, :])
+    block_list = jnp.sum(jnp.where(hit, numbers[None, :, None], 0), axis=1).astype(jnp.int32)
+    mask_bias = jnp.where(mask.T, 0.0, NEGATIVE).astype(low)
+    cosine, sine = rotation(take_own(depth_pos), HEAD)
+    sine = sine * jnp.where(jnp.arange(HEAD) < HEAD // 2, -1.0, 1.0)
+
+    normed_one, query, keyval_own = project(inputs_low, gain_one, qkv_full, bias_full, cosine, sine)
+    keyval = plane_order([keyval_own] + [swap(keyval_own, bits) for bits in OTHERS], chip)
+    heads_out, lse = attend_fast(block_list, block_count, query, keyval, mask_bias)
+    inputs = inputs_low.astype(full)
+    resid = inputs + jnp.dot(heads_out, out_full, preferred_element_type=full)
+    unit_two, inverse_two, normed_two = norm_parts(resid, gain_two)
+
+    normed_slots = slot_columns(normed_two, plane)
+    cotan_slots = slot_columns(grad_low, plane)
+    normed_blocks = [normed_slots] + [swap(normed_slots, bits) for bits in OTHERS]
+    cotan_blocks = [cotan_slots] + [swap(cotan_slots, bits) for bits in OTHERS]
+    results = []
+    for normed, cotan in zip(normed_blocks, cotan_blocks):
+        if results:
+            normed = after(normed, results[-1][4])
+        results.append(ffn_block(normed, cotan, gate_full, up_full, down_full))
+    hidden_b, gate_b, up_b, out_b, back_b = zip(*results)
+    grad_normed = [back_b[0]] + [swap(b, bits) for b, bits in zip(back_b[1:], OTHERS)]
+    ffn_out = [out_b[0]] + [swap(after(b, back_b[3]), bits) for b, bits in zip(out_b[1:], OTHERS)]
+    ffn_grads = []
+    for left, right in ((hidden_b, cotan_blocks), (gate_b, normed_blocks), (up_b, normed_blocks)):
+        if ffn_grads:
+            left = (after(left[0], parts),) + left[1:]
+        else:
+            left = (after(left[0], back_b[3]),) + left[1:]
+        parts = wgrad(left, right, 4)
+        mine = parts[0].astype(full) + swap(parts[1], CORE).astype(full)
+        ffn_grads.append(ring_sums(mine.astype(low)))
+    grad_down = ffn_grads[0][:own_units]
+    grad_wgate = ffn_grads[1].T[:, :own_units]
+    grad_wup = ffn_grads[2].T[:, :own_units]
+
+    grad_normed_two = slot_columns(sum(b.astype(full) for b in grad_normed), plane)
+    back_two, grad_gain_two = norm_back(grad_normed_two, unit_two, inverse_two, gain_two)
+    grad_resid = grad_low.astype(full) + back_two
+    grad_branch = grad_resid.astype(low)
+    grad_heads = jnp.dot(grad_branch, out_full.T, preferred_element_type=full).astype(low)
+    query_lin, keyval_part = attend_back_fast(
+        block_list, block_count, query, keyval, mask_bias, lse, heads_out, grad_heads, cosine, sine
+    )
+    grad_wout = jnp.dot(heads_out.T, grad_branch, preferred_element_type=full).astype(low)
+    grad_wout = lax.psum_scatter(grad_wout, ("gx", "gy"), scatter_dimension=1, tiled=True).astype(full)
+
+    def part_of(index):
+        return lax.dynamic_slice_in_dim(keyval_part, (chip ^ index) * rows, rows, 0)
+
+    keyval_grad = part_of(0).astype(full) + sum(
+        swap(part_of(index + 1), bits).astype(full) for index, bits in enumerate(OTHERS)
+    )
+    keys_grad = keyval_grad[:, :kwidth].reshape(rows, KV_HEADS, HEAD)
+    keys_lin = keys_grad * cosine[:, None, :] - jnp.roll(keys_grad, HEAD // 2, axis=-1) * sine[:, None, :]
+    keyval_lin = jnp.concatenate([keys_lin.reshape(rows, kwidth), keyval_grad[:, kwidth:]], axis=1).astype(low)
+    grad_linear = jnp.concatenate([query_lin, keyval_lin], axis=1)
+    grad_wqkv = jnp.dot(normed_one.T, grad_linear, preferred_element_type=full).astype(low)
+    grad_wqkv = lax.psum_scatter(grad_wqkv, ("gx", "gy"), scatter_dimension=0, tiled=True).astype(full)
+    grad_bias = jnp.sum(grad_linear.astype(full), axis=0)
+    grad_normed_one = jnp.dot(grad_linear, qkv_full.T, preferred_element_type=full)
+    unit_one, inverse_one, _ = norm_parts(inputs, gain_one)
+    back_one, grad_gain_one = norm_back(grad_normed_one, unit_one, inverse_one, gain_one)
+    grad_tokens = unpair_rows((grad_resid + back_one).astype(low), core)
+    layer_out = unpair_rows((resid + slot_columns(sum(b.astype(full) for b in ffn_out), plane)).astype(low), core)
+
+    packed = jnp.concatenate(
+        [grad_bias.reshape(32, nb), grad_gain_one.reshape(32, ng), grad_gain_two.reshape(32, ng)], axis=1
+    )
+    small = sum_small(packed, plane, me)
+    return (
+        layer_out,
+        grad_tokens,
+        grad_wqkv,
+        small[:nb],
+        grad_wout,
+        small[nb : nb + ng],
+        small[nb + ng :],
+        grad_wgate,
+        grad_wup,
+        grad_down,
+    )
+
+
 def solution(mesh):
     in_specs = (
         P("gx", "gy", None),
@@ -339,5 +931,9 @@
         P("gy", "gx"),
     )
     return jax.shard_map(
-        on_device, mesh=mesh, in_specs=in_specs, out_specs=out_specs, check_vma=False
-    )
+        on_core if tuple(mesh.shape.values()) == (4, 8) else on_device,
+        mesh=mesh,
+        in_specs=in_specs,
+        out_specs=out_specs,
+        check_vma=False,
+    )

time: 2170 us -> 1270 us (0.59)
  waiting for transfers between devices: 1280 us -> 577 us
  matrix products: 560 us -> 38.2 us
  Pallas kernels: 0 us -> 285 us
  starting transfers between devices: 1.45 us -> 128 us
  blocking collectives: 86.7 us -> 0 us
    reduce_scatter x11 -> x2, waiting for transfers between devices: 873 us -> 117 us  [the longest x1 117 us: on_core(): lax.psum_scatter(grad_wqkv, ('gx', 'gy'), scatter_dimension=0, tiled=True)]
    dot_general x54 -> x5, matrix products: 560 us -> 38.2 us  [the longest x1 10.6 us: on_core(): jnp.dot(grad_linear, qkv_full.T, preferred_element_type=full)]
    ppermute x0 -> x67, waiting for transfers between devices: none -> 459 us  [the longest x24 295 us: ring(): return lax.ppermute(array, 'gx', [(i, (i + 1) % 4) for i in range(4)])]
    all_gather x13 -> x2, waiting for transfers between devices: 403 us -> 0.01 us  [the longest x1 0.01 us: on_core(): qkv_full = lax.all_gather(w_qkv, ('gx', 'gy'), axis=0, tiled=True)]
    pallas_call x0 -> x10, Pallas kernels: none -> 285 us  [the longest x4 152 us: ffn_block(): pl.pallas_call(ffn_body, grid=(steps,), in_specs=[whole, whole, pl.BlockS...]
    ppermute x0 -> x67, starting transfers between devices: none -> 128 us  [the longest x43 107 us: swap(): return lax.ppermute(array, 'gy', [(i, i ^ bits) for i in range(8)])]
    concatenate x6 -> x7, other arithmetic: 7.29 us -> 97.7 us  [the longest x3 93.2 us: both_cores(): jnp.concatenate([mine] + [jnp.concatenate([swap(s, CORE) for s in slots],...]
    unnamed x2 -> x0, blocking collectives: 86.7 us -> none
  transfers between devices with their start and end apart: 26 -> 71, of which waited for: 19 -> 29; matrix products, arithmetic and copies ran while one was open for 28% -> 19% of each run, Pallas kernels for 0% -> 23%
where the time goes in v1:
time: 1270 us; the launch traced here: 1260 us
  waiting for transfers between devices  577 us (45%)
  Pallas kernels  285 us (22%)
  other arithmetic  168 us (13%)
  starting transfers between devices  128 us (10%)
  local copies, waits for them, and re-layouts  45.4 us (4%)
  matrix products  38.2 us (3%)
  between operations  15.1 us (1%)
    ppermute x24, waiting for transfers between devices, ring(): return lax.ppermute(array, 'gx', [(i, (i + 1) % 4) for i in range(4)])  295 us
    ppermute x43, waiting for transfers between devices, swap(): return lax.ppermute(array, 'gy', [(i, i ^ bits) for i in range(8)])  164 us
    pallas_call x4, Pallas kernels, ffn_block(): pl.pallas_call(ffn_body, grid=(steps,), in_specs=[whole, whole, pl.BlockS...  152 us
    reduce_scatter x1, waiting for transfers between devices, on_core(): lax.psum_scatter(grad_wqkv, ('gx', 'gy'), scatter_dimension=0, tiled=True)  117 us
    ppermute x43, starting transfers between devices, swap(): return lax.ppermute(array, 'gy', [(i, i ^ bits) for i in range(8)])  107 us
    concatenate x3, other arithmetic, both_cores(): jnp.concatenate([mine] + [jnp.concatenate([swap(s, CORE) for s in slots],...  93.2 us
    pallas_call x3, Pallas kernels, wgrad(): pl.pallas_call(wgrad_body, grid=(units // tile,), in_specs=[pl.BlockSpec(...  85.8 us
  transfers between devices with their start and end apart: 71, of which 29 were waited for; matrix products, arithmetic and copies ran while one was open for 19% of the time, Pallas kernels for 23%

profile of v1, /device:TPU:9, one launch (start us, length us, event | category | flops | bytes accessed | tf_op | source)
XLA Modules:
  0.0 1256.4 jit_solution(4177508607904768603)
XLA Ops:
  32.5 5.0 or_reduce_fusion
  43.0 11.6 collective-permute-done.2
  75.1 16.5 %collective-permute-done.12 = bf16[384,1152]{1,0:T(8,128)(2,1)} collective-permute-done((bf16[384,1152]{1,0:T(8,128)(2,1)}, bf16[384,1152]{1,0:T(8,128)(2,1)}, u32[]{:S(2)}, u32[]{:S(2)}) %collective-permute-start.12) | collective-permute-done | bytes 884768 | tf_op jit(solution)/shard_map/ppermute | solution.py:673
  95.7 6.5 collective-permute-start.15
  102.3 22.7 %collective-permute-done.25 = bf16[1152,384]{1,0:T(8,128)(2,1)} collective-permute-done((bf16[1152,384]{1,0:T(8,128)(2,1)S(1)}, bf16[1152,384]{1,0:T(8,128)(2,1)}, u32[]{:S(2)}, u32[]{:S(2)}) %collective-permute-start.25) | collective-permute-done | bytes 884768 | tf_op jit(solution)/shard_map/ppermute | solution.py:673
  127.9 16.0 %collective-permute-done.19 = bf16[384,1152]{1,0:T(8,128)(2,1)} collective-permute-done((bf16[384,1152]{1,0:T(8,128)(2,1)}, bf16[384,1152]{1,0:T(8,128)(2,1)}, u32[]{:S(2)}, u32[]{:S(2)}) %collective-permute-start.19) | collective-permute-done | bytes 884768 | tf_op jit(solution)/shard_map/ppermute | solution.py:673
  143.9 19.0 %collective-permute-done.13 = bf16[384,1152]{1,0:T(8,128)(2,1)} collective-permute-done((bf16[384,1152]{1,0:T(8,128)(2,1)}, bf16[384,1152]{1,0:T(8,128)(2,1)}, u32[]{:S(2)}, u32[]{:S(2)}) %collective-permute-start.13) | collective-permute-done | bytes 884768 | tf_op jit(solution)/shard_map/ppermute | solution.py:673
  173.6 8.2 collective-permute-done.26
  185.1 18.8 %collective-permute-done.20 = bf16[384,1152]{1,0:T(8,128)(2,1)} collective-permute-done((bf16[384,1152]{1,0:T(8,128)(2,1)}, bf16[384,1152]{1,0:T(8,128)(2,1)}, u32[]{:S(2)}, u32[]{:S(2)}) %collective-permute-start.20) | collective-permute-done | bytes 884768 | tf_op jit(solution)/shard_map/ppermute | solution.py:673
  205.6 11.1 maximum_maximum_fusion.wg_ref
  218.4 14.1 %collective-permute-done.27 = bf16[1152,384]{1,0:T(8,128)(2,1)S(1)} collective-permute-done((bf16[1152,384]{1,0:T(8,128)(2,1)}, bf16[1152,384]{1,0:T(8,128)(2,1)S(1)}, u32[]{:S(2)}, u32[]{:S(2)}) %collective-permute-start.27) | collective-permute-done | bytes 884768 | tf_op jit(solution)/shard_map/ppermute | solution.py:673
  234.5 43.3 %maximum_maximum_fusion.1.wu_ref = bf16[1536,2304]{1,0:T(8,128)(2,1)} fusion(bf16[384,1152]{1,0:T(8,128)(2,1)S(1)} %collective-permute-done.24, bf16[384,1152]{1,0:T(8,128)(2,1)S(1)} %collective-permute-done.23, bf16[384,1152]{1,0:T(8,128)(2,1)S(1)} %collective-permute-done.22, bf16[384,1152]{1,0:T(8,128)(2,1)S(1)} %collective-permute-done.21, ...), kind=kLoop, calls=%fused_computation.3 | loop fusion | flops 56623104 | bytes 14155776 | tf_op jit(solution)/shard_map/concatenate | solution.py:800
  277.8 9.4 project.1
  291.1 38.8 %maximum_maximum_fusion.2.wd_ref = bf16[2304,1536]{1,0:T(8,128)(2,1)} fusion(bf16[1152,384]{1,0:T(8,128)(2,1)S(1)} %collective-permute-done.31, bf16[1152,384]{1,0:T(8,128)(2,1)S(1)} %collective-permute-done.30, bf16[1152,384]{1,0:T(8,128)(2,1)S(1)} %collective-permute-done.29, bf16[1152,384]{1,0:T(8,128)(2,1)S(1)} %collective-permute-done.28, ...), kind=kLoop, calls=%fused_computation.4 | loop fusion | flops 56623104 | bytes 14155776 | tf_op jit(solution)/shard_map/concatenate | solution.py:800
  331.4 70.3 %collective-permute-done.8 = bf16[640,512]{1,0:T(8,128)(2,1)S(1)} collective-permute-done((bf16[640,512]{1,0:T(8,128)(2,1)S(1)}, bf16[640,512]{1,0:T(8,128)(2,1)S(1)}, u32[]{:S(2)}, u32[]{:S(2)}) %collective-permute-start.8) | collective-permute-done | bytes 655392 | tf_op jit(solution)/shard_map/ppermute | solution.py:669
  403.3 14.4 %tree_attention.1 = (bf16[640,1536]{1,0:T(8,128)(2,1)S(1)}, f32[5,2,1,768]{3,2,1,0:T(1,128)S(1)}) custom-call(s32[5,10]{1,0:T(8,128)S(1)} %select_reduce_fusion.5.list_ref, s32[5]{0:T(128)S(1)} %convert_reduce_fusion.2.count_ref, bf16[640,1536]{1,0:T(8,128)(2,1)S(1)} %get-tuple-element.83.q_ref, bf16[2560,512]{1,0:T(8,128)(2,1)} %copy-done.22, ...), custom_call_target="tpu_custom_call" | custom-call | flops 10066329600 | bytes 6553600 | tf_op jit(solution)/shard_map/tree_attention/pallas_call | solution.py:489
  419.5 6.9 multiply_reduce_fusion.2
  429.8 14.5 %collective-permute-start.32 = (bf16[640,1536]{1,0:T(8,128)(2,1)}, bf16[640,1536]{1,0:T(8,128)(2,1)}, u32[]{:S(2)}, u32[]{:S(2)}) collective-permute-start(bf16[640,1536]{1,0:T(8,128)(2,1)} %pad_maximum_fusion.2.n_ref.refs_4_), channel_id=1, source_target_pairs={{0,2},{1,3},{2,0},{3,1},{4,6},{5,7},{6,4},{7,5},{8,10},{9,11},{10,... | collective-permute-start | bytes 5898248 | tf_op jit(solution)/shard_map/ppermute | solution.py:669
  444.4 11.2 collective-permute-start.35
  455.6 37.6 %ffn_block.4 = (bf16[640,2304]{1,0:T(8,128)(2,1)}, bf16[640,2304]{1,0:T(8,128)(2,1)}, bf16[640,2304]{1,0:T(8,128)(2,1)}, bf16[640,1536]{1,0:T(8,128)(2,1)}, bf16[640,1536]{1,0:T(8,128)(2,1)}) custom-call(bf16[640,1536]{1,0:T(8,128)(2,1)} %pad_maximum_fusion.2.n_ref.refs_4_, bf16[640,1536]{1,0:T(8,128)(2,1)} %pad_maximum_fusion.3.c_ref.refs_4_, ...), custom_call_target="tpu_custom_call" | custom-call | flops 27179089920 | bytes 35979264 | tf_op jit(solution)/shard_map/ffn_block/pallas_call | solution.py:388
  493.3 6.6 collective-permute-start.34
  499.8 37.9 %ffn_block.5 = (bf16[640,2304]{1,0:T(8,128)(2,1)}, bf16[640,2304]{1,0:T(8,128)(2,1)}, bf16[640,2304]{1,0:T(8,128)(2,1)}, bf16[640,1536]{1,0:T(8,128)(2,1)}, bf16[640,1536]{1,0:T(8,128)(2,1)}) custom-call(bf16[640,1536]{1,0:T(8,128)(2,1)} %collective-permute-done.32.n_ref.refs_5_, bf16[640,1536]{1,0:T(8,128)(2,1)} %collective-permute-done.33.c_ref.refs_5_, ...), custom_call_target="tpu_custom_call" | custom-call | flops 27179089920 | bytes 35979264 | tf_op jit(solution)/shard_map/ffn_block/pallas_call | solution.py:388
  537.7 38.0 %ffn_block.6 = (bf16[640,2304]{1,0:T(8,128)(2,1)}, bf16[640,2304]{1,0:T(8,128)(2,1)}, bf16[640,2304]{1,0:T(8,128)(2,1)}, bf16[640,1536]{1,0:T(8,128)(2,1)}, bf16[640,1536]{1,0:T(8,128)(2,1)}) custom-call(bf16[640,1536]{1,0:T(8,128)(2,1)} %collective-permute-done.35.n_ref.refs_6_, bf16[640,1536]{1,0:T(8,128)(2,1)} %collective-permute-done.36.c_ref.refs_6_, ...), custom_call_target="tpu_custom_call" | custom-call | flops 27179089920 | bytes 35979264 | tf_op jit(solution)/shard_map/ffn_block/pallas_call | solution.py:388
  575.9 38.1 %ffn_block.7 = (bf16[640,2304]{1,0:T(8,128)(2,1)}, bf16[640,2304]{1,0:T(8,128)(2,1)}, bf16[640,2304]{1,0:T(8,128)(2,1)}, bf16[640,1536]{1,0:T(8,128)(2,1)}, bf16[640,1536]{1,0:T(8,128)(2,1)}) custom-call(bf16[640,1536]{1,0:T(8,128)(2,1)} %collective-permute-done.34.n_ref.refs_7_, bf16[640,1536]{1,0:T(8,128)(2,1)} %collective-permute-done.37.c_ref.refs_7_, ...), custom_call_target="tpu_custom_call" | custom-call | flops 27179089920 | bytes 35979264 | tf_op jit(solution)/shard_map/ffn_block/pallas_call | solution.py:388
  616.3 28.6 %ffn_wgrad.3 = bf16[2,4,1152,384]{3,2,1,0:T(8,128)(2,1)} custom-call(bf16[640,2304]{1,0:T(8,128)(2,1)} %get-tuple-element.107.refs_0_, bf16[640,2304]{1,0:T(8,128)(2,1)} %get-tuple-element.108.refs_1_, bf16[640,2304]{1,0:T(8,128)(2,1)} %get-tuple-element.109.refs_2_, bf16[640,2304]{1,0:T(8,128)(2,1)} %get-tuple-element.110.refs_3_, ...), custom_call_target="tpu_custom_call" | custom-call | flops 18119393280 | bytes 19660800 | tf_op jit(solution)/shard_map/ffn_wgrad/pallas_call | solution.py:426
  645.3 28.7 %ffn_wgrad.4 = bf16[2,4,1152,384]{3,2,1,0:T(8,128)(2,1)} custom-call(bf16[640,2304]{1,0:T(8,128)(2,1)} %get-tuple-element.111.refs_0_, bf16[640,2304]{1,0:T(8,128)(2,1)} %get-tuple-element.112.refs_1_, bf16[640,2304]{1,0:T(8,128)(2,1)} %get-tuple-element.113.refs_2_, bf16[640,2304]{1,0:T(8,128)(2,1)} %get-tuple-element.114.refs_3_, ...), custom_call_target="tpu_custom_call" | custom-call | flops 18119393280 | bytes 19660800 | tf_op jit(solution)/shard_map/ffn_wgrad/pallas_call | solution.py:426
  676.3 28.5 %ffn_wgrad.5 = bf16[2,4,1152,384]{3,2,1,0:T(8,128)(2,1)} custom-call(bf16[640,2304]{1,0:T(8,128)(2,1)} %get-tuple-element.116.refs_0_, bf16[640,2304]{1,0:T(8,128)(2,1)} %get-tuple-element.117.refs_1_, bf16[640,2304]{1,0:T(8,128)(2,1)} %get-tuple-element.118.refs_2_, bf16[640,2304]{1,0:T(8,128)(2,1)} %get-tuple-element.119.refs_3_, ...), custom_call_target="tpu_custom_call" | custom-call | flops 18119393280 | bytes 19660800 | tf_op jit(solution)/shard_map/ffn_wgrad/pallas_call | solution.py:426
  711.7 46.9 %collective-permute-done.39 = bf16[640,1536]{1,0:T(8,128)(2,1)} collective-permute-done((bf16[640,1536]{1,0:T(8,128)(2,1)}, bf16[640,1536]{1,0:T(8,128)(2,1)}, u32[]{:S(2)}, u32[]{:S(2)}) %collective-permute-start.39) | collective-permute-done | bytes 1966112 | tf_op jit(solution)/shard_map/ppermute | solution.py:669
  765.9 19.6 %collective-permute-done.42 = bf16[640,1536]{1,0:T(8,128)(2,1)S(1)} collective-permute-done((bf16[640,1536]{1,0:T(8,128)(2,1)}, bf16[640,1536]{1,0:T(8,128)(2,1)S(1)}, u32[]{:S(2)}, u32[]{:S(2)}) %collective-permute-start.42) | collective-permute-done | bytes 1966112 | tf_op jit(solution)/shard_map/ppermute | solution.py:669
  795.4 8.1 convolution_convert_fusion.2.do_ref
  803.5 23.9 %tree_attention_back.1 = (bf16[640,1536]{1,0:T(8,128)(2,1)}, bf16[2560,512]{1,0:T(8,128)(2,1)}) custom-call(s32[5,10]{1,0:T(8,128)} %copy-done.4, s32[5]{0:T(128)} %copy-done.5, bf16[640,1536]{1,0:T(8,128)(2,1)} %copy-done.6, bf16[2560,512]{1,0:T(8,128)(2,1)} %copy-done.22, bf16[2560,640]{1,0:T(8,128)(2,1)} %select_convert_fusion.bias_ref, ...), custom_call_target="tpu_custom_call" | custom-call | flops 25165824000 | bytes 13107200 | tf_op jit(solution)/shard_map/tree_attention_back/pallas_call | solution.py:580
  830.2 15.9 %collective-permute-start.45 = (bf16[640,512]{1,0:T(8,128)(2,1)}, bf16[640,512]{1,0:T(8,128)(2,1)S(1)}, u32[]{:S(2)}, u32[]{:S(2)}) collective-permute-start(bf16[640,512]{1,0:T(8,128)(2,1)} %get-tuple-element.146), channel_id=1, source_target_pairs={{0,2},{1,3},{2,0},{3,1},{4,6},{5,7},{6,4},{7,5},{8,10},{9,11},{10,... | collective-permute-start | bytes 1966088 | tf_op jit(solution)/shard_map/ppermute | solution.py:669
  846.1 8.9 collective-permute-start.46
  856.1 5.5 convolution_convert_fusion
  861.8 20.2 %collective-permute-done.46 = bf16[640,512]{1,0:T(8,128)(2,1)} collective-permute-done((bf16[640,512]{1,0:T(8,128)(2,1)}, bf16[640,512]{1,0:T(8,128)(2,1)}, u32[]{:S(2)}, u32[]{:S(2)}) %collective-permute-start.46) | collective-permute-done | bytes 655392 | tf_op jit(solution)/shard_map/ppermute | solution.py:669
  893.3 10.6 fusion.14
  914.1 7.2 convolution_convert_fusion.1
  924.6 4.9 fusion.13
  960.3 13.7 %collective-permute-done.60 = bf16[1152,384]{1,0:T(8,128)(2,1)} collective-permute-done((bf16[1152,384]{1,0:T(8,128)(2,1)S(1)}, bf16[1152,384]{1,0:T(8,128)(2,1)}, u32[]{:S(2)}, u32[]{:S(2)}) %collective-permute-start.60) | collective-permute-done | bytes 884768 | tf_op jit(solution)/shard_map/ppermute | solution.py:673
  975.7 19.1 %collective-permute-done.56 = bf16[1152,384]{1,0:T(8,128)(2,1)S(1)} collective-permute-done((bf16[1152,384]{1,0:T(8,128)(2,1)S(1)}, bf16[1152,384]{1,0:T(8,128)(2,1)S(1)}, u32[]{:S(2)}, u32[]{:S(2)}) %collective-permute-start.56) | collective-permute-done | bytes 884768 | tf_op jit(solution)/shard_map/ppermute | solution.py:673
  995.3 18.5 %collective-permute-done.64 = bf16[1152,384]{1,0:T(8,128)(2,1)S(1)} collective-permute-done((bf16[1152,384]{1,0:T(8,128)(2,1)S(1)}, bf16[1152,384]{1,0:T(8,128)(2,1)S(1)}, u32[]{:S(2)}, u32[]{:S(2)}) %collective-permute-start.64) | collective-permute-done | bytes 884768 | tf_op jit(solution)/shard_map/ppermute | solution.py:673
  1014.3 18.5 %collective-permute-done.61 = bf16[1152,384]{1,0:T(8,128)(2,1)S(1)} collective-permute-done((bf16[1152,384]{1,0:T(8,128)(2,1)S(1)}, bf16[1152,384]{1,0:T(8,128)(2,1)S(1)}, u32[]{:S(2)}, u32[]{:S(2)}) %collective-permute-start.61) | collective-permute-done | bytes 884768 | tf_op jit(solution)/shard_map/ppermute | solution.py:673
  1033.2 18.5 %collective-permute-done.57 = bf16[1152,384]{1,0:T(8,128)(2,1)S(1)} collective-permute-done((bf16[1152,384]{1,0:T(8,128)(2,1)S(1)}, bf16[1152,384]{1,0:T(8,128)(2,1)S(1)}, u32[]{:S(2)}, u32[]{:S(2)}) %collective-permute-start.57) | collective-permute-done | bytes 884768 | tf_op jit(solution)/shard_map/ppermute | solution.py:673
  1052.2 18.5 %collective-permute-done.65 = bf16[1152,384]{1,0:T(8,128)(2,1)S(1)} collective-permute-done((bf16[1152,384]{1,0:T(8,128)(2,1)S(1)}, bf16[1152,384]{1,0:T(8,128)(2,1)S(1)}, u32[]{:S(2)}, u32[]{:S(2)}) %collective-permute-start.65) | collective-permute-done | bytes 884768 | tf_op jit(solution)/shard_map/ppermute | solution.py:673
  1071.2 18.5 %collective-permute-done.62 = bf16[1152,384]{1,0:T(8,128)(2,1)S(1)} collective-permute-done((bf16[1152,384]{1,0:T(8,128)(2,1)S(1)}, bf16[1152,384]{1,0:T(8,128)(2,1)S(1)}, u32[]{:S(2)}, u32[]{:S(2)}) %collective-permute-start.62) | collective-permute-done | bytes 884768 | tf_op jit(solution)/shard_map/ppermute | solution.py:673
  1091.1 17.5 %collective-permute-done.58 = bf16[1152,384]{1,0:T(8,128)(2,1)S(1)} collective-permute-done((bf16[1152,384]{1,0:T(8,128)(2,1)S(1)}, bf16[1152,384]{1,0:T(8,128)(2,1)S(1)}, u32[]{:S(2)}, u32[]{:S(2)}) %collective-permute-start.58) | collective-permute-done | bytes 884768 | tf_op jit(solution)/shard_map/ppermute | solution.py:673
  1110.1 17.5 %collective-permute-done.66 = bf16[1152,384]{1,0:T(8,128)(2,1)S(1)} collective-permute-done((bf16[1152,384]{1,0:T(8,128)(2,1)S(1)}, bf16[1152,384]{1,0:T(8,128)(2,1)S(1)}, u32[]{:S(2)}, u32[]{:S(2)}) %collective-permute-start.66) | collective-permute-done | bytes 884768 | tf_op jit(solution)/shard_map/ppermute | solution.py:673
  1130.6 117.4 %reduce-scatter.3.cloned.1.call-done = bf16[48,2048]{1,0:T(8,128)(2,1)} async-done(((bf16[1536,2048]{1,0:T(8,128)(2,1)}), bf16[48,2048]{1,0:T(8,128)(2,1)}) %reduce-scatter.3.cloned.1.call-update) | async-done | bytes 196624 | tf_op jit(solution)/shard_map/reduce_scatter | solution.py:880
  (342 shorter events, 189.4 us)
Async XLA Ops:
  7.2 163.3 %all-gather.3.cloned.1.call-start = ((), (), s32[]{:S(2)}) async-start(), calls=%async_computation.2 | async-start | bytes 6488064 | tf_op jit(solution)/shard_map/all_gather | solution.py:787
  7.9 411.6 %all-gather.5.cloned.1.call-start = ((), (), s32[]{:S(2)}) async-start(), calls=%async_computation.3 | async-start | bytes 4866048 | tf_op jit(solution)/shard_map/all_gather | solution.py:788
  10.6 47.4 %collective-permute-start.11 = (bf16[384,1152]{1,0:T(8,128)(2,1)}, bf16[384,1152]{1,0:T(8,128)(2,1)}, u32[]{:S(2)}, u32[]{:S(2)}) collective-permute-start(bf16[384,1152]{1,0:T(8,128)(2,1)} %pad.22), channel_id=1, source_target_pairs={{0,8},{8,16},{16,24},{24,0},{1,9},{9,17},{17,25},{25,1},{2,10},{10... | collective-permute-start | bytes 2654216 | tf_op jit(solution)/shard_map/ppermute | solution.py:673
  11.9 83.8 %collective-permute-start.14 = (bf16[384,1152]{1,0:T(8,128)(2,1)}, bf16[384,1152]{1,0:T(8,128)(2,1)}, u32[]{:S(2)}, u32[]{:S(2)}) collective-permute-start(bf16[384,1152]{1,0:T(8,128)(2,1)} %pad.22), channel_id=1, source_target_pairs={{0,1},{1,0},{2,3},{3,2},{4,5},{5,4},{6,7},{7,6},{8,9},{9,8},{10,11... | collective-permute-start | bytes 2654216 | tf_op jit(solution)/shard_map/ppermute | solution.py:669
  25.3 46.2 %collective-permute-start.10 = (bf16[320,1536]{1,0:T(8,128)(2,1)}, bf16[320,1536]{1,0:T(8,128)(2,1)}, u32[]{:S(2)}, u32[]{:S(2)}) collective-permute-start(bf16[320,1536]{1,0:T(8,128)(2,1)} %get-tuple-element.158), channel_id=1, source_target_pairs={{0,1},{1,0},{2,3},{3,2},{4,5},{5,4},{6,7},{7,6},{8,9},{9,8},{10,11... | collective-permute-start | bytes 2949128 | tf_op jit(solution)/shard_map/ppermute | solution.py:669
  27.1 43.1 %collective-permute-start.18 = (bf16[384,1152]{1,0:T(8,128)(2,1)S(1)}, bf16[384,1152]{1,0:T(8,128)(2,1)}, u32[]{:S(2)}, u32[]{:S(2)}) collective-permute-start(bf16[384,1152]{1,0:T(8,128)(2,1)S(1)} %pad.23), channel_id=1, source_target_pairs={{0,8},{8,16},{16,24},{24,0},{1,9},{9,17},{17,25},{25,1},{2,10},{10... | collective-permute-start | bytes 2654216 | tf_op jit(solution)/shard_map/ppermute | solution.py:673
  68.3 56.7 %collective-permute-start = (bf16[320,1536]{1,0:T(8,128)(2,1)}, bf16[320,1536]{1,0:T(8,128)(2,1)}, u32[]{:S(2)}, u32[]{:S(2)}) collective-permute-start(bf16[320,1536]{1,0:T(8,128)(2,1)} %get-tuple-element.163), channel_id=1, source_target_pairs={{0,1},{1,0},{2,3},{3,2},{4,5},{5,4},{6,7},{7,6},{8,9},{9,8},{10,11... | collective-permute-start | bytes 2949128 | tf_op jit(solution)/shard_map/ppermute | solution.py:669
  70.2 54.7 %collective-permute-start.25 = (bf16[1152,384]{1,0:T(8,128)(2,1)S(1)}, bf16[1152,384]{1,0:T(8,128)(2,1)}, u32[]{:S(2)}, u32[]{:S(2)}) collective-permute-start(bf16[1152,384]{1,0:T(8,128)(2,1)S(1)} %pad.24), channel_id=1, source_target_pairs={{0,8},{8,16},{16,24},{24,0},{1,9},{9,17},{17,25},{25,1},{2,10},{10... | collective-permute-start | bytes 2654216 | tf_op jit(solution)/shard_map/ppermute | solution.py:673
  71.5 72.4 %collective-permute-start.19 = (bf16[384,1152]{1,0:T(8,128)(2,1)}, bf16[384,1152]{1,0:T(8,128)(2,1)}, u32[]{:S(2)}, u32[]{:S(2)}) collective-permute-start(bf16[384,1152]{1,0:T(8,128)(2,1)} %collective-permute-done.18), channel_id=1, source_target_pairs={{0,8},{8,16},{16,24},{24,0},{1,9},{9,17},{17,25},{25,1},{2,10},{10... | collective-permute-start | bytes 2654216 | tf_op jit(solution)/shard_map/ppermute | solution.py:673
  91.7 71.2 %collective-permute-start.13 = (bf16[384,1152]{1,0:T(8,128)(2,1)}, bf16[384,1152]{1,0:T(8,128)(2,1)}, u32[]{:S(2)}, u32[]{:S(2)}) collective-permute-start(bf16[384,1152]{1,0:T(8,128)(2,1)} %collective-permute-done.12), channel_id=1, source_target_pairs={{0,8},{8,16},{16,24},{24,0},{1,9},{9,17},{17,25},{25,1},{2,10},{10... | collective-permute-start | bytes 2654216 | tf_op jit(solution)/shard_map/ppermute | solution.py:673
  95.7 77.9 %collective-permute-start.15 = (bf16[384,1152]{1,0:T(8,128)(2,1)}, bf16[384,1152]{1,0:T(8,128)(2,1)}, u32[]{:S(2)}, u32[]{:S(2)}) collective-permute-start(bf16[384,1152]{1,0:T(8,128)(2,1)} %collective-permute-done.11), channel_id=1, source_target_pairs={{0,1},{1,0},{2,3},{3,2},{4,5},{5,4},{6,7},{7,6},{8,9},{9,8},{10,11... | collective-permute-start | bytes 2654216 | tf_op jit(solution)/shard_map/ppermute | solution.py:669
  125.0 56.9 %collective-permute-start.26 = (bf16[1152,384]{1,0:T(8,128)(2,1)}, bf16[1152,384]{1,0:T(8,128)(2,1)}, u32[]{:S(2)}, u32[]{:S(2)}) collective-permute-start(bf16[1152,384]{1,0:T(8,128)(2,1)} %collective-permute-done.25), channel_id=1, source_target_pairs={{0,8},{8,16},{16,24},{24,0},{1,9},{9,17},{17,25},{25,1},{2,10},{10... | collective-permute-start | bytes 2654216 | tf_op jit(solution)/shard_map/ppermute | solution.py:673
  125.0 60.1 %collective-permute-start.16 = (bf16[384,1152]{1,0:T(8,128)(2,1)}, bf16[384,1152]{1,0:T(8,128)(2,1)}, u32[]{:S(2)}, u32[]{:S(2)}) collective-permute-start(bf16[384,1152]{1,0:T(8,128)(2,1)} %collective-permute-done.12), channel_id=1, source_target_pairs={{0,1},{1,0},{2,3},{3,2},{4,5},{5,4},{6,7},{7,6},{8,9},{9,8},{10,11... | collective-permute-start | bytes 2654216 | tf_op jit(solution)/shard_map/ppermute | solution.py:669
  143.9 60.0 %collective-permute-start.20 = (bf16[384,1152]{1,0:T(8,128)(2,1)}, bf16[384,1152]{1,0:T(8,128)(2,1)}, u32[]{:S(2)}, u32[]{:S(2)}) collective-permute-start(bf16[384,1152]{1,0:T(8,128)(2,1)} %collective-permute-done.19), channel_id=1, source_target_pairs={{0,8},{8,16},{16,24},{24,0},{1,9},{9,17},{17,25},{25,1},{2,10},{10... | collective-permute-start | bytes 2654216 | tf_op jit(solution)/shard_map/ppermute | solution.py:673
  162.9 41.3 %collective-permute-start.17 = (bf16[384,1152]{1,0:T(8,128)(2,1)}, bf16[384,1152]{1,0:T(8,128)(2,1)}, u32[]{:S(2)}, u32[]{:S(2)}) collective-permute-start(bf16[384,1152]{1,0:T(8,128)(2,1)} %collective-permute-done.13), channel_id=1, source_target_pairs={{0,1},{1,0},{2,3},{3,2},{4,5},{5,4},{6,7},{7,6},{8,9},{9,8},{10,11... | collective-permute-start | bytes 2654216 | tf_op jit(solution)/shard_map/ppermute | solution.py:669
  170.6 958.4 %reduce-scatter.5.cloned.1.call-start = ((), (), s32[]{:S(2)}) async-start(), calls=%async_computation.5 | async-start | bytes 4866048 | tf_op jit(solution)/shard_map/reduce_scatter | solution.py:867
  173.6 43.1 %collective-permute-start.21 = (bf16[384,1152]{1,0:T(8,128)(2,1)}, bf16[384,1152]{1,0:T(8,128)(2,1)S(1)}, u32[]{:S(2)}, u32[]{:S(2)}) collective-permute-start(bf16[384,1152]{1,0:T(8,128)(2,1)} %copy-done.20), channel_id=1, source_target_pairs={{0,1},{1,0},{2,3},{3,2},{4,5},{5,4},{6,7},{7,6},{8,9},{9,8},{10,11... | collective-permute-start | bytes 2654216 | tf_op jit(solution)/shard_map/ppermute | solution.py:669
  216.6 70.6 %collective-permute-start.28 = (bf16[1152,384]{1,0:T(8,128)(2,1)S(1)}, bf16[1152,384]{1,0:T(8,128)(2,1)S(1)}, u32[]{:S(2)}, u32[]{:S(2)}) collective-permute-start(bf16[1152,384]{1,0:T(8,128)(2,1)S(1)} %pad.24), channel_id=1, source_target_pairs={{0,1},{1,0},{2,3},{3,2},{4,5},{5,4},{6,7},{7,6},{8,9},{9,8},{10,11... | collective-permute-start | bytes 2654216 | tf_op jit(solution)/shard_map/ppermute | solution.py:669
  216.7 71.7 %collective-permute-start.29 = (bf16[1152,384]{1,0:T(8,128)(2,1)}, bf16[1152,384]{1,0:T(8,128)(2,1)S(1)}, u32[]{:S(2)}, u32[]{:S(2)}) collective-permute-start(bf16[1152,384]{1,0:T(8,128)(2,1)} %collective-permute-done.25), channel_id=1, source_target_pairs={{0,1},{1,0},{2,3},{3,2},{4,5},{5,4},{6,7},{7,6},{8,9},{9,8},{10,11... | collective-permute-start | bytes 2654216 | tf_op jit(solution)/shard_map/ppermute | solution.py:669
  217.2 282.6 %collective-permute-start.33 = (bf16[640,1536]{1,0:T(8,128)(2,1)}, bf16[640,1536]{1,0:T(8,128)(2,1)}, u32[]{:S(2)}, u32[]{:S(2)}) collective-permute-start(bf16[640,1536]{1,0:T(8,128)(2,1)} %pad_maximum_fusion.3.c_ref.refs_4_), channel_id=1, source_target_pairs={{0,2},{1,3},{2,0},{3,1},{4,6},{5,7},{6,4},{7,5},{8,10},{9,11},{10,... | collective-permute-start | bytes 5898248 | tf_op jit(solution)/shard_map/ppermute | solution.py:669
  232.6 57.1 %collective-permute-start.30 = (bf16[1152,384]{1,0:T(8,128)(2,1)}, bf16[1152,384]{1,0:T(8,128)(2,1)S(1)}, u32[]{:S(2)}, u32[]{:S(2)}) collective-permute-start(bf16[1152,384]{1,0:T(8,128)(2,1)} %collective-permute-done.26), channel_id=1, source_target_pairs={{0,1},{1,0},{2,3},{3,2},{4,5},{5,4},{6,7},{7,6},{8,9},{9,8},{10,11... | collective-permute-start | bytes 2654216 | tf_op jit(solution)/shard_map/ppermute | solution.py:669
  234.5 55.4 %collective-permute-start.31 = (bf16[1152,384]{1,0:T(8,128)(2,1)S(1)}, bf16[1152,384]{1,0:T(8,128)(2,1)S(1)}, u32[]{:S(2)}, u32[]{:S(2)}) collective-permute-start(bf16[1152,384]{1,0:T(8,128)(2,1)S(1)} %collective-permute-done.27), channel_id=1, source_target_pairs={{0,1},{1,0},{2,3},{3,2},{4,5},{5,4},{6,7},{7,6},{8,9},{9,8},{10,11... | collective-permute-start | bytes 2654216 | tf_op jit(solution)/shard_map/ppermute | solution.py:669
  287.3 250.5 %collective-permute-start.36 = (bf16[640,1536]{1,0:T(8,128)(2,1)}, bf16[640,1536]{1,0:T(8,128)(2,1)}, u32[]{:S(2)}, u32[]{:S(2)}) collective-permute-start(bf16[640,1536]{1,0:T(8,128)(2,1)} %pad_maximum_fusion.3.c_ref.refs_4_), channel_id=1, source_target_pairs={{0,4},{1,5},{2,6},{3,7},{4,0},{5,1},{6,2},{7,3},{8,12},{9,13},{10,... | collective-permute-start | bytes 5898248 | tf_op jit(solution)/shard_map/ppermute | solution.py:669
  288.5 41.7 %collective-permute-start.7 = (bf16[640,512]{1,0:T(8,128)(2,1)S(1)}, bf16[640,512]{1,0:T(8,128)(2,1)S(1)}, u32[]{:S(2)}, u32[]{:S(2)}) collective-permute-start(bf16[640,512]{1,0:T(8,128)(2,1)S(1)} %get-tuple-element.84), channel_id=1, source_target_pairs={{0,2},{1,3},{2,0},{3,1},{4,6},{5,7},{6,4},{7,5},{8,10},{9,11},{10,... | collective-permute-start | bytes 1966088 | tf_op jit(solution)/shard_map/ppermute | solution.py:669
  289.7 112.0 %collective-permute-start.8 = (bf16[640,512]{1,0:T(8,128)(2,1)S(1)}, bf16[640,512]{1,0:T(8,128)(2,1)S(1)}, u32[]{:S(2)}, u32[]{:S(2)}) collective-permute-start(bf16[640,512]{1,0:T(8,128)(2,1)S(1)} %get-tuple-element.84), channel_id=1, source_target_pairs={{0,4},{1,5},{2,6},{3,7},{4,0},{5,1},{6,2},{7,3},{8,12},{9,13},{10,... | collective-permute-start | bytes 1966088 | tf_op jit(solution)/shard_map/ppermute | solution.py:669
  289.9 111.9 %collective-permute-start.9 = (bf16[640,512]{1,0:T(8,128)(2,1)S(1)}, bf16[640,512]{1,0:T(8,128)(2,1)S(1)}, u32[]{:S(2)}, u32[]{:S(2)}) collective-permute-start(bf16[640,512]{1,0:T(8,128)(2,1)S(1)} %get-tuple-element.84), channel_id=1, source_target_pairs={{0,6},{1,7},{2,4},{3,5},{4,2},{5,3},{6,0},{7,1},{8,14},{9,15},{10,... | collective-permute-start | bytes 1966088 | tf_op jit(solution)/shard_map/ppermute | solution.py:669
  330.1 245.7 %collective-permute-start.37 = (bf16[640,1536]{1,0:T(8,128)(2,1)}, bf16[640,1536]{1,0:T(8,128)(2,1)}, u32[]{:S(2)}, u32[]{:S(2)}) collective-permute-start(bf16[640,1536]{1,0:T(8,128)(2,1)} %pad_maximum_fusion.3.c_ref.refs_4_), channel_id=1, source_target_pairs={{0,6},{1,7},{2,4},{3,5},{4,2},{5,3},{6,0},{7,1},{8,14},{9,15},{10,... | collective-permute-start | bytes 5898248 | tf_op jit(solution)/shard_map/ppermute | solution.py:669
  429.8 63.4 %collective-permute-start.32 = (bf16[640,1536]{1,0:T(8,128)(2,1)}, bf16[640,1536]{1,0:T(8,128)(2,1)}, u32[]{:S(2)}, u32[]{:S(2)}) collective-permute-start(bf16[640,1536]{1,0:T(8,128)(2,1)} %pad_maximum_fusion.2.n_ref.refs_4_), channel_id=1, source_target_pairs={{0,2},{1,3},{2,0},{3,1},{4,6},{5,7},{6,4},{7,5},{8,10},{9,11},{10,... | collective-permute-start | bytes 5898248 | tf_op jit(solution)/shard_map/ppermute | solution.py:669
  444.4 93.3 %collective-permute-start.35 = (bf16[640,1536]{1,0:T(8,128)(2,1)}, bf16[640,1536]{1,0:T(8,128)(2,1)}, u32[]{:S(2)}, u32[]{:S(2)}) collective-permute-start(bf16[640,1536]{1,0:T(8,128)(2,1)} %pad_maximum_fusion.2.n_ref.refs_4_), channel_id=1, source_target_pairs={{0,4},{1,5},{2,6},{3,7},{4,0},{5,1},{6,2},{7,3},{8,12},{9,13},{10,... | collective-permute-start | bytes 5898248 | tf_op jit(solution)/shard_map/ppermute | solution.py:669
  493.3 82.6 %collective-permute-start.34 = (bf16[640,1536]{1,0:T(8,128)(2,1)}, bf16[640,1536]{1,0:T(8,128)(2,1)}, u32[]{:S(2)}, u32[]{:S(2)}) collective-permute-start(bf16[640,1536]{1,0:T(8,128)(2,1)} %pad_maximum_fusion.2.n_ref.refs_4_), channel_id=1, source_target_pairs={{0,6},{1,7},{2,4},{3,5},{4,2},{5,3},{6,0},{7,1},{8,14},{9,15},{10,... | collective-permute-start | bytes 5898248 | tf_op jit(solution)/shard_map/ppermute | solution.py:669
  575.8 190.1 %collective-permute-start.43 = (bf16[640,1536]{1,0:T(8,128)(2,1)}, bf16[640,1536]{1,0:T(8,128)(2,1)}, u32[]{:S(2)}, u32[]{:S(2)}) collective-permute-start(bf16[640,1536]{1,0:T(8,128)(2,1)} %get-tuple-element.93), channel_id=1, source_target_pairs={{0,4},{1,5},{2,6},{3,7},{4,0},{5,1},{6,2},{7,3},{8,12},{9,13},{10,... | collective-permute-start | bytes 5898248 | tf_op jit(solution)/shard_map/ppermute | solution.py:669
  614.0 151.8 %collective-permute-start.44 = (bf16[640,1536]{1,0:T(8,128)(2,1)}, bf16[640,1536]{1,0:T(8,128)(2,1)}, u32[]{:S(2)}, u32[]{:S(2)}) collective-permute-start(bf16[640,1536]{1,0:T(8,128)(2,1)} %get-tuple-element.95), channel_id=1, source_target_pairs={{0,6},{1,7},{2,4},{3,5},{4,2},{5,3},{6,0},{7,1},{8,14},{9,15},{10,... | collective-permute-start | bytes 5898248 | tf_op jit(solution)/shard_map/ppermute | solution.py:669
  644.9 59.9 %collective-permute-start.38 = (bf16[640,1536]{1,0:T(8,128)(2,1)}, bf16[640,1536]{1,0:T(8,128)(2,1)}, u32[]{:S(2)}, u32[]{:S(2)}) collective-permute-start(bf16[640,1536]{1,0:T(8,128)(2,1)} %get-tuple-element.96), channel_id=1, source_target_pairs={{0,2},{1,3},{2,0},{3,1},{4,6},{5,7},{6,4},{7,5},{8,10},{9,11},{10,... | collective-permute-start | bytes 5898248 | tf_op jit(solution)/shard_map/ppermute | solution.py:669
  674.0 84.6 %collective-permute-start.39 = (bf16[640,1536]{1,0:T(8,128)(2,1)}, bf16[640,1536]{1,0:T(8,128)(2,1)}, u32[]{:S(2)}, u32[]{:S(2)}) collective-permute-start(bf16[640,1536]{1,0:T(8,128)(2,1)} %get-tuple-element.98), channel_id=1, source_target_pairs={{0,4},{1,5},{2,6},{3,7},{4,0},{5,1},{6,2},{7,3},{8,12},{9,13},{10,... | collective-permute-start | bytes 5898248 | tf_op jit(solution)/shard_map/ppermute | solution.py:669
  674.0 87.6 %collective-permute-start.40 = (bf16[640,1536]{1,0:T(8,128)(2,1)}, bf16[640,1536]{1,0:T(8,128)(2,1)}, u32[]{:S(2)}, u32[]{:S(2)}) collective-permute-start(bf16[640,1536]{1,0:T(8,128)(2,1)} %get-tuple-element.100), channel_id=1, source_target_pairs={{0,6},{1,7},{2,4},{3,5},{4,2},{5,3},{6,0},{7,1},{8,14},{9,15},{10,... | collective-permute-start | bytes 5898248 | tf_op jit(solution)/shard_map/ppermute | solution.py:669
  704.8 80.7 %collective-permute-start.42 = (bf16[640,1536]{1,0:T(8,128)(2,1)}, bf16[640,1536]{1,0:T(8,128)(2,1)S(1)}, u32[]{:S(2)}, u32[]{:S(2)}) collective-permute-start(bf16[640,1536]{1,0:T(8,128)(2,1)} %get-tuple-element.91), channel_id=1, source_target_pairs={{0,2},{1,3},{2,0},{3,1},{4,6},{5,7},{6,4},{7,5},{8,10},{9,11},{10,... | collective-permute-start | bytes 5898248 | tf_op jit(solution)/shard_map/ppermute | solution.py:669
  758.5 193.3 %collective-permute-start.63 = (bf16[4,1152,384]{2,1,0:T(8,128)(2,1)}, bf16[4,1152,384]{2,1,0:T(8,128)(2,1)}, u32[]{:S(2)}, u32[]{:S(2)}) collective-permute-start(bf16[4,1152,384]{2,1,0:T(8,128)(2,1)} %slice_bitcast_fusion), channel_id=1, source_target_pairs={{0,1},{1,0},{2,3},{3,2},{4,5},{5,4},{6,7},{7,6},{8,9},{9,8},{10,11... | collective-permute-start | bytes 10616840 | tf_op jit(solution)/shard_map/ppermute | solution.py:669
  846.1 35.9 %collective-permute-start.46 = (bf16[640,512]{1,0:T(8,128)(2,1)}, bf16[640,512]{1,0:T(8,128)(2,1)}, u32[]{:S(2)}, u32[]{:S(2)}) collective-permute-start(bf16[640,512]{1,0:T(8,128)(2,1)} %get-tuple-element.148), channel_id=1, source_target_pairs={{0,4},{1,5},{2,6},{3,7},{4,0},{5,1},{6,2},{7,3},{8,12},{9,13},{10,... | collective-permute-start | bytes 1966088 | tf_op jit(solution)/shard_map/ppermute | solution.py:669
  861.7 386.3 %reduce-scatter.3.cloned.1.call-start = ((), (), s32[]{:S(2)}) async-start(), calls=%async_computation.4 | async-start | bytes 6488064 | tf_op jit(solution)/shard_map/reduce_scatter | solution.py:880
  909.7 36.8 %collective-permute-start.55 = (bf16[4,1152,384]{2,1,0:T(8,128)(2,1)}, bf16[4,1152,384]{2,1,0:T(8,128)(2,1)}, u32[]{:S(2)}, u32[]{:S(2)}) collective-permute-start(bf16[4,1152,384]{2,1,0:T(8,128)(2,1)} %slice_bitcast_fusion.4), channel_id=1, source_target_pairs={{0,1},{1,0},{2,3},{3,2},{4,5},{5,4},{6,7},{7,6},{8,9},{9,8},{10,11... | collective-permute-start | bytes 10616840 | tf_op jit(solution)/shard_map/ppermute | solution.py:669
  949.9 45.0 %collective-permute-start.56 = (bf16[1152,384]{1,0:T(8,128)(2,1)S(1)}, bf16[1152,384]{1,0:T(8,128)(2,1)S(1)}, u32[]{:S(2)}, u32[]{:S(2)}) collective-permute-start(bf16[1152,384]{1,0:T(8,128)(2,1)S(1)} %slice_bitcast_fusion.14), channel_id=1, source_target_pairs={{0,8},{8,16},{16,24},{24,0},{1,9},{9,17},{17,25},{25,1},{2,10},{10... | collective-permute-start | bytes 2654216 | tf_op jit(solution)/shard_map/ppermute | solution.py:673
  955.0 58.8 %collective-permute-start.64 = (bf16[1152,384]{1,0:T(8,128)(2,1)S(1)}, bf16[1152,384]{1,0:T(8,128)(2,1)S(1)}, u32[]{:S(2)}, u32[]{:S(2)}) collective-permute-start(bf16[1152,384]{1,0:T(8,128)(2,1)S(1)} %get-tuple-element.144), channel_id=1, source_target_pairs={{0,8},{8,16},{16,24},{24,0},{1,9},{9,17},{17,25},{25,1},{2,10},{10... | collective-permute-start | bytes 2654216 | tf_op jit(solution)/shard_map/ppermute | solution.py:673
  975.5 57.3 %collective-permute-start.61 = (bf16[1152,384]{1,0:T(8,128)(2,1)S(1)}, bf16[1152,384]{1,0:T(8,128)(2,1)S(1)}, u32[]{:S(2)}, u32[]{:S(2)}) collective-permute-start(bf16[1152,384]{1,0:T(8,128)(2,1)S(1)} %fusion.19), channel_id=1, source_target_pairs={{0,8},{8,16},{16,24},{24,0},{1,9},{9,17},{17,25},{25,1},{2,10},{10... | collective-permute-start | bytes 2654216 | tf_op jit(solution)/shard_map/ppermute | solution.py:673
  995.1 56.6 %collective-permute-start.57 = (bf16[1152,384]{1,0:T(8,128)(2,1)S(1)}, bf16[1152,384]{1,0:T(8,128)(2,1)S(1)}, u32[]{:S(2)}, u32[]{:S(2)}) collective-permute-start(bf16[1152,384]{1,0:T(8,128)(2,1)S(1)} %fusion.22), channel_id=1, source_target_pairs={{0,8},{8,16},{16,24},{24,0},{1,9},{9,17},{17,25},{25,1},{2,10},{10... | collective-permute-start | bytes 2654216 | tf_op jit(solution)/shard_map/ppermute | solution.py:673
  1014.1 56.6 %collective-permute-start.65 = (bf16[1152,384]{1,0:T(8,128)(2,1)S(1)}, bf16[1152,384]{1,0:T(8,128)(2,1)S(1)}, u32[]{:S(2)}, u32[]{:S(2)}) collective-permute-start(bf16[1152,384]{1,0:T(8,128)(2,1)S(1)} %fusion.17), channel_id=1, source_target_pairs={{0,8},{8,16},{16,24},{24,0},{1,9},{9,17},{17,25},{25,1},{2,10},{10... | collective-permute-start | bytes 2654216 | tf_op jit(solution)/shard_map/ppermute | solution.py:673
  1033.0 56.6 %collective-permute-start.62 = (bf16[1152,384]{1,0:T(8,128)(2,1)S(1)}, bf16[1152,384]{1,0:T(8,128)(2,1)S(1)}, u32[]{:S(2)}, u32[]{:S(2)}) collective-permute-start(bf16[1152,384]{1,0:T(8,128)(2,1)S(1)} %fusion.20), channel_id=1, source_target_pairs={{0,8},{8,16},{16,24},{24,0},{1,9},{9,17},{17,25},{25,1},{2,10},{10... | collective-permute-start | bytes 2654216 | tf_op jit(solution)/shard_map/ppermute | solution.py:673
  1052.0 56.6 %collective-permute-start.58 = (bf16[1152,384]{1,0:T(8,128)(2,1)S(1)}, bf16[1152,384]{1,0:T(8,128)(2,1)S(1)}, u32[]{:S(2)}, u32[]{:S(2)}) collective-permute-start(bf16[1152,384]{1,0:T(8,128)(2,1)S(1)} %fusion.23), channel_id=1, source_target_pairs={{0,8},{8,16},{16,24},{24,0},{1,9},{9,17},{17,25},{25,1},{2,10},{10... | collective-permute-start | bytes 2654216 | tf_op jit(solution)/shard_map/ppermute | solution.py:673
  1070.9 56.6 %collective-permute-start.66 = (bf16[1152,384]{1,0:T(8,128)(2,1)S(1)}, bf16[1152,384]{1,0:T(8,128)(2,1)S(1)}, u32[]{:S(2)}, u32[]{:S(2)}) collective-permute-start(bf16[1152,384]{1,0:T(8,128)(2,1)S(1)} %fusion.18), channel_id=1, source_target_pairs={{0,8},{8,16},{16,24},{24,0},{1,9},{9,17},{17,25},{25,1},{2,10},{10... | collective-permute-start | bytes 2654216 | tf_op jit(solution)/shard_map/ppermute | solution.py:673
  (68 other events, 2487.6 us)
Sparse Core Ops, SparseCore 0:
  10.9 112.1 all-gather.2
  170.7 99.3 all-gather.4
  861.8 118.0 reduce-scatter.4
  986.3 261.5 reduce-scatter.2

commit v2 on v1

--- a/solution.py
+++ b/solution.py
@@ -18,6 +18,7 @@
 FFN_CHUNK = 768
 FFN_PARTS = 2
 WG_TILE = 384
+PACE = 0.15
 LOG2E = 1.0 / math.log(2.0)
 
 
@@ -334,7 +335,7 @@
 
 
 def cost(flops, moved, trans=0):
-    return pl.CostEstimate(flops=int(flops), bytes_accessed=int(moved), transcendentals=int(trans))
+    return pl.CostEstimate(flops=int(flops * PACE), bytes_accessed=int(moved * PACE), transcendentals=int(trans * PACE))
 
 
 def params(mib):
@@ -345,31 +346,66 @@
     return 0.5 * jnp.tanh(0.5 * v) + 0.5
 
 
-def ffn_body(n_ref, c_ref, wg_ref, wu_ref, wd_ref, hid_ref, dg_ref, du_ref, f_ref, dn_ref, f_acc, dn_acc):
+def ffn_copies(chunk, pieces, held, sems):
+    units = pieces[0].shape[1]
+    tile = FFN_CHUNK // 2
+    slot = chunk % 2
+    copies = []
+    for part in range(2):
+        column = chunk * FFN_CHUNK + part * tile
+        owner, inside = column // units, column % units
+        for kind in range(3):
+            copies.append(
+                pltpu.make_async_copy(
+                    pieces[3 * owner + kind].at[:, pl.ds(inside, tile)],
+                    held.at[slot, kind, :, pl.ds(part * tile, tile)],
+                    sems.at[slot, part * 3 + kind],
+                )
+            )
+    return copies
+
+
+def ffn_body(n_ref, c_ref, *refs):
+    pieces = refs[:6]
+    hid_ref, dg_ref, du_ref, f_ref, dn_ref, f_acc, dn_acc, held, sems = refs[6:]
     step = pl.program_id(0)
+    chunks = 2 * pieces[0].shape[1] // FFN_CHUNK
 
     @pl.when(step == 0)
     def _():
+        for copy in ffn_copies(0, pieces, held, sems):
+            copy.start()
         f_acc[...] = jnp.zeros_like(f_acc)
         dn_acc[...] = jnp.zeros_like(dn_acc)
 
+    for chunk in range(chunks):
+
+        @pl.when(step == chunk)
+        def _():
+            if chunk + 1 < chunks:
+                for copy in ffn_copies(chunk + 1, pieces, held, sems):
+                    copy.start()
+            for copy in ffn_copies(chunk, pieces, held, sems):
+                copy.wait()
+
+    slot = step % 2
     rows = n_ref.shape[0]
     part = rows // FFN_PARTS
     for index in range(FFN_PARTS):
         take = pl.ds(index * part, part)
-        gate = dot_nn(n_ref[take, :], wg_ref[...])
-        upward = dot_nn(n_ref[take, :], wu_ref[...])
+        gate = dot_nn(n_ref[take, :], held[slot, 0])
+        upward = dot_nn(n_ref[take, :], held[slot, 1])
         sigma = sigmoid(gate)
         swish = gate * sigma
         hidden = (swish * upward).astype(jnp.bfloat16)
         hid_ref[take, :] = hidden
-        grad_hidden = dot_nt(c_ref[take, :], wd_ref[...])
+        grad_hidden = dot_nn(c_ref[take, :], held[slot, 2])
         grad_gate = (grad_hidden * upward * sigma * (1.0 + gate * (1.0 - sigma))).astype(jnp.bfloat16)
         grad_up = (grad_hidden * swish).astype(jnp.bfloat16)
         dg_ref[take, :] = grad_gate
         du_ref[take, :] = grad_up
-        f_acc[take, :] += dot_nn(hidden, wd_ref[...])
-        dn_acc[take, :] += dot_nt(grad_gate, wg_ref[...]) + dot_nt(grad_up, wu_ref[...])
+        f_acc[take, :] += dot_nt(hidden, held[slot, 2])
+        dn_acc[take, :] += dot_nt(grad_gate, held[slot, 0]) + dot_nt(grad_up, held[slot, 1])
 
     @pl.when(step == pl.num_programs(0) - 1)
     def _():
@@ -377,43 +413,42 @@
         dn_ref[...] = dn_acc[...].astype(dn_ref.dtype)
 
 
-def ffn_block(normed, cotan, w_gate, w_up, w_down):
+def ffn_block(normed, cotan, pieces):
     rows, width = normed.shape
-    units = w_gate.shape[1]
+    units = 2 * pieces[0].shape[1]
     chunk = FFN_CHUNK
-    steps = units // chunk
     whole = pl.BlockSpec((rows, width), lambda j: (0, 0))
     tall = pl.BlockSpec((rows, chunk), lambda j: (0, j))
     low = jnp.bfloat16
     return pl.pallas_call(
         ffn_body,
-        grid=(steps,),
-        in_specs=[
-            whole,
-            whole,
-            pl.BlockSpec((width, chunk), lambda j: (0, j)),
-            pl.BlockSpec((width, chunk), lambda j: (0, j)),
-            pl.BlockSpec((chunk, width), lambda j: (j, 0)),
-        ],
+        grid=(units // chunk,),
+        in_specs=[whole, whole] + [pl.BlockSpec(memory_space=pl.ANY)] * len(pieces),
         out_specs=[tall, tall, tall, whole, whole],
         out_shape=[jax.ShapeDtypeStruct((rows, units), low)] * 3
         + [jax.ShapeDtypeStruct((rows, width), low)] * 2,
-        scratch_shapes=[pltpu.VMEM((rows, width), jnp.float32)] * 2,
+        scratch_shapes=[pltpu.VMEM((rows, width), jnp.float32)] * 2
+        + [pltpu.VMEM((2, 3, width, chunk), low), pltpu.SemaphoreType.DMA((2, len(pieces)))],
         compiler_params=params(60),
         cost_estimate=cost(12 * rows * width * units, 6 * width * units + 6 * rows * (width + units)),
         name="ffn_block",
-    )(normed, cotan, w_gate, w_up, w_down)
-
-
-def wgrad_body(*refs):
-    count = (len(refs) - 1) // 2
-    out_ref = refs[-1]
-    slots, wide = out_ref.shape[1], out_ref.shape[3]
+    )(normed, cotan, *pieces)
+
+
+def wgrad_body(per_half, *refs):
+    count = (len(refs) - 2) // 2
     total = dot_tn(refs[0][...], refs[count][...])
     for index in range(1, count):
         total = total + dot_tn(refs[index][...], refs[count + index][...])
-    for slot in range(slots):
-        out_ref[0, slot] = total[:, slot * wide : (slot + 1) * wide].astype(out_ref.dtype)
+
+    def store(out_ref):
+        slots, _, wide = out_ref.shape
+        for slot in range(slots):
+            out_ref[slot] = total[:, slot * wide : (slot + 1) * wide].astype(out_ref.dtype)
+
+    first = pl.program_id(0) < per_half
+    pl.when(first)(lambda: store(refs[-2]))
+    pl.when(jnp.logical_not(first))(lambda: store(refs[-1]))
 
 
 def wgrad(lefts, rights, slots):
@@ -424,12 +459,15 @@
     wide = width // slots
     count = len(lefts)
     return pl.pallas_call(
-        wgrad_body,
+        lambda *refs: wgrad_body(per_half, *refs),
         grid=(units // tile,),
         in_specs=[pl.BlockSpec((rows, tile), lambda j: (0, j))] * count
         + [pl.BlockSpec((rows, width), lambda j: (0, 0))] * count,
-        out_specs=pl.BlockSpec((1, slots, tile, wide), lambda j: (j // per_half, 0, j % per_half, 0)),
-        out_shape=jax.ShapeDtypeStruct((2, slots, units // 2, wide), jnp.bfloat16),
+        out_specs=[
+            pl.BlockSpec((slots, tile, wide), lambda j: (0, jnp.minimum(j, per_half - 1), 0)),
+            pl.BlockSpec((slots, tile, wide), lambda j: (0, jnp.maximum(j - per_half, 0), 0)),
+        ],
+        out_shape=[jax.ShapeDtypeStruct((slots, units // 2, wide), jnp.bfloat16)] * 2,
         compiler_params=params(60),
         cost_estimate=cost(2 * count * rows * width * units, 2 * count * rows * (width + units)),
         name="ffn_wgrad",
@@ -640,7 +678,7 @@
         in_specs=[
             pl.BlockSpec((tile, width), moving),
             pl.BlockSpec((1, width), fixed),
-            pl.BlockSpec(w_qkv.shape, fixed),
+            pl.BlockSpec((width, qwidth + kwidth), fixed),
             pl.BlockSpec((1, qwidth + kwidth), fixed),
             pl.BlockSpec((tile, HEAD), moving),
             pl.BlockSpec((tile, HEAD), moving),
@@ -661,6 +699,96 @@
     )(inputs, gain, w_qkv, bias, cosine, sine)
 
 
+def spread_body(own, rows, whole, rows_x, rows_y, rows_d, sent, landed, kept):
+    me, plane = lax.axis_index("gy"), lax.axis_index("gx")
+    core = me + 1 - 2 * lax.rem(me, 2)
+    along_x = me + 2 - 4 * lax.rem(me // 2, 2)
+    along_y = me + 4 - 8 * (me // 4)
+    across = along_x + 4 - 8 * (along_x // 4)
+    places = [lax.rem(plane + 4 - k, 4) for k in range(4)]
+    ahead = [lax.rem(plane + k, 4) for k in range(4)]
+    barrier = pltpu.get_barrier_semaphore()
+    peers = [{"gy": core}, {"gy": along_x}, {"gy": along_y}] + [{"gx": ahead[k]} for k in (1, 2, 3)]
+    for peer in peers:
+        pl.semaphore_signal(barrier, inc=1, device_id=peer, device_id_type=pl.DeviceIdType.MESH)
+    pl.semaphore_wait(barrier, len(peers))
+    copies = []
+
+    def send(source, target, peer):
+        copy = pltpu.make_async_remote_copy(
+            source,
+            target,
+            sent.at[len(copies)],
+            landed.at[len(copies)],
+            device_id=peer,
+            device_id_type=pl.DeviceIdType.MESH,
+        )
+        copies.append(copy)
+        copy.start()
+        return copy
+
+    to_core, to_x, to_y = peers[:3]
+    from_z = [send(own, whole.at[plane, me], peers[2 + k]) for k in (1, 2, 3)]
+    local = pltpu.make_async_copy(own, whole.at[plane, me], kept)
+    local.start()
+    from_x, from_y, from_d, from_core = [], [], [], []
+    for k in range(4):
+        block = whole.at[places[k], me]
+        source = own if k == 0 else block
+        if k > 0:
+            from_z[k - 1].wait_recv()
+        from_x.append(send(source, block, to_x))
+        from_y.append(send(source, block, to_y))
+        from_core.append(send(source, block, to_core))
+    moved_x, moved_y = send(rows, rows_x, to_x), send(rows, rows_y, to_y)
+    for k in range(4):
+        block_x, block_y = whole.at[places[k], along_x], whole.at[places[k], along_y]
+        from_x[k].wait_recv()
+        if k < 2:
+            from_d.append(send(block_x, block_x, to_y))
+        from_core.append(send(block_x, block_x, to_core))
+        from_y[k].wait_recv()
+        if k >= 2:
+            from_d.append(send(block_y, block_y, to_x))
+        from_core.append(send(block_y, block_y, to_core))
+    for k in range(4):
+        block = whole.at[places[k], across]
+        from_d[k].wait_recv()
+        from_core.append(send(block, block, to_core))
+    half = rows.shape[0] // 2
+    first, second = pl.ds(0, half), pl.ds(half, half)
+    moved_x.wait_recv()
+    moved_d = [send(rows_x.at[first], rows_d.at[first], to_y)]
+    moved_y.wait_recv()
+    moved_d.append(send(rows_y.at[second], rows_d.at[second], to_x))
+    for copy in from_core + moved_d:
+        copy.wait_recv()
+    for copy in copies:
+        copy.wait_send()
+    local.wait()
+
+
+def spread(own, rows):
+    deep, wide = own.shape
+    anywhere = pl.BlockSpec(memory_space=pl.ANY)
+    whole, *others = pl.pallas_call(
+        spread_body,
+        in_specs=[anywhere] * 2,
+        out_specs=[anywhere] * 4,
+        out_shape=[jax.ShapeDtypeStruct((4, 8, deep, wide), own.dtype)]
+        + [jax.ShapeDtypeStruct(rows.shape, rows.dtype)] * 3,
+        scratch_shapes=[
+            pltpu.SemaphoreType.DMA((35,)),
+            pltpu.SemaphoreType.DMA((35,)),
+            pltpu.SemaphoreType.DMA,
+        ],
+        compiler_params=pltpu.CompilerParams(collective_id=0, has_side_effects=True),
+        cost_estimate=cost(0, 300 * 1024 * 1024),
+        name="spread",
+    )(own, rows)
+    return whole.reshape(32 * deep, wide), others
+
+
 CORE, ALONG_X, ALONG_Y, ACROSS = 1, 2, 4, 6
 OTHERS = (ALONG_X, ALONG_Y, ACROSS)
 
@@ -679,14 +807,6 @@
 
 def after(array, *earlier):
     return lax.optimization_barrier((array, *earlier))[0]
-
-
-def slot_columns(array, plane):
-    wide = array.shape[-1] // 4
-    return jnp.concatenate(
-        [lax.dynamic_slice_in_dim(array, lax.rem(plane + 4 - s, 4) * wide, wide, array.ndim - 1) for s in range(4)],
-        axis=array.ndim - 1,
-    )
 
 
 def pair_rows(pair, core):
@@ -699,13 +819,6 @@
     kept = lax.dynamic_slice_in_dim(rows, core * half, half, 0)
     got = swap(lax.dynamic_slice_in_dim(rows, (1 - core) * half, half, 0), CORE)
     return jnp.where(core == 0, jnp.stack([kept, got]), jnp.stack([got, kept]))
-
-
-def ring_slots(own):
-    slots = [own]
-    for _ in range(3):
-        slots.append(ring(slots[-1]))
-    return slots
 
 
 def ring_sums(slots):
@@ -723,18 +836,17 @@
     return whole
 
 
-def gather_small(row, plane, me):
-    slots = ring_slots(row)
-    rows = jnp.concatenate(slots)
-    rows = jnp.concatenate([pick(rows, lax.rem(plane + 4 - s, 4))[None] for s in range(4)])[:, None]
-    for level, bits in enumerate((CORE, ALONG_X, ALONG_Y)):
-        other = swap(rows, bits)
-        rows = jnp.where(
-            (me >> level) % 2 == 0,
-            jnp.concatenate([rows, other], axis=1),
-            jnp.concatenate([other, rows], axis=1),
-        )
-    return rows.reshape(32, row.shape[1])
+def sum_rows(rows, plane, me, order):
+    width = rows.shape[1]
+    rows = rows.reshape(4, 2, 2, 2, rows.shape[0] // 32, width)
+    axis = {ALONG_Y: 1, ALONG_X: 2, CORE: 3}
+    for bits in order:
+        bit = (me // bits) % 2
+        kept = lax.dynamic_slice_in_dim(rows, bit, 1, axis[bits])
+        sent = lax.dynamic_slice_in_dim(rows, 1 - bit, 1, axis[bits])
+        rows = (kept.astype(jnp.float32) + swap(sent, bits).astype(jnp.float32)).astype(rows.dtype)
+    rows = rows.reshape(4, -1, width)
+    return ring_sums([pick(rows, lax.rem(plane + 4 - s, 4)) for s in range(4)])
 
 
 def sum_small(rows, plane, me):
@@ -777,40 +889,40 @@
     offset = chip * rows
 
     nb, ng = qkv_bias.shape[0], gain_attn.shape[0]
-    packed = jnp.zeros((1, 256), low)
-    packed = packed.at[0, :nb].set(qkv_bias).at[0, nb : nb + ng].set(gain_attn)
-    packed = packed.at[0, nb + ng : nb + 2 * ng].set(gain_ffn)
-    small = gather_small(packed, plane, me).astype(full)
+    packed = jnp.concatenate([qkv_bias, gain_attn, gain_ffn]).reshape(-1, 1)
+    packed = jnp.pad(packed, ((0, 4 * ng - packed.shape[0]), (0, 0))).reshape(4, ng).T
+    packed = jnp.pad(packed, ((0, 0), (0, HEAD - 4)))
+    attn_own = jnp.concatenate([w_qkv, w_out.T, packed], axis=1)
+
+    inputs_low = pair_rows(tokens, core)
+    grad_low = pair_rows(cotangent, core)
+
+    seg_tree = pick(segment, core)
+    valid, upper_one, upper_two, depth_pos = tree_tables(seg_tree, pick(parent, core))
+    places = jnp.arange(slot_len, dtype=jnp.int32)
+
+    def take_own(array):
+        return lax.dynamic_slice_in_dim(array, offset, rows, 0)
+
+    cosine, sine = rotation(take_own(depth_pos), HEAD)
+    sine = sine * jnp.where(jnp.arange(HEAD) < HEAD // 2, -1.0, 1.0)
+
+    more = pad_units - own_units
+    shards = [jnp.pad(w, ((0, 0), (0, more))) for w in (w_gate, w_up, w_down.T)]
+    weights = [lax.all_gather(w, "gx", axis=0, tiled=True) for w in shards]
+    attn_all, cotan_others = spread(after(attn_own, inputs_low, cosine, sine), grad_low)
+    cotan_blocks = [grad_low] + cotan_others
+    qwide = qwidth + 2 * kwidth
+    small = attn_all[:, qwide + width :].reshape(32, ng, HEAD)[:, :, :4].transpose(0, 2, 1).reshape(32, 4 * ng)
+    small = small.astype(full)
     bias_full = small[:, :nb].reshape(1, -1)
     gain_one = small[:, nb : nb + ng].reshape(1, -1)
     gain_two = small[:, nb + ng : nb + 2 * ng].reshape(1, -1)
-    qkv_full = lax.all_gather(w_qkv, ("gx", "gy"), axis=0, tiled=True)
-    out_full = lax.all_gather(after(w_out, qkv_full), ("gx", "gy"), axis=1, tiled=True)
-
-    inputs_low = pair_rows(tokens, core)
-    grad_low = pair_rows(cotangent, core)
-
-    more = pad_units - own_units
-    gate_slots = ring_slots(jnp.pad(w_gate, ((0, 0), (0, more))))
-    up_slots = ring_slots(jnp.pad(w_up, ((0, 0), (0, more))))
-    down_slots = ring_slots(jnp.pad(w_down, ((0, more), (0, 0))))
-
-    def both_cores(slots, axis):
-        mine = jnp.concatenate(slots, axis=axis)
-        return jnp.concatenate([mine] + [jnp.concatenate([swap(s, CORE) for s in slots], axis=axis)], axis=1 - axis)
-
-    gate_full, up_full = both_cores(gate_slots, 0), both_cores(up_slots, 0)
-    down_full = both_cores(down_slots, 1)
-
-    seg_tree = pick(segment, core)
-    valid, upper_one, upper_two, depth_pos = tree_tables(seg_tree, pick(parent, core))
-    places = jnp.arange(slot_len, dtype=jnp.int32)
-
-    def take_own(array):
-        return lax.dynamic_slice_in_dim(array, offset, rows, 0)
-
+    out_turned = attn_all[:, qwide : qwide + width]
+
+    normed_one, query, keyval_own = project(inputs_low, gain_one, attn_all, bias_full, cosine, sine)
     mask = allowed(
-        take_own(seg_tree), take_own(upper_one), take_own(upper_two), take_own(places), seg_tree, valid, places
+        after(take_own(seg_tree), keyval_own), take_own(upper_one), take_own(upper_two), take_own(places), seg_tree, valid, places
     )
     qblocks, kblocks = rows // QUERY_TILE, slot_len // KEY_TILE
     active = mask.reshape(qblocks, QUERY_TILE, kblocks, KEY_TILE).any(axis=(1, 3))
@@ -820,56 +932,59 @@
     hit = active[:, :, None] & (rank[:, :, None] == numbers[None, None, :])
     block_list = jnp.sum(jnp.where(hit, numbers[None, :, None], 0), axis=1).astype(jnp.int32)
     mask_bias = jnp.where(mask.T, 0.0, NEGATIVE).astype(low)
-    cosine, sine = rotation(take_own(depth_pos), HEAD)
-    sine = sine * jnp.where(jnp.arange(HEAD) < HEAD // 2, -1.0, 1.0)
-
-    normed_one, query, keyval_own = project(inputs_low, gain_one, qkv_full, bias_full, cosine, sine)
+
     keyval = plane_order([keyval_own] + [swap(keyval_own, bits) for bits in OTHERS], chip)
+    other_weights = [swap(after(w, keyval), CORE) for w in weights[:2]]
     heads_out, lse = attend_fast(block_list, block_count, query, keyval, mask_bias)
     inputs = inputs_low.astype(full)
-    resid = inputs + jnp.dot(heads_out, out_full, preferred_element_type=full)
+    resid = inputs + lax.dot_general(heads_out, out_turned, (((1,), (1,)), ((), ())), preferred_element_type=full)
     unit_two, inverse_two, normed_two = norm_parts(resid, gain_two)
 
-    normed_slots = slot_columns(normed_two, plane)
-    cotan_slots = slot_columns(grad_low, plane)
-    normed_blocks = [normed_slots] + [swap(normed_slots, bits) for bits in OTHERS]
-    cotan_blocks = [cotan_slots] + [swap(cotan_slots, bits) for bits in OTHERS]
-    results = []
-    for normed, cotan in zip(normed_blocks, cotan_blocks):
-        if results:
-            normed = after(normed, results[-1][4])
-        results.append(ffn_block(normed, cotan, gate_full, up_full, down_full))
+    other_weights.append(swap(after(weights[2], heads_out), CORE))
+    pieces = weights + other_weights
+    normed_x, normed_y = swap(normed_two, ALONG_X), swap(normed_two, ALONG_Y)
+    results = [ffn_block(normed_two, cotan_blocks[0], pieces)]
+    normed_d = swap(after(normed_two, results[0][4]), ACROSS)
+    normed_blocks = [normed_two, normed_x, normed_y, normed_d]
+    for normed, cotan in zip(normed_blocks[1:], cotan_blocks[1:]):
+        results.append(ffn_block(after(normed, results[-1][4]), cotan, pieces))
     hidden_b, gate_b, up_b, out_b, back_b = zip(*results)
-    grad_normed = [back_b[0]] + [swap(b, bits) for b, bits in zip(back_b[1:], OTHERS)]
-    ffn_out = [out_b[0]] + [swap(after(b, back_b[3]), bits) for b, bits in zip(out_b[1:], OTHERS)]
-    ffn_grads = []
-    for left, right in ((hidden_b, cotan_blocks), (gate_b, normed_blocks), (up_b, normed_blocks)):
-        if ffn_grads:
-            left = (after(left[0], parts),) + left[1:]
-        else:
-            left = (after(left[0], back_b[3]),) + left[1:]
-        parts = wgrad(left, right, 4)
-        mine = parts[0].astype(full) + swap(parts[1], CORE).astype(full)
-        ffn_grads.append(ring_sums(mine.astype(low)))
-    grad_down = ffn_grads[0][:own_units]
-    grad_wgate = ffn_grads[1].T[:, :own_units]
-    grad_wup = ffn_grads[2].T[:, :own_units]
-
-    grad_normed_two = slot_columns(sum(b.astype(full) for b in grad_normed), plane)
+    back_got = [swap(b, bits) for b, bits in zip(back_b[1:], OTHERS)]
+
+    def both_halves(mine, other):
+        mine = (mine.astype(full) + other.astype(full)).astype(low)
+        mine = mine.reshape(-1, mine.shape[-1])
+        return mine, lax.psum_scatter(mine, "gx", scatter_dimension=0, tiled=True).astype(full)
+
+    down_mine, down_sent = wgrad((after(hidden_b[0], back_b[3]),) + hidden_b[1:], cotan_blocks, 4)
+    down_got = swap(down_sent, CORE)
+    gate_mine, gate_sent = wgrad((after(gate_b[0], down_sent, back_got[0]),) + gate_b[1:], normed_blocks, 4)
+    gate_got = swap(gate_sent, CORE)
+    down_sum, grad_down = both_halves(after(down_mine, gate_sent), down_got)
+
+    grad_normed_two = sum(after(b, gate_sent).astype(full) for b in [back_b[0]] + back_got)
     back_two, grad_gain_two = norm_back(grad_normed_two, unit_two, inverse_two, gain_two)
     grad_resid = grad_low.astype(full) + back_two
     grad_branch = grad_resid.astype(low)
-    grad_heads = jnp.dot(grad_branch, out_full.T, preferred_element_type=full).astype(low)
+    grad_heads = jnp.dot(grad_branch, out_turned, preferred_element_type=full).astype(low)
+    grad_wout = jnp.dot(grad_branch.T, heads_out, preferred_element_type=full).astype(low)
+    out_got = [swap(after(b, grad_normed_two), bits) for b, bits in zip(out_b[1:], OTHERS)]
+    gate_sum, grad_wgate = both_halves(gate_mine, gate_got)
+    grad_heads = after(grad_heads, grad_wout, gate_sum, down_sum)
     query_lin, keyval_part = attend_back_fast(
         block_list, block_count, query, keyval, mask_bias, lse, heads_out, grad_heads, cosine, sine
     )
-    grad_wout = jnp.dot(heads_out.T, grad_branch, preferred_element_type=full).astype(low)
-    grad_wout = lax.psum_scatter(grad_wout, ("gx", "gy"), scatter_dimension=1, tiled=True).astype(full)
+
+    grad_wout = sum_rows(grad_wout, plane, me, (CORE, ALONG_X, ALONG_Y)).T
+    up_mine, up_sent = wgrad((after(up_b[0], query_lin),) + up_b[1:], normed_blocks, 4)
+    up_sum, grad_wup = both_halves(up_mine, swap(up_sent, CORE))
+    grad_down = grad_down[:own_units]
+    grad_wgate, grad_wup = grad_wgate.T[:, :own_units], grad_wup.T[:, :own_units]
 
     def part_of(index):
         return lax.dynamic_slice_in_dim(keyval_part, (chip ^ index) * rows, rows, 0)
 
-    keyval_grad = part_of(0).astype(full) + sum(
+    keyval_grad = after(part_of(0), up_sent).astype(full) + sum(
         swap(part_of(index + 1), bits).astype(full) for index, bits in enumerate(OTHERS)
     )
     keys_grad = keyval_grad[:, :kwidth].reshape(rows, KV_HEADS, HEAD)
@@ -877,13 +992,21 @@
     keyval_lin = jnp.concatenate([keys_lin.reshape(rows, kwidth), keyval_grad[:, kwidth:]], axis=1).astype(low)
     grad_linear = jnp.concatenate([query_lin, keyval_lin], axis=1)
     grad_wqkv = jnp.dot(normed_one.T, grad_linear, preferred_element_type=full).astype(low)
-    grad_wqkv = lax.psum_scatter(grad_wqkv, ("gx", "gy"), scatter_dimension=0, tiled=True).astype(full)
+    middle = grad_wqkv.shape[1] // 2
+    grad_wqkv = jnp.concatenate(
+        [
+            sum_rows(grad_wqkv[:, :middle], plane, me, (CORE, ALONG_X, ALONG_Y)),
+            sum_rows(grad_wqkv[:, middle:], plane, me, (CORE, ALONG_Y, ALONG_X)),
+        ],
+        axis=1,
+    )
     grad_bias = jnp.sum(grad_linear.astype(full), axis=0)
-    grad_normed_one = jnp.dot(grad_linear, qkv_full.T, preferred_element_type=full)
+    grad_normed_one = jnp.dot(grad_linear, attn_all[:, :qwide].T, preferred_element_type=full)
     unit_one, inverse_one, _ = norm_parts(inputs, gain_one)
     back_one, grad_gain_one = norm_back(grad_normed_one, unit_one, inverse_one, gain_one)
     grad_tokens = unpair_rows((grad_resid + back_one).astype(low), core)
-    layer_out = unpair_rows((resid + slot_columns(sum(b.astype(full) for b in ffn_out), plane)).astype(low), core)
+    ffn_out = sum(after(b, query_lin).astype(full) for b in [out_b[0]] + out_got)
+    layer_out = unpair_rows((resid + ffn_out).astype(low), core)
 
     packed = jnp.concatenate(
         [grad_bias.reshape(32, nb), grad_gain_one.reshape(32, ng), grad_gain_two.reshape(32, ng)], axis=1

time: 1270 us -> 934 us (0.74)
  waiting for transfers between devices: 577 us -> 196 us
  Pallas kernels: 285 us -> 449 us
  other arithmetic: 168 us -> 76 us
  starting transfers between devices: 128 us -> 107 us
    ppermute x24 -> x12, waiting for transfers between devices: 295 us -> 42.3 us  [ring(): return lax.ppermute(array, 'gx', [(i, (i + 1) % 4) for i in range(4)])]
    pallas_call x7 -> x8, Pallas kernels: 237 us -> 403 us  [the longest x1 161 us: spread(): pl.pallas_call(spread_body, in_specs=[anywhere] * 2, out_specs=[anywhere]...]
    reduce_scatter x2 -> x3, waiting for transfers between devices: 117 us -> 0.69 us  [both_halves(): lax.psum_scatter(mine, 'gx', scatter_dimension=0, tiled=True).astype(full)]
    concatenate x6 -> x3, other arithmetic: 97.6 us -> 2.7 us  [the longest x1 1.85 us: on_core(): attn_own = jnp.concatenate([w_qkv, w_out.T, packed], axis=1)]
    ppermute x43 -> x37, starting transfers between devices: 107 us -> 82.7 us  [swap(): return lax.ppermute(array, 'gy', [(i, i ^ bits) for i in range(8)])]
    convert_element_type x6 -> x14, other arithmetic: 13.6 us -> 29 us  [the longest x3 14.3 us: both_halves(): mine = (mine.astype(full) + other.astype(full)).astype(low)]
    ppermute x43 -> x37, waiting for transfers between devices: 164 us -> 152 us  [swap(): return lax.ppermute(array, 'gy', [(i, i ^ bits) for i in range(8)])]
  transfers between devices with their start and end apart: 71 -> 55, of which waited for: 29 -> 24; matrix products, arithmetic and copies ran while one was open for 19% -> 15% of each run, Pallas kernels for 23% -> 46%
where the time goes in v2:
time: 934 us; the launch traced here: 921 us
  Pallas kernels  449 us (48%)
  waiting for transfers between devices  196 us (21%)
  starting transfers between devices  107 us (11%)
  other arithmetic  76 us (8%)
  local copies, waits for them, and re-layouts  40.1 us (4%)
  matrix products  37.4 us (4%)
  between operations  15.6 us (2%)
    pallas_call x1, Pallas kernels, spread(): pl.pallas_call(spread_body, in_specs=[anywhere] * 2, out_specs=[anywhere]...  161 us
    ppermute x37, waiting for transfers between devices, swap(): return lax.ppermute(array, 'gy', [(i, i ^ bits) for i in range(8)])  152 us
    pallas_call x4, Pallas kernels, ffn_block(): pl.pallas_call(ffn_body, grid=(units // chunk,), in_specs=[whole, whole]...  152 us
    pallas_call x3, Pallas kernels, wgrad(): pl.pallas_call(lambda *refs: wgrad_body(per_half, *refs), grid=(units //...  89.5 us
    ppermute x37, starting transfers between devices, swap(): return lax.ppermute(array, 'gy', [(i, i ^ bits) for i in range(8)])  82.7 us
    ppermute x12, waiting for transfers between devices, ring(): return lax.ppermute(array, 'gx', [(i, (i + 1) % 4) for i in range(4)])  42.3 us
    ppermute x12, starting transfers between devices, ring(): return lax.ppermute(array, 'gx', [(i, (i + 1) % 4) for i in range(4)])  24.2 us
    pallas_call x1, Pallas kernels, attend_back_fast(): pl.pallas_call(attend_back_body, grid_spec=pltpu.PrefetchScalarGridSpec(n...  23.4 us
  transfers between devices with their start and end apart: 55, of which 24 were waited for; matrix products, arithmetic and copies ran while one was open for 15% of the time, Pallas kernels for 46%

profile of v2, /device:TPU:9, one launch (start us, length us, event | category | flops | bytes accessed | tf_op | source)
XLA Modules:
  0.0 921.4 jit_solution(10676889361240998678)
XLA Ops:
  27.3 3.5 fusion.18
  30.8 3.4 maximum_select_fusion.1.rows.c_ref.refs_4_
  34.1 161.5 %spread.1 = (bf16[4,8,48,3712]{3,2,1,0:T(8,128)(2,1)}, bf16[640,1536]{1,0:T(8,128)(2,1)}, bf16[640,1536]{1,0:T(8,128)(2,1)}, bf16[640,1536]{1,0:T(8,128)(2,1)}) custom-call(bf16[48,3712]{1,0:T(8,128)(2,1)} %fusion.28.own, bf16[640,1536]{1,0:T(8,128)(2,1)} %maximum_select_fusion.1.rows.c_ref.refs_4_), custom_call_target="tpu_custom_call" | custom-call | bytes 47185920 | tf_op jit(solution)/shard_map/spread/pallas_call | solution.py:774
  197.4 9.1 project.1
  210.5 4.3 select_convert_fusion.bias_ref
  214.8 5.1 or_reduce_fusion
  225.0 11.9 %collective-permute-done.4 = bf16[640,512]{1,0:T(8,128)(2,1)} collective-permute-done((bf16[640,512]{1,0:T(8,128)(2,1)S(1)}, bf16[640,512]{1,0:T(8,128)(2,1)}, u32[]{:S(2)}, u32[]{:S(2)}) %collective-permute-start.4) | collective-permute-done | bytes 655392 | tf_op jit(solution)/shard_map/ppermute | solution.py:797
  239.5 14.2 %tree_attention.1 = (bf16[640,1536]{1,0:T(8,128)(2,1)S(1)}, f32[5,2,1,768]{3,2,1,0:T(1,128)S(1)}) custom-call(s32[5,10]{1,0:T(8,128)S(1)} %select_reduce_fusion.5.list_ref, s32[5]{0:T(128)S(1)} %convert_reduce_fusion.2.count_ref, bf16[640,1536]{1,0:T(8,128)(2,1)S(1)} %get-tuple-element.77.q_ref, bf16[2560,512]{1,0:T(8,128)(2,1)} %copy-done.20, ...), custom_call_target="tpu_custom_call" | custom-call | flops 1509949440 | bytes 983040 | tf_op jit(solution)/shard_map/tree_attention/pallas_call | solution.py:527
  255.1 3.7 collective-permute-start.7
  259.4 6.9 multiply_reduce_fusion.2
  268.2 14.6 %collective-permute-start.10 = (bf16[640,1536]{1,0:T(8,128)(2,1)S(1)}, bf16[640,1536]{1,0:T(8,128)(2,1)}, u32[]{:S(2)}, u32[]{:S(2)}) collective-permute-start(bf16[640,1536]{1,0:T(8,128)(2,1)S(1)} %multiply_convert_fusion.n_ref.refs_4_), channel_id=1, source_target_pairs={{0,2},{1,3},{2,0},{3,1},{4,6},{5,7},{6,4},{7,5},{8,10},{9,11},{10,... | collective-permute-start | bytes 5898248 | tf_op jit(solution)/shard_map/ppermute | solution.py:797
  282.8 9.3 %collective-permute-start.9 = (bf16[640,1536]{1,0:T(8,128)(2,1)S(1)}, bf16[640,1536]{1,0:T(8,128)(2,1)}, u32[]{:S(2)}, u32[]{:S(2)}) collective-permute-start(bf16[640,1536]{1,0:T(8,128)(2,1)S(1)} %multiply_convert_fusion.n_ref.refs_4_), channel_id=1, source_target_pairs={{0,4},{1,5},{2,6},{3,7},{4,0},{5,1},{6,2},{7,3},{8,12},{9,13},{10,... | collective-permute-start | bytes 5898248 | tf_op jit(solution)/shard_map/ppermute | solution.py:797
  292.2 38.0 %ffn_block.4 = (bf16[640,2304]{1,0:T(8,128)(2,1)}, bf16[640,2304]{1,0:T(8,128)(2,1)}, bf16[640,2304]{1,0:T(8,128)(2,1)}, bf16[640,1536]{1,0:T(8,128)(2,1)}, bf16[640,1536]{1,0:T(8,128)(2,1)}) custom-call(bf16[640,1536]{1,0:T(8,128)(2,1)} %copy-done.15, bf16[640,1536]{1,0:T(8,128)(2,1)} %maximum_select_fusion.1.rows.c_ref.refs_4_, ...), custom_call_target="tpu_custom_call" | custom-call | flops 4076863488 | bytes 5396889 | tf_op jit(solution)/shard_map/ffn_block/pallas_call | solution.py:423
  330.2 6.7 collective-permute-start.8
  336.9 37.9 %ffn_block.5 = (bf16[640,2304]{1,0:T(8,128)(2,1)}, bf16[640,2304]{1,0:T(8,128)(2,1)}, bf16[640,2304]{1,0:T(8,128)(2,1)}, bf16[640,1536]{1,0:T(8,128)(2,1)}, bf16[640,1536]{1,0:T(8,128)(2,1)}) custom-call(bf16[640,1536]{1,0:T(8,128)(2,1)} %collective-permute-done.10.n_ref.refs_5_, bf16[640,1536]{1,0:T(8,128)(2,1)} %get-tuple-element.89.c_ref.refs_5_, ...), custom_call_target="tpu_custom_call" | custom-call | flops 4076863488 | bytes 5396889 | tf_op jit(solution)/shard_map/ffn_block/pallas_call | solution.py:423
  376.0 38.0 %ffn_block.6 = (bf16[640,2304]{1,0:T(8,128)(2,1)}, bf16[640,2304]{1,0:T(8,128)(2,1)}, bf16[640,2304]{1,0:T(8,128)(2,1)}, bf16[640,1536]{1,0:T(8,128)(2,1)}, bf16[640,1536]{1,0:T(8,128)(2,1)}) custom-call(bf16[640,1536]{1,0:T(8,128)(2,1)} %collective-permute-done.9.n_ref.refs_6_, bf16[640,1536]{1,0:T(8,128)(2,1)} %get-tuple-element.92.c_ref.refs_6_, ...), custom_call_target="tpu_custom_call" | custom-call | flops 4076863488 | bytes 5396889 | tf_op jit(solution)/shard_map/ffn_block/pallas_call | solution.py:423
  414.0 37.8 %ffn_block.7 = (bf16[640,2304]{1,0:T(8,128)(2,1)}, bf16[640,2304]{1,0:T(8,128)(2,1)}, bf16[640,2304]{1,0:T(8,128)(2,1)}, bf16[640,1536]{1,0:T(8,128)(2,1)}, bf16[640,1536]{1,0:T(8,128)(2,1)}) custom-call(bf16[640,1536]{1,0:T(8,128)(2,1)} %collective-permute-done.8.n_ref.refs_7_, bf16[640,1536]{1,0:T(8,128)(2,1)} %get-tuple-element.95.c_ref.refs_7_, ...), custom_call_target="tpu_custom_call" | custom-call | flops 4076863488 | bytes 5396889 | tf_op jit(solution)/shard_map/ffn_block/pallas_call | solution.py:423
  451.8 29.7 %ffn_wgrad.3 = (bf16[4,1152,384]{2,1,0:T(8,128)(2,1)}, bf16[4,1152,384]{2,1,0:T(8,128)(2,1)}) custom-call(bf16[640,2304]{1,0:T(8,128)(2,1)} %get-tuple-element.97.refs_0_, bf16[640,2304]{1,0:T(8,128)(2,1)} %get-tuple-element.98.refs_1_, bf16[640,2304]{1,0:T(8,128)(2,1)} %get-tuple-element.99.refs_2_, bf16[640,2304]{1,0:T(8,128)(2,1)} %get-tuple-element.100.refs_3_, ...), custom_call_target="tpu_custom_call" | custom-call | flops 2717908992 | bytes 2949120 | tf_op jit(solution)/shard_map/ffn_wgrad/pallas_call | solution.py:461
  481.5 30.0 %ffn_wgrad.4 = (bf16[4,1152,384]{2,1,0:T(8,128)(2,1)}, bf16[4,1152,384]{2,1,0:T(8,128)(2,1)}) custom-call(bf16[640,2304]{1,0:T(8,128)(2,1)} %get-tuple-element.102.refs_0_, bf16[640,2304]{1,0:T(8,128)(2,1)} %get-tuple-element.103.refs_1_, bf16[640,2304]{1,0:T(8,128)(2,1)} %get-tuple-element.104.refs_2_, bf16[640,2304]{1,0:T(8,128)(2,1)} %get-tuple-element.105.refs_3_, ...), custom_call_target="tpu_custom_call" | custom-call | flops 2717908992 | bytes 2949120 | tf_op jit(solution)/shard_map/ffn_wgrad/pallas_call | solution.py:461
  513.8 4.6 collective-permute-done.14
  518.4 4.7 add_convert_fusion.2
  525.0 74.2 %collective-permute-done.12 = bf16[640,1536]{1,0:T(8,128)(2,1)} collective-permute-done((bf16[640,1536]{1,0:T(8,128)(2,1)}, bf16[640,1536]{1,0:T(8,128)(2,1)}, u32[]{:S(2)}, u32[]{:S(2)}) %collective-permute-start.12) | collective-permute-done | bytes 1966112 | tf_op jit(solution)/shard_map/ppermute | solution.py:797
  599.2 6.4 multiply_reduce_fusion
  609.8 4.5 convolution_convert_fusion.1
  614.3 8.4 fusion.21.do_ref
  626.9 4.7 add_convert_fusion.1
  631.7 23.4 %tree_attention_back.1 = (bf16[640,1536]{1,0:T(8,128)(2,1)}, bf16[2560,512]{1,0:T(8,128)(2,1)}) custom-call(s32[5,10]{1,0:T(8,128)} %copy-done.5, s32[5]{0:T(128)} %copy-done.6, bf16[640,1536]{1,0:T(8,128)(2,1)} %copy-done.4, bf16[2560,512]{1,0:T(8,128)(2,1)} %copy-done.20, bf16[2560,640]{1,0:T(8,128)(2,1)} %select_convert_fusion.bias_ref, ...), custom_call_target="tpu_custom_call" | custom-call | flops 3774873600 | bytes 1966080 | tf_op jit(solution)/shard_map/tree_attention_back/pallas_call | solution.py:618
  655.1 29.9 %ffn_wgrad.5 = (bf16[4,1152,384]{2,1,0:T(8,128)(2,1)}, bf16[4,1152,384]{2,1,0:T(8,128)(2,1)}) custom-call(bf16[640,2304]{1,0:T(8,128)(2,1)} %get-tuple-element.128.refs_0_, bf16[640,2304]{1,0:T(8,128)(2,1)} %get-tuple-element.129.refs_1_, bf16[640,2304]{1,0:T(8,128)(2,1)} %get-tuple-element.130.refs_2_, bf16[640,2304]{1,0:T(8,128)(2,1)} %get-tuple-element.131.refs_3_, ...), custom_call_target="tpu_custom_call" | custom-call | flops 2717908992 | bytes 2949120 | tf_op jit(solution)/shard_map/ffn_wgrad/pallas_call | solution.py:461
  686.8 14.1 %collective-permute-start.20 = (bf16[640,512]{1,0:T(8,128)(2,1)}, bf16[640,512]{1,0:T(8,128)(2,1)S(1)}, u32[]{:S(2)}, u32[]{:S(2)}) collective-permute-start(bf16[640,512]{1,0:T(8,128)(2,1)} %get-tuple-element.156), channel_id=1, source_target_pairs={{0,2},{1,3},{2,0},{3,1},{4,6},{5,7},{6,4},{7,5},{8,10},{9,11},{10,... | collective-permute-start | bytes 1966088 | tf_op jit(solution)/shard_map/ppermute | solution.py:797
  701.0 10.9 %collective-permute-start.21 = (bf16[640,512]{1,0:T(8,128)(2,1)}, bf16[640,512]{1,0:T(8,128)(2,1)S(1)}, u32[]{:S(2)}, u32[]{:S(2)}) collective-permute-start(bf16[640,512]{1,0:T(8,128)(2,1)} %get-tuple-element.155), channel_id=1, source_target_pairs={{0,4},{1,5},{2,6},{3,7},{4,0},{5,1},{6,2},{7,3},{8,12},{9,13},{10,... | collective-permute-start | bytes 1966088 | tf_op jit(solution)/shard_map/ppermute | solution.py:797
  713.1 5.1 add_convert_fusion.4
  720.6 19.2 %collective-permute-done.21 = bf16[640,512]{1,0:T(8,128)(2,1)S(1)} collective-permute-done((bf16[640,512]{1,0:T(8,128)(2,1)}, bf16[640,512]{1,0:T(8,128)(2,1)S(1)}, u32[]{:S(2)}, u32[]{:S(2)}) %collective-permute-start.21) | collective-permute-done | bytes 655392 | tf_op jit(solution)/shard_map/ppermute | solution.py:797
  745.3 10.5 %fusion.17 = (f32[1536]{0:T(1024)S(1)}, f32[640]{0:T(1024)S(1)}, f32[640,1536]{1,0:T(8,128)}) fusion(bf16[640,1536]{1,0:T(8,128)(2,1)} %get-tuple-element.149.x_ref, f32[640]{0:T(1024)S(1)} %copy-done.35, f32[1536]{0:T(1024)S(1)} %copy-done.33, bf16[1536,3712]{1,0:T(8,128)(2,1)} %bitcast.129, bf16[640,256]{1,0:T(8,128)(2,1)S(1)} %slice.144, ...), kind=kOutput, calls=%fused_computation.31 | convolution fusion | flops 4041275392 | bytes 14828544 | tf_op jit(solution)/shard_map/dot_general | solution.py:1004
  756.5 7.1 convolution_convert_fusion
  789.0 3.2 maximum_select_fusion.2
  793.9 19.3 %collective-permute-done.43 = bf16[4,2,1,1,48,1536]{5,4,3,2,1,0:T(8,128)(2,1)S(1)} collective-permute-done((bf16[4,2,1,1,48,1536]{5,4,3,2,1,0:T(8,128)(2,1)S(1)}, bf16[4,2,1,1,48,1536]{5,4,3,2,1,0:T(8,128)(2,1)S(1)}, u32[]{:S(2)}, u32[]{:S(2)}) %collective-permute-start.43) | collective-permute-done | bytes 1179680 | tf_op jit(solution)/shard_map/ppermute | solution.py:797
  815.4 4.8 add_convert_fusion
  820.2 8.4 collective-permute-done.44
  834.9 6.6 collective-permute-done.45
  841.6 3.8 collective-permute-start.46
  847.6 8.7 collective-permute-done.46
  859.9 5.0 collective-permute-done.31
  869.0 4.4 collective-permute-done.26
  874.8 6.2 collective-permute-done.27
  883.4 3.3 collective-permute-done.33
  886.7 3.3 collective-permute-start.34
  891.5 3.8 collective-permute-start.29
  900.8 3.2 collective-permute-done.29
  (308 shorter events, 128.6 us)
Async XLA Ops:
  7.2 247.9 %all-gather.8.cloned.1.call-start = ((), (), s32[]{:S(2)}) async-start(), calls=%async_computation.5 | async-start | bytes 4423680 | tf_op jit(solution)/shard_map/all_gather | solution.py:912
  9.9 248.9 %all-gather.4.cloned.1.call-start = ((), (), s32[]{:S(2)}) async-start(), calls=%async_computation.3 | async-start | bytes 4423680 | tf_op jit(solution)/shard_map/all_gather | solution.py:912
  12.5 246.5 %all-gather.6.cloned.1.call-start = ((), (), s32[]{:S(2)}) async-start(), calls=%async_computation.4 | async-start | bytes 4423680 | tf_op jit(solution)/shard_map/all_gather | solution.py:912
  15.1 15.6 %collective-permute-start.1 = (bf16[320,1536]{1,0:T(8,128)(2,1)}, bf16[320,1536]{1,0:T(8,128)(2,1)}, u32[]{:S(2)}, u32[]{:S(2)}) collective-permute-start(bf16[320,1536]{1,0:T(8,128)(2,1)} %get-tuple-element.162), channel_id=1, source_target_pairs={{0,1},{1,0},{2,3},{3,2},{4,5},{5,4},{6,7},{7,6},{8,9},{9,8},{10,11... | collective-permute-start | bytes 2949128 | tf_op jit(solution)/shard_map/ppermute | solution.py:797
  18.4 8.9 collective-permute-start
  21.2 885.1 %reduce-scatter.4.cloned.1.call-start = ((), (), s32[]{:S(2)}) async-start(), calls=%async_computation.6 | async-start | bytes 4423680 | tf_op jit(solution)/shard_map/reduce_scatter | solution.py:957
  207.9 14.8 %collective-permute-start.2 = (bf16[640,512]{1,0:T(8,128)(2,1)S(1)}, bf16[640,512]{1,0:T(8,128)(2,1)}, u32[]{:S(2)}, u32[]{:S(2)}) collective-permute-start(bf16[640,512]{1,0:T(8,128)(2,1)S(1)} %get-tuple-element.75), channel_id=1, source_target_pairs={{0,2},{1,3},{2,0},{3,1},{4,6},{5,7},{6,4},{7,5},{8,10},{9,11},{10,... | collective-permute-start | bytes 1966088 | tf_op jit(solution)/shard_map/ppermute | solution.py:797
  208.2 15.7 %collective-permute-start.3 = (bf16[640,512]{1,0:T(8,128)(2,1)S(1)}, bf16[640,512]{1,0:T(8,128)(2,1)}, u32[]{:S(2)}, u32[]{:S(2)}) collective-permute-start(bf16[640,512]{1,0:T(8,128)(2,1)S(1)} %get-tuple-element.75), channel_id=1, source_target_pairs={{0,4},{1,5},{2,6},{3,7},{4,0},{5,1},{6,2},{7,3},{8,12},{9,13},{10,... | collective-permute-start | bytes 1966088 | tf_op jit(solution)/shard_map/ppermute | solution.py:797
  209.4 27.5 %collective-permute-start.4 = (bf16[640,512]{1,0:T(8,128)(2,1)S(1)}, bf16[640,512]{1,0:T(8,128)(2,1)}, u32[]{:S(2)}, u32[]{:S(2)}) collective-permute-start(bf16[640,512]{1,0:T(8,128)(2,1)S(1)} %get-tuple-element.75), channel_id=1, source_target_pairs={{0,6},{1,7},{2,4},{3,5},{4,2},{5,3},{6,0},{7,1},{8,14},{9,15},{10,... | collective-permute-start | bytes 1966088 | tf_op jit(solution)/shard_map/ppermute | solution.py:797
  255.1 37.1 %collective-permute-start.7 = (bf16[1536,1152]{1,0:T(8,128)(2,1)}, bf16[1536,1152]{1,0:T(8,128)(2,1)}, u32[]{:S(2)}, u32[]{:S(2)}) collective-permute-start(bf16[1536,1152]{1,0:T(8,128)(2,1)} %all-gather.8.cloned.1.call-done.refs_2_), channel_id=1, source_target_pairs={{0,1},{1,0},{2,3},{3,2},{4,5},{5,4},{6,7},{7,6},{8,9},{9,8},{10,11... | collective-permute-start | bytes 10616840 | tf_op jit(solution)/shard_map/ppermute | solution.py:797
  258.8 33.3 %collective-permute-start.5 = (bf16[1536,1152]{1,0:T(8,128)(2,1)}, bf16[1536,1152]{1,0:T(8,128)(2,1)}, u32[]{:S(2)}, u32[]{:S(2)}) collective-permute-start(bf16[1536,1152]{1,0:T(8,128)(2,1)} %all-gather.4.cloned.1.call-done.refs_0_), channel_id=1, source_target_pairs={{0,1},{1,0},{2,3},{3,2},{4,5},{5,4},{6,7},{7,6},{8,9},{9,8},{10,11... | collective-permute-start | bytes 10616840 | tf_op jit(solution)/shard_map/ppermute | solution.py:797
  258.9 33.2 %collective-permute-start.6 = (bf16[1536,1152]{1,0:T(8,128)(2,1)}, bf16[1536,1152]{1,0:T(8,128)(2,1)}, u32[]{:S(2)}, u32[]{:S(2)}) collective-permute-start(bf16[1536,1152]{1,0:T(8,128)(2,1)} %all-gather.6.cloned.1.call-done.refs_1_), channel_id=1, source_target_pairs={{0,1},{1,0},{2,3},{3,2},{4,5},{5,4},{6,7},{7,6},{8,9},{9,8},{10,11... | collective-permute-start | bytes 10616840 | tf_op jit(solution)/shard_map/ppermute | solution.py:797
  268.2 68.6 %collective-permute-start.10 = (bf16[640,1536]{1,0:T(8,128)(2,1)S(1)}, bf16[640,1536]{1,0:T(8,128)(2,1)}, u32[]{:S(2)}, u32[]{:S(2)}) collective-permute-start(bf16[640,1536]{1,0:T(8,128)(2,1)S(1)} %multiply_convert_fusion.n_ref.refs_4_), channel_id=1, source_target_pairs={{0,2},{1,3},{2,0},{3,1},{4,6},{5,7},{6,4},{7,5},{8,10},{9,11},{10,... | collective-permute-start | bytes 5898248 | tf_op jit(solution)/shard_map/ppermute | solution.py:797
  282.8 93.1 %collective-permute-start.9 = (bf16[640,1536]{1,0:T(8,128)(2,1)S(1)}, bf16[640,1536]{1,0:T(8,128)(2,1)}, u32[]{:S(2)}, u32[]{:S(2)}) collective-permute-start(bf16[640,1536]{1,0:T(8,128)(2,1)S(1)} %multiply_convert_fusion.n_ref.refs_4_), channel_id=1, source_target_pairs={{0,4},{1,5},{2,6},{3,7},{4,0},{5,1},{6,2},{7,3},{8,12},{9,13},{10,... | collective-permute-start | bytes 5898248 | tf_op jit(solution)/shard_map/ppermute | solution.py:797
  330.2 83.8 %collective-permute-start.8 = (bf16[640,1536]{1,0:T(8,128)(2,1)}, bf16[640,1536]{1,0:T(8,128)(2,1)}, u32[]{:S(2)}, u32[]{:S(2)}) collective-permute-start(bf16[640,1536]{1,0:T(8,128)(2,1)} %copy-done.15), channel_id=1, source_target_pairs={{0,6},{1,7},{2,4},{3,5},{4,2},{5,3},{6,0},{7,1},{8,14},{9,15},{10,... | collective-permute-start | bytes 5898248 | tf_op jit(solution)/shard_map/ppermute | solution.py:797
  374.7 106.7 %collective-permute-start.11 = (bf16[640,1536]{1,0:T(8,128)(2,1)}, bf16[640,1536]{1,0:T(8,128)(2,1)}, u32[]{:S(2)}, u32[]{:S(2)}) collective-permute-start(bf16[640,1536]{1,0:T(8,128)(2,1)} %get-tuple-element.90), channel_id=1, source_target_pairs={{0,2},{1,3},{2,0},{3,1},{4,6},{5,7},{6,4},{7,5},{8,10},{9,11},{10,... | collective-permute-start | bytes 5898248 | tf_op jit(solution)/shard_map/ppermute | solution.py:797
  512.3 86.8 %collective-permute-start.12 = (bf16[640,1536]{1,0:T(8,128)(2,1)}, bf16[640,1536]{1,0:T(8,128)(2,1)}, u32[]{:S(2)}, u32[]{:S(2)}) collective-permute-start(bf16[640,1536]{1,0:T(8,128)(2,1)} %get-tuple-element.93), channel_id=1, source_target_pairs={{0,4},{1,5},{2,6},{3,7},{4,0},{5,1},{6,2},{7,3},{8,12},{9,13},{10,... | collective-permute-start | bytes 5898248 | tf_op jit(solution)/shard_map/ppermute | solution.py:797
  512.3 86.8 %collective-permute-start.13 = (bf16[640,1536]{1,0:T(8,128)(2,1)}, bf16[640,1536]{1,0:T(8,128)(2,1)}, u32[]{:S(2)}, u32[]{:S(2)}) collective-permute-start(bf16[640,1536]{1,0:T(8,128)(2,1)} %get-tuple-element.96), channel_id=1, source_target_pairs={{0,6},{1,7},{2,4},{3,5},{4,2},{5,3},{6,0},{7,1},{8,14},{9,15},{10,... | collective-permute-start | bytes 5898248 | tf_op jit(solution)/shard_map/ppermute | solution.py:797
  523.2 385.6 %reduce-scatter.8.cloned.1.call-start = ((), (), s32[]{:S(2)}) async-start(), calls=%async_computation.8 | async-start | bytes 4423680 | tf_op jit(solution)/shard_map/reduce_scatter | solution.py:957
  524.6 102.3 %collective-permute-start.15 = (bf16[4,1152,384]{2,1,0:T(8,128)(2,1)}, bf16[4,1152,384]{2,1,0:T(8,128)(2,1)}, u32[]{:S(2)}, u32[]{:S(2)}) collective-permute-start(bf16[4,1152,384]{2,1,0:T(8,128)(2,1)} %get-tuple-element.101), channel_id=1, source_target_pairs={{0,1},{1,0},{2,3},{3,2},{4,5},{5,4},{6,7},{7,6},{8,9},{9,8},{10,11... | collective-permute-start | bytes 10616840 | tf_op jit(solution)/shard_map/ppermute | solution.py:797
  605.6 81.3 %collective-permute-start.16 = (bf16[640,1536]{1,0:T(8,128)(2,1)}, bf16[640,1536]{1,0:T(8,128)(2,1)}, u32[]{:S(2)}, u32[]{:S(2)}) collective-permute-start(bf16[640,1536]{1,0:T(8,128)(2,1)} %get-tuple-element.118), channel_id=1, source_target_pairs={{0,2},{1,3},{2,0},{3,1},{4,6},{5,7},{6,4},{7,5},{8,10},{9,11},{10,... | collective-permute-start | bytes 5898248 | tf_op jit(solution)/shard_map/ppermute | solution.py:797
  605.9 95.1 %collective-permute-start.17 = (bf16[640,1536]{1,0:T(8,128)(2,1)}, bf16[640,1536]{1,0:T(8,128)(2,1)}, u32[]{:S(2)}, u32[]{:S(2)}) collective-permute-start(bf16[640,1536]{1,0:T(8,128)(2,1)} %get-tuple-element.121), channel_id=1, source_target_pairs={{0,4},{1,5},{2,6},{3,7},{4,0},{5,1},{6,2},{7,3},{8,12},{9,13},{10,... | collective-permute-start | bytes 5898248 | tf_op jit(solution)/shard_map/ppermute | solution.py:797
  606.0 105.9 %collective-permute-start.18 = (bf16[640,1536]{1,0:T(8,128)(2,1)}, bf16[640,1536]{1,0:T(8,128)(2,1)}, u32[]{:S(2)}, u32[]{:S(2)}) collective-permute-start(bf16[640,1536]{1,0:T(8,128)(2,1)} %get-tuple-element.124), channel_id=1, source_target_pairs={{0,6},{1,7},{2,4},{3,5},{4,2},{5,3},{6,0},{7,1},{8,14},{9,15},{10,... | collective-permute-start | bytes 5898248 | tf_op jit(solution)/shard_map/ppermute | solution.py:797
  624.4 157.7 %collective-permute-start.42 = (bf16[4,2,2,1,48,1536]{5,4,3,2,1,0:T(8,128)(2,1)}, bf16[4,2,2,1,48,1536]{5,4,3,2,1,0:T(8,128)(2,1)}, u32[]{:S(2)}, u32[]{:S(2)}) collective-permute-start(bf16[4,2,2,1,48,1536]{5,4,3,2,1,0:T(8,128)(2,1)} %constant_dynamic-slice_fusion.2), channel_id=1, source_target_pairs={{0,1},{1,0},{2,3},{3,2},{4,5},{5,4},{6,7},{7,6},{8,9},{9,8},{10,11... | collective-permute-start | bytes 7077896 | tf_op jit(solution)/shard_map/ppermute | solution.py:797
  685.0 130.4 %collective-permute-start.48 = (bf16[4,1152,384]{2,1,0:T(8,128)(2,1)}, bf16[4,1152,384]{2,1,0:T(8,128)(2,1)}, u32[]{:S(2)}, u32[]{:S(2)}) collective-permute-start(bf16[4,1152,384]{2,1,0:T(8,128)(2,1)} %get-tuple-element.132), channel_id=1, source_target_pairs={{0,1},{1,0},{2,3},{3,2},{4,5},{5,4},{6,7},{7,6},{8,9},{9,8},{10,11... | collective-permute-start | bytes 10616840 | tf_op jit(solution)/shard_map/ppermute | solution.py:797
  686.6 225.3 %reduce-scatter.6.cloned.1.call-start = ((), (), s32[]{:S(2)}) async-start(), calls=%async_computation.7 | async-start | bytes 4423680 | tf_op jit(solution)/shard_map/reduce_scatter | solution.py:957
  686.8 32.8 %collective-permute-start.20 = (bf16[640,512]{1,0:T(8,128)(2,1)}, bf16[640,512]{1,0:T(8,128)(2,1)S(1)}, u32[]{:S(2)}, u32[]{:S(2)}) collective-permute-start(bf16[640,512]{1,0:T(8,128)(2,1)} %get-tuple-element.156), channel_id=1, source_target_pairs={{0,2},{1,3},{2,0},{3,1},{4,6},{5,7},{6,4},{7,5},{8,10},{9,11},{10,... | collective-permute-start | bytes 1966088 | tf_op jit(solution)/shard_map/ppermute | solution.py:797
  701.0 38.9 %collective-permute-start.21 = (bf16[640,512]{1,0:T(8,128)(2,1)}, bf16[640,512]{1,0:T(8,128)(2,1)S(1)}, u32[]{:S(2)}, u32[]{:S(2)}) collective-permute-start(bf16[640,512]{1,0:T(8,128)(2,1)} %get-tuple-element.155), channel_id=1, source_target_pairs={{0,4},{1,5},{2,6},{3,7},{4,0},{5,1},{6,2},{7,3},{8,12},{9,13},{10,... | collective-permute-start | bytes 1966088 | tf_op jit(solution)/shard_map/ppermute | solution.py:797
  711.9 29.7 %collective-permute-start.22 = (bf16[640,512]{1,0:T(8,128)(2,1)S(1)}, bf16[640,512]{1,0:T(8,128)(2,1)S(1)}, u32[]{:S(2)}, u32[]{:S(2)}) collective-permute-start(bf16[640,512]{1,0:T(8,128)(2,1)S(1)} %get-tuple-element.154), channel_id=1, source_target_pairs={{0,6},{1,7},{2,4},{3,5},{4,2},{5,3},{6,0},{7,1},{8,14},{9,15},{10,... | collective-permute-start | bytes 1966088 | tf_op jit(solution)/shard_map/ppermute | solution.py:797
  719.6 68.2 %collective-permute-start.19 = (bf16[320,1536]{1,0:T(8,128)(2,1)}, bf16[320,1536]{1,0:T(8,128)(2,1)}, u32[]{:S(2)}, u32[]{:S(2)}) collective-permute-start(bf16[320,1536]{1,0:T(8,128)(2,1)} %get-tuple-element.160), channel_id=1, source_target_pairs={{0,1},{1,0},{2,3},{3,2},{4,5},{5,4},{6,7},{7,6},{8,9},{9,8},{10,11... | collective-permute-start | bytes 2949128 | tf_op jit(solution)/shard_map/ppermute | solution.py:797
  755.9 11.5 %collective-permute-start.36 = (f32[4,4,160]{2,1,0:T(4,128)S(1)}, f32[4,4,160]{2,1,0:T(4,128)S(1)}, u32[]{:S(2)}, u32[]{:S(2)}) collective-permute-start(f32[4,4,160]{2,1,0:T(4,128)S(1)} %constant_dynamic-slice_fusion.11), channel_id=1, source_target_pairs={{0,4},{1,5},{2,6},{3,7},{4,0},{5,1},{6,2},{7,3},{8,12},{9,13},{10,... | collective-permute-start | bytes 30728 | tf_op jit(solution)/shard_map/ppermute | solution.py:797
  765.9 66.3 %collective-permute-start.24 = (bf16[4,2,2,1,48,1024]{5,4,3,2,1,0:T(8,128)(2,1)}, bf16[4,2,2,1,48,1024]{5,4,3,2,1,0:T(8,128)(2,1)}, u32[]{:S(2)}, u32[]{:S(2)}) collective-permute-start(bf16[4,2,2,1,48,1024]{5,4,3,2,1,0:T(8,128)(2,1)} %constant_dynamic-slice_fusion.17), channel_id=1, source_target_pairs={{0,1},{1,0},{2,3},{3,2},{4,5},{5,4},{6,7},{7,6},{8,9},{9,8},{10,11... | collective-permute-start | bytes 4718600 | tf_op jit(solution)/shard_map/ppermute | solution.py:797
  780.3 12.0 %collective-permute-start.23 = (bf16[320,1536]{1,0:T(8,128)(2,1)S(1)}, bf16[320,1536]{1,0:T(8,128)(2,1)S(1)}, u32[]{:S(2)}, u32[]{:S(2)}) collective-permute-start(bf16[320,1536]{1,0:T(8,128)(2,1)S(1)} %get-tuple-element.158), channel_id=1, source_target_pairs={{0,1},{1,0},{2,3},{3,2},{4,5},{5,4},{6,7},{7,6},{8,9},{9,8},{10,11... | collective-permute-start | bytes 2949128 | tf_op jit(solution)/shard_map/ppermute | solution.py:797
  786.6 26.5 %collective-permute-start.43 = (bf16[4,2,1,1,48,1536]{5,4,3,2,1,0:T(8,128)(2,1)S(1)}, bf16[4,2,1,1,48,1536]{5,4,3,2,1,0:T(8,128)(2,1)S(1)}, u32[]{:S(2)}, u32[]{:S(2)}) collective-permute-start(bf16[4,2,1,1,48,1536]{5,4,3,2,1,0:T(8,128)(2,1)S(1)} %constant_dynamic-slice_fusion.1), channel_id=1, source_target_pairs={{0,2},{1,3},{2,0},{3,1},{4,6},{5,7},{6,4},{7,5},{8,10},{9,11},{10,... | collective-permute-start | bytes 3538952 | tf_op jit(solution)/shard_map/ppermute | solution.py:797
  787.8 57.5 %collective-permute-start.30 = (bf16[4,2,2,1,48,1024]{5,4,3,2,1,0:T(8,128)(2,1)}, bf16[4,2,2,1,48,1024]{5,4,3,2,1,0:T(8,128)(2,1)}, u32[]{:S(2)}, u32[]{:S(2)}) collective-permute-start(bf16[4,2,2,1,48,1024]{5,4,3,2,1,0:T(8,128)(2,1)} %constant_dynamic-slice_fusion.14), channel_id=1, source_target_pairs={{0,1},{1,0},{2,3},{3,2},{4,5},{5,4},{6,7},{7,6},{8,9},{9,8},{10,11... | collective-permute-start | bytes 4718600 | tf_op jit(solution)/shard_map/ppermute | solution.py:797
  815.3 13.3 %collective-permute-start.44 = (bf16[4,1,1,1,48,1536]{5,4,3,2,1,0:T(8,128)(2,1)}, bf16[4,1,1,1,48,1536]{5,4,3,2,1,0:T(8,128)(2,1)}, u32[]{:S(2)}, u32[]{:S(2)}) collective-permute-start(bf16[4,1,1,1,48,1536]{5,4,3,2,1,0:T(8,128)(2,1)} %constant_dynamic-slice_fusion), channel_id=1, source_target_pairs={{0,4},{1,5},{2,6},{3,7},{4,0},{5,1},{6,2},{7,3},{8,12},{9,13},{10,... | collective-permute-start | bytes 1769480 | tf_op jit(solution)/shard_map/ppermute | solution.py:797
  830.1 11.5 %collective-permute-start.45 = (bf16[48,1536]{1,0:T(8,128)(2,1)S(1)}, bf16[48,1536]{1,0:T(8,128)(2,1)S(1)}, u32[]{:S(2)}, u32[]{:S(2)}) collective-permute-start(bf16[48,1536]{1,0:T(8,128)(2,1)S(1)} %dynamic-slice_bitcast_fusion.6), channel_id=1, source_target_pairs={{0,8},{8,16},{16,24},{24,0},{1,9},{9,17},{17,25},{25,1},{2,10},{10... | collective-permute-start | bytes 442376 | tf_op jit(solution)/shard_map/ppermute | solution.py:801
  834.8 23.9 %collective-permute-start.25 = (bf16[4,2,1,1,48,1024]{5,4,3,2,1,0:T(8,128)(2,1)S(1)}, bf16[4,2,1,1,48,1024]{5,4,3,2,1,0:T(8,128)(2,1)S(1)}, u32[]{:S(2)}, u32[]{:S(2)}) collective-permute-start(bf16[4,2,1,1,48,1024]{5,4,3,2,1,0:T(8,128)(2,1)S(1)} %constant_dynamic-slice_fusion.16), channel_id=1, source_target_pairs={{0,2},{1,3},{2,0},{3,1},{4,6},{5,7},{6,4},{7,5},{8,10},{9,11},{10,... | collective-permute-start | bytes 2359304 | tf_op jit(solution)/shard_map/ppermute | solution.py:797
  841.6 14.8 %collective-permute-start.46 = (bf16[48,1536]{1,0:T(8,128)(2,1)S(1)}, bf16[48,1536]{1,0:T(8,128)(2,1)S(1)}, u32[]{:S(2)}, u32[]{:S(2)}) collective-permute-start(bf16[48,1536]{1,0:T(8,128)(2,1)S(1)} %fusion.29), channel_id=1, source_target_pairs={{0,8},{8,16},{16,24},{24,0},{1,9},{9,17},{17,25},{25,1},{2,10},{10... | collective-permute-start | bytes 442376 | tf_op jit(solution)/shard_map/ppermute | solution.py:801
  847.5 17.4 %collective-permute-start.31 = (bf16[4,1,2,1,48,1024]{5,4,3,2,1,0:T(8,128)(2,1)S(1)}, bf16[4,1,2,1,48,1024]{5,4,3,2,1,0:T(8,128)(2,1)S(1)}, u32[]{:S(2)}, u32[]{:S(2)}) collective-permute-start(bf16[4,1,2,1,48,1024]{5,4,3,2,1,0:T(8,128)(2,1)S(1)} %constant_dynamic-slice_fusion.13), channel_id=1, source_target_pairs={{0,4},{1,5},{2,6},{3,7},{4,0},{5,1},{6,2},{7,3},{8,12},{9,13},{10,... | collective-permute-start | bytes 2359304 | tf_op jit(solution)/shard_map/ppermute | solution.py:797
  856.4 11.9 %collective-permute-start.47 = (bf16[48,1536]{1,0:T(8,128)(2,1)S(1)}, bf16[48,1536]{1,0:T(8,128)(2,1)S(1)}, u32[]{:S(2)}, u32[]{:S(2)}) collective-permute-start(bf16[48,1536]{1,0:T(8,128)(2,1)S(1)} %fusion.30), channel_id=1, source_target_pairs={{0,8},{8,16},{16,24},{24,0},{1,9},{9,17},{17,25},{25,1},{2,10},{10... | collective-permute-start | bytes 442376 | tf_op jit(solution)/shard_map/ppermute | solution.py:801
  859.1 14.3 %collective-permute-start.26 = (bf16[4,1,1,1,48,1024]{5,4,3,2,1,0:T(8,128)(2,1)S(1)}, bf16[4,1,1,1,48,1024]{5,4,3,2,1,0:T(8,128)(2,1)S(1)}, u32[]{:S(2)}, u32[]{:S(2)}) collective-permute-start(bf16[4,1,1,1,48,1024]{5,4,3,2,1,0:T(8,128)(2,1)S(1)} %constant_dynamic-slice_fusion.15), channel_id=1, source_target_pairs={{0,4},{1,5},{2,6},{3,7},{4,0},{5,1},{6,2},{7,3},{8,12},{9,13},{10,... | collective-permute-start | bytes 1179656 | tf_op jit(solution)/shard_map/ppermute | solution.py:797
  865.3 9.0 collective-permute-start.32
  873.5 7.5 collective-permute-start.27
  874.5 12.2 %collective-permute-start.33 = (bf16[48,1024]{1,0:T(8,128)(2,1)S(1)}, bf16[48,1024]{1,0:T(8,128)(2,1)S(1)}, u32[]{:S(2)}, u32[]{:S(2)}) collective-permute-start(bf16[48,1024]{1,0:T(8,128)(2,1)S(1)} %dynamic-slice_bitcast_fusion.7), channel_id=1, source_target_pairs={{0,8},{8,16},{16,24},{24,0},{1,9},{9,17},{17,25},{25,1},{2,10},{10... | collective-permute-start | bytes 294920 | tf_op jit(solution)/shard_map/ppermute | solution.py:801
  881.1 10.4 %collective-permute-start.28 = (bf16[48,1024]{1,0:T(8,128)(2,1)S(1)}, bf16[48,1024]{1,0:T(8,128)(2,1)S(1)}, u32[]{:S(2)}, u32[]{:S(2)}) collective-permute-start(bf16[48,1024]{1,0:T(8,128)(2,1)S(1)} %fusion.34), channel_id=1, source_target_pairs={{0,8},{8,16},{16,24},{24,0},{1,9},{9,17},{17,25},{25,1},{2,10},{10... | collective-permute-start | bytes 294920 | tf_op jit(solution)/shard_map/ppermute | solution.py:801
  886.7 11.7 %collective-permute-start.34 = (bf16[48,1024]{1,0:T(8,128)(2,1)S(1)}, bf16[48,1024]{1,0:T(8,128)(2,1)S(1)}, u32[]{:S(2)}, u32[]{:S(2)}) collective-permute-start(bf16[48,1024]{1,0:T(8,128)(2,1)S(1)} %fusion.32), channel_id=1, source_target_pairs={{0,8},{8,16},{16,24},{24,0},{1,9},{9,17},{17,25},{25,1},{2,10},{10... | collective-permute-start | bytes 294920 | tf_op jit(solution)/shard_map/ppermute | solution.py:801
  891.5 12.5 %collective-permute-start.29 = (bf16[48,1024]{1,0:T(8,128)(2,1)S(1)}, bf16[48,1024]{1,0:T(8,128)(2,1)S(1)}, u32[]{:S(2)}, u32[]{:S(2)}) collective-permute-start(bf16[48,1024]{1,0:T(8,128)(2,1)S(1)} %fusion.35), channel_id=1, source_target_pairs={{0,8},{8,16},{16,24},{24,0},{1,9},{9,17},{17,25},{25,1},{2,10},{10... | collective-permute-start | bytes 294920 | tf_op jit(solution)/shard_map/ppermute | solution.py:801
  (51 other events, 868.2 us)
Sparse Core Ops, SparseCore 0:
  10.0 97.6 all-gather.7
  109.9 69.6 all-gather.3
  181.1 68.5 all-gather.5
  523.3 68.3 reduce-scatter.3
  686.7 91.9 reduce-scatter.7
  820.3 91.5 reduce-scatter.5

commit v3 on v2

--- a/solution.py
+++ b/solution.py
@@ -18,8 +18,12 @@
 FFN_CHUNK = 768
 FFN_PARTS = 2
 WG_TILE = 384
-PACE = 0.15
+PACE = 1.0
 LOG2E = 1.0 / math.log(2.0)
+
+CORE, ALONG_X, ALONG_Y, ACROSS = 1, 2, 4, 6
+OTHERS = (ALONG_X, ALONG_Y, ACROSS)
+RING = 8
 
 
 EPS = 1e-06
@@ -346,6 +350,100 @@
     return 0.5 * jnp.tanh(0.5 * v) + 0.5
 
 
+def peers_of():
+    me, plane = lax.axis_index("gy"), lax.axis_index("gx")
+    along_x = me + 2 - 4 * lax.rem(me // 2, 2)
+    return {
+        CORE: {"gy": me + 1 - 2 * lax.rem(me, 2)},
+        ALONG_X: {"gy": along_x},
+        ALONG_Y: {"gy": me + 4 - 8 * (me // 4)},
+        ACROSS: {"gy": along_x + 4 - 8 * (along_x // 4)},
+        RING: {"gx": lax.rem(plane + 1, 4)},
+        RING + 1: {"gx": lax.rem(plane + 2, 4)},
+        -RING: {"gx": lax.rem(plane + 3, 4)},
+    }
+
+
+def greet(bits_used):
+    peers = peers_of()
+    barrier = pltpu.get_barrier_semaphore()
+    greeted = [bits for bits in bits_used] + [-RING] * (RING in bits_used)
+    for bits in greeted:
+        pl.semaphore_signal(barrier, inc=1, device_id=peers[bits], device_id_type=pl.DeviceIdType.MESH)
+    pl.semaphore_wait(barrier, len(greeted))
+
+
+def side_copies(sides, sources, targets, sent, landed):
+    peers = peers_of()
+    copies = []
+    for parts, target in zip(sides, targets):
+        for _, take, fill, bits in parts:
+            copies.append(
+                pltpu.make_async_remote_copy(
+                    sources[len(copies)].at[pl.ds(*take)],
+                    target.at[pl.ds(*fill)],
+                    sent.at[len(copies)],
+                    landed.at[len(copies)],
+                    device_id=peers[bits],
+                    device_id_type=pl.DeviceIdType.MESH,
+                )
+            )
+    return copies
+
+
+def whole_side(array, bits):
+    return [(array, (0, array.shape[0]), (0, array.shape[0]), bits)]
+
+
+def rows_side(array, start, count, bits):
+    return [(array, (start, count), (0, count), bits)]
+
+
+def call_beside(body, sides, collective, operands, grid, in_specs, out_specs, out_shape, scratch_shapes, mib, estimate, name):
+    n_in, n_out, n_scratch = len(in_specs), len(out_specs), len(scratch_shapes)
+    flat = [part for parts in sides for part in parts]
+    bits_used = sorted({part[3] for part in flat})
+
+    def whole_body(*refs):
+        ins, refs = refs[:n_in], refs[n_in:]
+        sources, refs = refs[: len(flat)], refs[len(flat) :]
+        outs, refs = refs[:n_out], refs[n_out:]
+        targets, refs = refs[: len(sides)], refs[len(sides) :]
+        scratch, refs = refs[:n_scratch], refs[n_scratch:]
+        step, last = pl.program_id(0), pl.num_programs(0) - 1
+        if flat:
+
+            @pl.when(step == 0)
+            def _():
+                greet(bits_used)
+                for copy in side_copies(sides, sources, targets, *refs):
+                    copy.start()
+
+        body(*ins, *outs, *scratch)
+        if flat:
+
+            @pl.when(step == last)
+            def _():
+                for copy in side_copies(sides, sources, targets, *refs):
+                    copy.wait()
+
+    anywhere = pl.BlockSpec(memory_space=pl.ANY)
+    extra = {"collective_id": collective, "has_side_effects": True} if flat else {}
+    results = pl.pallas_call(
+        whole_body,
+        grid=grid,
+        in_specs=list(in_specs) + [anywhere] * len(flat),
+        out_specs=list(out_specs) + [anywhere] * len(sides),
+        out_shape=list(out_shape)
+        + [jax.ShapeDtypeStruct((sum(p[2][1] for p in parts),) + parts[0][0].shape[1:], parts[0][0].dtype) for parts in sides],
+        scratch_shapes=list(scratch_shapes) + ([pltpu.SemaphoreType.DMA((len(flat),))] * 2 if flat else []),
+        compiler_params=pltpu.CompilerParams(vmem_limit_bytes=mib * 1024 * 1024, **extra),
+        cost_estimate=estimate,
+        name=name,
+    )(*operands, *[part[0] for part in flat])
+    return results[:n_out], results[n_out:]
+
+
 def ffn_copies(chunk, pieces, held, sems):
     units = pieces[0].shape[1]
     tile = FFN_CHUNK // 2
@@ -413,26 +511,28 @@
         dn_ref[...] = dn_acc[...].astype(dn_ref.dtype)
 
 
-def ffn_block(normed, cotan, pieces):
+def ffn_block(normed, cotan, pieces, collective, sides=()):
     rows, width = normed.shape
     units = 2 * pieces[0].shape[1]
     chunk = FFN_CHUNK
     whole = pl.BlockSpec((rows, width), lambda j: (0, 0))
     tall = pl.BlockSpec((rows, chunk), lambda j: (0, j))
     low = jnp.bfloat16
-    return pl.pallas_call(
+    return call_beside(
         ffn_body,
-        grid=(units // chunk,),
-        in_specs=[whole, whole] + [pl.BlockSpec(memory_space=pl.ANY)] * len(pieces),
-        out_specs=[tall, tall, tall, whole, whole],
-        out_shape=[jax.ShapeDtypeStruct((rows, units), low)] * 3
-        + [jax.ShapeDtypeStruct((rows, width), low)] * 2,
-        scratch_shapes=[pltpu.VMEM((rows, width), jnp.float32)] * 2
+        sides,
+        collective,
+        (normed, cotan, *pieces),
+        (units // chunk,),
+        [whole, whole] + [pl.BlockSpec(memory_space=pl.ANY)] * len(pieces),
+        [tall, tall, tall, whole, whole],
+        [jax.ShapeDtypeStruct((rows, units), low)] * 3 + [jax.ShapeDtypeStruct((rows, width), low)] * 2,
+        [pltpu.VMEM((rows, width), jnp.float32)] * 2
         + [pltpu.VMEM((2, 3, width, chunk), low), pltpu.SemaphoreType.DMA((2, len(pieces)))],
-        compiler_params=params(60),
-        cost_estimate=cost(12 * rows * width * units, 6 * width * units + 6 * rows * (width + units)),
-        name="ffn_block",
-    )(normed, cotan, *pieces)
+        60,
+        cost(12 * rows * width * units, 6 * width * units + 6 * rows * (width + units)),
+        "ffn_block",
+    )
 
 
 def wgrad_body(per_half, *refs):
@@ -451,27 +551,31 @@
     pl.when(jnp.logical_not(first))(lambda: store(refs[-1]))
 
 
-def wgrad(lefts, rights, slots):
+def wgrad(lefts, rights, slots, collective, sides=()):
     rows, units = lefts[0].shape
     width = rights[0].shape[1]
     tile = WG_TILE
     per_half = units // 2 // tile
     wide = width // slots
     count = len(lefts)
-    return pl.pallas_call(
+    return call_beside(
         lambda *refs: wgrad_body(per_half, *refs),
-        grid=(units // tile,),
-        in_specs=[pl.BlockSpec((rows, tile), lambda j: (0, j))] * count
+        sides,
+        collective,
+        (*lefts, *rights),
+        (units // tile,),
+        [pl.BlockSpec((rows, tile), lambda j: (0, j))] * count
         + [pl.BlockSpec((rows, width), lambda j: (0, 0))] * count,
-        out_specs=[
+        [
             pl.BlockSpec((slots, tile, wide), lambda j: (0, jnp.minimum(j, per_half - 1), 0)),
             pl.BlockSpec((slots, tile, wide), lambda j: (0, jnp.maximum(j - per_half, 0), 0)),
         ],
-        out_shape=[jax.ShapeDtypeStruct((slots, units // 2, wide), jnp.bfloat16)] * 2,
-        compiler_params=params(60),
-        cost_estimate=cost(2 * count * rows * width * units, 2 * count * rows * (width + units)),
-        name="ffn_wgrad",
-    )(*lefts, *rights)
+        [jax.ShapeDtypeStruct((slots, units // 2, wide), jnp.bfloat16)] * 2,
+        [],
+        60,
+        cost(2 * count * rows * width * units, 2 * count * rows * (width + units)),
+        "ffn_wgrad",
+    )
 
 
 def group_rows(source_ref, group, per_group):
@@ -789,16 +893,160 @@
     return whole.reshape(32 * deep, wide), others
 
 
-CORE, ALONG_X, ALONG_Y, ACROSS = 1, 2, 4, 6
-OTHERS = (ALONG_X, ALONG_Y, ACROSS)
+def finish_body(wide_ref, out_ref, mine_ref, sent_ref, *refs):
+    results, scratch = refs[:3], refs[3:]
+    kept, got_core, got_first, got_second, got_ring = [scratch[i : i + 2] for i in range(0, 10, 2)]
+    units, got_units, units_ring, units_moving, sent, landed, local = scratch[10:]
+    me, plane = lax.axis_index("gy"), lax.axis_index("gx")
+    core, x, y = lax.rem(me, 2), lax.rem(me // 2, 2), me // 4
+    places = [lax.rem(plane + 4 - s, 4) for s in range(4)]
+    peers = peers_of()
+    full = jnp.float32
+    greet((CORE, ALONG_X, ALONG_Y, RING, RING + 1))
+    copies, loads = [], []
+
+    def send(source, target, bits):
+        copy = pltpu.make_async_remote_copy(
+            source,
+            target,
+            sent.at[len(copies)],
+            landed.at[len(copies)],
+            device_id=peers[bits],
+            device_id_type=pl.DeviceIdType.MESH,
+        )
+        copies.append(copy)
+        copy.start()
+        return copy
+
+    def load(source, target):
+        copy = pltpu.make_async_copy(source, target, local.at[len(loads)])
+        loads.append(copy)
+        copy.start()
+        return copy
+
+    inputs = (wide_ref, out_ref)
+    core_copies = [send(sent_ref, got_units, CORE)]
+    core_copies += [send(inputs[i].at[:, :, :, 1 - core], got_core[i], CORE) for i in range(2)]
+    held = [load(mine_ref, units)]
+    held += [load(inputs[i].at[:, :, :, core], kept[i]) for i in range(2)]
+
+    core_copies[0].wait_recv()
+    held[0].wait()
+
+    @pl.loop(0, 4)
+    def _(p):
+        units[p] += got_units[p]
+
+    units_copy = send(units.at[places[1]], units_ring.at[0], RING)
+    steps = []
+    for i in range(2):
+        core_copies[1 + i].wait_recv()
+        held[1 + i].wait()
+
+        @pl.loop(0, 4)
+        def _(p):
+            for a in range(2):
+                for b in range(2):
+                    kept[i][p, a, b] += got_core[i][p, a, b]
+
+        middle = kept[i].shape[-1] // 256 * 128
+        first, second = pl.ds(0, middle), pl.ds(middle, kept[i].shape[-1] - middle)
+        steps.append((
+            send(kept[i].at[:, :, 1 - x, :, first], got_first[i].at[:, :, :, first], ALONG_X),
+            send(kept[i].at[:, 1 - y, :, :, second], got_first[i].at[:, :, :, second], ALONG_Y),
+            first,
+            second,
+        ))
+    units_copy.wait_recv()
+    units_moving[0] = units[places[2]] + units_ring[0]
+    units_copy = send(units_moving.at[0], units_ring.at[1], RING)
+    nexts = []
+    for i in range(2):
+        first_copy, second_copy, first, second = steps[i]
+        first_copy.wait_recv()
+
+        @pl.loop(0, 4)
+        def _(p):
+            for a in range(2):
+                kept[i][p, a, x, :, first] += got_first[i][p, a, :, first]
+
+        third_copy = send(kept[i].at[:, 1 - y, x, :, first], got_second[i].at[:, :, first], ALONG_Y)
+        second_copy.wait_recv()
+
+        @pl.loop(0, 4)
+        def _(p):
+            for b in range(2):
+                kept[i][p, y, b, :, second] += got_first[i][p, b, :, second]
+
+        nexts.append((third_copy, send(kept[i].at[:, y, 1 - x, :, second], got_second[i].at[:, :, second], ALONG_X)))
+    units_copy.wait_recv()
+    units_moving[1] = units[places[3]] + units_ring[1]
+    units_copy = send(units_moving.at[1], units_ring.at[2], RING)
+    ring_copies = []
+    for i in range(2):
+        for copy in nexts[i]:
+            copy.wait_recv()
+
+        @pl.loop(0, 4)
+        def _(p):
+            kept[i][p, y, x] += got_second[i][p]
+
+        for k, bits in ((1, RING), (2, RING + 1), (3, -RING)):
+            there = lax.rem(plane + k, 4)
+            ring_copies.append(send(kept[i].at[there, y, x], got_ring[i].at[k - 1], bits))
+    for i in range(2):
+        total = kept[i][plane, y, x].astype(full)
+        for k in range(3):
+            ring_copies[3 * i + k].wait_recv()
+            total = total + got_ring[i][k].astype(full)
+        results[i][...] = total
+    units_copy.wait_recv()
+    results[2][...] = units[places[0]].astype(full) + units_ring[2].astype(full)
+    for copy in copies:
+        copy.wait_send()
+
+
+def finish(wide, out, mine, sent, collective):
+    low, full = jnp.bfloat16, jnp.float32
+    deep = wide.shape[0] // 32
+    wide, out = (a.reshape(4, 2, 2, 2, deep, a.shape[1]) for a in (wide, out))
+    columns = (wide.shape[-1], out.shape[-1])
+    block = mine.shape[1:]
+    anywhere = pl.BlockSpec(memory_space=pl.ANY)
+    inside = pl.BlockSpec(memory_space=pltpu.VMEM)
+
+    def pairs(*lead):
+        return [pltpu.VMEM((*lead, deep, c), low) for c in columns]
+
+    return pl.pallas_call(
+        finish_body,
+        in_specs=[anywhere] * 4,
+        out_specs=[inside] * 3,
+        out_shape=[jax.ShapeDtypeStruct((deep, c), full) for c in columns] + [jax.ShapeDtypeStruct(block, full)],
+        scratch_shapes=[
+            *pairs(4, 2, 2),
+            *pairs(4, 2, 2),
+            *pairs(4, 2),
+            *pairs(4),
+            *pairs(3),
+            pltpu.VMEM((4, *block), low),
+            pltpu.VMEM((4, *block), low),
+            pltpu.VMEM((3, *block), low),
+            pltpu.VMEM((2, *block), low),
+            pltpu.SemaphoreType.DMA((20,)),
+            pltpu.SemaphoreType.DMA((20,)),
+            pltpu.SemaphoreType.DMA((3,)),
+        ],
+        compiler_params=pltpu.CompilerParams(
+            vmem_limit_bytes=56 * 1024 * 1024, collective_id=collective, has_side_effects=True
+        ),
+        cost_estimate=cost(0, 200 * 1024 * 1024),
+        name="finish",
+    )(wide, out, mine, sent)
 
 
 def swap(array, bits):
     return lax.ppermute(array, "gy", [(i, i ^ bits) for i in range(8)])
-
-
-def ring(array):
-    return lax.ppermute(array, "gx", [(i, (i + 1) % 4) for i in range(4)])
 
 
 def pick(array, index):
@@ -819,13 +1067,6 @@
     kept = lax.dynamic_slice_in_dim(rows, core * half, half, 0)
     got = swap(lax.dynamic_slice_in_dim(rows, (1 - core) * half, half, 0), CORE)
     return jnp.where(core == 0, jnp.stack([kept, got]), jnp.stack([got, kept]))
-
-
-def ring_sums(slots):
-    moving = ring(slots[1])
-    for s in (2, 3):
-        moving = ring((slots[s].astype(jnp.float32) + moving.astype(jnp.float32)).astype(jnp.bfloat16))
-    return slots[0].astype(jnp.float32) + moving.astype(jnp.float32)
 
 
 def plane_order(blocks, chip):
@@ -834,33 +1075,6 @@
     for index, block in enumerate(blocks):
         whole = lax.dynamic_update_slice_in_dim(whole, block, (chip ^ index) * rows, 0)
     return whole
-
-
-def sum_rows(rows, plane, me, order):
-    width = rows.shape[1]
-    rows = rows.reshape(4, 2, 2, 2, rows.shape[0] // 32, width)
-    axis = {ALONG_Y: 1, ALONG_X: 2, CORE: 3}
-    for bits in order:
-        bit = (me // bits) % 2
-        kept = lax.dynamic_slice_in_dim(rows, bit, 1, axis[bits])
-        sent = lax.dynamic_slice_in_dim(rows, 1 - bit, 1, axis[bits])
-        rows = (kept.astype(jnp.float32) + swap(sent, bits).astype(jnp.float32)).astype(rows.dtype)
-    rows = rows.reshape(4, -1, width)
-    return ring_sums([pick(rows, lax.rem(plane + 4 - s, 4)) for s in range(4)])
-
-
-def sum_small(rows, plane, me):
-    rows = rows.reshape(4, 8, rows.shape[1])
-    for level, bits in ((2, ALONG_Y), (1, ALONG_X), (0, CORE)):
-        half = rows.shape[1] // 2
-        bit = (me >> level) % 2
-        kept = lax.dynamic_slice_in_dim(rows, bit * half, half, 1)
-        rows = kept + swap(lax.dynamic_slice_in_dim(rows, (1 - bit) * half, half, 1), bits)
-    slots = [pick(rows, lax.rem(plane + 4 - s, 4)) for s in range(4)]
-    moving = ring(slots[1])
-    for s in (2, 3):
-        moving = ring(slots[s] + moving)
-    return (slots[0] + moving)[0]
 
 
 def on_core(
@@ -942,64 +1156,72 @@
 
     other_weights.append(swap(after(weights[2], heads_out), CORE))
     pieces = weights + other_weights
-    normed_x, normed_y = swap(normed_two, ALONG_X), swap(normed_two, ALONG_Y)
-    results = [ffn_block(normed_two, cotan_blocks[0], pieces)]
-    normed_d = swap(after(normed_two, results[0][4]), ACROSS)
+    half = rows // 2
+    first, second = (0, half), (half, half)
+    own, (normed_x, normed_y) = ffn_block(
+        normed_two, cotan_blocks[0], pieces, 1, [whole_side(normed_two, ALONG_X), whole_side(normed_two, ALONG_Y)]
+    )
+    passed_on = [(normed_x, first, first, ALONG_Y), (normed_y, second, second, ALONG_X)]
+    near_x, (normed_d,) = ffn_block(normed_x, cotan_blocks[1], pieces, 2, [passed_on])
+    near_y, (back_x,) = ffn_block(
+        after(normed_y, near_x[4]), cotan_blocks[2], pieces, 3, [rows_side(near_x[4], 0, 512, ALONG_X)]
+    )
+    far, (back_y, back_x_end) = ffn_block(
+        normed_d,
+        cotan_blocks[3],
+        pieces,
+        4,
+        [rows_side(near_y[4], 0, 512, ALONG_Y), rows_side(near_x[4], 512, rows - 512, ALONG_X)],
+    )
     normed_blocks = [normed_two, normed_x, normed_y, normed_d]
-    for normed, cotan in zip(normed_blocks[1:], cotan_blocks[1:]):
-        results.append(ffn_block(after(normed, results[-1][4]), cotan, pieces))
-    hidden_b, gate_b, up_b, out_b, back_b = zip(*results)
-    back_got = [swap(b, bits) for b, bits in zip(back_b[1:], OTHERS)]
-
-    def both_halves(mine, other):
-        mine = (mine.astype(full) + other.astype(full)).astype(low)
-        mine = mine.reshape(-1, mine.shape[-1])
-        return mine, lax.psum_scatter(mine, "gx", scatter_dimension=0, tiled=True).astype(full)
-
-    down_mine, down_sent = wgrad((after(hidden_b[0], back_b[3]),) + hidden_b[1:], cotan_blocks, 4)
-    down_got = swap(down_sent, CORE)
-    gate_mine, gate_sent = wgrad((after(gate_b[0], down_sent, back_got[0]),) + gate_b[1:], normed_blocks, 4)
+    hidden_b, gate_b, up_b, out_b, back_b = zip(own, near_x, near_y, far)
+
+    (down_mine, down_sent), (back_d,) = wgrad(hidden_b, cotan_blocks, 4, 5, [rows_side(back_b[3], 0, 384, ACROSS)])
+    (gate_mine, gate_sent), (down_got, back_d_end, back_y_end) = wgrad(
+        gate_b,
+        normed_blocks,
+        4,
+        6,
+        [
+            whole_side(down_sent, CORE),
+            rows_side(after(back_b[3], back_d), 384, rows - 384, ACROSS),
+            rows_side(after(back_b[2], back_d), 512, rows - 512, ALONG_Y),
+        ],
+    )
     gate_got = swap(gate_sent, CORE)
-    down_sum, grad_down = both_halves(after(down_mine, gate_sent), down_got)
-
-    grad_normed_two = sum(after(b, gate_sent).astype(full) for b in [back_b[0]] + back_got)
+    down_sum = down_mine.astype(full) + down_got.astype(full)
+    back_x, back_y, back_d = (
+        jnp.concatenate(pair)
+        for pair in ((back_x, back_x_end), (back_y, back_y_end), (back_d, back_d_end))
+    )
+
+    grad_normed_two = sum(after(b, gate_sent).astype(full) for b in (back_b[0], back_x, back_y, back_d))
     back_two, grad_gain_two = norm_back(grad_normed_two, unit_two, inverse_two, gain_two)
     grad_resid = grad_low.astype(full) + back_two
     grad_branch = grad_resid.astype(low)
     grad_heads = jnp.dot(grad_branch, out_turned, preferred_element_type=full).astype(low)
     grad_wout = jnp.dot(grad_branch.T, heads_out, preferred_element_type=full).astype(low)
     out_got = [swap(after(b, grad_normed_two), bits) for b, bits in zip(out_b[1:], OTHERS)]
-    gate_sum, grad_wgate = both_halves(gate_mine, gate_got)
-    grad_heads = after(grad_heads, grad_wout, gate_sum, down_sum)
+    gate_sum = gate_mine.astype(full) + gate_got.astype(full)
+    both = jnp.concatenate([down_sum, gate_sum], axis=1).astype(low)
+    grad_heads = after(grad_heads, grad_wout, both)
+    both = lax.psum_scatter(both, "gx", scatter_dimension=0, tiled=True)[0].astype(full)
+    grad_down, grad_wgate = both[:own_units], both[pad_units : pad_units + own_units].T
     query_lin, keyval_part = attend_back_fast(
         block_list, block_count, query, keyval, mask_bias, lse, heads_out, grad_heads, cosine, sine
     )
 
-    grad_wout = sum_rows(grad_wout, plane, me, (CORE, ALONG_X, ALONG_Y)).T
-    up_mine, up_sent = wgrad((after(up_b[0], query_lin),) + up_b[1:], normed_blocks, 4)
-    up_sum, grad_wup = both_halves(up_mine, swap(up_sent, CORE))
-    grad_down = grad_down[:own_units]
-    grad_wgate, grad_wup = grad_wgate.T[:, :own_units], grad_wup.T[:, :own_units]
-
-    def part_of(index):
-        return lax.dynamic_slice_in_dim(keyval_part, (chip ^ index) * rows, rows, 0)
-
-    keyval_grad = after(part_of(0), up_sent).astype(full) + sum(
-        swap(part_of(index + 1), bits).astype(full) for index, bits in enumerate(OTHERS)
-    )
+    parts = [lax.dynamic_slice_in_dim(keyval_part, (chip ^ i) * rows, rows, 0) for i in range(4)]
+    (up_mine, up_sent), others = wgrad(
+        up_b, normed_blocks, 4, 7, [whole_side(part, bits) for part, bits in zip(parts[1:], OTHERS)]
+    )
+
+    keyval_grad = sum(part.astype(full) for part in (parts[0], *others))
     keys_grad = keyval_grad[:, :kwidth].reshape(rows, KV_HEADS, HEAD)
     keys_lin = keys_grad * cosine[:, None, :] - jnp.roll(keys_grad, HEAD // 2, axis=-1) * sine[:, None, :]
     keyval_lin = jnp.concatenate([keys_lin.reshape(rows, kwidth), keyval_grad[:, kwidth:]], axis=1).astype(low)
     grad_linear = jnp.concatenate([query_lin, keyval_lin], axis=1)
     grad_wqkv = jnp.dot(normed_one.T, grad_linear, preferred_element_type=full).astype(low)
-    middle = grad_wqkv.shape[1] // 2
-    grad_wqkv = jnp.concatenate(
-        [
-            sum_rows(grad_wqkv[:, :middle], plane, me, (CORE, ALONG_X, ALONG_Y)),
-            sum_rows(grad_wqkv[:, middle:], plane, me, (CORE, ALONG_Y, ALONG_X)),
-        ],
-        axis=1,
-    )
     grad_bias = jnp.sum(grad_linear.astype(full), axis=0)
     grad_normed_one = jnp.dot(grad_linear, attn_all[:, :qwide].T, preferred_element_type=full)
     unit_one, inverse_one, _ = norm_parts(inputs, gain_one)
@@ -1011,7 +1233,14 @@
     packed = jnp.concatenate(
         [grad_bias.reshape(32, nb), grad_gain_one.reshape(32, ng), grad_gain_two.reshape(32, ng)], axis=1
     )
-    small = sum_small(packed, plane, me)
+    packed = jnp.pad(packed, ((0, 0), (0, 4 * ng - packed.shape[1]))).reshape(32, 4, ng).transpose(0, 2, 1)
+    packed = jnp.pad(packed.reshape(32 * ng, 4), ((0, 0), (0, HEAD - 4))).astype(low)
+    wide, grad_wout, grad_wup = finish(
+        jnp.concatenate([grad_wqkv, packed], axis=1), grad_wout, up_mine, up_sent, 8
+    )
+    grad_wqkv, grad_wout = wide[:, :qwide], grad_wout.T
+    small = wide[:, qwide : qwide + 4].T.reshape(-1)
+    grad_wup = grad_wup.T[:, :own_units]
     return (
         layer_out,
         grad_tokens,
@@ -1019,7 +1248,7 @@
         small[:nb],
         grad_wout,
         small[nb : nb + ng],
-        small[nb + ng :],
+        small[nb + ng : nb + 2 * ng],
         grad_wgate,
         grad_wup,
         grad_down,

time: 934 us -> 865 us (0.926)
  Pallas kernels: 449 us -> 652 us
  waiting for transfers between devices: 196 us -> 18.5 us
  starting transfers between devices: 107 us -> 13.5 us
  local copies, waits for them, and re-layouts: 40.1 us -> 49.7 us
    pallas_call x7 -> x8, Pallas kernels: 241 us -> 444 us  [the longest x7 330 us: call_beside(): pl.pallas_call(whole_body, grid=grid, in_specs=list(in_specs) + [anywhere...]
    ppermute x37 -> x14, waiting for transfers between devices: 152 us -> 18.4 us  [swap(): return lax.ppermute(array, 'gy', [(i, i ^ bits) for i in range(8)])]
    ppermute x37 -> x14, starting transfers between devices: 82.7 us -> 13.3 us  [swap(): return lax.ppermute(array, 'gy', [(i, i ^ bits) for i in range(8)])]
    ppermute x12 -> x0, waiting for transfers between devices: 42.3 us -> none  [ring(): return lax.ppermute(array, 'gx', [(i, (i + 1) % 4) for i in range(4)])]
    ppermute x12 -> x0, starting transfers between devices: 24.2 us -> none  [ring(): return lax.ppermute(array, 'gx', [(i, (i + 1) % 4) for i in range(4)])]
    convert_element_type x18 -> x1, other arithmetic: 24 us -> 1.71 us  [on_core(): lax.psum_scatter(both, 'gx', scatter_dimension=0, tiled=True)[0]]
    concatenate x1 -> x5, other arithmetic: 0.77 us -> 11.4 us  [the longest x1 6.7 us: on_core(): both = jnp.concatenate([down_sum, gate_sum], axis=1).astype(low)]
  transfers between devices with their start and end apart: 55 -> 18, of which waited for: 24 -> 4; matrix products, arithmetic and copies ran while one was open for 15% -> 15% of each run, Pallas kernels for 46% -> 46%
where the time goes in v3:
time: 865 us; the launch traced here: 859 us
  Pallas kernels  652 us (75%)
  other arithmetic  72.8 us (8%)
  local copies, waits for them, and re-layouts  49.7 us (6%)
  matrix products  37.2 us (4%)
  waiting for transfers between devices  18.5 us (2%)
  between operations  14.9 us (2%)
  starting transfers between devices  13.5 us (2%)
    pallas_call x7, Pallas kernels, call_beside(): pl.pallas_call(whole_body, grid=grid, in_specs=list(in_specs) + [anywhere...  330 us
    pallas_call x1, Pallas kernels, spread(): pl.pallas_call(spread_body, in_specs=[anywhere] * 2, out_specs=[anywhere]...  161 us
    pallas_call x1, Pallas kernels, finish(): pl.pallas_call(finish_body, in_specs=[anywhere] * 4, out_specs=[inside] *...  114 us
    pallas_call x1, Pallas kernels, attend_back_fast(): pl.pallas_call(attend_back_body, grid_spec=pltpu.PrefetchScalarGridSpec(n...  23.8 us
    ppermute x14, waiting for transfers between devices, swap(): return lax.ppermute(array, 'gy', [(i, i ^ bits) for i in range(8)])  18.4 us
    unnamed x108, local copies, waits for them, and re-layouts  18.2 us
  transfers between devices with their start and end apart: 18, of which 4 were waited for; matrix products, arithmetic and copies ran while one was open for 15% of the time, Pallas kernels for 46%

profile of v3, /device:TPU:9, one launch (start us, length us, event | category | flops | bytes accessed | tf_op | source)
XLA Modules:
  0.0 858.6 jit_solution(11509647208884146546)
XLA Ops:
  7.2 1.7 copy.37
  12.5 2.6 dynamic-slice_bitcast_fusion.3
  15.8 2.6 dynamic-slice_bitcast_fusion.4
  18.5 1.8 copy.36
  25.1 4.0 fusion.20
  29.2 3.4 maximum_select_fusion.1.rows.refs_1_.refs_4_
  32.5 160.8 %spread.1 = (bf16[4,8,48,3712]{3,2,1,0:T(8,128)(2,1)}, bf16[640,1536]{1,0:T(8,128)(2,1)}, bf16[640,1536]{1,0:T(8,128)(2,1)}, bf16[640,1536]{1,0:T(8,128)(2,1)}) custom-call(bf16[48,3712]{1,0:T(8,128)(2,1)} %fusion.30.own, bf16[640,1536]{1,0:T(8,128)(2,1)} %maximum_select_fusion.1.rows.refs_1_.refs_4_), custom_call_target="tpu_custom_call" | custom-call | bytes 314572800 | tf_op jit(solution)/shard_map/spread/pallas_call | solution.py:878
  195.7 9.1 %project.1 = (bf16[640,1536]{1,0:T(8,128)(2,1)S(1)}, bf16[640,1536]{1,0:T(8,128)(2,1)S(1)}, bf16[640,512]{1,0:T(8,128)(2,1)S(1)}) custom-call(bf16[640,1536]{1,0:T(8,128)(2,1)} %get-tuple-element.169.x_ref, f32[1,1536]{1,0:T(1,128)S(1)} %reshape.246.gain_ref, bf16[1536,3712]{1,0:T(8,128)(2,1)} %bitcast.85, f32[1,2048]{1,0:T(1,128)S(1)} %reshape.247.b_ref, ...), custom_call_target="tpu_custom_call" | custom-call | flops 4026531840 | bytes 14155776 | tf_op jit(solution)/shard_map/project/pallas_call | solution.py:779
  208.7 4.3 select_convert_fusion.bias_ref
  213.1 5.0 or_reduce_fusion
  218.7 1.6 collective-permute-done.2
  222.6 11.6 %collective-permute-done.4 = bf16[640,512]{1,0:T(8,128)(2,1)} collective-permute-done((bf16[640,512]{1,0:T(8,128)(2,1)S(1)}, bf16[640,512]{1,0:T(8,128)(2,1)}, u32[]{:S(2)}, u32[]{:S(2)}) %collective-permute-start.4) | collective-permute-done | bytes 655392 | tf_op jit(solution)/shard_map/ppermute | solution.py:1049
  235.4 1.5 copy-done.21
  236.9 14.2 %tree_attention.1 = (bf16[640,1536]{1,0:T(8,128)(2,1)S(1)}, f32[5,2,1,768]{3,2,1,0:T(1,128)S(1)}) custom-call(s32[5,10]{1,0:T(8,128)S(1)} %select_reduce_fusion.5.list_ref, s32[5]{0:T(128)S(1)} %convert_reduce_fusion.1.count_ref, bf16[640,1536]{1,0:T(8,128)(2,1)S(1)} %copy-done.7, bf16[2560,512]{1,0:T(8,128)(2,1)} %copy-done.21, ...), custom_call_target="tpu_custom_call" | custom-call | flops 10066329600 | bytes 6553600 | tf_op jit(solution)/shard_map/tree_attention/pallas_call | solution.py:631
  253.0 4.3 collective-permute-start.7
  257.9 6.9 multiply_reduce_fusion.2
  264.9 1.8 copy-done.10
  266.7 1.7 multiply_convert_fusion.refs_0_.refs_8_.refs_9_.refs_4_
  268.6 5.1 collective-permute-done.6.refs_6_
  273.6 71.1 %ffn_block.4 = (bf16[640,2304]{1,0:T(8,128)(2,1)}, bf16[640,2304]{1,0:T(8,128)(2,1)}, bf16[640,2304]{1,0:T(8,128)(2,1)}, bf16[640,1536]{1,0:T(8,128)(2,1)}, bf16...) custom-call(bf16[640,1536]{1,0:T(8,128)(2,1)} %multiply_convert_fusion.refs_0_.refs_8_.refs_9_.refs_4_, ...), custom_call_target="tpu_custom_call" | custom-call | flops 27179089920 | bytes 35979264 | tf_op jit(solution)/shard_map/ffn_block/pallas_call | solution.py:432
  344.8 38.3 %ffn_block.5 = (bf16[640,2304]{1,0:T(8,128)(2,1)}, bf16[640,2304]{1,0:T(8,128)(2,1)}, bf16[640,2304]{1,0:T(8,128)(2,1)}, bf16[640,1536]{1,0:T(8,128)(2,1)}, bf16...) custom-call(bf16[640,1536]{1,0:T(8,128)(2,1)} %get-tuple-element.96.refs_0_.refs_8_.refs_5_, ...), custom_call_target="tpu_custom_call" | custom-call | flops 27179089920 | bytes 35979264 | tf_op jit(solution)/shard_map/ffn_block/pallas_call | solution.py:432
  383.1 40.7 %ffn_block.6 = (bf16[640,2304]{1,0:T(8,128)(2,1)}, bf16[640,2304]{1,0:T(8,128)(2,1)}, bf16[640,2304]{1,0:T(8,128)(2,1)}, bf16[640,1536]{1,0:T(8,128)(2,1)}, bf16...) custom-call(bf16[640,1536]{1,0:T(8,128)(2,1)} %get-tuple-element.101.refs_9_.refs_0_.refs_6_, ...), custom_call_target="tpu_custom_call" | custom-call | flops 27179089920 | bytes 35979264 | tf_op jit(solution)/shard_map/ffn_block/pallas_call | solution.py:432
  423.8 39.5 %ffn_block.7 = (bf16[640,2304]{1,0:T(8,128)(2,1)}, bf16[640,2304]{1,0:T(8,128)(2,1)}, bf16[640,2304]{1,0:T(8,128)(2,1)}, bf16[640,1536]{1,0:T(8,128)(2,1)}, bf16...) custom-call(bf16[640,1536]{1,0:T(8,128)(2,1)} %get-tuple-element.104.refs_0_.refs_7_, ...), custom_call_target="tpu_custom_call" | custom-call | flops 27179089920 | bytes 35979264 | tf_op jit(solution)/shard_map/ffn_block/pallas_call | solution.py:432
  463.3 31.2 %ffn_wgrad.3 = (bf16[4,1152,384]{2,1,0:T(8,128)(2,1)}, bf16[4,1152,384]{2,1,0:T(8,128)(2,1)}, bf16[384,1536]{1,0:T(8,128)(2,1)}) custom-call(bf16[640,2304]{1,0:T(8,128)(2,1)} %get-tuple-element.108.refs_0_, bf16[640,2304]{1,0:T(8,128)(2,1)} %get-tuple-element.109.refs_1_, bf16[640,2304]{1,0:T(8,128)(2,1)} %get-tuple-element.110.refs_2_, ...), custom_call_target="tpu_custom_call" | custom-call | flops 18119393280 | bytes 19660800 | tf_op jit(solution)/shard_map/ffn_wgrad/pallas_call | solution.py:432
  494.6 36.5 %ffn_wgrad.4 = (bf16[4,1152,384]{2,1,0:T(8,128)(2,1)}, bf16[4,1152,384]{2,1,0:T(8,128)(2,1)}, bf16[4,1152,384]{2,1,0:T(8,128)(2,1)}, bf16[256,1536]{1,0:T(8,128)(2,1)}, bf16[128,1536]{1,0:T(8,128)(2,1)}) custom-call(bf16[640,2304]{1,0:T(8,128)(2,1)} %get-tuple-element.95.refs_0_, bf16[640,2304]{1,0:T(8,128)(2,1)} %get-tuple-element.99.refs_1_, ...), custom_call_target="tpu_custom_call" | custom-call | flops 18119393280 | bytes 19660800 | tf_op jit(solution)/shard_map/ffn_wgrad/pallas_call | solution.py:432
  535.8 1.6 copy-done.11
  538.0 3.7 multiply_reduce_fusion
  541.8 2.8 add_convert_fusion.1
  544.6 4.7 add_convert_fusion
  549.3 6.7 pad_maximum_fusion
  556.0 6.9 multiply_add_fusion
  565.7 8.7 %convolution_convert_fusion.1 = bf16[1536,1536]{1,0:T(8,128)(2,1)} fusion(bf16[640,1536]{1,0:T(8,128)(2,1)} %copy-done.8, f32[640,1536]{1,0:T(8,128)} %multiply_add_fusion), kind=kOutput, calls=%fused_computation.3 | convolution fusion | flops 3023241216 | bytes 10616832 | tf_op jit(solution)/shard_map/dot_general | solution.py:1203
  574.4 6.7 fusion.23.do_ref
  581.1 23.8 %tree_attention_back.1 = (bf16[640,1536]{1,0:T(8,128)(2,1)}, bf16[2560,512]{1,0:T(8,128)(2,1)}) custom-call(s32[5,10]{1,0:T(8,128)} %copy-done.4, s32[5]{0:T(128)} %copy-done.5, bf16[640,1536]{1,0:T(8,128)(2,1)} %copy-done.6, bf16[2560,512]{1,0:T(8,128)(2,1)} %copy-done.21, bf16[2560,640]{1,0:T(8,128)(2,1)} %select_convert_fusion.bias_ref, ...), custom_call_target="tpu_custom_call" | custom-call | flops 25165824000 | bytes 13107200 | tf_op jit(solution)/shard_map/tree_attention_back/pallas_call | solution.py:722
  604.9 2.8 constant_dynamic-slice_fusion.1
  607.7 73.1 %ffn_wgrad.5 = (bf16[4,1152,384]{2,1,0:T(8,128)(2,1)}, bf16[4,1152,384]{2,1,0:T(8,128)(2,1)}, bf16[640,512]{1,0:T(8,128)(2,1)}, bf16[640,512]{1,0:T(8,128)(2,1)}, bf16[640,512]{1,0:T(8,128)(2,1)}) custom-call(bf16[640,2304]{1,0:T(8,128)(2,1)} %get-tuple-element.143.refs_0_, bf16[640,2304]{1,0:T(8,128)(2,1)} %get-tuple-element.144.refs_1_, ...), custom_call_target="tpu_custom_call" | custom-call | flops 18119393280 | bytes 19660800 | tf_op jit(solution)/shard_map/ffn_wgrad/pallas_call | solution.py:432
  680.8 2.0 convert_add_fusion.2
  689.6 9.2 %fusion.19 = (bf16[1536]{0:T(1024)(128)(2,1)S(1)}, f32[640]{0:T(1024)S(1)}, f32[640,1536]{1,0:T(8,128)}) fusion(bf16[640,1536]{1,0:T(8,128)(2,1)S(1)} %copy-done.14, f32[640]{0:T(1024)S(1)} %add_rsqrt_fusion, f32[1536]{0:T(1024)S(1)} %copy-done.46, bf16[1536,3712]{1,0:T(8,128)(2,1)} %bitcast.88, bf16[640,256]{1,0:T(8,128)(2,1)S(1)} %copy-done.30, ...), kind=kOutput, calls=%fused_computation.32 | convolution fusion | flops 4041275392 | bytes 14825472 | tf_op jit(solution)/shard_map/dot_general | solution.py:1226
  699.9 5.0 fusion.18
  707.4 4.0 add_convert_fusion.2
  713.8 5.8 convolution_convert_fusion
  719.5 3.2 fusion.1
  722.7 113.6 %finish.1 = (f32[48,2176]{1,0:T(8,128)}, f32[48,1536]{1,0:T(8,128)}, f32[1152,384]{1,0:T(8,128)}) custom-call(bf16[4,2,2,2,48,2176]{5,4,3,2,1,0:T(8,128)(2,1)} %bitcast.69, bf16[4,2,2,2,48,1536]{5,4,3,2,1,0:T(8,128)(2,1)} %bitcast.70, bf16[4,1152,384]{2,1,0:T(8,128)(2,1)} %get-tuple-element.151.mine_ref, bf16[4,1152,384]{2,1,0:T(8,128)(2,1)} %get-tuple-element.152.sent_ref), custom_call_target="tpu_custom_call" | custom-call | bytes 209715200 | tf_op jit(solution)/shard_map/finish/pallas_call | solution.py:1021
  836.4 2.9 slice.99
  841.3 3.1 maximum_select_fusion.3
  844.4 3.1 maximum_select_fusion.2
  847.4 1.7 convert_element_type.156
  849.2 2.0 slice_bitcast_fusion
  (217 shorter events, 45.4 us)
Async XLA Ops:
  7.2 2.8 copy-start.33
  7.2 245.8 %all-gather.8.cloned.1.call-start = ((), (), s32[]{:S(2)}) async-start(), calls=%async_computation.3 | async-start | bytes 4423680 | tf_op jit(solution)/shard_map/all_gather | solution.py:1126
  9.9 247.4 %all-gather.4.cloned.1.call-start = ((), (), s32[]{:S(2)}) async-start(), calls=%async_computation.1 | async-start | bytes 4423680 | tf_op jit(solution)/shard_map/all_gather | solution.py:1126
  12.5 244.9 %all-gather.6.cloned.1.call-start = ((), (), s32[]{:S(2)}) async-start(), calls=%async_computation.2 | async-start | bytes 4423680 | tf_op jit(solution)/shard_map/all_gather | solution.py:1126
  15.1 6.2 copy-start.47
  15.1 6.5 copy-start.51
  15.1 14.1 %collective-permute-start.1 = (bf16[320,1536]{1,0:T(8,128)(2,1)}, bf16[320,1536]{1,0:T(8,128)(2,1)}, u32[]{:S(2)}, u32[]{:S(2)}) collective-permute-start(bf16[320,1536]{1,0:T(8,128)(2,1)} %get-tuple-element.181), channel_id=1, source_target_pairs={{0,1},{1,0},{2,3},{3,2},{4,5},{5,4},{6,7},{7,6},{8,9},{9,8},{10,11... | collective-permute-start | bytes 2949128 | tf_op jit(solution)/shard_map/ppermute | solution.py:1049
  18.4 5.4 copy-start.48
  18.4 5.5 copy-start.49
  18.4 5.5 copy-start.50
  18.4 6.0 copy-start.38
  18.4 6.0 copy-start.41
  18.4 6.8 collective-permute-start
  21.3 826.2 %reduce-scatter.2.cloned.1.call-start = ((), (), s32[]{:S(2)}) async-start(), calls=%async_computation.4 | async-start | bytes 8847360 | tf_op jit(solution)/shard_map/reduce_scatter | solution.py:1208
  23.8 171.8 %copy-start = (f32[640,128]{1,0:T(8,128)}, f32[640,128]{1,0:T(8,128)S(1)}, u32[]{:S(2)}) copy-start(f32[640,128]{1,0:T(8,128)S(1)} %get-tuple-element.199.sin_ref) | copy-start | bytes 983044
  23.8 171.8 %copy-start.2 = (f32[640,128]{1,0:T(8,128)}, f32[640,128]{1,0:T(8,128)S(1)}, u32[]{:S(2)}) copy-start(f32[640,128]{1,0:T(8,128)S(1)} %get-tuple-element.198.cos_ref) | copy-start | bytes 983044
  206.1 14.2 %collective-permute-start.2 = (bf16[640,512]{1,0:T(8,128)(2,1)S(1)}, bf16[640,512]{1,0:T(8,128)(2,1)}, u32[]{:S(2)}, u32[]{:S(2)}) collective-permute-start(bf16[640,512]{1,0:T(8,128)(2,1)S(1)} %get-tuple-element.85), channel_id=1, source_target_pairs={{0,2},{1,3},{2,0},{3,1},{4,6},{5,7},{6,4},{7,5},{8,10},{9,11},{10,... | collective-permute-start | bytes 1966088 | tf_op jit(solution)/shard_map/ppermute | solution.py:1049
  206.1 15.3 %collective-permute-start.3 = (bf16[640,512]{1,0:T(8,128)(2,1)S(1)}, bf16[640,512]{1,0:T(8,128)(2,1)}, u32[]{:S(2)}, u32[]{:S(2)}) collective-permute-start(bf16[640,512]{1,0:T(8,128)(2,1)S(1)} %get-tuple-element.85), channel_id=1, source_target_pairs={{0,4},{1,5},{2,6},{3,7},{4,0},{5,1},{6,2},{7,3},{8,12},{9,13},{10,... | collective-permute-start | bytes 1966088 | tf_op jit(solution)/shard_map/ppermute | solution.py:1049
  207.6 26.7 %collective-permute-start.4 = (bf16[640,512]{1,0:T(8,128)(2,1)S(1)}, bf16[640,512]{1,0:T(8,128)(2,1)}, u32[]{:S(2)}, u32[]{:S(2)}) collective-permute-start(bf16[640,512]{1,0:T(8,128)(2,1)S(1)} %get-tuple-element.85), channel_id=1, source_target_pairs={{0,6},{1,7},{2,4},{3,5},{4,2},{5,3},{6,0},{7,1},{8,14},{9,15},{10,... | collective-permute-start | bytes 1966088 | tf_op jit(solution)/shard_map/ppermute | solution.py:1049
  218.4 17.0 %copy-start.5 = (s32[5]{0:T(128)}, s32[5]{0:T(128)S(1)}, u32[]{:S(2)}) copy-start(s32[5]{0:T(128)S(1)} %convert_reduce_fusion.1.count_ref) | copy-start | bytes 64
  218.5 16.9 %copy-start.4 = (s32[5,10]{1,0:T(8,128)}, s32[5,10]{1,0:T(8,128)S(1)}, u32[]{:S(2)}) copy-start(s32[5,10]{1,0:T(8,128)S(1)} %select_reduce_fusion.5.list_ref) | copy-start | bytes 604
  218.5 18.4 %copy-start.7 = (bf16[640,1536]{1,0:T(8,128)(2,1)S(1)}, bf16[640,1536]{1,0:T(8,128)(2,1)}, u32[]{:S(2)}) copy-start(bf16[640,1536]{1,0:T(8,128)(2,1)} %copy-done.6) | copy-start | bytes 5898244
  253.0 15.4 %collective-permute-start.7 = (bf16[1536,1152]{1,0:T(8,128)(2,1)}, bf16[1536,1152]{1,0:T(8,128)(2,1)}, u32[]{:S(2)}, u32[]{:S(2)}) collective-permute-start(bf16[1536,1152]{1,0:T(8,128)(2,1)} %all-gather.8.cloned.1.call-done.refs_4_), channel_id=1, source_target_pairs={{0,1},{1,0},{2,3},{3,2},{4,5},{5,4},{6,7},{7,6},{8,9},{9,8},{10,11... | collective-permute-start | bytes 10616840 | tf_op jit(solution)/shard_map/ppermute | solution.py:1049
  257.3 11.2 %collective-permute-start.5 = (bf16[1536,1152]{1,0:T(8,128)(2,1)}, bf16[1536,1152]{1,0:T(8,128)(2,1)}, u32[]{:S(2)}, u32[]{:S(2)}) collective-permute-start(bf16[1536,1152]{1,0:T(8,128)(2,1)} %all-gather.4.cloned.1.call-done.refs_2_), channel_id=1, source_target_pairs={{0,1},{1,0},{2,3},{3,2},{4,5},{5,4},{6,7},{7,6},{8,9},{9,8},{10,11... | collective-permute-start | bytes 10616840 | tf_op jit(solution)/shard_map/ppermute | solution.py:1049
  257.3 16.3 %collective-permute-start.6 = (bf16[1536,1152]{1,0:T(8,128)(2,1)}, bf16[1536,1152]{1,0:T(8,128)(2,1)}, u32[]{:S(2)}, u32[]{:S(2)}) collective-permute-start(bf16[1536,1152]{1,0:T(8,128)(2,1)} %all-gather.6.cloned.1.call-done.refs_3_), channel_id=1, source_target_pairs={{0,1},{1,0},{2,3},{3,2},{4,5},{5,4},{6,7},{7,6},{8,9},{9,8},{10,11... | collective-permute-start | bytes 10616840 | tf_op jit(solution)/shard_map/ppermute | solution.py:1049
  257.9 6.9 copy-start.42
  264.8 3.5 copy-start.44
  494.6 37.9 %copy-start.40 = (f32[32,48]{1,0:T(8,128)S(1)}, f32[32,48]{1,0:T(8,128)}, u32[]{:S(2)}) copy-start(f32[32,48]{1,0:T(8,128)} %copy-done.39) | copy-start | bytes 18436
  494.6 39.4 %copy-start.26 = (bf16[512,1536]{1,0:T(8,128)(2,1)S(1)}, bf16[512,1536]{1,0:T(8,128)(2,1)}, u32[]{:S(2)}) copy-start(bf16[512,1536]{1,0:T(8,128)(2,1)} %get-tuple-element.119) | copy-start | bytes 4718596
  531.1 13.5 %collective-permute-start.8 = (bf16[4,1152,384]{2,1,0:T(8,128)(2,1)}, bf16[4,1152,384]{2,1,0:T(8,128)(2,1)}, u32[]{:S(2)}, u32[]{:S(2)}) collective-permute-start(bf16[4,1152,384]{2,1,0:T(8,128)(2,1)} %get-tuple-element.117), channel_id=1, source_target_pairs={{0,1},{1,0},{2,3},{3,2},{4,5},{5,4},{6,7},{7,6},{8,9},{9,8},{10,11... | collective-permute-start | bytes 10616840 | tf_op jit(solution)/shard_map/ppermute | solution.py:1049
  535.2 2.8 copy-start.25
  535.2 2.8 copy-start.43
  535.3 2.8 copy-start.45
  538.0 3.7 copy-start.18
  538.0 3.8 copy-start.20
  541.8 2.8 copy-start.19
  563.0 143.5 %collective-permute-start.9 = (bf16[640,1536]{1,0:T(8,128)(2,1)}, bf16[640,1536]{1,0:T(8,128)(2,1)}, u32[]{:S(2)}, u32[]{:S(2)}) collective-permute-start(bf16[640,1536]{1,0:T(8,128)(2,1)} %get-tuple-element.134), channel_id=1, source_target_pairs={{0,2},{1,3},{2,0},{3,1},{4,6},{5,7},{6,4},{7,5},{8,10},{9,11},{10,... | collective-permute-start | bytes 5898248 | tf_op jit(solution)/shard_map/ppermute | solution.py:1049
  564.0 142.5 %collective-permute-start.10 = (bf16[640,1536]{1,0:T(8,128)(2,1)}, bf16[640,1536]{1,0:T(8,128)(2,1)}, u32[]{:S(2)}, u32[]{:S(2)}) collective-permute-start(bf16[640,1536]{1,0:T(8,128)(2,1)} %get-tuple-element.137), channel_id=1, source_target_pairs={{0,4},{1,5},{2,6},{3,7},{4,0},{5,1},{6,2},{7,3},{8,12},{9,13},{10,... | collective-permute-start | bytes 5898248 | tf_op jit(solution)/shard_map/ppermute | solution.py:1049
  564.5 9.9 %copy-start.13 = (f32[640,1536]{1,0:T(8,128)S(1)}, f32[640,1536]{1,0:T(8,128)}, u32[]{:S(2)}) copy-start(f32[640,1536]{1,0:T(8,128)} %multiply_add_fusion) | copy-start | bytes 11796484
  564.5 142.0 %collective-permute-start.11 = (bf16[640,1536]{1,0:T(8,128)(2,1)}, bf16[640,1536]{1,0:T(8,128)(2,1)}, u32[]{:S(2)}, u32[]{:S(2)}) collective-permute-start(bf16[640,1536]{1,0:T(8,128)(2,1)} %get-tuple-element.140), channel_id=1, source_target_pairs={{0,6},{1,7},{2,4},{3,5},{4,2},{5,3},{6,0},{7,1},{8,14},{9,15},{10,... | collective-permute-start | bytes 5898248 | tf_op jit(solution)/shard_map/ppermute | solution.py:1049
  682.8 4.2 copy-start.1
  684.1 3.8 copy-start.3
  688.4 10.4 %copy-start.28 = (bf16[640,256]{1,0:T(8,128)(2,1)}, bf16[640,256]{1,0:T(8,128)(2,1)S(1)}, u32[]{:S(2)}) copy-start(bf16[640,256]{1,0:T(8,128)(2,1)S(1)} %fusion.29) | copy-start | bytes 983044
  699.9 6.7 copy-start.24
  706.0 135.3 %collective-permute-start.13 = (bf16[320,1536]{1,0:T(8,128)(2,1)}, bf16[320,1536]{1,0:T(8,128)(2,1)}, u32[]{:S(2)}, u32[]{:S(2)}) collective-permute-start(bf16[320,1536]{1,0:T(8,128)(2,1)} %get-tuple-element.177), channel_id=1, source_target_pairs={{0,1},{1,0},{2,3},{3,2},{4,5},{5,4},{6,7},{7,6},{8,9},{9,8},{10,11... | collective-permute-start | bytes 2949128 | tf_op jit(solution)/shard_map/ppermute | solution.py:1049
  712.9 131.5 %collective-permute-start.12 = (bf16[320,1536]{1,0:T(8,128)(2,1)}, bf16[320,1536]{1,0:T(8,128)(2,1)}, u32[]{:S(2)}, u32[]{:S(2)}) collective-permute-start(bf16[320,1536]{1,0:T(8,128)(2,1)} %get-tuple-element.179), channel_id=1, source_target_pairs={{0,1},{1,0},{2,3},{3,2},{4,5},{5,4},{6,7},{7,6},{8,9},{9,8},{10,11... | collective-permute-start | bytes 2949128 | tf_op jit(solution)/shard_map/ppermute | solution.py:1049
  836.4 2.9 copy-start.35
  836.4 8.0 copy-start.17
  (22 other events, 40.5 us)
Sparse Core Ops, SparseCore 0:
  10.0 97.6 all-gather.7
  109.9 69.6 all-gather.3
  181.1 68.5 all-gather.5
  556.1 132.2 reduce-scatter.1

commit v4 on v3

--- a/solution.py
+++ b/solution.py
@@ -15,6 +15,7 @@
 QUERY_TILE = 128
 KEY_TILE = 256
 ROW_TILE = 128
+BRANCH_CUTS = (4, 3)
 FFN_CHUNK = 768
 FFN_PARTS = 2
 WG_TILE = 384
@@ -598,10 +599,10 @@
     def body(n, carry):
         rows = pl.ds(pl.multiple_of(list_ref[block, n] * KEY_TILE, KEY_TILE), KEY_TILE)
         bias = jnp.concatenate([bias_ref[rows, :].astype(jnp.float32)] * per_group, axis=1)
+        products = [dot_nt(kv_ref[rows, g * HEAD : (g + 1) * HEAD], qs[g]) for g in range(KV_HEADS)]
         for group in range(KV_HEADS):
-            keys = kv_ref[rows, group * HEAD : (group + 1) * HEAD]
             values = kv_ref[rows, (KV_HEADS + group) * HEAD : (KV_HEADS + group + 1) * HEAD]
-            scores = dot_nt(keys, qs[group]) * factor + bias
+            scores = products[group] * factor + bias
             old = top[group]
             new = jnp.maximum(old, jnp.max(scores, axis=0, keepdims=True))
             probs = jnp.exp2(scores - new)
@@ -803,94 +804,200 @@
     )(inputs, gain, w_qkv, bias, cosine, sine)
 
 
-def spread_body(own, rows, whole, rows_x, rows_y, rows_d, sent, landed, kept):
+def spread_body(*refs):
+    owns, rows, whole, rows_x, rows_y, rows_d, sent, landed, kept = refs[:4], *refs[4:]
     me, plane = lax.axis_index("gy"), lax.axis_index("gx")
-    core = me + 1 - 2 * lax.rem(me, 2)
-    along_x = me + 2 - 4 * lax.rem(me // 2, 2)
-    along_y = me + 4 - 8 * (me // 4)
-    across = along_x + 4 - 8 * (along_x // 4)
+    peers = peers_of()
+    along_x, along_y, across = (peers[bits]["gy"] for bits in OTHERS)
     places = [lax.rem(plane + 4 - k, 4) for k in range(4)]
-    ahead = [lax.rem(plane + k, 4) for k in range(4)]
-    barrier = pltpu.get_barrier_semaphore()
-    peers = [{"gy": core}, {"gy": along_x}, {"gy": along_y}] + [{"gx": ahead[k]} for k in (1, 2, 3)]
-    for peer in peers:
-        pl.semaphore_signal(barrier, inc=1, device_id=peer, device_id_type=pl.DeviceIdType.MESH)
-    pl.semaphore_wait(barrier, len(peers))
+    greet((CORE, ALONG_X, ALONG_Y))
     copies = []
 
-    def send(source, target, peer):
+    def send(source, target, bits):
         copy = pltpu.make_async_remote_copy(
             source,
             target,
             sent.at[len(copies)],
             landed.at[len(copies)],
-            device_id=peer,
+            device_id=peers[bits],
             device_id_type=pl.DeviceIdType.MESH,
         )
         copies.append(copy)
         copy.start()
         return copy
 
-    to_core, to_x, to_y = peers[:3]
-    from_z = [send(own, whole.at[plane, me], peers[2 + k]) for k in (1, 2, 3)]
-    local = pltpu.make_async_copy(own, whole.at[plane, me], kept)
-    local.start()
-    from_x, from_y, from_d, from_core = [], [], [], []
+    from_x, from_y, from_d, from_core, local = [], [], [], [], []
     for k in range(4):
         block = whole.at[places[k], me]
-        source = own if k == 0 else block
-        if k > 0:
-            from_z[k - 1].wait_recv()
-        from_x.append(send(source, block, to_x))
-        from_y.append(send(source, block, to_y))
-        from_core.append(send(source, block, to_core))
-    moved_x, moved_y = send(rows, rows_x, to_x), send(rows, rows_y, to_y)
+        from_x.append(send(owns[k], block, ALONG_X))
+        from_y.append(send(owns[k], block, ALONG_Y))
+        from_core.append(send(owns[k], block, CORE))
+        local.append(pltpu.make_async_copy(owns[k], block, kept.at[k]))
+        local[k].start()
+    moved_x, moved_y = send(rows, rows_x, ALONG_X), send(rows, rows_y, ALONG_Y)
     for k in range(4):
         block_x, block_y = whole.at[places[k], along_x], whole.at[places[k], along_y]
         from_x[k].wait_recv()
         if k < 2:
-            from_d.append(send(block_x, block_x, to_y))
-        from_core.append(send(block_x, block_x, to_core))
+            from_d.append(send(block_x, block_x, ALONG_Y))
+        from_core.append(send(block_x, block_x, CORE))
         from_y[k].wait_recv()
         if k >= 2:
-            from_d.append(send(block_y, block_y, to_x))
-        from_core.append(send(block_y, block_y, to_core))
+            from_d.append(send(block_y, block_y, ALONG_X))
+        from_core.append(send(block_y, block_y, CORE))
     for k in range(4):
         block = whole.at[places[k], across]
         from_d[k].wait_recv()
-        from_core.append(send(block, block, to_core))
+        from_core.append(send(block, block, CORE))
     half = rows.shape[0] // 2
     first, second = pl.ds(0, half), pl.ds(half, half)
     moved_x.wait_recv()
-    moved_d = [send(rows_x.at[first], rows_d.at[first], to_y)]
+    moved_d = [send(rows_x.at[first], rows_d.at[first], ALONG_Y)]
     moved_y.wait_recv()
-    moved_d.append(send(rows_y.at[second], rows_d.at[second], to_x))
+    moved_d.append(send(rows_y.at[second], rows_d.at[second], ALONG_X))
     for copy in from_core + moved_d:
         copy.wait_recv()
     for copy in copies:
         copy.wait_send()
-    local.wait()
-
-
-def spread(own, rows):
-    deep, wide = own.shape
+    for copy in local:
+        copy.wait()
+
+
+def spread(owns, rows):
+    deep, wide = owns[0].shape
     anywhere = pl.BlockSpec(memory_space=pl.ANY)
     whole, *others = pl.pallas_call(
         spread_body,
-        in_specs=[anywhere] * 2,
+        in_specs=[anywhere] * 5,
         out_specs=[anywhere] * 4,
-        out_shape=[jax.ShapeDtypeStruct((4, 8, deep, wide), own.dtype)]
+        out_shape=[jax.ShapeDtypeStruct((4, 8, deep, wide), rows.dtype)]
         + [jax.ShapeDtypeStruct(rows.shape, rows.dtype)] * 3,
         scratch_shapes=[
-            pltpu.SemaphoreType.DMA((35,)),
-            pltpu.SemaphoreType.DMA((35,)),
-            pltpu.SemaphoreType.DMA,
+            pltpu.SemaphoreType.DMA((32,)),
+            pltpu.SemaphoreType.DMA((32,)),
+            pltpu.SemaphoreType.DMA((4,)),
         ],
         compiler_params=pltpu.CompilerParams(collective_id=0, has_side_effects=True),
         cost_estimate=cost(0, 300 * 1024 * 1024),
         name="spread",
-    )(own, rows)
+    )(*owns, rows)
     return whole.reshape(32 * deep, wide), others
+
+
+def unit_back(grad_normed, values, gain):
+    inverse = lax.rsqrt(jnp.mean(values * values, axis=-1, keepdims=True) + EPS)
+    unit = values * inverse
+    scaled = grad_normed * gain
+    back = inverse * (scaled - unit * jnp.mean(scaled * unit, axis=-1, keepdims=True))
+    return back, jnp.sum(grad_normed * unit, axis=0, keepdims=True)
+
+
+def branch_back_body(own_ref, xa_ref, xb_ref, ya_ref, yb_ref, resid_ref, cot_ref, gain_ref, heads_ref, *refs):
+    turned, (resid_out, heads_out, gain_out, weight_out, branch) = refs[:-5], refs[-5:]
+    step, full = pl.program_id(0), jnp.float32
+    tile = own_ref.shape[0]
+    from_x = jnp.where(step < BRANCH_CUTS[0], xa_ref[...].astype(full), xb_ref[...].astype(full))
+    from_y = jnp.where(step < BRANCH_CUTS[1], ya_ref[...].astype(full), yb_ref[...].astype(full))
+    grad_normed = own_ref[...].astype(full) + from_x + from_y
+    back, gain_part = unit_back(grad_normed, resid_ref[...], gain_ref[...])
+    grad_resid = cot_ref[...].astype(full) + back
+    resid_out[...] = grad_resid
+    low = grad_resid.astype(jnp.bfloat16)
+    branch[pl.ds(pl.multiple_of(step * tile, tile), tile), :] = low
+    gain_out[...] = jnp.where(step == 0, 0.0, gain_out[...]) + gain_part
+    wide = turned[0].shape[1]
+    for index, piece in enumerate(turned):
+        heads_out[:, index * wide : (index + 1) * wide] = dot_nn(low, piece[...]).astype(jnp.bfloat16)
+
+    @pl.when(step == pl.num_programs(0) - 1)
+    def _():
+        weight_out[...] = dot_tn(branch[...], heads_ref[...]).astype(jnp.bfloat16)
+
+
+def branch_back(own, from_x, from_y, resid, cotan, gain, heads, weights, first_column):
+    rows, width = own.shape
+    tile, wide = ROW_TILE, 512
+    steps = rows // tile
+    low, full = jnp.bfloat16, jnp.float32
+    moving = pl.BlockSpec((tile, width), lambda i: (i, 0))
+    fixed = pl.BlockSpec((1, width), lambda i: (0, 0))
+    first, then = [], []
+    for count in BRANCH_CUTS:
+        first.append(pl.BlockSpec((tile, width), lambda i, n=count: (jnp.minimum(i, n - 1), 0)))
+        then.append(pl.BlockSpec((tile, width), lambda i, n=count: (jnp.maximum(i - n, 0), 0)))
+    return pl.pallas_call(
+        branch_back_body,
+        grid=(steps,),
+        in_specs=[moving, first[0], then[0], first[1], then[1], moving, moving, fixed]
+        + [pl.BlockSpec((rows, width), lambda i: (0, 0))]
+        + [pl.BlockSpec((width, wide), lambda i, j=j: (0, first_column // wide + j)) for j in range(width // wide)],
+        out_specs=[moving, moving, fixed, pl.BlockSpec((width, width), lambda i: (0, 0))],
+        out_shape=[
+            jax.ShapeDtypeStruct((rows, width), full),
+            jax.ShapeDtypeStruct((rows, width), low),
+            jax.ShapeDtypeStruct((1, width), full),
+            jax.ShapeDtypeStruct((width, width), low),
+        ],
+        scratch_shapes=[pltpu.VMEM((rows, width), low)],
+        compiler_params=params(56),
+        cost_estimate=cost(4 * rows * width * width, 20 * rows * width + 4 * width * width),
+        name="branch_back",
+    )(own, *from_x, *from_y, resid, cotan, gain, heads, *[weights] * (width // wide))
+
+
+def project_back_body(q_ref, own_ref, x_ref, y_ref, d_ref, cos_ref, sin_ref, w_ref, in_ref, gain_ref, resid_ref, normed_ref,
+                      tokens_out, bias_out, gain_out, weight_out, linear):
+    step, full = pl.program_id(0), jnp.float32
+    tile, qwidth = q_ref.shape
+    total = own_ref[...].astype(full) + x_ref[...].astype(full) + y_ref[...].astype(full) + d_ref[...].astype(full)
+    pieces = [q_ref[...]]
+    for head in range(2 * KV_HEADS):
+        lane = total[:, head * HEAD : (head + 1) * HEAD]
+        if head < KV_HEADS:
+            lane = lane * cos_ref[...] - pltpu.roll(lane, HEAD // 2, 1) * sin_ref[...]
+        pieces.append(lane.astype(jnp.bfloat16))
+    lin = jnp.concatenate(pieces, axis=1)
+    linear[pl.ds(pl.multiple_of(step * tile, tile), tile), :] = lin
+    bias_part = jnp.sum(lin.astype(full), axis=0, keepdims=True)
+    bias_out[...] = jnp.where(step == 0, 0.0, bias_out[...]) + bias_part
+    back, gain_part = unit_back(dot_nt(lin, w_ref[...]), in_ref[...].astype(full), gain_ref[...])
+    gain_out[...] = jnp.where(step == 0, 0.0, gain_out[...]) + gain_part
+    tokens_out[...] = (resid_ref[...] + back).astype(jnp.bfloat16)
+
+    @pl.when(step == pl.num_programs(0) - 1)
+    def _():
+        weight_out[...] = dot_tn(normed_ref[...], linear[...]).astype(jnp.bfloat16)
+
+
+def project_back(query_lin, parts, cosine, sine, weights, inputs, gain, grad_resid, normed):
+    rows, width = inputs.shape
+    qwidth, kwidth = query_lin.shape[1], parts[0].shape[1]
+    qwide, tile = qwidth + kwidth, ROW_TILE
+    low, full = jnp.bfloat16, jnp.float32
+
+    def moving(columns):
+        return pl.BlockSpec((tile, columns), lambda i: (i, 0))
+
+    def fixed(high, columns):
+        return pl.BlockSpec((high, columns), lambda i: (0, 0))
+
+    return pl.pallas_call(
+        project_back_body,
+        grid=(rows // tile,),
+        in_specs=[moving(qwidth)] + [moving(kwidth)] * 4 + [moving(HEAD)] * 2
+        + [fixed(width, qwide), moving(width), fixed(1, width), moving(width), fixed(rows, width)],
+        out_specs=[moving(width), fixed(1, qwide), fixed(1, width), fixed(width, qwide)],
+        out_shape=[
+            jax.ShapeDtypeStruct((rows, width), low),
+            jax.ShapeDtypeStruct((1, qwide), full),
+            jax.ShapeDtypeStruct((1, width), full),
+            jax.ShapeDtypeStruct((width, qwide), low),
+        ],
+        scratch_shapes=[pltpu.VMEM((rows, qwide), low)],
+        compiler_params=params(56),
+        cost_estimate=cost(4 * rows * width * qwide, 20 * rows * width + 4 * width * qwide),
+        name="project_back",
+    )(query_lin, *parts, cosine, sine, weights, inputs, gain, grad_resid, normed)
 
 
 def finish_body(wide_ref, out_ref, mine_ref, sent_ref, *refs):
@@ -1107,6 +1214,9 @@
     packed = jnp.pad(packed, ((0, 4 * ng - packed.shape[0]), (0, 0))).reshape(4, ng).T
     packed = jnp.pad(packed, ((0, 0), (0, HEAD - 4)))
     attn_own = jnp.concatenate([w_qkv, w_out.T, packed], axis=1)
+    attn_slots = [attn_own] + [
+        lax.ppermute(attn_own, "gx", [(i, (i + k) % 4) for i in range(4)]) for k in (1, 2, 3)
+    ]
 
     inputs_low = pair_rows(tokens, core)
     grad_low = pair_rows(cotangent, core)
@@ -1123,8 +1233,8 @@
 
     more = pad_units - own_units
     shards = [jnp.pad(w, ((0, 0), (0, more))) for w in (w_gate, w_up, w_down.T)]
-    weights = [lax.all_gather(w, "gx", axis=0, tiled=True) for w in shards]
-    attn_all, cotan_others = spread(after(attn_own, inputs_low, cosine, sine), grad_low)
+    weights = [lax.all_gather(after(w, *attn_slots, inputs_low, grad_low), "gx", axis=0, tiled=True) for w in shards]
+    attn_all, cotan_others = spread([after(s, inputs_low, cosine, sine, *shards) for s in attn_slots], grad_low)
     cotan_blocks = [grad_low] + cotan_others
     qwide = qwidth + 2 * kwidth
     small = attn_all[:, qwide + width :].reshape(32, ng, HEAD)[:, :, :4].transpose(0, 2, 1).reshape(32, 4 * ng)
@@ -1152,7 +1262,7 @@
     heads_out, lse = attend_fast(block_list, block_count, query, keyval, mask_bias)
     inputs = inputs_low.astype(full)
     resid = inputs + lax.dot_general(heads_out, out_turned, (((1,), (1,)), ((), ())), preferred_element_type=full)
-    unit_two, inverse_two, normed_two = norm_parts(resid, gain_two)
+    normed_two = norm_parts(resid, gain_two)[2]
 
     other_weights.append(swap(after(weights[2], heads_out), CORE))
     pieces = weights + other_weights
@@ -1163,45 +1273,58 @@
     )
     passed_on = [(normed_x, first, first, ALONG_Y), (normed_y, second, second, ALONG_X)]
     near_x, (normed_d,) = ffn_block(normed_x, cotan_blocks[1], pieces, 2, [passed_on])
-    near_y, (back_x,) = ffn_block(
-        after(normed_y, near_x[4]), cotan_blocks[2], pieces, 3, [rows_side(near_x[4], 0, 512, ALONG_X)]
-    )
-    far, (back_y, back_x_end) = ffn_block(
-        normed_d,
-        cotan_blocks[3],
-        pieces,
-        4,
-        [rows_side(near_y[4], 0, 512, ALONG_Y), rows_side(near_x[4], 512, rows - 512, ALONG_X)],
+    cut, early = (count * ROW_TILE for count in BRANCH_CUTS)
+    rest, few = rows - cut, rows // 10 * 3
+    far, (back_x,) = ffn_block(normed_d, cotan_blocks[3], pieces, 3, [rows_side(near_x[4], 0, cut, ALONG_X)])
+    near_y, (back_d,) = ffn_block(
+        after(normed_y, far[4]), cotan_blocks[2], pieces, 4, [rows_side(far[4], 0, cut, ALONG_X)]
     )
     normed_blocks = [normed_two, normed_x, normed_y, normed_d]
     hidden_b, gate_b, up_b, out_b, back_b = zip(own, near_x, near_y, far)
 
-    (down_mine, down_sent), (back_d,) = wgrad(hidden_b, cotan_blocks, 4, 5, [rows_side(back_b[3], 0, 384, ACROSS)])
-    (gate_mine, gate_sent), (down_got, back_d_end, back_y_end) = wgrad(
+    def join(mine, passed):
+        return (mine.astype(full) + passed.astype(full)).astype(low)
+
+    (down_mine, down_sent), (back_x_end, back_d_end, out_d_end, back_y) = wgrad(
+        hidden_b,
+        cotan_blocks,
+        4,
+        5,
+        [
+            rows_side(back_b[1], cut, rest, ALONG_X),
+            rows_side(back_b[3], cut, rest, ALONG_X),
+            rows_side(out_b[3], 0, few, ALONG_X),
+            rows_side(join(back_b[2][:early], back_d[:early]), 0, early, ALONG_Y),
+        ],
+    )
+    late = join(back_b[2][early:], jnp.concatenate([back_d[early:], back_d_end]))
+    (gate_mine, gate_sent), (down_got, out_d, back_y_end) = wgrad(
         gate_b,
         normed_blocks,
         4,
         6,
         [
             whole_side(down_sent, CORE),
-            rows_side(after(back_b[3], back_d), 384, rows - 384, ACROSS),
-            rows_side(after(back_b[2], back_d), 512, rows - 512, ALONG_Y),
+            rows_side(out_b[3], few, rows - few, ALONG_X),
+            rows_side(late, 0, rows - early, ALONG_Y),
         ],
     )
     gate_got = swap(gate_sent, CORE)
     down_sum = down_mine.astype(full) + down_got.astype(full)
-    back_x, back_y, back_d = (
-        jnp.concatenate(pair)
-        for pair in ((back_x, back_x_end), (back_y, back_y_end), (back_d, back_d_end))
-    )
-
-    grad_normed_two = sum(after(b, gate_sent).astype(full) for b in (back_b[0], back_x, back_y, back_d))
-    back_two, grad_gain_two = norm_back(grad_normed_two, unit_two, inverse_two, gain_two)
-    grad_resid = grad_low.astype(full) + back_two
-    grad_branch = grad_resid.astype(low)
-    grad_heads = jnp.dot(grad_branch, out_turned, preferred_element_type=full).astype(low)
-    grad_wout = jnp.dot(grad_branch.T, heads_out, preferred_element_type=full).astype(low)
-    out_got = [swap(after(b, grad_normed_two), bits) for b, bits in zip(out_b[1:], OTHERS)]
+    out_d = jnp.concatenate([out_d_end, out_d])
+
+    grad_resid, grad_heads, grad_gain_two, grad_wout = branch_back(
+        back_b[0],
+        (back_x, back_x_end),
+        (back_y, back_y_end),
+        resid,
+        grad_low,
+        gain_two,
+        heads_out,
+        attn_all,
+        qwide,
+    )
+    out_got = [swap(after(out_b[1], gate_sent), ALONG_X), swap(join(out_b[2], out_d), ALONG_Y)]
     gate_sum = gate_mine.astype(full) + gate_got.astype(full)
     both = jnp.concatenate([down_sum, gate_sum], axis=1).astype(low)
     grad_heads = after(grad_heads, grad_wout, both)
@@ -1216,17 +1339,10 @@
         up_b, normed_blocks, 4, 7, [whole_side(part, bits) for part, bits in zip(parts[1:], OTHERS)]
     )
 
-    keyval_grad = sum(part.astype(full) for part in (parts[0], *others))
-    keys_grad = keyval_grad[:, :kwidth].reshape(rows, KV_HEADS, HEAD)
-    keys_lin = keys_grad * cosine[:, None, :] - jnp.roll(keys_grad, HEAD // 2, axis=-1) * sine[:, None, :]
-    keyval_lin = jnp.concatenate([keys_lin.reshape(rows, kwidth), keyval_grad[:, kwidth:]], axis=1).astype(low)
-    grad_linear = jnp.concatenate([query_lin, keyval_lin], axis=1)
-    grad_wqkv = jnp.dot(normed_one.T, grad_linear, preferred_element_type=full).astype(low)
-    grad_bias = jnp.sum(grad_linear.astype(full), axis=0)
-    grad_normed_one = jnp.dot(grad_linear, attn_all[:, :qwide].T, preferred_element_type=full)
-    unit_one, inverse_one, _ = norm_parts(inputs, gain_one)
-    back_one, grad_gain_one = norm_back(grad_normed_one, unit_one, inverse_one, gain_one)
-    grad_tokens = unpair_rows((grad_resid + back_one).astype(low), core)
+    grad_rows, grad_bias, grad_gain_one, grad_wqkv = project_back(
+        query_lin, (parts[0], *others), cosine, sine, attn_all, inputs_low, gain_one, grad_resid, normed_one
+    )
+    grad_tokens = unpair_rows(grad_rows, core)
     ffn_out = sum(after(b, query_lin).astype(full) for b in [out_b[0]] + out_got)
     layer_out = unpair_rows((resid + ffn_out).astype(low), core)
 

time: 865 us -> 825 us (0.954)
  waiting for transfers between devices: 18.5 us -> 75.8 us
  Pallas kernels: 652 us -> 614 us
  matrix products: 37.2 us -> 6.33 us
  local copies, waits for them, and re-layouts: 49.7 us -> 36.4 us
  other arithmetic: 72.8 us -> 60.5 us
    dot_general x4 -> x0, matrix products: 30.3 us -> none  [the longest x1 9.18 us: on_core(): jnp.dot(grad_linear, attn_all[:, :qwide].T, preferred_element_type=full)]
    all_gather x3, waiting for transfers between devices: 0.01 us -> 29.1 us  [on_core(): lax.all_gather(after(w, *attn_slots, inputs_low, grad_low), 'gx', axis=0,...]
    pallas_call x7, Pallas kernels: 330 us -> 306 us  [call_beside(): pl.pallas_call(whole_body, grid=grid, in_specs=list(in_specs) + [anywhere...]
    ppermute x0 -> x3, waiting for transfers between devices: none -> 18.6 us  [on_core(): lax.ppermute(attn_own, 'gx', [(i, (i + k) % 4) for i in range(4)])]
    pallas_call x1, Pallas kernels: 114 us -> 104 us  [finish(): pl.pallas_call(finish_body, in_specs=[anywhere] * 4, out_specs=[inside] *...]
    ppermute x14 -> x13, waiting for transfers between devices: 18.4 us -> 27.9 us  [swap(): return lax.ppermute(array, 'gy', [(i, i ^ bits) for i in range(8)])]
    add x2 -> x0, other arithmetic: 8.92 us -> none  [the longest x1 6.9 us: on_core(): grad_resid = grad_low.astype(full) + back_two]
    unnamed x108 -> x72, local copies, waits for them, and re-layouts: 18.2 us -> 11.5 us
  transfers between devices with their start and end apart: 18 -> 20, of which waited for: 4 -> 8; matrix products, arithmetic and copies ran while one was open for 15% -> 9% of each run, Pallas kernels for 46% -> 45%
where the time goes in v4:
time: 825 us; the launch traced here: 820 us
  Pallas kernels  614 us (74%)
  waiting for transfers between devices  75.8 us (9%)
  other arithmetic  60.5 us (7%)
  local copies, waits for them, and re-layouts  36.4 us (4%)
  between operations  14.7 us (2%)
  starting transfers between devices  12.9 us (2%)
    pallas_call x7, Pallas kernels, call_beside(): pl.pallas_call(whole_body, grid=grid, in_specs=list(in_specs) + [anywhere...  306 us
    pallas_call x1, Pallas kernels, spread(): pl.pallas_call(spread_body, in_specs=[anywhere] * 5, out_specs=[anywhere]...  115 us
    pallas_call x1, Pallas kernels, finish(): pl.pallas_call(finish_body, in_specs=[anywhere] * 4, out_specs=[inside] *...  104 us
    all_gather x3, waiting for transfers between devices, on_core(): lax.all_gather(after(w, *attn_slots, inputs_low, grad_low), 'gx', axis=0,...  29.1 us
    ppermute x13, waiting for transfers between devices, swap(): return lax.ppermute(array, 'gy', [(i, i ^ bits) for i in range(8)])  27.9 us
    pallas_call x1, Pallas kernels, project_back(): pl.pallas_call(project_back_body, grid=(rows // tile,), in_specs=[moving(...  24.7 us
    pallas_call x1, Pallas kernels, attend_back_fast(): pl.pallas_call(attend_back_body, grid_spec=pltpu.PrefetchScalarGridSpec(n...  24 us
    pallas_call x1, Pallas kernels, branch_back(): pl.pallas_call(branch_back_body, grid=(steps,), in_specs=[moving, first[0...  19.6 us
  transfers between devices with their start and end apart: 20, of which 8 were waited for; matrix products, arithmetic and copies ran while one was open for 9% of the time, Pallas kernels for 45%

profile of v4, /device:TPU:9, one launch (start us, length us, event | category | flops | bytes accessed | tf_op | source)
XLA Modules:
  0.0 820.2 jit_solution(17394588106425062770)
XLA Ops:
  7.3 2.7 dynamic-slice_bitcast_fusion.5
  12.3 2.5 collective-permute-start.2
  14.7 2.2 collective-permute-start.1
  16.9 1.6 copy.35
  19.5 3.4 maximum_select_fusion.x_ref.in_ref
  22.9 3.4 maximum_select_fusion.1.refs_4_.refs_1_.cot_ref
  26.3 11.0 %collective-permute-done.2.refs_2_ = bf16[48,3712]{1,0:T(8,128)(2,1)} collective-permute-done((bf16[48,3712]{1,0:T(8,128)(2,1)S(1)}, bf16[48,3712]{1,0:T(8,128)(2,1)}, u32[]{:S(2)}, u32[]{:S(2)}) %collective-permute-start.2) | collective-permute-done | bytes 356384 | tf_op jit(solution)/shard_map/ppermute | solution.py:1218
  37.4 7.6 collective-permute-done.1.refs_1_
  45.1 1.5 copy.34
  47.8 1.5 copy.36
  53.0 114.6 %spread.1 = (bf16[4,8,48,3712]{3,2,1,0:T(8,128)(2,1)}, bf16[640,1536]{1,0:T(8,128)(2,1)}, bf16[640,1536]{1,0:T(8,128)(2,1)}, bf16[640,1536]{1,0:T(8,128)(2,1)}) custom-call(bf16[48,3712]{1,0:T(8,128)(2,1)} %copy-done.17, bf16[48,3712]{1,0:T(8,128)(2,1)} %collective-permute-done.1.refs_1_, bf16[48,3712]{1,0:T(8,128)(2,1)} %collective-permute-done.2.refs_2_, ...), custom_call_target="tpu_custom_call" | custom-call | bytes 314572800 | tf_op jit(solution)/shard_map/spread/pallas_call | solution.py:869
  169.5 8.9 %project.1 = (bf16[640,1536]{1,0:T(8,128)(2,1)S(1)}, bf16[640,1536]{1,0:T(8,128)(2,1)S(1)}, bf16[640,512]{1,0:T(8,128)(2,1)S(1)}) custom-call(bf16[640,1536]{1,0:T(8,128)(2,1)} %maximum_select_fusion.x_ref.in_ref, f32[1,1536]{1,0:T(1,128)S(1)} %reshape.184.gain_ref, bf16[1536,3712]{1,0:T(8,128)(2,1)} %bitcast.58, f32[1,2048]{1,0:T(1,128)S(1)} %reshape.185.b_ref, ...), custom_call_target="tpu_custom_call" | custom-call | flops 4026531840 | bytes 14155776 | tf_op jit(solution)/shard_map/project/pallas_call | solution.py:780
  183.6 4.3 select_convert_fusion.bias_ref
  187.9 5.0 or_reduce_fusion
  193.6 15.0 %collective-permute-done.5 = bf16[640,512]{1,0:T(8,128)(2,1)S(1)} collective-permute-done((bf16[640,512]{1,0:T(8,128)(2,1)S(1)}, bf16[640,512]{1,0:T(8,128)(2,1)S(1)}, u32[]{:S(2)}, u32[]{:S(2)}) %collective-permute-start.5) | collective-permute-done | bytes 655392 | tf_op jit(solution)/shard_map/ppermute | solution.py:1156
  208.7 4.0 collective-permute-done.6
  214.3 12.0 %tree_attention.1 = (bf16[640,1536]{1,0:T(8,128)(2,1)S(1)}, f32[5,2,1,768]{3,2,1,0:T(1,128)S(1)}) custom-call(s32[5,10]{1,0:T(8,128)S(1)} %select_reduce_fusion.5.list_ref, s32[5]{0:T(128)S(1)} %convert_reduce_fusion.4.count_ref, bf16[640,1536]{1,0:T(8,128)(2,1)S(1)} %copy-done.8, bf16[2560,512]{1,0:T(8,128)(2,1)} %copy-done.13, ...), custom_call_target="tpu_custom_call" | custom-call | flops 10066329600 | bytes 6553600 | tf_op jit(solution)/shard_map/tree_attention/pallas_call | solution.py:632
  226.9 29.1 %all-gather.8.cloned.1.call-done.refs_4_ = bf16[1536,1152]{1,0:T(8,128)(2,1)} async-done(((bf16[384,1152]{1,0:T(8,128)(2,1)}), bf16[1536,1152]{1,0:T(8,128)(2,1)}) %all-gather.8.cloned.1.call-update) | async-done | bytes 3538960 | tf_op jit(solution)/shard_map/all_gather | solution.py:1236
  257.1 6.3 multiply_reduce_fusion
  263.5 2.1 multiply_convert_fusion.refs_0_.refs_8_.refs_9_.refs_4_
  265.9 1.9 collective-permute-done.8.refs_5_
  267.8 5.1 collective-permute-done.9.refs_6_
  272.9 50.9 %ffn_block.4 = (bf16[640,2304]{1,0:T(8,128)(2,1)}, bf16[640,2304]{1,0:T(8,128)(2,1)}, bf16[640,2304]{1,0:T(8,128)(2,1)}, bf16[640,1536]{1,0:T(8,128)(2,1)}, bf16...) custom-call(bf16[640,1536]{1,0:T(8,128)(2,1)} %multiply_convert_fusion.refs_0_.refs_8_.refs_9_.refs_4_, ...), custom_call_target="tpu_custom_call" | custom-call | flops 27179089920 | bytes 35979264 | tf_op jit(solution)/shard_map/ffn_block/pallas_call | solution.py:433
  323.7 38.2 %ffn_block.5 = (bf16[640,2304]{1,0:T(8,128)(2,1)}, bf16[640,2304]{1,0:T(8,128)(2,1)}, bf16[640,2304]{1,0:T(8,128)(2,1)}, bf16[640,1536]{1,0:T(8,128)(2,1)}, bf16...) custom-call(bf16[640,1536]{1,0:T(8,128)(2,1)} %get-tuple-element.108.refs_0_.refs_8_.refs_5_, ...), custom_call_target="tpu_custom_call" | custom-call | flops 27179089920 | bytes 35979264 | tf_op jit(solution)/shard_map/ffn_block/pallas_call | solution.py:433
  362.0 40.4 %ffn_block.6 = (bf16[640,2304]{1,0:T(8,128)(2,1)}, bf16[640,2304]{1,0:T(8,128)(2,1)}, bf16[640,2304]{1,0:T(8,128)(2,1)}, bf16[640,1536]{1,0:T(8,128)(2,1)}, bf16...) custom-call(bf16[640,1536]{1,0:T(8,128)(2,1)} %get-tuple-element.111.refs_0_.refs_7_, ...), custom_call_target="tpu_custom_call" | custom-call | flops 27179089920 | bytes 35979264 | tf_op jit(solution)/shard_map/ffn_block/pallas_call | solution.py:433
  402.4 39.3 %ffn_block.7 = (bf16[640,2304]{1,0:T(8,128)(2,1)}, bf16[640,2304]{1,0:T(8,128)(2,1)}, bf16[640,2304]{1,0:T(8,128)(2,1)}, bf16[640,1536]{1,0:T(8,128)(2,1)}, bf16...) custom-call(bf16[640,1536]{1,0:T(8,128)(2,1)} %get-tuple-element.118.refs_9_.refs_0_.refs_6_, ...), custom_call_target="tpu_custom_call" | custom-call | flops 27179089920 | bytes 35979264 | tf_op jit(solution)/shard_map/ffn_block/pallas_call | solution.py:433
  442.7 2.9 add_convert_fusion.4.refs_11_
  445.6 34.3 %ffn_wgrad.3 = (bf16[4,1152,384]{2,1,0:T(8,128)(2,1)}, bf16[4,1152,384]{2,1,0:T(8,128)(2,1)}, bf16[128,1536]{1,0:T(8,128)(2,1)}, bf16[128,1536]{1,0:T(8,128)(2,1...) custom-call(bf16[640,2304]{1,0:T(8,128)(2,1)} %get-tuple-element.115.refs_0_, ...), custom_call_target="tpu_custom_call" | custom-call | flops 18119393280 | bytes 19660800 | tf_op jit(solution)/shard_map/ffn_wgrad/pallas_call | solution.py:433
  480.0 2.3 add_convert_fusion.5.refs_10_
  482.3 41.5 %ffn_wgrad.4 = (bf16[4,1152,384]{2,1,0:T(8,128)(2,1)}, bf16[4,1152,384]{2,1,0:T(8,128)(2,1)}, bf16[4,1152,384]{2,1,0:T(8,128)(2,1)}, bf16[448,1536]{1,0:T(8,128)(2,1)}, bf16[256,1536]{1,0:T(8,128)(2,1)}) custom-call(bf16[640,2304]{1,0:T(8,128)(2,1)} %get-tuple-element.127.refs_0_, bf16[640,2304]{1,0:T(8,128)(2,1)} %get-tuple-element.128.refs_1_, ...), custom_call_target="tpu_custom_call" | custom-call | flops 18119393280 | bytes 19660800 | tf_op jit(solution)/shard_map/ffn_wgrad/pallas_call | solution.py:433
  525.0 4.1 add_convert_fusion.1
  529.1 2.0 collective-permute-done.11
  531.1 2.8 add_convert_fusion
  533.8 5.6 pad_maximum_fusion
  541.2 3.4 add_convert_fusion.3
  545.7 19.6 %branch_back.1 = (f32[640,1536]{1,0:T(8,128)}, bf16[640,1536]{1,0:T(8,128)(2,1)}, f32[1,1536]{1,0:T(1,128)}, bf16[1536,1536]{1,0:T(8,128)(2,1)}) custom-call(bf16[640,1536]{1,0:T(8,128)(2,1)} %get-tuple-element.107.own_ref, bf16[512,1536]{1,0:T(8,128)(2,1)} %get-tuple-element.114.xa_ref, bf16[128,1536]{1,0:T(8,128)(2,1)} %get-tuple-element.125.xb_ref, ...), custom_call_target="tpu_custom_call" | custom-call | flops 6039797760 | bytes 29097984 | tf_op jit(solution)/shard_map/branch_back/pallas_call | solution.py:928
  566.2 24.0 %tree_attention_back.1 = (bf16[640,1536]{1,0:T(8,128)(2,1)}, bf16[2560,512]{1,0:T(8,128)(2,1)}) custom-call(s32[5,10]{1,0:T(8,128)} %copy-done.4, s32[5]{0:T(128)} %copy-done.5, bf16[640,1536]{1,0:T(8,128)(2,1)} %copy-done.7, bf16[2560,512]{1,0:T(8,128)(2,1)} %copy-done.13, bf16[2560,640]{1,0:T(8,128)(2,1)} %select_convert_fusion.bias_ref, ...), custom_call_target="tpu_custom_call" | custom-call | flops 25165824000 | bytes 13107200 | tf_op jit(solution)/shard_map/tree_attention_back/pallas_call | solution.py:723
  590.2 3.9 constant_dynamic-slice_fusion.1
  594.1 61.2 %ffn_wgrad.5 = (bf16[4,1152,384]{2,1,0:T(8,128)(2,1)}, bf16[4,1152,384]{2,1,0:T(8,128)(2,1)}, bf16[640,512]{1,0:T(8,128)(2,1)}, bf16[640,512]{1,0:T(8,128)(2,1)}, bf16[640,512]{1,0:T(8,128)(2,1)}) custom-call(bf16[640,2304]{1,0:T(8,128)(2,1)} %get-tuple-element.151.refs_0_, bf16[640,2304]{1,0:T(8,128)(2,1)} %get-tuple-element.152.refs_1_, ...), custom_call_target="tpu_custom_call" | custom-call | flops 18119393280 | bytes 19660800 | tf_op jit(solution)/shard_map/ffn_wgrad/pallas_call | solution.py:433
  655.4 24.7 %project_back.1 = (bf16[640,1536]{1,0:T(8,128)(2,1)}, f32[1,2048]{1,0:T(1,128)}, f32[1,1536]{1,0:T(1,128)}, bf16[1536,2048]{1,0:T(8,128)(2,1)}) custom-call(bf16[640,1536]{1,0:T(8,128)(2,1)} %get-tuple-element.141.q_ref, bf16[640,512]{1,0:T(8,128)(2,1)} %get-tuple-element.185.own_ref, bf16[640,512]{1,0:T(8,128)(2,1)} %get-tuple-element.155.x_ref, ...), custom_call_target="tpu_custom_call" | custom-call | flops 8053063680 | bytes 32243712 | tf_op jit(solution)/shard_map/project_back/pallas_call | solution.py:984
  682.3 5.1 add_convert_fusion.2
  691.0 3.1 fusion.1
  694.1 103.8 %finish.1 = (f32[48,2176]{1,0:T(8,128)}, f32[48,1536]{1,0:T(8,128)}, f32[1152,384]{1,0:T(8,128)}) custom-call(bf16[4,2,2,2,48,2176]{5,4,3,2,1,0:T(8,128)(2,1)} %bitcast.64, bf16[4,2,2,2,48,1536]{5,4,3,2,1,0:T(8,128)(2,1)} %bitcast.67, bf16[4,1152,384]{2,1,0:T(8,128)(2,1)} %get-tuple-element.165.mine_ref, bf16[4,1152,384]{2,1,0:T(8,128)(2,1)} %get-tuple-element.166.sent_ref), custom_call_target="tpu_custom_call" | custom-call | bytes 209715200 | tf_op jit(solution)/shard_map/finish/pallas_call | solution.py:1128
  797.9 2.9 slice.87
  802.8 3.1 maximum_select_fusion.2
  806.0 3.1 maximum_select_fusion.3
  809.0 1.7 convert_element_type.127
  810.8 2.0 slice_bitcast_fusion
  (173 shorter events, 33.9 us)
Async XLA Ops:
  7.2 219.7 %all-gather.6.cloned.1.call-start = ((), (), s32[]{:S(2)}) async-start(), calls=%async_computation.2 | async-start | bytes 4423680 | tf_op jit(solution)/shard_map/all_gather | solution.py:1236
  7.2 3.5 copy-start.14
  10.0 1.9 copy-start.28
  10.0 1.9 copy-start.29
  10.0 1.9 copy-start.30
  10.0 2.2 copy-start.23
  10.0 2.2 copy-start.26
  10.0 9.5 %collective-permute-start = (bf16[320,1536]{1,0:T(8,128)(2,1)}, bf16[320,1536]{1,0:T(8,128)(2,1)}, u32[]{:S(2)}, u32[]{:S(2)}) collective-permute-start(bf16[320,1536]{1,0:T(8,128)(2,1)} %get-tuple-element.193), channel_id=1, source_target_pairs={{0,1},{1,0},{2,3},{3,2},{4,5},{5,4},{6,7},{7,6},{8,9},{9,8},{10,11... | collective-permute-start | bytes 2949128 | tf_op jit(solution)/shard_map/ppermute | solution.py:1156
  11.8 11.1 %collective-permute-start.4 = (bf16[320,1536]{1,0:T(8,128)(2,1)}, bf16[320,1536]{1,0:T(8,128)(2,1)}, u32[]{:S(2)}, u32[]{:S(2)}) collective-permute-start(bf16[320,1536]{1,0:T(8,128)(2,1)} %get-tuple-element.191), channel_id=1, source_target_pairs={{0,1},{1,0},{2,3},{3,2},{4,5},{5,4},{6,7},{7,6},{8,9},{9,8},{10,11... | collective-permute-start | bytes 2949128 | tf_op jit(solution)/shard_map/ppermute | solution.py:1156
  12.2 10.7 %copy-start.17 = (bf16[48,3712]{1,0:T(8,128)(2,1)}, bf16[48,3712]{1,0:T(8,128)(2,1)S(1)}, u32[]{:S(2)}) copy-start(bf16[48,3712]{1,0:T(8,128)(2,1)S(1)} %fusion.8.refs_0_) | copy-start | bytes 1069060
  12.2 14.1 %collective-permute-start.3 = (bf16[48,3712]{1,0:T(8,128)(2,1)S(1)}, bf16[48,3712]{1,0:T(8,128)(2,1)}, u32[]{:S(2)}, u32[]{:S(2)}) collective-permute-start(bf16[48,3712]{1,0:T(8,128)(2,1)S(1)} %fusion.8.refs_0_), channel_id=1, source_target_pairs={{0,24},{8,0},{16,8},{24,16},{1,25},{9,1},{17,9},{25,17},{2,26},{10... | collective-permute-start | bytes 1069064 | tf_op jit(solution)/shard_map/ppermute | solution.py:1218
  12.3 25.1 %collective-permute-start.2 = (bf16[48,3712]{1,0:T(8,128)(2,1)S(1)}, bf16[48,3712]{1,0:T(8,128)(2,1)}, u32[]{:S(2)}, u32[]{:S(2)}) collective-permute-start(bf16[48,3712]{1,0:T(8,128)(2,1)S(1)} %fusion.8.refs_0_), channel_id=1, source_target_pairs={{0,16},{8,24},{16,0},{24,8},{1,17},{9,25},{17,1},{25,9},{2,18},{10... | collective-permute-start | bytes 1069064 | tf_op jit(solution)/shard_map/ppermute | solution.py:1218
  14.7 30.2 %collective-permute-start.1 = (bf16[48,3712]{1,0:T(8,128)(2,1)S(1)}, bf16[48,3712]{1,0:T(8,128)(2,1)}, u32[]{:S(2)}, u32[]{:S(2)}) collective-permute-start(bf16[48,3712]{1,0:T(8,128)(2,1)S(1)} %fusion.8.refs_0_), channel_id=1, source_target_pairs={{0,8},{8,16},{16,24},{24,0},{1,9},{9,17},{17,25},{25,1},{2,10},{10... | collective-permute-start | bytes 1069064 | tf_op jit(solution)/shard_map/ppermute | solution.py:1218
  22.9 22.2 %copy-start.19 = (bf16[384,1120]{0,1:T(8,128)(2,1)S(1)}, bf16[384,1120]{0,1:T(8,128)(2,1)}, u32[]{:S(2)}) copy-start(bf16[384,1120]{0,1:T(8,128)(2,1)} %param.21) | copy-start | bytes 2580484
  26.3 21.3 %copy-start.27 = (s32[2,2560]{1,0:T(2,128)S(1)}, s32[2,2560]{1,0:T(2,128)}, u32[]{:S(2)}) copy-start(s32[2,2560]{1,0:T(2,128)} %param.14) | copy-start | bytes 61444
  26.3 21.5 %copy-start.20 = (bf16[1120,384]{1,0:T(8,128)(2,1)S(1)}, bf16[1120,384]{1,0:T(8,128)(2,1)}, u32[]{:S(2)}) copy-start(bf16[1120,384]{1,0:T(8,128)(2,1)} %param.23) | copy-start | bytes 2580484
  45.0 181.9 %all-gather.4.cloned.1.call-start = ((), (), s32[]{:S(2)}) async-start(), calls=%async_computation.1 | async-start | bytes 4423680 | tf_op jit(solution)/shard_map/all_gather | solution.py:1236
  47.5 2.8 copy-start.31
  47.6 208.4 %all-gather.8.cloned.1.call-start = ((), (), s32[]{:S(2)}) async-start(), calls=%async_computation.3 | async-start | bytes 4423680 | tf_op jit(solution)/shard_map/all_gather | solution.py:1236
  51.0 758.1 %reduce-scatter.2.cloned.1.call-start = ((), (), s32[]{:S(2)}) async-start(), calls=%async_computation.4 | async-start | bytes 8847360 | tf_op jit(solution)/shard_map/reduce_scatter | solution.py:1331
  53.0 116.4 %copy-start.1 = (f32[640,128]{1,0:T(8,128)}, f32[640,128]{1,0:T(8,128)S(1)}, u32[]{:S(2)}) copy-start(f32[640,128]{1,0:T(8,128)S(1)} %get-tuple-element.203.cos_ref) | copy-start | bytes 983044
  53.0 116.4 %copy-start.2 = (f32[640,128]{1,0:T(8,128)}, f32[640,128]{1,0:T(8,128)S(1)}, u32[]{:S(2)}) copy-start(f32[640,128]{1,0:T(8,128)S(1)} %get-tuple-element.204.sin_ref) | copy-start | bytes 983044
  169.3 87.7 %copy-start.24 = (f32[32,48]{1,0:T(8,128)}, f32[32,48]{1,0:T(8,128)S(1)}, u32[]{:S(2)}) copy-start(f32[32,48]{1,0:T(8,128)S(1)} %get-tuple-element.194) | copy-start | bytes 18436
  169.4 8.9 %copy-start.3 = (f32[1,1536]{1,0:T(1,128)}, f32[1,1536]{1,0:T(1,128)S(1)}, u32[]{:S(2)}) copy-start(f32[1,1536]{1,0:T(1,128)S(1)} %reshape.184.gain_ref) | copy-start | bytes 18436
  181.0 31.8 %collective-permute-start.7 = (bf16[640,512]{1,0:T(8,128)(2,1)S(1)}, bf16[640,512]{1,0:T(8,128)(2,1)S(1)}, u32[]{:S(2)}, u32[]{:S(2)}) collective-permute-start(bf16[640,512]{1,0:T(8,128)(2,1)S(1)} %get-tuple-element.95), channel_id=1, source_target_pairs={{0,6},{1,7},{2,4},{3,5},{4,2},{5,3},{6,0},{7,1},{8,14},{9,15},{10,... | collective-permute-start | bytes 1966088 | tf_op jit(solution)/shard_map/ppermute | solution.py:1156
  182.2 30.5 %collective-permute-start.6 = (bf16[640,512]{1,0:T(8,128)(2,1)S(1)}, bf16[640,512]{1,0:T(8,128)(2,1)S(1)}, u32[]{:S(2)}, u32[]{:S(2)}) collective-permute-start(bf16[640,512]{1,0:T(8,128)(2,1)S(1)} %get-tuple-element.95), channel_id=1, source_target_pairs={{0,4},{1,5},{2,6},{3,7},{4,0},{5,1},{6,2},{7,3},{8,12},{9,13},{10,... | collective-permute-start | bytes 1966088 | tf_op jit(solution)/shard_map/ppermute | solution.py:1156
  182.2 26.5 %collective-permute-start.5 = (bf16[640,512]{1,0:T(8,128)(2,1)S(1)}, bf16[640,512]{1,0:T(8,128)(2,1)S(1)}, u32[]{:S(2)}, u32[]{:S(2)}) collective-permute-start(bf16[640,512]{1,0:T(8,128)(2,1)S(1)} %get-tuple-element.95), channel_id=1, source_target_pairs={{0,2},{1,3},{2,0},{3,1},{4,6},{5,7},{6,4},{7,5},{8,10},{9,11},{10,... | collective-permute-start | bytes 1966088 | tf_op jit(solution)/shard_map/ppermute | solution.py:1156
  193.2 19.6 %copy-start.5 = (s32[5]{0:T(128)}, s32[5]{0:T(128)S(1)}, u32[]{:S(2)}) copy-start(s32[5]{0:T(128)S(1)} %convert_reduce_fusion.4.count_ref) | copy-start | bytes 64
  193.4 19.5 %copy-start.4 = (s32[5,10]{1,0:T(8,128)}, s32[5,10]{1,0:T(8,128)S(1)}, u32[]{:S(2)}) copy-start(s32[5,10]{1,0:T(8,128)S(1)} %select_reduce_fusion.5.list_ref) | copy-start | bytes 604
  193.5 20.7 %copy-start.8 = (bf16[640,1536]{1,0:T(8,128)(2,1)S(1)}, bf16[640,1536]{1,0:T(8,128)(2,1)}, u32[]{:S(2)}) copy-start(bf16[640,1536]{1,0:T(8,128)(2,1)} %copy-done.7) | copy-start | bytes 5898244
  226.9 36.6 %copy-start = (bf16[640,1536]{1,0:T(8,128)(2,1)}, bf16[640,1536]{1,0:T(8,128)(2,1)S(1)}, u32[]{:S(2)}) copy-start(bf16[640,1536]{1,0:T(8,128)(2,1)S(1)} %get-tuple-element.98.heads_ref.o_ref) | copy-start | bytes 5898244
  256.0 10.0 %collective-permute-start.10 = (bf16[1536,1152]{1,0:T(8,128)(2,1)}, bf16[1536,1152]{1,0:T(8,128)(2,1)}, u32[]{:S(2)}, u32[]{:S(2)}) collective-permute-start(bf16[1536,1152]{1,0:T(8,128)(2,1)} %all-gather.8.cloned.1.call-done.refs_4_), channel_id=1, source_target_pairs={{0,1},{1,0},{2,3},{3,2},{4,5},{5,4},{6,7},{7,6},{8,9},{9,8},{10,11... | collective-permute-start | bytes 10616840 | tf_op jit(solution)/shard_map/ppermute | solution.py:1156
  256.5 11.3 %collective-permute-start.8 = (bf16[1536,1152]{1,0:T(8,128)(2,1)}, bf16[1536,1152]{1,0:T(8,128)(2,1)}, u32[]{:S(2)}, u32[]{:S(2)}) collective-permute-start(bf16[1536,1152]{1,0:T(8,128)(2,1)} %all-gather.4.cloned.1.call-done.refs_2_), channel_id=1, source_target_pairs={{0,1},{1,0},{2,3},{3,2},{4,5},{5,4},{6,7},{7,6},{8,9},{9,8},{10,11... | collective-permute-start | bytes 10616840 | tf_op jit(solution)/shard_map/ppermute | solution.py:1156
  256.5 16.3 %collective-permute-start.9 = (bf16[1536,1152]{1,0:T(8,128)(2,1)}, bf16[1536,1152]{1,0:T(8,128)(2,1)}, u32[]{:S(2)}, u32[]{:S(2)}) collective-permute-start(bf16[1536,1152]{1,0:T(8,128)(2,1)} %all-gather.6.cloned.1.call-done.refs_3_), channel_id=1, source_target_pairs={{0,1},{1,0},{2,3},{3,2},{4,5},{5,4},{6,7},{7,6},{8,9},{9,8},{10,11... | collective-permute-start | bytes 10616840 | tf_op jit(solution)/shard_map/ppermute | solution.py:1156
  263.5 2.5 copy-start.10
  523.8 7.2 collective-permute-start.11
  525.0 6.1 copy-start.12
  540.8 49.3 %collective-permute-start.12 = (bf16[640,1536]{1,0:T(8,128)(2,1)}, bf16[640,1536]{1,0:T(8,128)(2,1)S(1)}, u32[]{:S(2)}, u32[]{:S(2)}) collective-permute-start(bf16[640,1536]{1,0:T(8,128)(2,1)} %get-tuple-element.144), channel_id=1, source_target_pairs={{0,2},{1,3},{2,0},{3,1},{4,6},{5,7},{6,4},{7,5},{8,10},{9,11},{10,... | collective-permute-start | bytes 5898248 | tf_op jit(solution)/shard_map/ppermute | solution.py:1156
  544.6 45.6 %collective-permute-start.13 = (bf16[640,1536]{1,0:T(8,128)(2,1)}, bf16[640,1536]{1,0:T(8,128)(2,1)}, u32[]{:S(2)}, u32[]{:S(2)}) collective-permute-start(bf16[640,1536]{1,0:T(8,128)(2,1)} %add_convert_fusion.3), channel_id=1, source_target_pairs={{0,4},{1,5},{2,6},{3,7},{4,0},{5,1},{6,2},{7,3},{8,12},{9,13},{10,... | collective-permute-start | bytes 5898248 | tf_op jit(solution)/shard_map/ppermute | solution.py:1156
  590.2 3.9 copy-start.15
  681.9 9.1 %slice-start = ((s8[6291456]{0:T(1024)(128)(4,1)}), s8[2097152]{0:T(1024)(128)(4,1)S(1)}, s32[]{:S(2)}) async-start(s8[6291456]{0:T(1024)(128)(4,1)} %bitcast.65), calls=%async_computation.5 | async-start | bytes 4194304
  682.2 8.8 %slice-start.1 = ((s8[6291456]{0:T(1024)(128)(4,1)}), s8[4194304]{0:T(1024)(128)(4,1)S(1)}, s32[]{:S(2)}) async-start(s8[6291456]{0:T(1024)(128)(4,1)} %bitcast.65), calls=%async_computation.6 | async-start | bytes 8388608
  687.3 2.3 copy-start.16
  688.7 114.1 %collective-permute-start.14 = (bf16[320,1536]{1,0:T(8,128)(2,1)}, bf16[320,1536]{1,0:T(8,128)(2,1)}, u32[]{:S(2)}, u32[]{:S(2)}) collective-permute-start(bf16[320,1536]{1,0:T(8,128)(2,1)} %get-tuple-element.189), channel_id=1, source_target_pairs={{0,1},{1,0},{2,3},{3,2},{4,5},{5,4},{6,7},{7,6},{8,9},{9,8},{10,11... | collective-permute-start | bytes 2949128 | tf_op jit(solution)/shard_map/ppermute | solution.py:1156
  690.7 115.3 %collective-permute-start.15 = (bf16[320,1536]{1,0:T(8,128)(2,1)}, bf16[320,1536]{1,0:T(8,128)(2,1)}, u32[]{:S(2)}, u32[]{:S(2)}) collective-permute-start(bf16[320,1536]{1,0:T(8,128)(2,1)} %get-tuple-element.187), channel_id=1, source_target_pairs={{0,1},{1,0},{2,3},{3,2},{4,5},{5,4},{6,7},{7,6},{8,9},{9,8},{10,11... | collective-permute-start | bytes 2949128 | tf_op jit(solution)/shard_map/ppermute | solution.py:1156
  797.9 2.9 copy-start.21
  797.9 4.9 copy-start.11
  810.8 2.0 copy-start.22
  (6 other events, 7.1 us)
Sparse Core Ops, SparseCore 0:
  45.1 69.2 all-gather.5
  116.6 68.5 all-gather.3
  187.4 68.5 all-gather.7
  539.6 123.2 reduce-scatter.1

commit v5 on v4

--- a/solution.py
+++ b/solution.py
@@ -379,6 +379,8 @@
     copies = []
     for parts, target in zip(sides, targets):
         for _, take, fill, bits in parts:
+            if take is None:
+                take = (pl.multiple_of(peers[bits]["gy"] // 2 * fill[1], fill[1]), fill[1])
             copies.append(
                 pltpu.make_async_remote_copy(
                     sources[len(copies)].at[pl.ds(*take)],
@@ -398,6 +400,10 @@
 
 def rows_side(array, start, count, bits):
     return [(array, (start, count), (0, count), bits)]
+
+
+def chip_side(array, bits):
+    return [(array, None, (0, array.shape[0] // 4), bits)]
 
 
 def call_beside(body, sides, collective, operands, grid, in_specs, out_specs, out_shape, scratch_shapes, mib, estimate, name):
@@ -490,15 +496,24 @@
     slot = step % 2
     rows = n_ref.shape[0]
     part = rows // FFN_PARTS
-    for index in range(FFN_PARTS):
-        take = pl.ds(index * part, part)
-        gate = dot_nn(n_ref[take, :], held[slot, 0])
-        upward = dot_nn(n_ref[take, :], held[slot, 1])
+    takes = [pl.ds(index * part, part) for index in range(FFN_PARTS)]
+
+    def products(take):
+        return (
+            dot_nn(n_ref[take, :], held[slot, 0]),
+            dot_nn(n_ref[take, :], held[slot, 1]),
+            dot_nn(c_ref[take, :], held[slot, 2]),
+        )
+
+    later = products(takes[0])
+    for index, take in enumerate(takes):
+        gate, upward, grad_hidden = later
+        if index + 1 < FFN_PARTS:
+            later = products(takes[index + 1])
         sigma = sigmoid(gate)
         swish = gate * sigma
         hidden = (swish * upward).astype(jnp.bfloat16)
         hid_ref[take, :] = hidden
-        grad_hidden = dot_nn(c_ref[take, :], held[slot, 2])
         grad_gate = (grad_hidden * upward * sigma * (1.0 + gate * (1.0 - sigma))).astype(jnp.bfloat16)
         grad_up = (grad_hidden * swish).astype(jnp.bfloat16)
         dg_ref[take, :] = grad_gate
@@ -966,10 +981,10 @@
 
     @pl.when(step == pl.num_programs(0) - 1)
     def _():
-        weight_out[...] = dot_tn(normed_ref[...], linear[...]).astype(jnp.bfloat16)
-
-
-def project_back(query_lin, parts, cosine, sine, weights, inputs, gain, grad_resid, normed):
+        weight_out[:, : linear.shape[1]] = dot_tn(normed_ref[...], linear[...]).astype(jnp.bfloat16)
+
+
+def project_back(query_lin, parts, cosine, sine, weights, inputs, gain, grad_resid, normed, collective, sides):
     rows, width = inputs.shape
     qwidth, kwidth = query_lin.shape[1], parts[0].shape[1]
     qwide, tile = qwidth + kwidth, ROW_TILE
@@ -981,26 +996,31 @@
     def fixed(high, columns):
         return pl.BlockSpec((high, columns), lambda i: (0, 0))
 
-    return pl.pallas_call(
+    return call_beside(
         project_back_body,
-        grid=(rows // tile,),
-        in_specs=[moving(qwidth)] + [moving(kwidth)] * 4 + [moving(HEAD)] * 2
+        sides,
+        collective,
+        (query_lin, *parts, cosine, sine, weights, inputs, gain, grad_resid, normed),
+        (rows // tile,),
+        [moving(qwidth)]
+        + [moving(kwidth)] * 4
+        + [moving(HEAD)] * 2
         + [fixed(width, qwide), moving(width), fixed(1, width), moving(width), fixed(rows, width)],
-        out_specs=[moving(width), fixed(1, qwide), fixed(1, width), fixed(width, qwide)],
-        out_shape=[
+        [moving(width), fixed(1, qwide), fixed(1, width), fixed(width, qwide + HEAD)],
+        [
             jax.ShapeDtypeStruct((rows, width), low),
             jax.ShapeDtypeStruct((1, qwide), full),
             jax.ShapeDtypeStruct((1, width), full),
-            jax.ShapeDtypeStruct((width, qwide), low),
+            jax.ShapeDtypeStruct((width, qwide + HEAD), low),
         ],
-        scratch_shapes=[pltpu.VMEM((rows, qwide), low)],
-        compiler_params=params(56),
-        cost_estimate=cost(4 * rows * width * qwide, 20 * rows * width + 4 * width * qwide),
-        name="project_back",
-    )(query_lin, *parts, cosine, sine, weights, inputs, gain, grad_resid, normed)
-
-
-def finish_body(wide_ref, out_ref, mine_ref, sent_ref, *refs):
+        [pltpu.VMEM((rows, qwide), low)],
+        56,
+        cost(4 * rows * width * qwide, 20 * rows * width + 4 * width * qwide),
+        "project_back",
+    )
+
+
+def finish_body(wide_ref, out_ref, mine_ref, other_ref, *refs):
     results, scratch = refs[:3], refs[3:]
     kept, got_core, got_first, got_second, got_ring = [scratch[i : i + 2] for i in range(0, 10, 2)]
     units, got_units, units_ring, units_moving, sent, landed, local = scratch[10:]
@@ -1032,13 +1052,12 @@
         return copy
 
     inputs = (wide_ref, out_ref)
-    core_copies = [send(sent_ref, got_units, CORE)]
-    core_copies += [send(inputs[i].at[:, :, :, 1 - core], got_core[i], CORE) for i in range(2)]
-    held = [load(mine_ref, units)]
-    held += [load(inputs[i].at[:, :, :, core], kept[i]) for i in range(2)]
-
-    core_copies[0].wait_recv()
-    held[0].wait()
+    core_copies = [send(inputs[i].at[:, :, :, 1 - core], got_core[i], CORE) for i in range(2)]
+    unit_loads = [load(mine_ref, units), load(other_ref, got_units)]
+    held = [load(inputs[i].at[:, :, :, core], kept[i]) for i in range(2)]
+
+    for copy in unit_loads:
+        copy.wait()
 
     @pl.loop(0, 4)
     def _(p):
@@ -1047,8 +1066,8 @@
     units_copy = send(units.at[places[1]], units_ring.at[0], RING)
     steps = []
     for i in range(2):
-        core_copies[1 + i].wait_recv()
-        held[1 + i].wait()
+        core_copies[i].wait_recv()
+        held[i].wait()
 
         @pl.loop(0, 4)
         def _(p):
@@ -1113,7 +1132,7 @@
         copy.wait_send()
 
 
-def finish(wide, out, mine, sent, collective):
+def finish(wide, out, mine, other, collective):
     low, full = jnp.bfloat16, jnp.float32
     deep = wide.shape[0] // 32
     wide, out = (a.reshape(4, 2, 2, 2, deep, a.shape[1]) for a in (wide, out))
@@ -1140,16 +1159,16 @@
             pltpu.VMEM((4, *block), low),
             pltpu.VMEM((3, *block), low),
             pltpu.VMEM((2, *block), low),
-            pltpu.SemaphoreType.DMA((20,)),
-            pltpu.SemaphoreType.DMA((20,)),
-            pltpu.SemaphoreType.DMA((3,)),
+            pltpu.SemaphoreType.DMA((19,)),
+            pltpu.SemaphoreType.DMA((19,)),
+            pltpu.SemaphoreType.DMA((4,)),
         ],
         compiler_params=pltpu.CompilerParams(
             vmem_limit_bytes=56 * 1024 * 1024, collective_id=collective, has_side_effects=True
         ),
         cost_estimate=cost(0, 200 * 1024 * 1024),
         name="finish",
-    )(wide, out, mine, sent)
+    )(wide, out, mine, other)
 
 
 def swap(array, bits):
@@ -1233,7 +1252,10 @@
 
     more = pad_units - own_units
     shards = [jnp.pad(w, ((0, 0), (0, more))) for w in (w_gate, w_up, w_down.T)]
-    weights = [lax.all_gather(after(w, *attn_slots, inputs_low, grad_low), "gx", axis=0, tiled=True) for w in shards]
+    weights = [
+        lax.all_gather(after(w, *attn_slots, inputs_low, grad_low), "gx", axis=0, tiled=True) for w in shards[:2]
+    ]
+    weights.append(lax.all_gather(after(shards[2], weights[0]), "gx", axis=0, tiled=True))
     attn_all, cotan_others = spread([after(s, inputs_low, cosine, sine, *shards) for s in attn_slots], grad_low)
     cotan_blocks = [grad_low] + cotan_others
     qwide = qwidth + 2 * kwidth
@@ -1259,6 +1281,7 @@
 
     keyval = plane_order([keyval_own] + [swap(keyval_own, bits) for bits in OTHERS], chip)
     other_weights = [swap(after(w, keyval), CORE) for w in weights[:2]]
+    query = after(query, *other_weights)
     heads_out, lse = attend_fast(block_list, block_count, query, keyval, mask_bias)
     inputs = inputs_low.astype(full)
     resid = inputs + lax.dot_general(heads_out, out_turned, (((1,), (1,)), ((), ())), preferred_element_type=full)
@@ -1334,13 +1357,23 @@
         block_list, block_count, query, keyval, mask_bias, lse, heads_out, grad_heads, cosine, sine
     )
 
-    parts = [lax.dynamic_slice_in_dim(keyval_part, (chip ^ i) * rows, rows, 0) for i in range(4)]
+    keyval_own = lax.dynamic_slice_in_dim(keyval_part, offset, rows, 0)
     (up_mine, up_sent), others = wgrad(
-        up_b, normed_blocks, 4, 7, [whole_side(part, bits) for part, bits in zip(parts[1:], OTHERS)]
-    )
-
-    grad_rows, grad_bias, grad_gain_one, grad_wqkv = project_back(
-        query_lin, (parts[0], *others), cosine, sine, attn_all, inputs_low, gain_one, grad_resid, normed_one
+        up_b, normed_blocks, 4, 7, [chip_side(keyval_part, bits) for bits in OTHERS]
+    )
+
+    (grad_rows, grad_bias, grad_gain_one, grad_wqkv), (up_got,) = project_back(
+        query_lin,
+        (keyval_own, *others),
+        cosine,
+        sine,
+        attn_all,
+        inputs_low,
+        gain_one,
+        grad_resid,
+        normed_one,
+        9,
+        [whole_side(up_sent, CORE)],
     )
     grad_tokens = unpair_rows(grad_rows, core)
     ffn_out = sum(after(b, query_lin).astype(full) for b in [out_b[0]] + out_got)
@@ -1352,7 +1385,7 @@
     packed = jnp.pad(packed, ((0, 0), (0, 4 * ng - packed.shape[1]))).reshape(32, 4, ng).transpose(0, 2, 1)
     packed = jnp.pad(packed.reshape(32 * ng, 4), ((0, 0), (0, HEAD - 4))).astype(low)
     wide, grad_wout, grad_wup = finish(
-        jnp.concatenate([grad_wqkv, packed], axis=1), grad_wout, up_mine, up_sent, 8
+        lax.dynamic_update_slice_in_dim(grad_wqkv, packed, qwide, 1), grad_wout, up_mine, up_got, 8
     )
     grad_wqkv, grad_wout = wide[:, :qwide], grad_wout.T
     small = wide[:, qwide : qwide + 4].T.reshape(-1)

time: 825 us -> 813 us (0.985)
  waiting for transfers between devices: 75.8 us -> 60.2 us
    all_gather x3 -> x2, waiting for transfers between devices: 29.1 us -> 0.01 us  [on_core(): lax.all_gather(after(w, *attn_slots, inputs_low, grad_low), 'gx', axis=0,...]
    pallas_call x7 -> x8, Pallas kernels: 306 us -> 333 us  [call_beside(): pl.pallas_call(whole_body, grid=grid, in_specs=list(in_specs) + [anywhere...]
    pallas_call x1 -> x0, Pallas kernels: 24.7 us -> none  [project_back(): pl.pallas_call(project_back_body, grid=(rows // tile,), in_specs=[moving(...]
    all_gather x0 -> x1, waiting for transfers between devices: none -> 16.9 us  [on_core(): lax.all_gather(after(shards[2], weights[0]), 'gx', axis=0, tiled=True)]
  transfers between devices with their start and end apart: 20 -> 20, of which waited for: 8 -> 7; matrix products, arithmetic and copies ran while one was open for 9% -> 9% of each run, Pallas kernels for 45% -> 46%
where the time goes in v5:
time: 813 us; the launch traced here: 807 us
  Pallas kernels  613 us (75%)
  waiting for transfers between devices  60.2 us (7%)
  other arithmetic  56.6 us (7%)
  local copies, waits for them, and re-layouts  40.4 us (5%)
  starting transfers between devices  15.5 us (2%)
  between operations  14.6 us (2%)
    pallas_call x8, Pallas kernels, call_beside(): pl.pallas_call(whole_body, grid=grid, in_specs=list(in_specs) + [anywhere...  333 us
    pallas_call x1, Pallas kernels, spread(): pl.pallas_call(spread_body, in_specs=[anywhere] * 5, out_specs=[anywhere]...  115 us
    pallas_call x1, Pallas kernels, finish(): pl.pallas_call(finish_body, in_specs=[anywhere] * 4, out_specs=[inside] *...  102 us
    ppermute x13, waiting for transfers between devices, swap(): return lax.ppermute(array, 'gy', [(i, i ^ bits) for i in range(8)])  24.6 us
    pallas_call x1, Pallas kernels, attend_back_fast(): pl.pallas_call(attend_back_body, grid_spec=pltpu.PrefetchScalarGridSpec(n...  24 us
    pallas_call x1, Pallas kernels, branch_back(): pl.pallas_call(branch_back_body, grid=(steps,), in_specs=[moving, first[0...  19.4 us
    ppermute x3, waiting for transfers between devices, on_core(): lax.ppermute(attn_own, 'gx', [(i, (i + k) % 4) for i in range(4)])  18.6 us
    all_gather x1, waiting for transfers between devices, on_core(): lax.all_gather(after(shards[2], weights[0]), 'gx', axis=0, tiled=True)  16.9 us
  transfers between devices with their start and end apart: 20, of which 7 were waited for; matrix products, arithmetic and copies ran while one was open for 9% of the time, Pallas kernels for 46%

profile of v5, /device:TPU:9, one launch (start us, length us, event | category | flops | bytes accessed | tf_op | source)
XLA Modules:
  0.0 806.9 jit_solution(11547138062857918105)
XLA Ops:
  7.3 2.7 dynamic-slice_bitcast_fusion.5
  12.3 2.5 collective-permute-start.2
  14.7 2.2 collective-permute-start.1
  16.9 1.6 copy.34
  19.5 3.4 maximum_select_fusion.x_ref.refs_8_
  22.9 3.4 maximum_select_fusion.1.refs_4_.refs_1_.cot_ref
  26.3 11.0 %collective-permute-done.2.refs_2_ = bf16[48,3712]{1,0:T(8,128)(2,1)} collective-permute-done((bf16[48,3712]{1,0:T(8,128)(2,1)S(1)}, bf16[48,3712]{1,0:T(8,128)(2,1)}, u32[]{:S(2)}, u32[]{:S(2)}) %collective-permute-start.2) | collective-permute-done | bytes 356384 | tf_op jit(solution)/shard_map/ppermute | solution.py:1237
  37.4 7.6 collective-permute-done.1.refs_1_
  45.1 1.5 copy.35
  52.5 114.6 %spread.1 = (bf16[4,8,48,3712]{3,2,1,0:T(8,128)(2,1)}, bf16[640,1536]{1,0:T(8,128)(2,1)}, bf16[640,1536]{1,0:T(8,128)(2,1)}, bf16[640,1536]{1,0:T(8,128)(2,1)}) custom-call(bf16[48,3712]{1,0:T(8,128)(2,1)} %copy-done.16, bf16[48,3712]{1,0:T(8,128)(2,1)} %collective-permute-done.1.refs_1_, bf16[48,3712]{1,0:T(8,128)(2,1)} %collective-permute-done.2.refs_2_, ...), custom_call_target="tpu_custom_call" | custom-call | bytes 314572800 | tf_op jit(solution)/shard_map/spread/pallas_call | solution.py:884
  169.0 8.9 %project.1 = (bf16[640,1536]{1,0:T(8,128)(2,1)S(1)}, bf16[640,1536]{1,0:T(8,128)(2,1)S(1)}, bf16[640,512]{1,0:T(8,128)(2,1)S(1)}) custom-call(bf16[640,1536]{1,0:T(8,128)(2,1)} %maximum_select_fusion.x_ref.refs_8_, f32[1,1536]{1,0:T(1,128)S(1)} %reshape.184.gain_ref.refs_9_, bf16[1536,3712]{1,0:T(8,128)(2,1)} %bitcast.58, f32[1,2048]{1,0:T(1,128)S(1)} %reshape.185.b_ref, ...), custom_call_target="tpu_custom_call" | custom-call | flops 4026531840 | bytes 14155776 | tf_op jit(solution)/shard_map/project/pallas_call | solution.py:795
  180.6 1.5 collective-permute-start.6
  183.5 1.6 broadcast_in_dim.158
  186.1 9.0 %collective-permute-done.5 = bf16[640,512]{1,0:T(8,128)(2,1)S(1)} collective-permute-done((bf16[640,512]{1,0:T(8,128)(2,1)S(1)}, bf16[640,512]{1,0:T(8,128)(2,1)S(1)}, u32[]{:S(2)}, u32[]{:S(2)}) %collective-permute-start.5) | collective-permute-done | bytes 655392 | tf_op jit(solution)/shard_map/ppermute | solution.py:1175
  196.9 12.3 %collective-permute-done.7 = bf16[640,512]{1,0:T(8,128)(2,1)S(1)} collective-permute-done((bf16[640,512]{1,0:T(8,128)(2,1)S(1)}, bf16[640,512]{1,0:T(8,128)(2,1)S(1)}, u32[]{:S(2)}, u32[]{:S(2)}) %collective-permute-start.7) | collective-permute-done | bytes 655392 | tf_op jit(solution)/shard_map/ppermute | solution.py:1175
  210.1 3.4 collective-permute-start.8
  213.8 5.1 or_reduce_fusion
  219.3 4.3 select_convert_fusion.bias_ref
  224.8 1.5 copy-done.8
  226.4 12.0 %tree_attention.1 = (bf16[640,1536]{1,0:T(8,128)(2,1)S(1)}, f32[5,2,1,768]{3,2,1,0:T(1,128)S(1)}) custom-call(s32[5,10]{1,0:T(8,128)S(1)} %select_reduce_fusion.5.list_ref, s32[5]{0:T(128)S(1)} %convert_reduce_fusion.4.count_ref, bf16[640,1536]{1,0:T(8,128)(2,1)S(1)} %copy-done.8, bf16[2560,512]{1,0:T(8,128)(2,1)} %constant_dynamic-update-slice_fusion.kv_ref, ...), custom_call_target="tpu_custom_call" | custom-call | flops 10066329600 | bytes 6553600 | tf_op jit(solution)/shard_map/tree_attention/pallas_call | solution.py:647
  239.0 16.9 %all-gather.8.cloned.1.call-done.refs_4_ = bf16[1536,1152]{1,0:T(8,128)(2,1)} async-done(((bf16[384,1152]{1,0:T(8,128)(2,1)}), bf16[1536,1152]{1,0:T(8,128)(2,1)}) %all-gather.8.cloned.1.call-update) | async-done | bytes 3538960 | tf_op jit(solution)/shard_map/all_gather | solution.py:1258
  256.5 6.3 multiply_reduce_fusion
  262.9 2.1 multiply_convert_fusion.refs_0_.refs_8_.refs_9_.refs_4_
  265.4 52.0 %ffn_block.4 = (bf16[640,2304]{1,0:T(8,128)(2,1)}, bf16[640,2304]{1,0:T(8,128)(2,1)}, bf16[640,2304]{1,0:T(8,128)(2,1)}, bf16[640,1536]{1,0:T(8,128)(2,1)}, bf16...) custom-call(bf16[640,1536]{1,0:T(8,128)(2,1)} %multiply_convert_fusion.refs_0_.refs_8_.refs_9_.refs_4_, ...), custom_call_target="tpu_custom_call" | custom-call | flops 27179089920 | bytes 35979264 | tf_op jit(solution)/shard_map/ffn_block/pallas_call | solution.py:439
  317.5 39.2 %ffn_block.5 = (bf16[640,2304]{1,0:T(8,128)(2,1)}, bf16[640,2304]{1,0:T(8,128)(2,1)}, bf16[640,2304]{1,0:T(8,128)(2,1)}, bf16[640,1536]{1,0:T(8,128)(2,1)}, bf16...) custom-call(bf16[640,1536]{1,0:T(8,128)(2,1)} %get-tuple-element.111.refs_0_.refs_8_.refs_5_, ...), custom_call_target="tpu_custom_call" | custom-call | flops 27179089920 | bytes 35979264 | tf_op jit(solution)/shard_map/ffn_block/pallas_call | solution.py:439
  356.7 40.1 %ffn_block.6 = (bf16[640,2304]{1,0:T(8,128)(2,1)}, bf16[640,2304]{1,0:T(8,128)(2,1)}, bf16[640,2304]{1,0:T(8,128)(2,1)}, bf16[640,1536]{1,0:T(8,128)(2,1)}, bf16...) custom-call(bf16[640,1536]{1,0:T(8,128)(2,1)} %get-tuple-element.114.refs_0_.refs_7_, ...), custom_call_target="tpu_custom_call" | custom-call | flops 27179089920 | bytes 35979264 | tf_op jit(solution)/shard_map/ffn_block/pallas_call | solution.py:439
  396.8 38.9 %ffn_block.7 = (bf16[640,2304]{1,0:T(8,128)(2,1)}, bf16[640,2304]{1,0:T(8,128)(2,1)}, bf16[640,2304]{1,0:T(8,128)(2,1)}, bf16[640,1536]{1,0:T(8,128)(2,1)}, bf16...) custom-call(bf16[640,1536]{1,0:T(8,128)(2,1)} %get-tuple-element.121.refs_9_.refs_0_.refs_6_, ...), custom_call_target="tpu_custom_call" | custom-call | flops 27179089920 | bytes 35979264 | tf_op jit(solution)/shard_map/ffn_block/pallas_call | solution.py:439
  436.8 2.9 add_convert_fusion.4.refs_11_
  439.7 34.0 %ffn_wgrad.3 = (bf16[4,1152,384]{2,1,0:T(8,128)(2,1)}, bf16[4,1152,384]{2,1,0:T(8,128)(2,1)}, bf16[128,1536]{1,0:T(8,128)(2,1)}, bf16[128,1536]{1,0:T(8,128)(2,1...) custom-call(bf16[640,2304]{1,0:T(8,128)(2,1)} %get-tuple-element.118.refs_0_, ...), custom_call_target="tpu_custom_call" | custom-call | flops 18119393280 | bytes 19660800 | tf_op jit(solution)/shard_map/ffn_wgrad/pallas_call | solution.py:439
  473.7 2.3 add_convert_fusion.5.refs_10_
  476.0 41.4 %ffn_wgrad.4 = (bf16[4,1152,384]{2,1,0:T(8,128)(2,1)}, bf16[4,1152,384]{2,1,0:T(8,128)(2,1)}, bf16[4,1152,384]{2,1,0:T(8,128)(2,1)}, bf16[448,1536]{1,0:T(8,128)(2,1)}, bf16[256,1536]{1,0:T(8,128)(2,1)}) custom-call(bf16[640,2304]{1,0:T(8,128)(2,1)} %get-tuple-element.130.refs_0_, bf16[640,2304]{1,0:T(8,128)(2,1)} %get-tuple-element.131.refs_1_, ...), custom_call_target="tpu_custom_call" | custom-call | flops 18119393280 | bytes 19660800 | tf_op jit(solution)/shard_map/ffn_wgrad/pallas_call | solution.py:439
  518.9 4.1 add_convert_fusion.1
  522.9 2.0 collective-permute-done.11
  524.9 2.8 add_convert_fusion
  527.7 5.5 pad_maximum_fusion
  535.1 3.5 add_convert_fusion.3
  539.6 19.4 %branch_back.1 = (f32[640,1536]{1,0:T(8,128)}, bf16[640,1536]{1,0:T(8,128)(2,1)}, f32[1,1536]{1,0:T(1,128)}, bf16[1536,1536]{1,0:T(8,128)(2,1)}) custom-call(bf16[640,1536]{1,0:T(8,128)(2,1)} %get-tuple-element.110.own_ref, bf16[512,1536]{1,0:T(8,128)(2,1)} %get-tuple-element.117.xa_ref, bf16[128,1536]{1,0:T(8,128)(2,1)} %get-tuple-element.128.xb_ref, ...), custom_call_target="tpu_custom_call" | custom-call | flops 6039797760 | bytes 29097984 | tf_op jit(solution)/shard_map/branch_back/pallas_call | solution.py:943
  559.8 24.0 %tree_attention_back.1 = (bf16[640,1536]{1,0:T(8,128)(2,1)}, bf16[2560,512]{1,0:T(8,128)(2,1)}) custom-call(s32[5,10]{1,0:T(8,128)} %copy-done.4, s32[5]{0:T(128)} %copy-done.5, bf16[640,1536]{1,0:T(8,128)(2,1)} %copy-done.7, bf16[2560,512]{1,0:T(8,128)(2,1)} %constant_dynamic-update-slice_fusion.kv_ref, bf16[2560,640]{1,0:T(8,128)(2,1)} %select_convert_fusion.bias_ref, ...), custom_call_target="tpu_custom_call" | custom-call | flops 25165824000 | bytes 13107200 | tf_op jit(solution)/shard_map/tree_attention_back/pallas_call | solution.py:738
  583.8 2.5 constant_dynamic-slice_fusion.1.refs_1_
  586.3 59.2 %ffn_wgrad.5 = (bf16[4,1152,384]{2,1,0:T(8,128)(2,1)}, bf16[4,1152,384]{2,1,0:T(8,128)(2,1)}, bf16[640,512]{1,0:T(8,128)(2,1)}, bf16[640,512]{1,0:T(8,128)(2,1)}, bf16[640,512]{1,0:T(8,128)(2,1)}) custom-call(bf16[640,2304]{1,0:T(8,128)(2,1)} %get-tuple-element.154.refs_0_, bf16[640,2304]{1,0:T(8,128)(2,1)} %get-tuple-element.155.refs_1_, ...), custom_call_target="tpu_custom_call" | custom-call | flops 18119393280 | bytes 19660800 | tf_op jit(solution)/shard_map/ffn_wgrad/pallas_call | solution.py:439
  645.5 27.7 %project_back.1 = (bf16[640,1536]{1,0:T(8,128)(2,1)}, f32[1,2048]{1,0:T(1,128)}, f32[1,1536]{1,0:T(1,128)}, bf16[1536,2176]{1,0:T(8,128)(2,1)}, bf16[4,1152,384]{2,1,0:T(8,128)(2,1)}) custom-call(bf16[640,1536]{1,0:T(8,128)(2,1)} %get-tuple-element.144.refs_0_, bf16[640,512]{1,0:T(8,128)(2,1)} %constant_dynamic-slice_fusion.1.refs_1_, ...), custom_call_target="tpu_custom_call" | custom-call | flops 8053063680 | bytes 32243712 | tf_op jit(solution)/shard_map/project_back/pallas_call | solution.py:439
  674.9 4.3 add_convert_fusion.2
  683.2 101.5 %finish.1 = (f32[48,2176]{1,0:T(8,128)}, f32[48,1536]{1,0:T(8,128)}, f32[1152,384]{1,0:T(8,128)}) custom-call(bf16[4,2,2,2,48,2176]{5,4,3,2,1,0:T(8,128)(2,1)} %bitcast.64, bf16[4,2,2,2,48,1536]{5,4,3,2,1,0:T(8,128)(2,1)} %bitcast.65, bf16[4,1152,384]{2,1,0:T(8,128)(2,1)} %get-tuple-element.169.mine_ref, bf16[4,1152,384]{2,1,0:T(8,128)(2,1)} %get-tuple-element.170.other_ref), custom_call_target="tpu_custom_call" | custom-call | bytes 209715200 | tf_op jit(solution)/shard_map/finish/pallas_call | solution.py:1147
  784.7 2.8 slice.87
  789.6 3.1 maximum_select_fusion.2
  792.7 3.1 maximum_select_fusion.3
  795.8 1.7 convert_element_type.127
  797.5 2.0 slice_bitcast_fusion
  (166 shorter events, 36.7 us)
Async XLA Ops:
  7.2 174.9 %all-gather.4.cloned.1.call-start = ((), (), s32[]{:S(2)}) async-start(), calls=%async_computation.1 | async-start | bytes 4423680 | tf_op jit(solution)/shard_map/all_gather | solution.py:1256
  7.2 3.5 copy-start.12
  10.0 1.9 copy-start.27
  10.0 1.9 copy-start.28
  10.0 1.9 copy-start.29
  10.0 2.2 copy-start.22
  10.0 2.2 copy-start.25
  10.0 9.5 %collective-permute-start = (bf16[320,1536]{1,0:T(8,128)(2,1)}, bf16[320,1536]{1,0:T(8,128)(2,1)}, u32[]{:S(2)}, u32[]{:S(2)}) collective-permute-start(bf16[320,1536]{1,0:T(8,128)(2,1)} %get-tuple-element.193), channel_id=1, source_target_pairs={{0,1},{1,0},{2,3},{3,2},{4,5},{5,4},{6,7},{7,6},{8,9},{9,8},{10,11... | collective-permute-start | bytes 2949128 | tf_op jit(solution)/shard_map/ppermute | solution.py:1175
  11.8 11.1 %collective-permute-start.4 = (bf16[320,1536]{1,0:T(8,128)(2,1)}, bf16[320,1536]{1,0:T(8,128)(2,1)}, u32[]{:S(2)}, u32[]{:S(2)}) collective-permute-start(bf16[320,1536]{1,0:T(8,128)(2,1)} %get-tuple-element.191), channel_id=1, source_target_pairs={{0,1},{1,0},{2,3},{3,2},{4,5},{5,4},{6,7},{7,6},{8,9},{9,8},{10,11... | collective-permute-start | bytes 2949128 | tf_op jit(solution)/shard_map/ppermute | solution.py:1175
  12.2 10.7 %copy-start.16 = (bf16[48,3712]{1,0:T(8,128)(2,1)}, bf16[48,3712]{1,0:T(8,128)(2,1)S(1)}, u32[]{:S(2)}) copy-start(bf16[48,3712]{1,0:T(8,128)(2,1)S(1)} %fusion.6.refs_0_) | copy-start | bytes 1069060
  12.2 14.1 %collective-permute-start.3 = (bf16[48,3712]{1,0:T(8,128)(2,1)S(1)}, bf16[48,3712]{1,0:T(8,128)(2,1)}, u32[]{:S(2)}, u32[]{:S(2)}) collective-permute-start(bf16[48,3712]{1,0:T(8,128)(2,1)S(1)} %fusion.6.refs_0_), channel_id=1, source_target_pairs={{0,24},{8,0},{16,8},{24,16},{1,25},{9,1},{17,9},{25,17},{2,26},{10... | collective-permute-start | bytes 1069064 | tf_op jit(solution)/shard_map/ppermute | solution.py:1237
  12.3 25.1 %collective-permute-start.2 = (bf16[48,3712]{1,0:T(8,128)(2,1)S(1)}, bf16[48,3712]{1,0:T(8,128)(2,1)}, u32[]{:S(2)}, u32[]{:S(2)}) collective-permute-start(bf16[48,3712]{1,0:T(8,128)(2,1)S(1)} %fusion.6.refs_0_), channel_id=1, source_target_pairs={{0,16},{8,24},{16,0},{24,8},{1,17},{9,25},{17,1},{25,9},{2,18},{10... | collective-permute-start | bytes 1069064 | tf_op jit(solution)/shard_map/ppermute | solution.py:1237
  14.7 30.2 %collective-permute-start.1 = (bf16[48,3712]{1,0:T(8,128)(2,1)S(1)}, bf16[48,3712]{1,0:T(8,128)(2,1)}, u32[]{:S(2)}, u32[]{:S(2)}) collective-permute-start(bf16[48,3712]{1,0:T(8,128)(2,1)S(1)} %fusion.6.refs_0_), channel_id=1, source_target_pairs={{0,8},{8,16},{16,24},{24,0},{1,9},{9,17},{17,25},{25,1},{2,10},{10... | collective-permute-start | bytes 1069064 | tf_op jit(solution)/shard_map/ppermute | solution.py:1237
  22.9 22.2 %copy-start.18 = (bf16[384,1120]{0,1:T(8,128)(2,1)S(1)}, bf16[384,1120]{0,1:T(8,128)(2,1)}, u32[]{:S(2)}) copy-start(bf16[384,1120]{0,1:T(8,128)(2,1)} %param.22) | copy-start | bytes 2580484
  26.3 21.3 %copy-start.19 = (bf16[1120,384]{1,0:T(8,128)(2,1)S(1)}, bf16[1120,384]{1,0:T(8,128)(2,1)}, u32[]{:S(2)}) copy-start(bf16[1120,384]{1,0:T(8,128)(2,1)} %param.23) | copy-start | bytes 2580484
  45.0 165.1 %all-gather.6.cloned.1.call-start = ((), (), s32[]{:S(2)}) async-start(), calls=%async_computation.2 | async-start | bytes 4423680 | tf_op jit(solution)/shard_map/all_gather | solution.py:1256
  47.5 2.6 copy-start.26
  47.5 2.6 copy-start.30
  47.6 208.4 %all-gather.8.cloned.1.call-start = ((), (), s32[]{:S(2)}) async-start(), calls=%async_computation.3 | async-start | bytes 4423680 | tf_op jit(solution)/shard_map/all_gather | solution.py:1258
  52.5 116.4 %copy-start.1 = (f32[640,128]{1,0:T(8,128)}, f32[640,128]{1,0:T(8,128)S(1)}, u32[]{:S(2)}) copy-start(f32[640,128]{1,0:T(8,128)S(1)} %get-tuple-element.203.cos_ref.refs_5_) | copy-start | bytes 983044
  52.5 116.4 %copy-start.2 = (f32[640,128]{1,0:T(8,128)}, f32[640,128]{1,0:T(8,128)S(1)}, u32[]{:S(2)}) copy-start(f32[640,128]{1,0:T(8,128)S(1)} %get-tuple-element.204.sin_ref.refs_6_) | copy-start | bytes 983044
  168.8 87.6 %copy-start.23 = (f32[32,48]{1,0:T(8,128)}, f32[32,48]{1,0:T(8,128)S(1)}, u32[]{:S(2)}) copy-start(f32[32,48]{1,0:T(8,128)S(1)} %get-tuple-element.194) | copy-start | bytes 18436
  169.0 8.9 %copy-start.3 = (f32[1,1536]{1,0:T(1,128)}, f32[1,1536]{1,0:T(1,128)S(1)}, u32[]{:S(2)}) copy-start(f32[1,1536]{1,0:T(1,128)S(1)} %reshape.184.gain_ref.refs_9_) | copy-start | bytes 18436
  179.2 1.3 copy-start.7
  180.6 14.5 %collective-permute-start.5 = (bf16[640,512]{1,0:T(8,128)(2,1)S(1)}, bf16[640,512]{1,0:T(8,128)(2,1)S(1)}, u32[]{:S(2)}, u32[]{:S(2)}) collective-permute-start(bf16[640,512]{1,0:T(8,128)(2,1)S(1)} %get-tuple-element.97), channel_id=1, source_target_pairs={{0,2},{1,3},{2,0},{3,1},{4,6},{5,7},{6,4},{7,5},{8,10},{9,11},{10,... | collective-permute-start | bytes 1966088 | tf_op jit(solution)/shard_map/ppermute | solution.py:1175
  180.6 15.5 %collective-permute-start.6 = (bf16[640,512]{1,0:T(8,128)(2,1)S(1)}, bf16[640,512]{1,0:T(8,128)(2,1)S(1)}, u32[]{:S(2)}, u32[]{:S(2)}) collective-permute-start(bf16[640,512]{1,0:T(8,128)(2,1)S(1)} %get-tuple-element.97), channel_id=1, source_target_pairs={{0,4},{1,5},{2,6},{3,7},{4,0},{5,1},{6,2},{7,3},{8,12},{9,13},{10,... | collective-permute-start | bytes 1966088 | tf_op jit(solution)/shard_map/ppermute | solution.py:1175
  182.1 613.7 %reduce-scatter.2.cloned.1.call-start = ((), (), s32[]{:S(2)}) async-start(), calls=%async_computation.4 | async-start | bytes 8847360 | tf_op jit(solution)/shard_map/reduce_scatter | solution.py:1354
  182.3 26.9 %collective-permute-start.7 = (bf16[640,512]{1,0:T(8,128)(2,1)S(1)}, bf16[640,512]{1,0:T(8,128)(2,1)S(1)}, u32[]{:S(2)}, u32[]{:S(2)}) collective-permute-start(bf16[640,512]{1,0:T(8,128)(2,1)S(1)} %get-tuple-element.97), channel_id=1, source_target_pairs={{0,6},{1,7},{2,4},{3,5},{4,2},{5,3},{6,0},{7,1},{8,14},{9,15},{10,... | collective-permute-start | bytes 1966088 | tf_op jit(solution)/shard_map/ppermute | solution.py:1175
  210.1 13.4 %collective-permute-start.8 = (bf16[1536,1152]{1,0:T(8,128)(2,1)}, bf16[1536,1152]{1,0:T(8,128)(2,1)}, u32[]{:S(2)}, u32[]{:S(2)}) collective-permute-start(bf16[1536,1152]{1,0:T(8,128)(2,1)} %all-gather.4.cloned.1.call-done.refs_2_), channel_id=1, source_target_pairs={{0,1},{1,0},{2,3},{3,2},{4,5},{5,4},{6,7},{7,6},{8,9},{9,8},{10,11... | collective-permute-start | bytes 10616840 | tf_op jit(solution)/shard_map/ppermute | solution.py:1175
  213.6 11.3 %collective-permute-start.9 = (bf16[1536,1152]{1,0:T(8,128)(2,1)}, bf16[1536,1152]{1,0:T(8,128)(2,1)}, u32[]{:S(2)}, u32[]{:S(2)}) collective-permute-start(bf16[1536,1152]{1,0:T(8,128)(2,1)} %all-gather.6.cloned.1.call-done.refs_3_), channel_id=1, source_target_pairs={{0,1},{1,0},{2,3},{3,2},{4,5},{5,4},{6,7},{7,6},{8,9},{9,8},{10,11... | collective-permute-start | bytes 10616840 | tf_op jit(solution)/shard_map/ppermute | solution.py:1175
  219.1 5.7 copy-start.5
  219.3 5.6 copy-start.4
  224.8 1.5 copy-start.8
  239.0 23.9 %copy-start = (bf16[640,1536]{1,0:T(8,128)(2,1)}, bf16[640,1536]{1,0:T(8,128)(2,1)S(1)}, u32[]{:S(2)}) copy-start(bf16[640,1536]{1,0:T(8,128)(2,1)S(1)} %get-tuple-element.105.heads_ref.o_ref) | copy-start | bytes 5898244
  255.9 9.5 %collective-permute-start.10 = (bf16[1536,1152]{1,0:T(8,128)(2,1)}, bf16[1536,1152]{1,0:T(8,128)(2,1)}, u32[]{:S(2)}, u32[]{:S(2)}) collective-permute-start(bf16[1536,1152]{1,0:T(8,128)(2,1)} %all-gather.8.cloned.1.call-done.refs_4_), channel_id=1, source_target_pairs={{0,1},{1,0},{2,3},{3,2},{4,5},{5,4},{6,7},{7,6},{8,9},{9,8},{10,11... | collective-permute-start | bytes 10616840 | tf_op jit(solution)/shard_map/ppermute | solution.py:1175
  262.9 2.5 copy-start.10
  517.4 7.5 collective-permute-start.11
  518.9 6.1 copy-start.11
  533.2 1.9 copy-start.17
  534.6 49.2 %collective-permute-start.12 = (bf16[640,1536]{1,0:T(8,128)(2,1)}, bf16[640,1536]{1,0:T(8,128)(2,1)S(1)}, u32[]{:S(2)}, u32[]{:S(2)}) collective-permute-start(bf16[640,1536]{1,0:T(8,128)(2,1)} %get-tuple-element.147), channel_id=1, source_target_pairs={{0,2},{1,3},{2,0},{3,1},{4,6},{5,7},{6,4},{7,5},{8,10},{9,11},{10,... | collective-permute-start | bytes 5898248 | tf_op jit(solution)/shard_map/ppermute | solution.py:1175
  538.6 45.2 %collective-permute-start.13 = (bf16[640,1536]{1,0:T(8,128)(2,1)}, bf16[640,1536]{1,0:T(8,128)(2,1)}, u32[]{:S(2)}, u32[]{:S(2)}) collective-permute-start(bf16[640,1536]{1,0:T(8,128)(2,1)} %add_convert_fusion.3), channel_id=1, source_target_pairs={{0,4},{1,5},{2,6},{3,7},{4,0},{5,1},{6,2},{7,3},{8,12},{9,13},{10,... | collective-permute-start | bytes 5898248 | tf_op jit(solution)/shard_map/ppermute | solution.py:1175
  583.8 61.7 %copy-start.14 = (bf16[640,1536]{1,0:T(8,128)(2,1)}, bf16[640,1536]{1,0:T(8,128)(2,1)S(1)}, u32[]{:S(2)}) copy-start(bf16[640,1536]{1,0:T(8,128)(2,1)S(1)} %collective-permute-done.12) | copy-start | bytes 5898244
  645.5 29.4 %copy-start.13 = (bf16[640,1536]{1,0:T(8,128)(2,1)S(1)}, bf16[640,1536]{1,0:T(8,128)(2,1)}, u32[]{:S(2)}) copy-start(bf16[640,1536]{1,0:T(8,128)(2,1)} %get-tuple-element.145) | copy-start | bytes 5898244
  679.2 1.5 copy-start.15
  679.4 110.2 %collective-permute-start.14 = (bf16[320,1536]{1,0:T(8,128)(2,1)S(1)}, bf16[320,1536]{1,0:T(8,128)(2,1)}, u32[]{:S(2)}, u32[]{:S(2)}) collective-permute-start(bf16[320,1536]{1,0:T(8,128)(2,1)S(1)} %get-tuple-element.189), channel_id=1, source_target_pairs={{0,1},{1,0},{2,3},{3,2},{4,5},{5,4},{6,7},{7,6},{8,9},{9,8},{10,11... | collective-permute-start | bytes 2949128 | tf_op jit(solution)/shard_map/ppermute | solution.py:1175
  681.8 110.9 %collective-permute-start.15 = (bf16[320,1536]{1,0:T(8,128)(2,1)}, bf16[320,1536]{1,0:T(8,128)(2,1)}, u32[]{:S(2)}, u32[]{:S(2)}) collective-permute-start(bf16[320,1536]{1,0:T(8,128)(2,1)} %get-tuple-element.187), channel_id=1, source_target_pairs={{0,1},{1,0},{2,3},{3,2},{4,5},{5,4},{6,7},{7,6},{8,9},{9,8},{10,11... | collective-permute-start | bytes 2949128 | tf_op jit(solution)/shard_map/ppermute | solution.py:1175
  784.7 2.8 copy-start.20
  797.5 2.0 copy-start.21
  (3 other events, 2.6 us)
Sparse Core Ops, SparseCore 0:
  45.1 69.2 all-gather.3
  116.5 68.5 all-gather.5
  187.3 68.5 all-gather.7
  533.4 123.0 reduce-scatter.1

commit v6 on v5

--- a/solution.py
+++ b/solution.py
@@ -1020,10 +1020,10 @@
     )
 
 
-def finish_body(wide_ref, out_ref, mine_ref, other_ref, *refs):
-    results, scratch = refs[:3], refs[3:]
+def finish_body(wide_ref, out_ref, mine_ref, other_ref, both_ref, layer_ref, tokens_ref, *refs):
+    results, rows_out, scratch = refs[:5], refs[5:7], refs[7:]
     kept, got_core, got_first, got_second, got_ring = [scratch[i : i + 2] for i in range(0, 10, 2)]
-    units, got_units, units_ring, units_moving, sent, landed, local = scratch[10:]
+    units, got_units, units_ring, units_moving, both, sent, landed, local = scratch[10:]
     me, plane = lax.axis_index("gy"), lax.axis_index("gx")
     core, x, y = lax.rem(me, 2), lax.rem(me // 2, 2), me // 4
     places = [lax.rem(plane + 4 - s, 4) for s in range(4)]
@@ -1054,6 +1054,7 @@
     inputs = (wide_ref, out_ref)
     core_copies = [send(inputs[i].at[:, :, :, 1 - core], got_core[i], CORE) for i in range(2)]
     unit_loads = [load(mine_ref, units), load(other_ref, got_units)]
+    both_load = load(both_ref, both)
     held = [load(inputs[i].at[:, :, :, core], kept[i]) for i in range(2)]
 
     for copy in unit_loads:
@@ -1086,6 +1087,15 @@
     units_copy.wait_recv()
     units_moving[0] = units[places[2]] + units_ring[0]
     units_copy = send(units_moving.at[0], units_ring.at[1], RING)
+    half = layer_ref.shape[0] // 2
+    row_copies = []
+    for source, target in ((layer_ref, rows_out[0]), (tokens_ref, rows_out[1])):
+        row_copies.append(send(source.at[pl.ds((1 - core) * half, half)], target.at[core], CORE))
+        held.append(load(source.at[pl.ds(core * half, half)], target.at[core]))
+    both_load.wait()
+    high, own = both.shape[0] // 2, results[3].shape[0]
+    results[3][...] = both[0:own, :].astype(full)
+    results[4][...] = both[high : high + own, :].astype(full)
     nexts = []
     for i in range(2):
         first_copy, second_copy, first, second = steps[i]
@@ -1120,19 +1130,23 @@
         for k, bits in ((1, RING), (2, RING + 1), (3, -RING)):
             there = lax.rem(plane + k, 4)
             ring_copies.append(send(kept[i].at[there, y, x], got_ring[i].at[k - 1], bits))
+    units_copy.wait_recv()
+    results[2][...] = units[places[0], 0:own, :].astype(full) + units_ring[2, 0:own, :].astype(full)
     for i in range(2):
         total = kept[i][plane, y, x].astype(full)
         for k in range(3):
             ring_copies[3 * i + k].wait_recv()
             total = total + got_ring[i][k].astype(full)
         results[i][...] = total
-    units_copy.wait_recv()
-    results[2][...] = units[places[0]].astype(full) + units_ring[2].astype(full)
+    for copy in row_copies:
+        copy.wait_recv()
+    for copy in held[2:]:
+        copy.wait()
     for copy in copies:
         copy.wait_send()
 
 
-def finish(wide, out, mine, other, collective):
+def finish(wide, out, mine, other, both, layer, tokens, own_units, collective):
     low, full = jnp.bfloat16, jnp.float32
     deep = wide.shape[0] // 32
     wide, out = (a.reshape(4, 2, 2, 2, deep, a.shape[1]) for a in (wide, out))
@@ -1146,9 +1160,11 @@
 
     return pl.pallas_call(
         finish_body,
-        in_specs=[anywhere] * 4,
-        out_specs=[inside] * 3,
-        out_shape=[jax.ShapeDtypeStruct((deep, c), full) for c in columns] + [jax.ShapeDtypeStruct(block, full)],
+        in_specs=[anywhere] * 7,
+        out_specs=[inside] * 5 + [anywhere] * 2,
+        out_shape=[jax.ShapeDtypeStruct((deep, c), full) for c in columns]
+        + [jax.ShapeDtypeStruct((own_units, block[1]), full)] * 3
+        + [jax.ShapeDtypeStruct((2, rows.shape[0] // 2, rows.shape[1]), low) for rows in (layer, tokens)],
         scratch_shapes=[
             *pairs(4, 2, 2),
             *pairs(4, 2, 2),
@@ -1159,16 +1175,17 @@
             pltpu.VMEM((4, *block), low),
             pltpu.VMEM((3, *block), low),
             pltpu.VMEM((2, *block), low),
-            pltpu.SemaphoreType.DMA((19,)),
-            pltpu.SemaphoreType.DMA((19,)),
-            pltpu.SemaphoreType.DMA((4,)),
+            pltpu.VMEM(both.shape, low),
+            pltpu.SemaphoreType.DMA((21,)),
+            pltpu.SemaphoreType.DMA((21,)),
+            pltpu.SemaphoreType.DMA((7,)),
         ],
         compiler_params=pltpu.CompilerParams(
             vmem_limit_bytes=56 * 1024 * 1024, collective_id=collective, has_side_effects=True
         ),
         cost_estimate=cost(0, 200 * 1024 * 1024),
         name="finish",
-    )(wide, out, mine, other)
+    )(wide, out, mine, other, both, layer, tokens)
 
 
 def swap(array, bits):
@@ -1186,13 +1203,6 @@
 def pair_rows(pair, core):
     kept, got = pick(pair, core), swap(pick(pair, 1 - core), CORE)
     return jnp.where(core == 0, jnp.concatenate([kept, got]), jnp.concatenate([got, kept]))
-
-
-def unpair_rows(rows, core):
-    half = rows.shape[0] // 2
-    kept = lax.dynamic_slice_in_dim(rows, core * half, half, 0)
-    got = swap(lax.dynamic_slice_in_dim(rows, (1 - core) * half, half, 0), CORE)
-    return jnp.where(core == 0, jnp.stack([kept, got]), jnp.stack([got, kept]))
 
 
 def plane_order(blocks, chip):
@@ -1351,8 +1361,7 @@
     gate_sum = gate_mine.astype(full) + gate_got.astype(full)
     both = jnp.concatenate([down_sum, gate_sum], axis=1).astype(low)
     grad_heads = after(grad_heads, grad_wout, both)
-    both = lax.psum_scatter(both, "gx", scatter_dimension=0, tiled=True)[0].astype(full)
-    grad_down, grad_wgate = both[:own_units], both[pad_units : pad_units + own_units].T
+    both = lax.psum_scatter(both, "gx", scatter_dimension=0, tiled=True)[0]
     query_lin, keyval_part = attend_back_fast(
         block_list, block_count, query, keyval, mask_bias, lse, heads_out, grad_heads, cosine, sine
     )
@@ -1375,21 +1384,28 @@
         9,
         [whole_side(up_sent, CORE)],
     )
-    grad_tokens = unpair_rows(grad_rows, core)
     ffn_out = sum(after(b, query_lin).astype(full) for b in [out_b[0]] + out_got)
-    layer_out = unpair_rows((resid + ffn_out).astype(low), core)
+    layer_rows = (resid + ffn_out).astype(low)
 
     packed = jnp.concatenate(
         [grad_bias.reshape(32, nb), grad_gain_one.reshape(32, ng), grad_gain_two.reshape(32, ng)], axis=1
     )
     packed = jnp.pad(packed, ((0, 0), (0, 4 * ng - packed.shape[1]))).reshape(32, 4, ng).transpose(0, 2, 1)
     packed = jnp.pad(packed.reshape(32 * ng, 4), ((0, 0), (0, HEAD - 4))).astype(low)
-    wide, grad_wout, grad_wup = finish(
-        lax.dynamic_update_slice_in_dim(grad_wqkv, packed, qwide, 1), grad_wout, up_mine, up_got, 8
+    wide, grad_wout, grad_wup, grad_down, grad_wgate, layer_out, grad_tokens = finish(
+        lax.dynamic_update_slice_in_dim(grad_wqkv, packed, qwide, 1),
+        grad_wout,
+        up_mine,
+        up_got,
+        both,
+        layer_rows,
+        grad_rows,
+        own_units,
+        8,
     )
     grad_wqkv, grad_wout = wide[:, :qwide], grad_wout.T
     small = wide[:, qwide : qwide + 4].T.reshape(-1)
-    grad_wup = grad_wup.T[:, :own_units]
+    grad_wgate, grad_wup = grad_wgate.T, grad_wup.T
     return (
         layer_out,
         grad_tokens,

time: 813 us -> 810 us (level)
    unnamed x66 -> x75, local copies, waits for them, and re-layouts: 12.5 us -> 19.3 us
    ppermute x13 -> x11, waiting for transfers between devices: 24.6 us -> 24.6 us  [swap(): return lax.ppermute(array, 'gy', [(i, i ^ bits) for i in range(8)])]
  transfers between devices with their start and end apart: 20 -> 18, of which waited for: 7 -> 7; matrix products, arithmetic and copies ran while one was open for 9% -> 8% of each run, Pallas kernels for 46% -> 33%
where the time goes in v6:
time: 810 us; the launch traced here: 803 us
  Pallas kernels  613 us (76%)
  waiting for transfers between devices  60.2 us (7%)
  other arithmetic  50.2 us (6%)
  local copies, waits for them, and re-layouts  43.1 us (5%)
  starting transfers between devices  15.5 us (2%)
  between operations  14.6 us (2%)
    pallas_call x8, Pallas kernels, call_beside(): pl.pallas_call(whole_body, grid=grid, in_specs=list(in_specs) + [anywhere...  334 us
    pallas_call x1, Pallas kernels, spread(): pl.pallas_call(spread_body, in_specs=[anywhere] * 5, out_specs=[anywhere]...  115 us
    pallas_call x1, Pallas kernels, finish(): pl.pallas_call(finish_body, in_specs=[anywhere] * 7, out_specs=[inside] *...  100 us
    ppermute x11, waiting for transfers between devices, swap(): return lax.ppermute(array, 'gy', [(i, i ^ bits) for i in range(8)])  24.6 us
    pallas_call x1, Pallas kernels, attend_back_fast(): pl.pallas_call(attend_back_body, grid_spec=pltpu.PrefetchScalarGridSpec(n...  23.9 us
    unnamed x75, local copies, waits for them, and re-layouts  19.3 us
    pallas_call x1, Pallas kernels, branch_back(): pl.pallas_call(branch_back_body, grid=(steps,), in_specs=[moving, first[0...  18.7 us
    ppermute x3, waiting for transfers between devices, on_core(): lax.ppermute(attn_own, 'gx', [(i, (i + k) % 4) for i in range(4)])  18.6 us
  transfers between devices with their start and end apart: 18, of which 7 were waited for; matrix products, arithmetic and copies ran while one was open for 8% of the time, Pallas kernels for 33%

profile of v6, /device:TPU:9, one launch (start us, length us, event | category | flops | bytes accessed | tf_op | source)
XLA Modules:
  0.0 802.7 jit_solution(11800033739251263944)
XLA Ops:
  7.3 2.7 dynamic-slice_bitcast_fusion.3
  12.3 2.5 collective-permute-start.2
  14.7 2.2 collective-permute-start.1
  16.9 1.6 copy.34
  19.5 3.4 maximum_select_fusion.x_ref.refs_8_
  22.9 3.4 maximum_select_fusion.1.refs_4_.refs_1_.cot_ref
  26.4 11.0 %collective-permute-done.2.refs_2_ = bf16[48,3712]{1,0:T(8,128)(2,1)} collective-permute-done((bf16[48,3712]{1,0:T(8,128)(2,1)S(1)}, bf16[48,3712]{1,0:T(8,128)(2,1)}, u32[]{:S(2)}, u32[]{:S(2)}) %collective-permute-start.2) | collective-permute-done | bytes 356384 | tf_op jit(solution)/shard_map/ppermute | solution.py:1247
  37.4 7.6 collective-permute-done.1.refs_1_
  45.1 1.5 copy.35
  47.6 1.5 copy.36
  52.5 114.6 %spread.1 = (bf16[4,8,48,3712]{3,2,1,0:T(8,128)(2,1)}, bf16[640,1536]{1,0:T(8,128)(2,1)}, bf16[640,1536]{1,0:T(8,128)(2,1)}, bf16[640,1536]{1,0:T(8,128)(2,1)}) custom-call(bf16[48,3712]{1,0:T(8,128)(2,1)} %copy-done.19, bf16[48,3712]{1,0:T(8,128)(2,1)} %collective-permute-done.1.refs_1_, bf16[48,3712]{1,0:T(8,128)(2,1)} %collective-permute-done.2.refs_2_, ...), custom_call_target="tpu_custom_call" | custom-call | bytes 314572800 | tf_op jit(solution)/shard_map/spread/pallas_call | solution.py:884
  169.0 8.9 %project.1 = (bf16[640,1536]{1,0:T(8,128)(2,1)S(1)}, bf16[640,1536]{1,0:T(8,128)(2,1)S(1)}, bf16[640,512]{1,0:T(8,128)(2,1)S(1)}) custom-call(bf16[640,1536]{1,0:T(8,128)(2,1)} %maximum_select_fusion.x_ref.refs_8_, f32[1,1536]{1,0:T(1,128)S(1)} %reshape.181.gain_ref.refs_9_, bf16[1536,3712]{1,0:T(8,128)(2,1)} %bitcast.48, f32[1,2048]{1,0:T(1,128)S(1)} %reshape.182.b_ref, ...), custom_call_target="tpu_custom_call" | custom-call | flops 4026531840 | bytes 14155776 | tf_op jit(solution)/shard_map/project/pallas_call | solution.py:795
  177.9 1.3 copy-done.6
  180.5 1.5 collective-permute-start.6
  183.5 1.6 broadcast_in_dim.158
  186.1 9.0 %collective-permute-done.5 = bf16[640,512]{1,0:T(8,128)(2,1)S(1)} collective-permute-done((bf16[640,512]{1,0:T(8,128)(2,1)S(1)}, bf16[640,512]{1,0:T(8,128)(2,1)S(1)}, u32[]{:S(2)}, u32[]{:S(2)}) %collective-permute-start.5) | collective-permute-done | bytes 655392 | tf_op jit(solution)/shard_map/ppermute | solution.py:1192
  196.9 12.3 %collective-permute-done.7 = bf16[640,512]{1,0:T(8,128)(2,1)S(1)} collective-permute-done((bf16[640,512]{1,0:T(8,128)(2,1)S(1)}, bf16[640,512]{1,0:T(8,128)(2,1)S(1)}, u32[]{:S(2)}, u32[]{:S(2)}) %collective-permute-start.7) | collective-permute-done | bytes 655392 | tf_op jit(solution)/shard_map/ppermute | solution.py:1192
  210.1 3.5 collective-permute-start.8
  213.7 5.1 or_reduce_fusion
  219.2 4.3 select_convert_fusion.bias_ref
  224.8 1.5 copy-done.8
  226.3 12.0 %tree_attention.1 = (bf16[640,1536]{1,0:T(8,128)(2,1)S(1)}, f32[5,2,1,768]{3,2,1,0:T(1,128)S(1)}) custom-call(s32[5,10]{1,0:T(8,128)S(1)} %select_reduce_fusion.5.list_ref, s32[5]{0:T(128)S(1)} %convert_reduce_fusion.4.count_ref, bf16[640,1536]{1,0:T(8,128)(2,1)S(1)} %copy-done.8, bf16[2560,512]{1,0:T(8,128)(2,1)} %constant_dynamic-update-slice_fusion.kv_ref, ...), custom_call_target="tpu_custom_call" | custom-call | flops 10066329600 | bytes 6553600 | tf_op jit(solution)/shard_map/tree_attention/pallas_call | solution.py:647
  239.0 16.9 %all-gather.8.cloned.1.call-done.refs_4_ = bf16[1536,1152]{1,0:T(8,128)(2,1)} async-done(((bf16[384,1152]{1,0:T(8,128)(2,1)}), bf16[1536,1152]{1,0:T(8,128)(2,1)}) %all-gather.8.cloned.1.call-update) | async-done | bytes 3538960 | tf_op jit(solution)/shard_map/all_gather | solution.py:1268
  256.5 6.3 multiply_reduce_fusion
  262.9 2.1 multiply_convert_fusion.refs_0_.refs_8_.refs_9_.refs_4_
  265.4 53.0 %ffn_block.4 = (bf16[640,2304]{1,0:T(8,128)(2,1)}, bf16[640,2304]{1,0:T(8,128)(2,1)}, bf16[640,2304]{1,0:T(8,128)(2,1)}, bf16[640,1536]{1,0:T(8,128)(2,1)}, bf16...) custom-call(bf16[640,1536]{1,0:T(8,128)(2,1)} %multiply_convert_fusion.refs_0_.refs_8_.refs_9_.refs_4_, ...), custom_call_target="tpu_custom_call" | custom-call | flops 27179089920 | bytes 35979264 | tf_op jit(solution)/shard_map/ffn_block/pallas_call | solution.py:439
  318.5 39.3 %ffn_block.5 = (bf16[640,2304]{1,0:T(8,128)(2,1)}, bf16[640,2304]{1,0:T(8,128)(2,1)}, bf16[640,2304]{1,0:T(8,128)(2,1)}, bf16[640,1536]{1,0:T(8,128)(2,1)}, bf16...) custom-call(bf16[640,1536]{1,0:T(8,128)(2,1)} %get-tuple-element.114.refs_0_.refs_8_.refs_5_, ...), custom_call_target="tpu_custom_call" | custom-call | flops 27179089920 | bytes 35979264 | tf_op jit(solution)/shard_map/ffn_block/pallas_call | solution.py:439
  357.7 40.9 %ffn_block.6 = (bf16[640,2304]{1,0:T(8,128)(2,1)}, bf16[640,2304]{1,0:T(8,128)(2,1)}, bf16[640,2304]{1,0:T(8,128)(2,1)}, bf16[640,1536]{1,0:T(8,128)(2,1)}, bf16...) custom-call(bf16[640,1536]{1,0:T(8,128)(2,1)} %get-tuple-element.117.refs_0_.refs_7_, ...), custom_call_target="tpu_custom_call" | custom-call | flops 27179089920 | bytes 35979264 | tf_op jit(solution)/shard_map/ffn_block/pallas_call | solution.py:439
  398.7 39.8 %ffn_block.7 = (bf16[640,2304]{1,0:T(8,128)(2,1)}, bf16[640,2304]{1,0:T(8,128)(2,1)}, bf16[640,2304]{1,0:T(8,128)(2,1)}, bf16[640,1536]{1,0:T(8,128)(2,1)}, bf16...) custom-call(bf16[640,1536]{1,0:T(8,128)(2,1)} %get-tuple-element.124.refs_9_.refs_0_.refs_6_, ...), custom_call_target="tpu_custom_call" | custom-call | flops 27179089920 | bytes 35979264 | tf_op jit(solution)/shard_map/ffn_block/pallas_call | solution.py:439
  439.5 2.9 add_convert_fusion.4.refs_11_
  442.4 34.7 %ffn_wgrad.3 = (bf16[4,1152,384]{2,1,0:T(8,128)(2,1)}, bf16[4,1152,384]{2,1,0:T(8,128)(2,1)}, bf16[128,1536]{1,0:T(8,128)(2,1)}, bf16[128,1536]{1,0:T(8,128)(2,1...) custom-call(bf16[640,2304]{1,0:T(8,128)(2,1)} %get-tuple-element.121.refs_0_, ...), custom_call_target="tpu_custom_call" | custom-call | flops 18119393280 | bytes 19660800 | tf_op jit(solution)/shard_map/ffn_wgrad/pallas_call | solution.py:439
  477.1 2.3 add_convert_fusion.5.refs_10_
  479.4 40.6 %ffn_wgrad.4 = (bf16[4,1152,384]{2,1,0:T(8,128)(2,1)}, bf16[4,1152,384]{2,1,0:T(8,128)(2,1)}, bf16[4,1152,384]{2,1,0:T(8,128)(2,1)}, bf16[448,1536]{1,0:T(8,128)(2,1)}, bf16[256,1536]{1,0:T(8,128)(2,1)}) custom-call(bf16[640,2304]{1,0:T(8,128)(2,1)} %get-tuple-element.133.refs_0_, bf16[640,2304]{1,0:T(8,128)(2,1)} %get-tuple-element.134.refs_1_, ...), custom_call_target="tpu_custom_call" | custom-call | flops 18119393280 | bytes 19660800 | tf_op jit(solution)/shard_map/ffn_wgrad/pallas_call | solution.py:439
  520.0 1.5 collective-permute-start.11
  521.5 4.1 add_convert_fusion.1
  525.5 2.0 collective-permute-done.11
  527.5 2.8 add_convert_fusion
  530.3 5.5 pad_maximum_fusion
  537.8 3.5 add_convert_fusion.3
  542.2 18.7 %branch_back.1 = (f32[640,1536]{1,0:T(8,128)}, bf16[640,1536]{1,0:T(8,128)(2,1)}, f32[1,1536]{1,0:T(1,128)}, bf16[1536,1536]{1,0:T(8,128)(2,1)}) custom-call(bf16[640,1536]{1,0:T(8,128)(2,1)} %get-tuple-element.113.own_ref, bf16[512,1536]{1,0:T(8,128)(2,1)} %get-tuple-element.120.xa_ref, bf16[128,1536]{1,0:T(8,128)(2,1)} %get-tuple-element.131.xb_ref, ...), custom_call_target="tpu_custom_call" | custom-call | flops 6039797760 | bytes 29097984 | tf_op jit(solution)/shard_map/branch_back/pallas_call | solution.py:943
  561.7 23.9 %tree_attention_back.1 = (bf16[640,1536]{1,0:T(8,128)(2,1)}, bf16[2560,512]{1,0:T(8,128)(2,1)}) custom-call(s32[5,10]{1,0:T(8,128)} %copy-done.4, s32[5]{0:T(128)} %copy-done.5, bf16[640,1536]{1,0:T(8,128)(2,1)} %copy-done.7, bf16[2560,512]{1,0:T(8,128)(2,1)} %constant_dynamic-update-slice_fusion.kv_ref, bf16[2560,640]{1,0:T(8,128)(2,1)} %select_convert_fusion.bias_ref, ...), custom_call_target="tpu_custom_call" | custom-call | flops 25165824000 | bytes 13107200 | tf_op jit(solution)/shard_map/tree_attention_back/pallas_call | solution.py:738
  585.6 2.5 constant_dynamic-slice_fusion.refs_1_
  588.1 61.0 %ffn_wgrad.5 = (bf16[4,1152,384]{2,1,0:T(8,128)(2,1)}, bf16[4,1152,384]{2,1,0:T(8,128)(2,1)}, bf16[640,512]{1,0:T(8,128)(2,1)}, bf16[640,512]{1,0:T(8,128)(2,1)}, bf16[640,512]{1,0:T(8,128)(2,1)}) custom-call(bf16[640,2304]{1,0:T(8,128)(2,1)} %get-tuple-element.149.refs_0_, bf16[640,2304]{1,0:T(8,128)(2,1)} %get-tuple-element.150.refs_1_, ...), custom_call_target="tpu_custom_call" | custom-call | flops 18119393280 | bytes 19660800 | tf_op jit(solution)/shard_map/ffn_wgrad/pallas_call | solution.py:439
  649.1 25.0 %project_back.1 = (bf16[640,1536]{1,0:T(8,128)(2,1)}, f32[1,2048]{1,0:T(1,128)}, f32[1,1536]{1,0:T(1,128)}, bf16[1536,2176]{1,0:T(8,128)(2,1)}, bf16[4,1152,384]{2,1,0:T(8,128)(2,1)}) custom-call(bf16[640,1536]{1,0:T(8,128)(2,1)} %get-tuple-element.147.refs_0_, bf16[640,512]{1,0:T(8,128)(2,1)} %constant_dynamic-slice_fusion.refs_1_, ...), custom_call_target="tpu_custom_call" | custom-call | flops 8053063680 | bytes 32243712 | tf_op jit(solution)/shard_map/project_back/pallas_call | solution.py:439
  677.2 5.6 add_convert_fusion.2.layer_ref
  682.8 100.5 %finish.1 = (f32[48,2176]{1,0:T(8,128)}, f32[48,1536]{1,0:T(8,128)}, f32[1120,384]{1,0:T(8,128)}, f32[1120,384]{1,0:T(8,128)}, f32[1120,384]{1,0:T(8,128)}, /*in...) custom-call(bf16[4,2,2,2,48,2176]{5,4,3,2,1,0:T(8,128)(2,1)} %bitcast.54, ...), custom_call_target="tpu_custom_call" | custom-call | bytes 209715200 | tf_op jit(solution)/shard_map/finish/pallas_call | solution.py:1161
  784.1 1.8 slice.55
  787.2 2.9 copy.51
  (164 shorter events, 35.1 us)
Async XLA Ops:
  7.2 174.8 %all-gather.4.cloned.1.call-start = ((), (), s32[]{:S(2)}) async-start(), calls=%async_computation.1 | async-start | bytes 4423680 | tf_op jit(solution)/shard_map/all_gather | solution.py:1266
  7.2 3.5 copy-start.12
  10.0 1.9 copy-start.29
  10.0 1.9 copy-start.30
  10.0 1.9 copy-start.31
  10.0 2.2 copy-start.24
  10.0 2.2 copy-start.27
  10.0 9.5 %collective-permute-start = (bf16[320,1536]{1,0:T(8,128)(2,1)}, bf16[320,1536]{1,0:T(8,128)(2,1)}, u32[]{:S(2)}, u32[]{:S(2)}) collective-permute-start(bf16[320,1536]{1,0:T(8,128)(2,1)} %get-tuple-element.195), channel_id=1, source_target_pairs={{0,1},{1,0},{2,3},{3,2},{4,5},{5,4},{6,7},{7,6},{8,9},{9,8},{10,11... | collective-permute-start | bytes 2949128 | tf_op jit(solution)/shard_map/ppermute | solution.py:1192
  11.8 11.1 %collective-permute-start.4 = (bf16[320,1536]{1,0:T(8,128)(2,1)}, bf16[320,1536]{1,0:T(8,128)(2,1)}, u32[]{:S(2)}, u32[]{:S(2)}) collective-permute-start(bf16[320,1536]{1,0:T(8,128)(2,1)} %get-tuple-element.193), channel_id=1, source_target_pairs={{0,1},{1,0},{2,3},{3,2},{4,5},{5,4},{6,7},{7,6},{8,9},{9,8},{10,11... | collective-permute-start | bytes 2949128 | tf_op jit(solution)/shard_map/ppermute | solution.py:1192
  12.2 10.7 %copy-start.19 = (bf16[48,3712]{1,0:T(8,128)(2,1)}, bf16[48,3712]{1,0:T(8,128)(2,1)S(1)}, u32[]{:S(2)}) copy-start(bf16[48,3712]{1,0:T(8,128)(2,1)S(1)} %fusion.6.refs_0_) | copy-start | bytes 1069060
  12.2 14.2 %collective-permute-start.3 = (bf16[48,3712]{1,0:T(8,128)(2,1)S(1)}, bf16[48,3712]{1,0:T(8,128)(2,1)}, u32[]{:S(2)}, u32[]{:S(2)}) collective-permute-start(bf16[48,3712]{1,0:T(8,128)(2,1)S(1)} %fusion.6.refs_0_), channel_id=1, source_target_pairs={{0,24},{8,0},{16,8},{24,16},{1,25},{9,1},{17,9},{25,17},{2,26},{10... | collective-permute-start | bytes 1069064 | tf_op jit(solution)/shard_map/ppermute | solution.py:1247
  12.3 25.1 %collective-permute-start.2 = (bf16[48,3712]{1,0:T(8,128)(2,1)S(1)}, bf16[48,3712]{1,0:T(8,128)(2,1)}, u32[]{:S(2)}, u32[]{:S(2)}) collective-permute-start(bf16[48,3712]{1,0:T(8,128)(2,1)S(1)} %fusion.6.refs_0_), channel_id=1, source_target_pairs={{0,16},{8,24},{16,0},{24,8},{1,17},{9,25},{17,1},{25,9},{2,18},{10... | collective-permute-start | bytes 1069064 | tf_op jit(solution)/shard_map/ppermute | solution.py:1247
  14.7 30.2 %collective-permute-start.1 = (bf16[48,3712]{1,0:T(8,128)(2,1)S(1)}, bf16[48,3712]{1,0:T(8,128)(2,1)}, u32[]{:S(2)}, u32[]{:S(2)}) collective-permute-start(bf16[48,3712]{1,0:T(8,128)(2,1)S(1)} %fusion.6.refs_0_), channel_id=1, source_target_pairs={{0,8},{8,16},{16,24},{24,0},{1,9},{9,17},{17,25},{25,1},{2,10},{10... | collective-permute-start | bytes 1069064 | tf_op jit(solution)/shard_map/ppermute | solution.py:1247
  22.9 22.1 %copy-start.21 = (bf16[384,1120]{0,1:T(8,128)(2,1)S(1)}, bf16[384,1120]{0,1:T(8,128)(2,1)}, u32[]{:S(2)}) copy-start(bf16[384,1120]{0,1:T(8,128)(2,1)} %param.22) | copy-start | bytes 2580484
  26.4 21.3 %copy-start.22 = (bf16[1120,384]{1,0:T(8,128)(2,1)S(1)}, bf16[1120,384]{1,0:T(8,128)(2,1)}, u32[]{:S(2)}) copy-start(bf16[1120,384]{1,0:T(8,128)(2,1)} %param.23) | copy-start | bytes 2580484
  45.0 165.0 %all-gather.6.cloned.1.call-start = ((), (), s32[]{:S(2)}) async-start(), calls=%async_computation.2 | async-start | bytes 4423680 | tf_op jit(solution)/shard_map/all_gather | solution.py:1266
  47.5 2.6 copy-start.28
  47.5 2.6 copy-start.32
  47.6 208.4 %all-gather.8.cloned.1.call-start = ((), (), s32[]{:S(2)}) async-start(), calls=%async_computation.3 | async-start | bytes 4423680 | tf_op jit(solution)/shard_map/all_gather | solution.py:1268
  52.5 116.4 %copy-start.1 = (f32[640,128]{1,0:T(8,128)}, f32[640,128]{1,0:T(8,128)S(1)}, u32[]{:S(2)}) copy-start(f32[640,128]{1,0:T(8,128)S(1)} %get-tuple-element.205.cos_ref.refs_5_) | copy-start | bytes 983044
  52.5 116.4 %copy-start.2 = (f32[640,128]{1,0:T(8,128)}, f32[640,128]{1,0:T(8,128)S(1)}, u32[]{:S(2)}) copy-start(f32[640,128]{1,0:T(8,128)S(1)} %get-tuple-element.206.sin_ref.refs_6_) | copy-start | bytes 983044
  168.8 87.6 %copy-start.25 = (f32[32,48]{1,0:T(8,128)}, f32[32,48]{1,0:T(8,128)S(1)}, u32[]{:S(2)}) copy-start(f32[32,48]{1,0:T(8,128)S(1)} %get-tuple-element.196) | copy-start | bytes 18436
  169.0 8.9 %copy-start.3 = (f32[1,1536]{1,0:T(1,128)}, f32[1,1536]{1,0:T(1,128)S(1)}, u32[]{:S(2)}) copy-start(f32[1,1536]{1,0:T(1,128)S(1)} %reshape.181.gain_ref.refs_9_) | copy-start | bytes 18436
  177.9 1.3 copy-start.6
  179.2 1.3 copy-start.7
  180.5 14.5 %collective-permute-start.5 = (bf16[640,512]{1,0:T(8,128)(2,1)S(1)}, bf16[640,512]{1,0:T(8,128)(2,1)S(1)}, u32[]{:S(2)}, u32[]{:S(2)}) collective-permute-start(bf16[640,512]{1,0:T(8,128)(2,1)S(1)} %get-tuple-element.101), channel_id=1, source_target_pairs={{0,2},{1,3},{2,0},{3,1},{4,6},{5,7},{6,4},{7,5},{8,10},{9,11},{10,... | collective-permute-start | bytes 1966088 | tf_op jit(solution)/shard_map/ppermute | solution.py:1192
  180.5 15.4 %collective-permute-start.6 = (bf16[640,512]{1,0:T(8,128)(2,1)S(1)}, bf16[640,512]{1,0:T(8,128)(2,1)S(1)}, u32[]{:S(2)}, u32[]{:S(2)}) collective-permute-start(bf16[640,512]{1,0:T(8,128)(2,1)S(1)} %get-tuple-element.101), channel_id=1, source_target_pairs={{0,4},{1,5},{2,6},{3,7},{4,0},{5,1},{6,2},{7,3},{8,12},{9,13},{10,... | collective-permute-start | bytes 1966088 | tf_op jit(solution)/shard_map/ppermute | solution.py:1192
  182.0 500.7 %reduce-scatter.2.cloned.1.call-start = ((), (), s32[]{:S(2)}) async-start(), calls=%async_computation.4 | async-start | bytes 8847360 | tf_op jit(solution)/shard_map/reduce_scatter | solution.py:1364
  182.3 26.9 %collective-permute-start.7 = (bf16[640,512]{1,0:T(8,128)(2,1)S(1)}, bf16[640,512]{1,0:T(8,128)(2,1)S(1)}, u32[]{:S(2)}, u32[]{:S(2)}) collective-permute-start(bf16[640,512]{1,0:T(8,128)(2,1)S(1)} %get-tuple-element.101), channel_id=1, source_target_pairs={{0,6},{1,7},{2,4},{3,5},{4,2},{5,3},{6,0},{7,1},{8,14},{9,15},{10,... | collective-permute-start | bytes 1966088 | tf_op jit(solution)/shard_map/ppermute | solution.py:1192
  210.1 13.5 %collective-permute-start.8 = (bf16[1536,1152]{1,0:T(8,128)(2,1)}, bf16[1536,1152]{1,0:T(8,128)(2,1)}, u32[]{:S(2)}, u32[]{:S(2)}) collective-permute-start(bf16[1536,1152]{1,0:T(8,128)(2,1)} %all-gather.4.cloned.1.call-done.refs_2_), channel_id=1, source_target_pairs={{0,1},{1,0},{2,3},{3,2},{4,5},{5,4},{6,7},{7,6},{8,9},{9,8},{10,11... | collective-permute-start | bytes 10616840 | tf_op jit(solution)/shard_map/ppermute | solution.py:1192
  213.5 11.3 %collective-permute-start.9 = (bf16[1536,1152]{1,0:T(8,128)(2,1)}, bf16[1536,1152]{1,0:T(8,128)(2,1)}, u32[]{:S(2)}, u32[]{:S(2)}) collective-permute-start(bf16[1536,1152]{1,0:T(8,128)(2,1)} %all-gather.6.cloned.1.call-done.refs_3_), channel_id=1, source_target_pairs={{0,1},{1,0},{2,3},{3,2},{4,5},{5,4},{6,7},{7,6},{8,9},{9,8},{10,11... | collective-permute-start | bytes 10616840 | tf_op jit(solution)/shard_map/ppermute | solution.py:1192
  219.1 5.7 copy-start.5
  219.2 5.6 copy-start.4
  224.8 1.5 copy-start.8
  239.0 23.9 %copy-start = (bf16[640,1536]{1,0:T(8,128)(2,1)}, bf16[640,1536]{1,0:T(8,128)(2,1)S(1)}, u32[]{:S(2)}) copy-start(bf16[640,1536]{1,0:T(8,128)(2,1)S(1)} %get-tuple-element.110.heads_ref.o_ref) | copy-start | bytes 5898244
  255.9 9.5 %collective-permute-start.10 = (bf16[1536,1152]{1,0:T(8,128)(2,1)}, bf16[1536,1152]{1,0:T(8,128)(2,1)}, u32[]{:S(2)}, u32[]{:S(2)}) collective-permute-start(bf16[1536,1152]{1,0:T(8,128)(2,1)} %all-gather.8.cloned.1.call-done.refs_4_), channel_id=1, source_target_pairs={{0,1},{1,0},{2,3},{3,2},{4,5},{5,4},{6,7},{7,6},{8,9},{9,8},{10,11... | collective-permute-start | bytes 10616840 | tf_op jit(solution)/shard_map/ppermute | solution.py:1192
  262.9 2.5 copy-start.10
  520.0 7.5 collective-permute-start.11
  521.5 6.1 copy-start.11
  535.8 1.9 copy-start.20
  537.2 48.4 %collective-permute-start.12 = (bf16[640,1536]{1,0:T(8,128)(2,1)}, bf16[640,1536]{1,0:T(8,128)(2,1)S(1)}, u32[]{:S(2)}, u32[]{:S(2)}) collective-permute-start(bf16[640,1536]{1,0:T(8,128)(2,1)} %get-tuple-element.168), channel_id=1, source_target_pairs={{0,2},{1,3},{2,0},{3,1},{4,6},{5,7},{6,4},{7,5},{8,10},{9,11},{10,... | collective-permute-start | bytes 5898248 | tf_op jit(solution)/shard_map/ppermute | solution.py:1192
  541.3 44.3 %collective-permute-start.13 = (bf16[640,1536]{1,0:T(8,128)(2,1)}, bf16[640,1536]{1,0:T(8,128)(2,1)}, u32[]{:S(2)}, u32[]{:S(2)}) collective-permute-start(bf16[640,1536]{1,0:T(8,128)(2,1)} %add_convert_fusion.3), channel_id=1, source_target_pairs={{0,4},{1,5},{2,6},{3,7},{4,0},{5,1},{6,2},{7,3},{8,12},{9,13},{10,... | collective-permute-start | bytes 5898248 | tf_op jit(solution)/shard_map/ppermute | solution.py:1192
  585.6 63.5 %copy-start.14 = (bf16[640,1536]{1,0:T(8,128)(2,1)}, bf16[640,1536]{1,0:T(8,128)(2,1)S(1)}, u32[]{:S(2)}) copy-start(bf16[640,1536]{1,0:T(8,128)(2,1)S(1)} %collective-permute-done.12) | copy-start | bytes 5898244
  649.1 28.1 %copy-start.13 = (bf16[640,1536]{1,0:T(8,128)(2,1)S(1)}, bf16[640,1536]{1,0:T(8,128)(2,1)}, u32[]{:S(2)}) copy-start(bf16[640,1536]{1,0:T(8,128)(2,1)} %get-tuple-element.166) | copy-start | bytes 5898244
  783.2 6.9 copy-start.15
  790.1 2.3 copy-start.18
  791.4 2.2 copy-start.17
  792.4 2.4 copy-start.16
  (3 other events, 2.6 us)
Sparse Core Ops, SparseCore 0:
  45.1 69.2 all-gather.3
  116.5 68.5 all-gather.5
  187.3 68.5 all-gather.7
  536.0 121.3 reduce-scatter.1

commit v7 on v6

--- a/solution.py
+++ b/solution.py
@@ -1020,10 +1020,30 @@
     )
 
 
-def finish_body(wide_ref, out_ref, mine_ref, other_ref, both_ref, layer_ref, tokens_ref, *refs):
-    results, rows_out, scratch = refs[:5], refs[5:7], refs[7:]
+def both_body(first_mine, first_other, second_mine, second_other, out_ref):
+    deep = first_mine.shape[1]
+    out_ref[0, :deep] = (first_mine[0].astype(jnp.float32) + first_other[0].astype(jnp.float32)).astype(out_ref.dtype)
+    out_ref[0, deep:] = (second_mine[0].astype(jnp.float32) + second_other[0].astype(jnp.float32)).astype(out_ref.dtype)
+
+
+def both_sums(*arrays):
+    planes, deep, wide = arrays[0].shape
+    return pl.pallas_call(
+        both_body,
+        grid=(planes,),
+        in_specs=[pl.BlockSpec((1, deep, wide), lambda i: (i, 0, 0))] * 4,
+        out_specs=pl.BlockSpec((1, 2 * deep, wide), lambda i: (i, 0, 0)),
+        out_shape=jax.ShapeDtypeStruct((planes, 2 * deep, wide), arrays[0].dtype),
+        compiler_params=params(48),
+        cost_estimate=cost(0, 12 * planes * deep * wide),
+        name="both_back",
+    )(*arrays)
+
+
+def finish_body(wide_ref, out_ref, mine_ref, other_ref, both_ref, tokens_ref, resid_ref, *refs):
+    layer_refs, results, rows_out, scratch = refs[:3], refs[3:8], refs[8:10], refs[10:]
     kept, got_core, got_first, got_second, got_ring = [scratch[i : i + 2] for i in range(0, 10, 2)]
-    units, got_units, units_ring, units_moving, both, sent, landed, local = scratch[10:]
+    units, got_units, units_ring, units_moving, both, layer, resid, *layer_parts, sent, landed, local = scratch[10:]
     me, plane = lax.axis_index("gy"), lax.axis_index("gx")
     core, x, y = lax.rem(me, 2), lax.rem(me // 2, 2), me // 4
     places = [lax.rem(plane + 4 - s, 4) for s in range(4)]
@@ -1055,6 +1075,7 @@
     core_copies = [send(inputs[i].at[:, :, :, 1 - core], got_core[i], CORE) for i in range(2)]
     unit_loads = [load(mine_ref, units), load(other_ref, got_units)]
     both_load = load(both_ref, both)
+    layer_loads = [load(a, b) for a, b in zip((resid_ref, *layer_refs), (resid, *layer_parts))]
     held = [load(inputs[i].at[:, :, :, core], kept[i]) for i in range(2)]
 
     for copy in unit_loads:
@@ -1087,9 +1108,18 @@
     units_copy.wait_recv()
     units_moving[0] = units[places[2]] + units_ring[0]
     units_copy = send(units_moving.at[0], units_ring.at[1], RING)
-    half = layer_ref.shape[0] // 2
+    for copy in layer_loads:
+        copy.wait()
+
+    @pl.loop(0, resid.shape[0] // ROW_TILE)
+    def _(p):
+        take = pl.ds(pl.multiple_of(p * ROW_TILE, ROW_TILE), ROW_TILE)
+        total = layer_parts[0][take, :].astype(full) + layer_parts[1][take, :].astype(full)
+        layer[take, :] = (resid[take, :] + (total + layer_parts[2][take, :].astype(full))).astype(jnp.bfloat16)
+
+    half = resid.shape[0] // 2
     row_copies = []
-    for source, target in ((layer_ref, rows_out[0]), (tokens_ref, rows_out[1])):
+    for source, target in ((layer, rows_out[0]), (tokens_ref, rows_out[1])):
         row_copies.append(send(source.at[pl.ds((1 - core) * half, half)], target.at[core], CORE))
         held.append(load(source.at[pl.ds(core * half, half)], target.at[core]))
     both_load.wait()
@@ -1146,7 +1176,7 @@
         copy.wait_send()
 
 
-def finish(wide, out, mine, other, both, layer, tokens, own_units, collective):
+def finish(wide, out, mine, other, both, tokens, resid, layer_parts, own_units, collective):
     low, full = jnp.bfloat16, jnp.float32
     deep = wide.shape[0] // 32
     wide, out = (a.reshape(4, 2, 2, 2, deep, a.shape[1]) for a in (wide, out))
@@ -1160,11 +1190,11 @@
 
     return pl.pallas_call(
         finish_body,
-        in_specs=[anywhere] * 7,
+        in_specs=[anywhere] * 10,
         out_specs=[inside] * 5 + [anywhere] * 2,
         out_shape=[jax.ShapeDtypeStruct((deep, c), full) for c in columns]
         + [jax.ShapeDtypeStruct((own_units, block[1]), full)] * 3
-        + [jax.ShapeDtypeStruct((2, rows.shape[0] // 2, rows.shape[1]), low) for rows in (layer, tokens)],
+        + [jax.ShapeDtypeStruct((2, tokens.shape[0] // 2, tokens.shape[1]), low)] * 2,
         scratch_shapes=[
             *pairs(4, 2, 2),
             *pairs(4, 2, 2),
@@ -1176,16 +1206,19 @@
             pltpu.VMEM((3, *block), low),
             pltpu.VMEM((2, *block), low),
             pltpu.VMEM(both.shape, low),
+            pltpu.VMEM(tokens.shape, low),
+            pltpu.VMEM(resid.shape, full),
+            *[pltpu.VMEM(tokens.shape, low)] * 3,
             pltpu.SemaphoreType.DMA((21,)),
             pltpu.SemaphoreType.DMA((21,)),
-            pltpu.SemaphoreType.DMA((7,)),
+            pltpu.SemaphoreType.DMA((11,)),
         ],
         compiler_params=pltpu.CompilerParams(
-            vmem_limit_bytes=56 * 1024 * 1024, collective_id=collective, has_side_effects=True
+            vmem_limit_bytes=60 * 1024 * 1024, collective_id=collective, has_side_effects=True
         ),
         cost_estimate=cost(0, 200 * 1024 * 1024),
         name="finish",
-    )(wide, out, mine, other, both, layer, tokens)
+    )(wide, out, mine, other, both, tokens, resid, *layer_parts)
 
 
 def swap(array, bits):
@@ -1343,7 +1376,6 @@
         ],
     )
     gate_got = swap(gate_sent, CORE)
-    down_sum = down_mine.astype(full) + down_got.astype(full)
     out_d = jnp.concatenate([out_d_end, out_d])
 
     grad_resid, grad_heads, grad_gain_two, grad_wout = branch_back(
@@ -1358,8 +1390,7 @@
         qwide,
     )
     out_got = [swap(after(out_b[1], gate_sent), ALONG_X), swap(join(out_b[2], out_d), ALONG_Y)]
-    gate_sum = gate_mine.astype(full) + gate_got.astype(full)
-    both = jnp.concatenate([down_sum, gate_sum], axis=1).astype(low)
+    both = both_sums(down_mine, down_got, gate_mine, gate_got)
     grad_heads = after(grad_heads, grad_wout, both)
     both = lax.psum_scatter(both, "gx", scatter_dimension=0, tiled=True)[0]
     query_lin, keyval_part = attend_back_fast(
@@ -1384,9 +1415,6 @@
         9,
         [whole_side(up_sent, CORE)],
     )
-    ffn_out = sum(after(b, query_lin).astype(full) for b in [out_b[0]] + out_got)
-    layer_rows = (resid + ffn_out).astype(low)
-
     packed = jnp.concatenate(
         [grad_bias.reshape(32, nb), grad_gain_one.reshape(32, ng), grad_gain_two.reshape(32, ng)], axis=1
     )
@@ -1398,8 +1426,9 @@
         up_mine,
         up_got,
         both,
-        layer_rows,
         grad_rows,
+        resid,
+        (out_b[0], *out_got),
         own_units,
         8,
     )

time: 810 us -> 806 us (level)
  other arithmetic: 50.2 us -> 30.6 us
  Pallas kernels: 613 us -> 624 us
    pallas_call x1 -> x2, Pallas kernels: 100 us -> 114 us  [the longest x1 106 us: finish(): pl.pallas_call(finish_body, in_specs=[anywhere] * 10, out_specs=[inside]...]
    unnamed x75 -> x73, local copies, waits for them, and re-layouts: 19.3 us -> 22.3 us
  transfers between devices with their start and end apart: 18 -> 18, of which waited for: 7 -> 7; matrix products, arithmetic and copies ran while one was open for 8% -> 7% of each run, Pallas kernels for 33% -> 33%
where the time goes in v7:
time: 806 us; the launch traced here: 801 us
  Pallas kernels  624 us (77%)
  waiting for transfers between devices  64.1 us (8%)
  local copies, waits for them, and re-layouts  45.6 us (6%)
  other arithmetic  30.6 us (4%)
  starting transfers between devices  15.5 us (2%)
  between operations  14.8 us (2%)
    pallas_call x8, Pallas kernels, call_beside(): pl.pallas_call(whole_body, grid=grid, in_specs=list(in_specs) + [anywhere...  332 us
    pallas_call x1, Pallas kernels, spread(): pl.pallas_call(spread_body, in_specs=[anywhere] * 5, out_specs=[anywhere]...  115 us
    pallas_call x1, Pallas kernels, finish(): pl.pallas_call(finish_body, in_specs=[anywhere] * 10, out_specs=[inside]...  106 us
    ppermute x11, waiting for transfers between devices, swap(): return lax.ppermute(array, 'gy', [(i, i ^ bits) for i in range(8)])  28.5 us
    pallas_call x1, Pallas kernels, attend_back_fast(): pl.pallas_call(attend_back_body, grid_spec=pltpu.PrefetchScalarGridSpec(n...  23.5 us
    unnamed x73, local copies, waits for them, and re-layouts  22.3 us
    pallas_call x1, Pallas kernels, branch_back(): pl.pallas_call(branch_back_body, grid=(steps,), in_specs=[moving, first[0...  19.3 us
    ppermute x3, waiting for transfers between devices, on_core(): lax.ppermute(attn_own, 'gx', [(i, (i + k) % 4) for i in range(4)])  18.6 us
  transfers between devices with their start and end apart: 18, of which 7 were waited for; matrix products, arithmetic and copies ran while one was open for 7% of the time, Pallas kernels for 33%

profile of v7, /device:TPU:9, one launch (start us, length us, event | category | flops | bytes accessed | tf_op | source)
XLA Modules:
  0.0 801.3 jit_solution(13689605114871027116)
XLA Ops:
  7.3 2.7 dynamic-slice_bitcast_fusion.3
  12.3 2.5 collective-permute-start.2
  14.7 2.2 collective-permute-start.1
  16.9 1.6 copy.34
  19.5 3.4 maximum_select_fusion.x_ref.refs_8_
  22.9 3.4 maximum_select_fusion.1.refs_4_.refs_1_.cot_ref
  26.4 11.0 %collective-permute-done.2.refs_2_ = bf16[48,3712]{1,0:T(8,128)(2,1)} collective-permute-done((bf16[48,3712]{1,0:T(8,128)(2,1)S(1)}, bf16[48,3712]{1,0:T(8,128)(2,1)}, u32[]{:S(2)}, u32[]{:S(2)}) %collective-permute-start.2) | collective-permute-done | bytes 356384 | tf_op jit(solution)/shard_map/ppermute | solution.py:1280
  37.4 7.6 collective-permute-done.1.refs_1_
  45.1 1.5 copy.35
  47.7 1.5 copy.36
  52.5 114.6 %spread.1 = (bf16[4,8,48,3712]{3,2,1,0:T(8,128)(2,1)}, bf16[640,1536]{1,0:T(8,128)(2,1)}, bf16[640,1536]{1,0:T(8,128)(2,1)}, bf16[640,1536]{1,0:T(8,128)(2,1)}) custom-call(bf16[48,3712]{1,0:T(8,128)(2,1)} %copy-done.18, bf16[48,3712]{1,0:T(8,128)(2,1)} %collective-permute-done.1.refs_1_, bf16[48,3712]{1,0:T(8,128)(2,1)} %collective-permute-done.2.refs_2_, ...), custom_call_target="tpu_custom_call" | custom-call | bytes 314572800 | tf_op jit(solution)/shard_map/spread/pallas_call | solution.py:884
  169.0 8.9 %project.1 = (bf16[640,1536]{1,0:T(8,128)(2,1)S(1)}, bf16[640,1536]{1,0:T(8,128)(2,1)S(1)}, bf16[640,512]{1,0:T(8,128)(2,1)S(1)}) custom-call(bf16[640,1536]{1,0:T(8,128)(2,1)} %maximum_select_fusion.x_ref.refs_8_, f32[1,1536]{1,0:T(1,128)S(1)} %reshape.181.gain_ref.refs_9_, bf16[1536,3712]{1,0:T(8,128)(2,1)} %bitcast.48, f32[1,2048]{1,0:T(1,128)S(1)} %reshape.182.b_ref, ...), custom_call_target="tpu_custom_call" | custom-call | flops 4026531840 | bytes 14155776 | tf_op jit(solution)/shard_map/project/pallas_call | solution.py:795
  177.9 1.3 copy-done.7
  179.2 1.3 copy-done.8
  180.5 1.5 collective-permute-start.6
  183.5 1.7 broadcast_in_dim.158
  186.1 9.0 %collective-permute-done.5 = bf16[640,512]{1,0:T(8,128)(2,1)S(1)} collective-permute-done((bf16[640,512]{1,0:T(8,128)(2,1)S(1)}, bf16[640,512]{1,0:T(8,128)(2,1)S(1)}, u32[]{:S(2)}, u32[]{:S(2)}) %collective-permute-start.5) | collective-permute-done | bytes 655392 | tf_op jit(solution)/shard_map/ppermute | solution.py:1225
  197.0 12.2 %collective-permute-done.7 = bf16[640,512]{1,0:T(8,128)(2,1)S(1)} collective-permute-done((bf16[640,512]{1,0:T(8,128)(2,1)S(1)}, bf16[640,512]{1,0:T(8,128)(2,1)S(1)}, u32[]{:S(2)}, u32[]{:S(2)}) %collective-permute-start.7) | collective-permute-done | bytes 655392 | tf_op jit(solution)/shard_map/ppermute | solution.py:1225
  210.1 3.5 collective-permute-start.8
  213.8 5.1 or_reduce_fusion
  219.3 4.3 select_convert_fusion.bias_ref
  224.8 1.5 copy-done.9
  226.4 12.0 %tree_attention.1 = (bf16[640,1536]{1,0:T(8,128)(2,1)S(1)}, f32[5,2,1,768]{3,2,1,0:T(1,128)S(1)}) custom-call(s32[5,10]{1,0:T(8,128)S(1)} %select_reduce_fusion.5.list_ref, s32[5]{0:T(128)S(1)} %convert_reduce_fusion.4.count_ref, bf16[640,1536]{1,0:T(8,128)(2,1)S(1)} %copy-done.9, bf16[2560,512]{1,0:T(8,128)(2,1)} %constant_dynamic-update-slice_fusion.kv_ref, ...), custom_call_target="tpu_custom_call" | custom-call | flops 10066329600 | bytes 6553600 | tf_op jit(solution)/shard_map/tree_attention/pallas_call | solution.py:647
  239.1 16.9 %all-gather.8.cloned.1.call-done.refs_4_ = bf16[1536,1152]{1,0:T(8,128)(2,1)} async-done(((bf16[384,1152]{1,0:T(8,128)(2,1)}), bf16[1536,1152]{1,0:T(8,128)(2,1)}) %all-gather.8.cloned.1.call-update) | async-done | bytes 3538960 | tf_op jit(solution)/shard_map/all_gather | solution.py:1301
  256.5 6.3 multiply_reduce_fusion
  262.9 1.9 multiply_convert_fusion.refs_0_.refs_8_.refs_9_.refs_4_
  265.4 51.6 %ffn_block.4 = (bf16[640,2304]{1,0:T(8,128)(2,1)}, bf16[640,2304]{1,0:T(8,128)(2,1)}, bf16[640,2304]{1,0:T(8,128)(2,1)}, bf16[640,1536]{1,0:T(8,128)(2,1)}, bf16...) custom-call(bf16[640,1536]{1,0:T(8,128)(2,1)} %multiply_convert_fusion.refs_0_.refs_8_.refs_9_.refs_4_, ...), custom_call_target="tpu_custom_call" | custom-call | flops 27179089920 | bytes 35979264 | tf_op jit(solution)/shard_map/ffn_block/pallas_call | solution.py:439
  317.0 39.2 %ffn_block.5 = (bf16[640,2304]{1,0:T(8,128)(2,1)}, bf16[640,2304]{1,0:T(8,128)(2,1)}, bf16[640,2304]{1,0:T(8,128)(2,1)}, bf16[640,1536]{1,0:T(8,128)(2,1)}, bf16...) custom-call(bf16[640,1536]{1,0:T(8,128)(2,1)} %get-tuple-element.111.refs_0_.refs_8_.refs_5_, ...), custom_call_target="tpu_custom_call" | custom-call | flops 27179089920 | bytes 35979264 | tf_op jit(solution)/shard_map/ffn_block/pallas_call | solution.py:439
  356.2 40.4 %ffn_block.6 = (bf16[640,2304]{1,0:T(8,128)(2,1)}, bf16[640,2304]{1,0:T(8,128)(2,1)}, bf16[640,2304]{1,0:T(8,128)(2,1)}, bf16[640,1536]{1,0:T(8,128)(2,1)}, bf16...) custom-call(bf16[640,1536]{1,0:T(8,128)(2,1)} %get-tuple-element.114.refs_0_.refs_7_, ...), custom_call_target="tpu_custom_call" | custom-call | flops 27179089920 | bytes 35979264 | tf_op jit(solution)/shard_map/ffn_block/pallas_call | solution.py:439
  396.6 39.1 %ffn_block.7 = (bf16[640,2304]{1,0:T(8,128)(2,1)}, bf16[640,2304]{1,0:T(8,128)(2,1)}, bf16[640,2304]{1,0:T(8,128)(2,1)}, bf16[640,1536]{1,0:T(8,128)(2,1)}, bf16...) custom-call(bf16[640,1536]{1,0:T(8,128)(2,1)} %get-tuple-element.121.refs_9_.refs_0_.refs_6_, ...), custom_call_target="tpu_custom_call" | custom-call | flops 27179089920 | bytes 35979264 | tf_op jit(solution)/shard_map/ffn_block/pallas_call | solution.py:439
  436.8 2.9 add_convert_fusion.1.refs_11_
  439.7 34.3 %ffn_wgrad.3 = (bf16[4,1152,384]{2,1,0:T(8,128)(2,1)}, bf16[4,1152,384]{2,1,0:T(8,128)(2,1)}, bf16[128,1536]{1,0:T(8,128)(2,1)}, bf16[128,1536]{1,0:T(8,128)(2,1...) custom-call(bf16[640,2304]{1,0:T(8,128)(2,1)} %get-tuple-element.118.refs_0_, ...), custom_call_target="tpu_custom_call" | custom-call | flops 18119393280 | bytes 19660800 | tf_op jit(solution)/shard_map/ffn_wgrad/pallas_call | solution.py:439
  474.0 2.3 add_convert_fusion.2.refs_10_
  476.4 41.3 %ffn_wgrad.4 = (bf16[4,1152,384]{2,1,0:T(8,128)(2,1)}, bf16[4,1152,384]{2,1,0:T(8,128)(2,1)}, bf16[4,1152,384]{2,1,0:T(8,128)(2,1)}, bf16[448,1536]{1,0:T(8,128)(2,1)}, bf16[256,1536]{1,0:T(8,128)(2,1)}) custom-call(bf16[640,2304]{1,0:T(8,128)(2,1)} %get-tuple-element.130.refs_0_, bf16[640,2304]{1,0:T(8,128)(2,1)} %get-tuple-element.131.refs_1_, ...), custom_call_target="tpu_custom_call" | custom-call | flops 18119393280 | bytes 19660800 | tf_op jit(solution)/shard_map/ffn_wgrad/pallas_call | solution.py:439
  517.7 1.4 collective-permute-start.11
  519.1 6.1 collective-permute-done.11.second_other
  525.2 1.9 copy-done.12
  527.0 7.7 both_back.1
  536.6 2.1 add_convert_fusion
  539.8 19.3 %branch_back.1 = (f32[640,1536]{1,0:T(8,128)}, bf16[640,1536]{1,0:T(8,128)(2,1)}, f32[1,1536]{1,0:T(1,128)}, bf16[1536,1536]{1,0:T(8,128)(2,1)}) custom-call(bf16[640,1536]{1,0:T(8,128)(2,1)} %get-tuple-element.110.own_ref, bf16[512,1536]{1,0:T(8,128)(2,1)} %get-tuple-element.117.xa_ref, bf16[128,1536]{1,0:T(8,128)(2,1)} %get-tuple-element.128.xb_ref, ...), custom_call_target="tpu_custom_call" | custom-call | flops 6039797760 | bytes 29097984 | tf_op jit(solution)/shard_map/branch_back/pallas_call | solution.py:943
  559.9 23.5 %tree_attention_back.1 = (bf16[640,1536]{1,0:T(8,128)(2,1)}, bf16[2560,512]{1,0:T(8,128)(2,1)}) custom-call(s32[5,10]{1,0:T(8,128)} %copy-done.5, s32[5]{0:T(128)} %copy-done.6, bf16[640,1536]{1,0:T(8,128)(2,1)} %copy-done.8, bf16[2560,512]{1,0:T(8,128)(2,1)} %constant_dynamic-update-slice_fusion.kv_ref, bf16[2560,640]{1,0:T(8,128)(2,1)} %select_convert_fusion.bias_ref, ...), custom_call_target="tpu_custom_call" | custom-call | flops 25165824000 | bytes 13107200 | tf_op jit(solution)/shard_map/tree_attention_back/pallas_call | solution.py:738
  583.4 58.9 %ffn_wgrad.5 = (bf16[4,1152,384]{2,1,0:T(8,128)(2,1)}, bf16[4,1152,384]{2,1,0:T(8,128)(2,1)}, bf16[640,512]{1,0:T(8,128)(2,1)}, bf16[640,512]{1,0:T(8,128)(2,1)}, bf16[640,512]{1,0:T(8,128)(2,1)}) custom-call(bf16[640,2304]{1,0:T(8,128)(2,1)} %get-tuple-element.146.refs_0_, bf16[640,2304]{1,0:T(8,128)(2,1)} %get-tuple-element.147.refs_1_, ...), custom_call_target="tpu_custom_call" | custom-call | flops 18119393280 | bytes 19660800 | tf_op jit(solution)/shard_map/ffn_wgrad/pallas_call | solution.py:439
  642.2 2.0 constant_dynamic-slice_fusion.refs_1_
  644.2 27.1 %project_back.1 = (bf16[640,1536]{1,0:T(8,128)(2,1)}, f32[1,2048]{1,0:T(1,128)}, f32[1,1536]{1,0:T(1,128)}, bf16[1536,2176]{1,0:T(8,128)(2,1)}, bf16[4,1152,384]{2,1,0:T(8,128)(2,1)}) custom-call(bf16[640,1536]{1,0:T(8,128)(2,1)} %get-tuple-element.144.refs_0_, bf16[640,512]{1,0:T(8,128)(2,1)} %constant_dynamic-slice_fusion.refs_1_, ...), custom_call_target="tpu_custom_call" | custom-call | flops 8053063680 | bytes 32243712 | tf_op jit(solution)/shard_map/project_back/pallas_call | solution.py:439
  674.4 106.3 %finish.1 = (f32[48,2176]{1,0:T(8,128)}, f32[48,1536]{1,0:T(8,128)}, f32[1120,384]{1,0:T(8,128)}, f32[1120,384]{1,0:T(8,128)}, f32[1120,384]{1,0:T(8,128)}, /*in...) custom-call(bf16[4,2,2,2,48,2176]{5,4,3,2,1,0:T(8,128)(2,1)} %bitcast.54, ...), custom_call_target="tpu_custom_call" | custom-call | bytes 209715200 | tf_op jit(solution)/shard_map/finish/pallas_call | solution.py:1191
  781.5 1.8 slice.55
  784.5 3.1 copy.51
  787.6 1.3 copy.52
  (159 shorter events, 33.6 us)
Async XLA Ops:
  7.2 174.8 %all-gather.4.cloned.1.call-start = ((), (), s32[]{:S(2)}) async-start(), calls=%async_computation.1 | async-start | bytes 4423680 | tf_op jit(solution)/shard_map/all_gather | solution.py:1299
  7.2 3.5 copy-start.13
  10.0 1.9 copy-start.28
  10.0 1.9 copy-start.29
  10.0 1.9 copy-start.30
  10.0 2.2 copy-start.23
  10.0 2.2 copy-start.26
  10.0 9.5 %collective-permute-start = (bf16[320,1536]{1,0:T(8,128)(2,1)}, bf16[320,1536]{1,0:T(8,128)(2,1)}, u32[]{:S(2)}, u32[]{:S(2)}) collective-permute-start(bf16[320,1536]{1,0:T(8,128)(2,1)} %get-tuple-element.189), channel_id=1, source_target_pairs={{0,1},{1,0},{2,3},{3,2},{4,5},{5,4},{6,7},{7,6},{8,9},{9,8},{10,11... | collective-permute-start | bytes 2949128 | tf_op jit(solution)/shard_map/ppermute | solution.py:1225
  11.8 11.1 %collective-permute-start.4 = (bf16[320,1536]{1,0:T(8,128)(2,1)}, bf16[320,1536]{1,0:T(8,128)(2,1)}, u32[]{:S(2)}, u32[]{:S(2)}) collective-permute-start(bf16[320,1536]{1,0:T(8,128)(2,1)} %get-tuple-element.187), channel_id=1, source_target_pairs={{0,1},{1,0},{2,3},{3,2},{4,5},{5,4},{6,7},{7,6},{8,9},{9,8},{10,11... | collective-permute-start | bytes 2949128 | tf_op jit(solution)/shard_map/ppermute | solution.py:1225
  12.2 10.7 %copy-start.18 = (bf16[48,3712]{1,0:T(8,128)(2,1)}, bf16[48,3712]{1,0:T(8,128)(2,1)S(1)}, u32[]{:S(2)}) copy-start(bf16[48,3712]{1,0:T(8,128)(2,1)S(1)} %fusion.6.refs_0_) | copy-start | bytes 1069060
  12.2 14.2 %collective-permute-start.3 = (bf16[48,3712]{1,0:T(8,128)(2,1)S(1)}, bf16[48,3712]{1,0:T(8,128)(2,1)}, u32[]{:S(2)}, u32[]{:S(2)}) collective-permute-start(bf16[48,3712]{1,0:T(8,128)(2,1)S(1)} %fusion.6.refs_0_), channel_id=1, source_target_pairs={{0,24},{8,0},{16,8},{24,16},{1,25},{9,1},{17,9},{25,17},{2,26},{10... | collective-permute-start | bytes 1069064 | tf_op jit(solution)/shard_map/ppermute | solution.py:1280
  12.3 25.1 %collective-permute-start.2 = (bf16[48,3712]{1,0:T(8,128)(2,1)S(1)}, bf16[48,3712]{1,0:T(8,128)(2,1)}, u32[]{:S(2)}, u32[]{:S(2)}) collective-permute-start(bf16[48,3712]{1,0:T(8,128)(2,1)S(1)} %fusion.6.refs_0_), channel_id=1, source_target_pairs={{0,16},{8,24},{16,0},{24,8},{1,17},{9,25},{17,1},{25,9},{2,18},{10... | collective-permute-start | bytes 1069064 | tf_op jit(solution)/shard_map/ppermute | solution.py:1280
  14.7 30.2 %collective-permute-start.1 = (bf16[48,3712]{1,0:T(8,128)(2,1)S(1)}, bf16[48,3712]{1,0:T(8,128)(2,1)}, u32[]{:S(2)}, u32[]{:S(2)}) collective-permute-start(bf16[48,3712]{1,0:T(8,128)(2,1)S(1)} %fusion.6.refs_0_), channel_id=1, source_target_pairs={{0,8},{8,16},{16,24},{24,0},{1,9},{9,17},{17,25},{25,1},{2,10},{10... | collective-permute-start | bytes 1069064 | tf_op jit(solution)/shard_map/ppermute | solution.py:1280
  22.9 22.1 %copy-start.20 = (bf16[384,1120]{0,1:T(8,128)(2,1)S(1)}, bf16[384,1120]{0,1:T(8,128)(2,1)}, u32[]{:S(2)}) copy-start(bf16[384,1120]{0,1:T(8,128)(2,1)} %param.22) | copy-start | bytes 2580484
  45.0 2.6 copy-start.21
  45.0 165.0 %all-gather.6.cloned.1.call-start = ((), (), s32[]{:S(2)}) async-start(), calls=%async_computation.2 | async-start | bytes 4423680 | tf_op jit(solution)/shard_map/all_gather | solution.py:1299
  47.6 2.6 copy-start.27
  47.6 2.6 copy-start.31
  47.6 208.3 %all-gather.8.cloned.1.call-start = ((), (), s32[]{:S(2)}) async-start(), calls=%async_computation.3 | async-start | bytes 4423680 | tf_op jit(solution)/shard_map/all_gather | solution.py:1301
  52.5 116.4 %copy-start.2 = (f32[640,128]{1,0:T(8,128)}, f32[640,128]{1,0:T(8,128)S(1)}, u32[]{:S(2)}) copy-start(f32[640,128]{1,0:T(8,128)S(1)} %get-tuple-element.199.cos_ref.refs_5_) | copy-start | bytes 983044
  52.5 116.4 %copy-start.3 = (f32[640,128]{1,0:T(8,128)}, f32[640,128]{1,0:T(8,128)S(1)}, u32[]{:S(2)}) copy-start(f32[640,128]{1,0:T(8,128)S(1)} %get-tuple-element.200.sin_ref.refs_6_) | copy-start | bytes 983044
  168.9 87.6 %copy-start.24 = (f32[32,48]{1,0:T(8,128)}, f32[32,48]{1,0:T(8,128)S(1)}, u32[]{:S(2)}) copy-start(f32[32,48]{1,0:T(8,128)S(1)} %get-tuple-element.190) | copy-start | bytes 18436
  169.0 8.9 %copy-start.4 = (f32[1,1536]{1,0:T(1,128)}, f32[1,1536]{1,0:T(1,128)S(1)}, u32[]{:S(2)}) copy-start(f32[1,1536]{1,0:T(1,128)S(1)} %reshape.181.gain_ref.refs_9_) | copy-start | bytes 18436
  177.9 1.3 copy-start.7
  179.2 1.3 copy-start.8
  180.5 14.5 %collective-permute-start.5 = (bf16[640,512]{1,0:T(8,128)(2,1)S(1)}, bf16[640,512]{1,0:T(8,128)(2,1)S(1)}, u32[]{:S(2)}, u32[]{:S(2)}) collective-permute-start(bf16[640,512]{1,0:T(8,128)(2,1)S(1)} %get-tuple-element.98), channel_id=1, source_target_pairs={{0,2},{1,3},{2,0},{3,1},{4,6},{5,7},{6,4},{7,5},{8,10},{9,11},{10,... | collective-permute-start | bytes 1966088 | tf_op jit(solution)/shard_map/ppermute | solution.py:1225
  180.5 15.5 %collective-permute-start.6 = (bf16[640,512]{1,0:T(8,128)(2,1)S(1)}, bf16[640,512]{1,0:T(8,128)(2,1)S(1)}, u32[]{:S(2)}, u32[]{:S(2)}) collective-permute-start(bf16[640,512]{1,0:T(8,128)(2,1)S(1)} %get-tuple-element.98), channel_id=1, source_target_pairs={{0,4},{1,5},{2,6},{3,7},{4,0},{5,1},{6,2},{7,3},{8,12},{9,13},{10,... | collective-permute-start | bytes 1966088 | tf_op jit(solution)/shard_map/ppermute | solution.py:1225
  182.0 492.3 %reduce-scatter.2.cloned.1.call-start = ((), (), s32[]{:S(2)}) async-start(), calls=%async_computation.4 | async-start | bytes 8847360 | tf_op jit(solution)/shard_map/reduce_scatter | solution.py:1395
  182.3 26.9 %collective-permute-start.7 = (bf16[640,512]{1,0:T(8,128)(2,1)S(1)}, bf16[640,512]{1,0:T(8,128)(2,1)S(1)}, u32[]{:S(2)}, u32[]{:S(2)}) collective-permute-start(bf16[640,512]{1,0:T(8,128)(2,1)S(1)} %get-tuple-element.98), channel_id=1, source_target_pairs={{0,6},{1,7},{2,4},{3,5},{4,2},{5,3},{6,0},{7,1},{8,14},{9,15},{10,... | collective-permute-start | bytes 1966088 | tf_op jit(solution)/shard_map/ppermute | solution.py:1225
  210.1 13.5 %collective-permute-start.8 = (bf16[1536,1152]{1,0:T(8,128)(2,1)}, bf16[1536,1152]{1,0:T(8,128)(2,1)}, u32[]{:S(2)}, u32[]{:S(2)}) collective-permute-start(bf16[1536,1152]{1,0:T(8,128)(2,1)} %all-gather.4.cloned.1.call-done.refs_2_), channel_id=1, source_target_pairs={{0,1},{1,0},{2,3},{3,2},{4,5},{5,4},{6,7},{7,6},{8,9},{9,8},{10,11... | collective-permute-start | bytes 10616840 | tf_op jit(solution)/shard_map/ppermute | solution.py:1225
  213.6 11.3 %collective-permute-start.9 = (bf16[1536,1152]{1,0:T(8,128)(2,1)}, bf16[1536,1152]{1,0:T(8,128)(2,1)}, u32[]{:S(2)}, u32[]{:S(2)}) collective-permute-start(bf16[1536,1152]{1,0:T(8,128)(2,1)} %all-gather.6.cloned.1.call-done.refs_3_), channel_id=1, source_target_pairs={{0,1},{1,0},{2,3},{3,2},{4,5},{5,4},{6,7},{7,6},{8,9},{9,8},{10,11... | collective-permute-start | bytes 10616840 | tf_op jit(solution)/shard_map/ppermute | solution.py:1225
  219.1 5.7 copy-start.6
  219.3 5.6 copy-start.5
  224.8 1.5 copy-start.9
  239.1 23.8 %copy-start.1 = (bf16[640,1536]{1,0:T(8,128)(2,1)}, bf16[640,1536]{1,0:T(8,128)(2,1)S(1)}, u32[]{:S(2)}) copy-start(bf16[640,1536]{1,0:T(8,128)(2,1)S(1)} %get-tuple-element.107.heads_ref.o_ref) | copy-start | bytes 5898244
  255.9 9.4 %collective-permute-start.10 = (bf16[1536,1152]{1,0:T(8,128)(2,1)}, bf16[1536,1152]{1,0:T(8,128)(2,1)}, u32[]{:S(2)}, u32[]{:S(2)}) collective-permute-start(bf16[1536,1152]{1,0:T(8,128)(2,1)} %all-gather.8.cloned.1.call-done.refs_4_), channel_id=1, source_target_pairs={{0,1},{1,0},{2,3},{3,2},{4,5},{5,4},{6,7},{7,6},{8,9},{9,8},{10,11... | collective-permute-start | bytes 10616840 | tf_op jit(solution)/shard_map/ppermute | solution.py:1225
  262.9 2.5 copy-start.11
  476.4 50.7 %copy-start = (bf16[4,1152,384]{2,1,0:T(8,128)(2,1)S(1)}, bf16[4,1152,384]{2,1,0:T(8,128)(2,1)}, u32[]{:S(2)}) copy-start(bf16[4,1152,384]{2,1,0:T(8,128)(2,1)} %get-tuple-element.139.first_mine) | copy-start | bytes 10616836
  517.7 7.5 collective-permute-start.11
  525.2 1.9 copy-start.12
  534.7 1.9 copy-start.19
  536.1 138.3 %collective-permute-start.12 = (bf16[640,1536]{1,0:T(8,128)(2,1)}, bf16[640,1536]{1,0:T(8,128)(2,1)}, u32[]{:S(2)}, u32[]{:S(2)}) collective-permute-start(bf16[640,1536]{1,0:T(8,128)(2,1)} %get-tuple-element.165), channel_id=1, source_target_pairs={{0,2},{1,3},{2,0},{3,1},{4,6},{5,7},{6,4},{7,5},{8,10},{9,11},{10,... | collective-permute-start | bytes 5898248 | tf_op jit(solution)/shard_map/ppermute | solution.py:1225
  538.7 135.7 %collective-permute-start.13 = (bf16[640,1536]{1,0:T(8,128)(2,1)S(1)}, bf16[640,1536]{1,0:T(8,128)(2,1)}, u32[]{:S(2)}, u32[]{:S(2)}) collective-permute-start(bf16[640,1536]{1,0:T(8,128)(2,1)S(1)} %add_convert_fusion), channel_id=1, source_target_pairs={{0,4},{1,5},{2,6},{3,7},{4,0},{5,1},{6,2},{7,3},{8,12},{9,13},{10,... | collective-permute-start | bytes 5898248 | tf_op jit(solution)/shard_map/ppermute | solution.py:1225
  784.5 3.1 copy-start.14
  787.6 1.3 copy-start.22
  787.6 2.3 copy-start.17
  788.9 2.2 copy-start.16
  791.1 2.1 copy-start.15
  (2 other events, 1.3 us)
Sparse Core Ops, SparseCore 0:
  45.1 69.2 all-gather.3
  116.5 68.5 all-gather.5
  187.3 68.5 all-gather.7
  534.8 125.6 reduce-scatter.1

commit v8 on v7

--- a/solution.py
+++ b/solution.py
@@ -1390,7 +1390,7 @@
         qwide,
     )
     out_got = [swap(after(out_b[1], gate_sent), ALONG_X), swap(join(out_b[2], out_d), ALONG_Y)]
-    both = both_sums(down_mine, down_got, gate_mine, gate_got)
+    both = both_sums(down_mine, down_got, after(gate_mine, grad_heads), gate_got)
     grad_heads = after(grad_heads, grad_wout, both)
     both = lax.psum_scatter(both, "gx", scatter_dimension=0, tiled=True)[0]
     query_lin, keyval_part = attend_back_fast(

time: 806 us -> 798 us (0.990)
    unnamed x73 -> x75, local copies, waits for them, and re-layouts: 22.3 us -> 22 us
  transfers between devices with their start and end apart: 18 -> 18, of which waited for: 7 -> 7; matrix products, arithmetic and copies ran while one was open for 7% -> 6% of each run, Pallas kernels for 33% -> 33%
where the time goes in v8:
time: 798 us; the launch traced here: 791 us
  Pallas kernels  616 us (77%)
  waiting for transfers between devices  62.7 us (8%)
  local copies, waits for them, and re-layouts  45.3 us (6%)
  other arithmetic  30 us (4%)
  starting transfers between devices  15.9 us (2%)
  between operations  14.8 us (2%)
    pallas_call x8, Pallas kernels, call_beside(): pl.pallas_call(whole_body, grid=grid, in_specs=list(in_specs) + [anywhere...  330 us
    pallas_call x1, Pallas kernels, spread(): pl.pallas_call(spread_body, in_specs=[anywhere] * 5, out_specs=[anywhere]...  115 us
    pallas_call x1, Pallas kernels, finish(): pl.pallas_call(finish_body, in_specs=[anywhere] * 10, out_specs=[inside]...  99.7 us
    pallas_call x1, Pallas kernels, attend_back_fast(): pl.pallas_call(attend_back_body, grid_spec=pltpu.PrefetchScalarGridSpec(n...  24.4 us
    ppermute x11, waiting for transfers between devices, swap(): return lax.ppermute(array, 'gy', [(i, i ^ bits) for i in range(8)])  22.5 us
    unnamed x75, local copies, waits for them, and re-layouts  22 us
    pallas_call x1, Pallas kernels, branch_back(): pl.pallas_call(branch_back_body, grid=(steps,), in_specs=[moving, first[0...  18.8 us
    ppermute x3, waiting for transfers between devices, on_core(): lax.ppermute(attn_own, 'gx', [(i, (i + k) % 4) for i in range(4)])  18.6 us
  transfers between devices with their start and end apart: 18, of which 7 were waited for; matrix products, arithmetic and copies ran while one was open for 6% of the time, Pallas kernels for 33%

profile of v8, /device:TPU:9, one launch (start us, length us, event | category | flops | bytes accessed | tf_op | source)
XLA Modules:
  0.0 791.0 jit_solution(1343173553429834773)
XLA Ops:
  7.3 2.7 dynamic-slice_bitcast_fusion.3
  12.3 2.5 collective-permute-start.2
  14.7 2.2 collective-permute-start.1
  16.9 1.6 copy.34
  19.5 3.4 maximum_select_fusion.x_ref.refs_8_
  22.9 3.4 maximum_select_fusion.1.refs_4_.refs_1_.cot_ref
  26.4 11.0 %collective-permute-done.2.refs_2_ = bf16[48,3712]{1,0:T(8,128)(2,1)} collective-permute-done((bf16[48,3712]{1,0:T(8,128)(2,1)S(1)}, bf16[48,3712]{1,0:T(8,128)(2,1)}, u32[]{:S(2)}, u32[]{:S(2)}) %collective-permute-start.2) | collective-permute-done | bytes 356384 | tf_op jit(solution)/shard_map/ppermute | solution.py:1280
  37.4 7.6 collective-permute-done.1.refs_1_
  45.1 1.5 copy.35
  47.7 1.5 copy.36
  52.5 114.6 %spread.1 = (bf16[4,8,48,3712]{3,2,1,0:T(8,128)(2,1)}, bf16[640,1536]{1,0:T(8,128)(2,1)}, bf16[640,1536]{1,0:T(8,128)(2,1)}, bf16[640,1536]{1,0:T(8,128)(2,1)}) custom-call(bf16[48,3712]{1,0:T(8,128)(2,1)} %copy-done.18, bf16[48,3712]{1,0:T(8,128)(2,1)} %collective-permute-done.1.refs_1_, bf16[48,3712]{1,0:T(8,128)(2,1)} %collective-permute-done.2.refs_2_, ...), custom_call_target="tpu_custom_call" | custom-call | bytes 314572800 | tf_op jit(solution)/shard_map/spread/pallas_call | solution.py:884
  169.0 8.9 %project.1 = (bf16[640,1536]{1,0:T(8,128)(2,1)S(1)}, bf16[640,1536]{1,0:T(8,128)(2,1)S(1)}, bf16[640,512]{1,0:T(8,128)(2,1)S(1)}) custom-call(bf16[640,1536]{1,0:T(8,128)(2,1)} %maximum_select_fusion.x_ref.refs_8_, f32[1,1536]{1,0:T(1,128)S(1)} %reshape.181.gain_ref.refs_9_, bf16[1536,3712]{1,0:T(8,128)(2,1)} %bitcast.48, f32[1,2048]{1,0:T(1,128)S(1)} %reshape.182.b_ref, ...), custom_call_target="tpu_custom_call" | custom-call | flops 4026531840 | bytes 14155776 | tf_op jit(solution)/shard_map/project/pallas_call | solution.py:795
  177.9 1.3 copy-done.7
  179.2 1.3 copy-done.8
  180.6 1.5 collective-permute-start.6
  183.5 1.7 broadcast_in_dim.158
  186.1 9.0 %collective-permute-done.5 = bf16[640,512]{1,0:T(8,128)(2,1)S(1)} collective-permute-done((bf16[640,512]{1,0:T(8,128)(2,1)S(1)}, bf16[640,512]{1,0:T(8,128)(2,1)S(1)}, u32[]{:S(2)}, u32[]{:S(2)}) %collective-permute-start.5) | collective-permute-done | bytes 655392 | tf_op jit(solution)/shard_map/ppermute | solution.py:1225
  197.0 12.2 %collective-permute-done.7 = bf16[640,512]{1,0:T(8,128)(2,1)S(1)} collective-permute-done((bf16[640,512]{1,0:T(8,128)(2,1)S(1)}, bf16[640,512]{1,0:T(8,128)(2,1)S(1)}, u32[]{:S(2)}, u32[]{:S(2)}) %collective-permute-start.7) | collective-permute-done | bytes 655392 | tf_op jit(solution)/shard_map/ppermute | solution.py:1225
  210.1 3.5 collective-permute-start.8
  213.8 5.1 or_reduce_fusion
  219.3 4.3 select_convert_fusion.bias_ref
  223.6 1.3 collective-permute-done.9.refs_6_
  224.8 1.5 copy-done.9
  226.4 12.0 %tree_attention.1 = (bf16[640,1536]{1,0:T(8,128)(2,1)S(1)}, f32[5,2,1,768]{3,2,1,0:T(1,128)S(1)}) custom-call(s32[5,10]{1,0:T(8,128)S(1)} %select_reduce_fusion.5.list_ref, s32[5]{0:T(128)S(1)} %convert_reduce_fusion.4.count_ref, bf16[640,1536]{1,0:T(8,128)(2,1)S(1)} %copy-done.9, bf16[2560,512]{1,0:T(8,128)(2,1)} %constant_dynamic-update-slice_fusion.kv_ref, ...), custom_call_target="tpu_custom_call" | custom-call | flops 10066329600 | bytes 6553600 | tf_op jit(solution)/shard_map/tree_attention/pallas_call | solution.py:647
  239.1 16.9 %all-gather.8.cloned.1.call-done.refs_4_ = bf16[1536,1152]{1,0:T(8,128)(2,1)} async-done(((bf16[384,1152]{1,0:T(8,128)(2,1)}), bf16[1536,1152]{1,0:T(8,128)(2,1)}) %all-gather.8.cloned.1.call-update) | async-done | bytes 3538960 | tf_op jit(solution)/shard_map/all_gather | solution.py:1301
  256.5 6.3 multiply_reduce_fusion
  262.9 1.9 multiply_convert_fusion.refs_0_.refs_8_.refs_9_.refs_4_
  265.4 51.2 %ffn_block.4 = (bf16[640,2304]{1,0:T(8,128)(2,1)}, bf16[640,2304]{1,0:T(8,128)(2,1)}, bf16[640,2304]{1,0:T(8,128)(2,1)}, bf16[640,1536]{1,0:T(8,128)(2,1)}, bf16...) custom-call(bf16[640,1536]{1,0:T(8,128)(2,1)} %multiply_convert_fusion.refs_0_.refs_8_.refs_9_.refs_4_, ...), custom_call_target="tpu_custom_call" | custom-call | flops 27179089920 | bytes 35979264 | tf_op jit(solution)/shard_map/ffn_block/pallas_call | solution.py:439
  316.6 38.7 %ffn_block.5 = (bf16[640,2304]{1,0:T(8,128)(2,1)}, bf16[640,2304]{1,0:T(8,128)(2,1)}, bf16[640,2304]{1,0:T(8,128)(2,1)}, bf16[640,1536]{1,0:T(8,128)(2,1)}, bf16...) custom-call(bf16[640,1536]{1,0:T(8,128)(2,1)} %get-tuple-element.112.refs_0_.refs_8_.refs_5_, ...), custom_call_target="tpu_custom_call" | custom-call | flops 27179089920 | bytes 35979264 | tf_op jit(solution)/shard_map/ffn_block/pallas_call | solution.py:439
  355.3 40.4 %ffn_block.6 = (bf16[640,2304]{1,0:T(8,128)(2,1)}, bf16[640,2304]{1,0:T(8,128)(2,1)}, bf16[640,2304]{1,0:T(8,128)(2,1)}, bf16[640,1536]{1,0:T(8,128)(2,1)}, bf16...) custom-call(bf16[640,1536]{1,0:T(8,128)(2,1)} %get-tuple-element.115.refs_0_.refs_7_, ...), custom_call_target="tpu_custom_call" | custom-call | flops 27179089920 | bytes 35979264 | tf_op jit(solution)/shard_map/ffn_block/pallas_call | solution.py:439
  395.7 39.1 %ffn_block.7 = (bf16[640,2304]{1,0:T(8,128)(2,1)}, bf16[640,2304]{1,0:T(8,128)(2,1)}, bf16[640,2304]{1,0:T(8,128)(2,1)}, bf16[640,1536]{1,0:T(8,128)(2,1)}, bf16...) custom-call(bf16[640,1536]{1,0:T(8,128)(2,1)} %get-tuple-element.122.refs_9_.refs_0_.refs_6_, ...), custom_call_target="tpu_custom_call" | custom-call | flops 27179089920 | bytes 35979264 | tf_op jit(solution)/shard_map/ffn_block/pallas_call | solution.py:439
  435.8 2.9 add_convert_fusion.1.refs_11_
  438.7 34.3 %ffn_wgrad.3 = (bf16[4,1152,384]{2,1,0:T(8,128)(2,1)}, bf16[4,1152,384]{2,1,0:T(8,128)(2,1)}, bf16[128,1536]{1,0:T(8,128)(2,1)}, bf16[128,1536]{1,0:T(8,128)(2,1...) custom-call(bf16[640,2304]{1,0:T(8,128)(2,1)} %get-tuple-element.119.refs_0_, ...), custom_call_target="tpu_custom_call" | custom-call | flops 18119393280 | bytes 19660800 | tf_op jit(solution)/shard_map/ffn_wgrad/pallas_call | solution.py:439
  473.1 2.3 add_convert_fusion.2.refs_10_
  475.4 40.6 %ffn_wgrad.4 = (bf16[4,1152,384]{2,1,0:T(8,128)(2,1)}, bf16[4,1152,384]{2,1,0:T(8,128)(2,1)}, bf16[4,1152,384]{2,1,0:T(8,128)(2,1)}, bf16[448,1536]{1,0:T(8,128)(2,1)}, bf16[256,1536]{1,0:T(8,128)(2,1)}) custom-call(bf16[640,2304]{1,0:T(8,128)(2,1)} %get-tuple-element.131.refs_0_, bf16[640,2304]{1,0:T(8,128)(2,1)} %get-tuple-element.132.refs_1_, ...), custom_call_target="tpu_custom_call" | custom-call | flops 18119393280 | bytes 19660800 | tf_op jit(solution)/shard_map/ffn_wgrad/pallas_call | solution.py:439
  516.0 1.7 collective-permute-start.11
  518.4 18.8 %branch_back.1 = (f32[640,1536]{1,0:T(8,128)}, bf16[640,1536]{1,0:T(8,128)(2,1)}, f32[1,1536]{1,0:T(1,128)}, bf16[1536,1536]{1,0:T(8,128)(2,1)}) custom-call(bf16[640,1536]{1,0:T(8,128)(2,1)} %get-tuple-element.111.own_ref, bf16[512,1536]{1,0:T(8,128)(2,1)} %get-tuple-element.118.xa_ref, bf16[128,1536]{1,0:T(8,128)(2,1)} %get-tuple-element.129.xb_ref, ...), custom_call_target="tpu_custom_call" | custom-call | flops 6039797760 | bytes 29097984 | tf_op jit(solution)/shard_map/branch_back/pallas_call | solution.py:943
  537.2 1.8 copy-done.12
  539.0 7.6 both_back.1
  547.9 2.2 add_convert_fusion
  551.0 24.4 %tree_attention_back.1 = (bf16[640,1536]{1,0:T(8,128)(2,1)}, bf16[2560,512]{1,0:T(8,128)(2,1)}) custom-call(s32[5,10]{1,0:T(8,128)} %copy-done.5, s32[5]{0:T(128)} %copy-done.6, bf16[640,1536]{1,0:T(8,128)(2,1)} %copy-done.8, bf16[2560,512]{1,0:T(8,128)(2,1)} %constant_dynamic-update-slice_fusion.kv_ref, bf16[2560,640]{1,0:T(8,128)(2,1)} %select_convert_fusion.bias_ref, ...), custom_call_target="tpu_custom_call" | custom-call | flops 25165824000 | bytes 13107200 | tf_op jit(solution)/shard_map/tree_attention_back/pallas_call | solution.py:738
  575.4 59.4 %ffn_wgrad.5 = (bf16[4,1152,384]{2,1,0:T(8,128)(2,1)}, bf16[4,1152,384]{2,1,0:T(8,128)(2,1)}, bf16[640,512]{1,0:T(8,128)(2,1)}, bf16[640,512]{1,0:T(8,128)(2,1)}, bf16[640,512]{1,0:T(8,128)(2,1)}) custom-call(bf16[640,2304]{1,0:T(8,128)(2,1)} %get-tuple-element.148.refs_0_, bf16[640,2304]{1,0:T(8,128)(2,1)} %get-tuple-element.149.refs_1_, ...), custom_call_target="tpu_custom_call" | custom-call | flops 18119393280 | bytes 19660800 | tf_op jit(solution)/shard_map/ffn_wgrad/pallas_call | solution.py:439
  634.8 2.0 constant_dynamic-slice_fusion.refs_1_
  636.8 26.1 %project_back.1 = (bf16[640,1536]{1,0:T(8,128)(2,1)}, f32[1,2048]{1,0:T(1,128)}, f32[1,1536]{1,0:T(1,128)}, bf16[1536,2176]{1,0:T(8,128)(2,1)}, bf16[4,1152,384]{2,1,0:T(8,128)(2,1)}) custom-call(bf16[640,1536]{1,0:T(8,128)(2,1)} %get-tuple-element.146.refs_0_, bf16[640,512]{1,0:T(8,128)(2,1)} %constant_dynamic-slice_fusion.refs_1_, ...), custom_call_target="tpu_custom_call" | custom-call | flops 8053063680 | bytes 32243712 | tf_op jit(solution)/shard_map/project_back/pallas_call | solution.py:439
  665.9 4.7 reduce-scatter.2.cloned.1.call-done
  670.6 99.7 %finish.1 = (f32[48,2176]{1,0:T(8,128)}, f32[48,1536]{1,0:T(8,128)}, f32[1120,384]{1,0:T(8,128)}, f32[1120,384]{1,0:T(8,128)}, f32[1120,384]{1,0:T(8,128)}, /*in...) custom-call(bf16[4,2,2,2,48,2176]{5,4,3,2,1,0:T(8,128)(2,1)} %bitcast.54, ...), custom_call_target="tpu_custom_call" | custom-call | bytes 209715200 | tf_op jit(solution)/shard_map/finish/pallas_call | solution.py:1191
  771.1 1.8 slice.55
  774.1 3.1 copy.51
  (161 shorter events, 32.7 us)
Async XLA Ops:
  7.2 174.9 %all-gather.4.cloned.1.call-start = ((), (), s32[]{:S(2)}) async-start(), calls=%async_computation.1 | async-start | bytes 4423680 | tf_op jit(solution)/shard_map/all_gather | solution.py:1299
  7.2 3.5 copy-start.13
  10.0 1.9 copy-start.29
  10.0 1.9 copy-start.30
  10.0 1.9 copy-start.31
  10.0 2.2 copy-start.23
  10.0 2.2 copy-start.26
  10.0 9.5 %collective-permute-start = (bf16[320,1536]{1,0:T(8,128)(2,1)}, bf16[320,1536]{1,0:T(8,128)(2,1)}, u32[]{:S(2)}, u32[]{:S(2)}) collective-permute-start(bf16[320,1536]{1,0:T(8,128)(2,1)} %get-tuple-element.191), channel_id=1, source_target_pairs={{0,1},{1,0},{2,3},{3,2},{4,5},{5,4},{6,7},{7,6},{8,9},{9,8},{10,11... | collective-permute-start | bytes 2949128 | tf_op jit(solution)/shard_map/ppermute | solution.py:1225
  11.8 11.1 %collective-permute-start.4 = (bf16[320,1536]{1,0:T(8,128)(2,1)}, bf16[320,1536]{1,0:T(8,128)(2,1)}, u32[]{:S(2)}, u32[]{:S(2)}) collective-permute-start(bf16[320,1536]{1,0:T(8,128)(2,1)} %get-tuple-element.189), channel_id=1, source_target_pairs={{0,1},{1,0},{2,3},{3,2},{4,5},{5,4},{6,7},{7,6},{8,9},{9,8},{10,11... | collective-permute-start | bytes 2949128 | tf_op jit(solution)/shard_map/ppermute | solution.py:1225
  12.2 10.7 %copy-start.18 = (bf16[48,3712]{1,0:T(8,128)(2,1)}, bf16[48,3712]{1,0:T(8,128)(2,1)S(1)}, u32[]{:S(2)}) copy-start(bf16[48,3712]{1,0:T(8,128)(2,1)S(1)} %fusion.6.refs_0_) | copy-start | bytes 1069060
  12.2 14.2 %collective-permute-start.3 = (bf16[48,3712]{1,0:T(8,128)(2,1)S(1)}, bf16[48,3712]{1,0:T(8,128)(2,1)}, u32[]{:S(2)}, u32[]{:S(2)}) collective-permute-start(bf16[48,3712]{1,0:T(8,128)(2,1)S(1)} %fusion.6.refs_0_), channel_id=1, source_target_pairs={{0,24},{8,0},{16,8},{24,16},{1,25},{9,1},{17,9},{25,17},{2,26},{10... | collective-permute-start | bytes 1069064 | tf_op jit(solution)/shard_map/ppermute | solution.py:1280
  12.3 25.1 %collective-permute-start.2 = (bf16[48,3712]{1,0:T(8,128)(2,1)S(1)}, bf16[48,3712]{1,0:T(8,128)(2,1)}, u32[]{:S(2)}, u32[]{:S(2)}) collective-permute-start(bf16[48,3712]{1,0:T(8,128)(2,1)S(1)} %fusion.6.refs_0_), channel_id=1, source_target_pairs={{0,16},{8,24},{16,0},{24,8},{1,17},{9,25},{17,1},{25,9},{2,18},{10... | collective-permute-start | bytes 1069064 | tf_op jit(solution)/shard_map/ppermute | solution.py:1280
  14.7 30.2 %collective-permute-start.1 = (bf16[48,3712]{1,0:T(8,128)(2,1)S(1)}, bf16[48,3712]{1,0:T(8,128)(2,1)}, u32[]{:S(2)}, u32[]{:S(2)}) collective-permute-start(bf16[48,3712]{1,0:T(8,128)(2,1)S(1)} %fusion.6.refs_0_), channel_id=1, source_target_pairs={{0,8},{8,16},{16,24},{24,0},{1,9},{9,17},{17,25},{25,1},{2,10},{10... | collective-permute-start | bytes 1069064 | tf_op jit(solution)/shard_map/ppermute | solution.py:1280
  22.9 22.1 %copy-start.20 = (bf16[384,1120]{0,1:T(8,128)(2,1)S(1)}, bf16[384,1120]{0,1:T(8,128)(2,1)}, u32[]{:S(2)}) copy-start(bf16[384,1120]{0,1:T(8,128)(2,1)} %param.22) | copy-start | bytes 2580484
  45.0 2.6 copy-start.21
  45.0 165.1 %all-gather.6.cloned.1.call-start = ((), (), s32[]{:S(2)}) async-start(), calls=%async_computation.2 | async-start | bytes 4423680 | tf_op jit(solution)/shard_map/all_gather | solution.py:1299
  47.6 2.6 copy-start.27
  47.6 2.6 copy-start.32
  47.6 208.3 %all-gather.8.cloned.1.call-start = ((), (), s32[]{:S(2)}) async-start(), calls=%async_computation.3 | async-start | bytes 4423680 | tf_op jit(solution)/shard_map/all_gather | solution.py:1301
  52.5 116.4 %copy-start.2 = (f32[640,128]{1,0:T(8,128)}, f32[640,128]{1,0:T(8,128)S(1)}, u32[]{:S(2)}) copy-start(f32[640,128]{1,0:T(8,128)S(1)} %get-tuple-element.201.cos_ref.refs_5_) | copy-start | bytes 983044
  52.5 116.4 %copy-start.3 = (f32[640,128]{1,0:T(8,128)}, f32[640,128]{1,0:T(8,128)S(1)}, u32[]{:S(2)}) copy-start(f32[640,128]{1,0:T(8,128)S(1)} %get-tuple-element.202.sin_ref.refs_6_) | copy-start | bytes 983044
  168.9 87.6 %copy-start.24 = (f32[32,48]{1,0:T(8,128)}, f32[32,48]{1,0:T(8,128)S(1)}, u32[]{:S(2)}) copy-start(f32[32,48]{1,0:T(8,128)S(1)} %get-tuple-element.192) | copy-start | bytes 18436
  169.0 8.9 %copy-start.4 = (f32[1,1536]{1,0:T(1,128)}, f32[1,1536]{1,0:T(1,128)S(1)}, u32[]{:S(2)}) copy-start(f32[1,1536]{1,0:T(1,128)S(1)} %reshape.181.gain_ref.refs_9_) | copy-start | bytes 18436
  179.2 1.3 copy-start.8
  180.6 14.5 %collective-permute-start.5 = (bf16[640,512]{1,0:T(8,128)(2,1)S(1)}, bf16[640,512]{1,0:T(8,128)(2,1)S(1)}, u32[]{:S(2)}, u32[]{:S(2)}) collective-permute-start(bf16[640,512]{1,0:T(8,128)(2,1)S(1)} %get-tuple-element.99), channel_id=1, source_target_pairs={{0,2},{1,3},{2,0},{3,1},{4,6},{5,7},{6,4},{7,5},{8,10},{9,11},{10,... | collective-permute-start | bytes 1966088 | tf_op jit(solution)/shard_map/ppermute | solution.py:1225
  180.6 15.5 %collective-permute-start.6 = (bf16[640,512]{1,0:T(8,128)(2,1)S(1)}, bf16[640,512]{1,0:T(8,128)(2,1)S(1)}, u32[]{:S(2)}, u32[]{:S(2)}) collective-permute-start(bf16[640,512]{1,0:T(8,128)(2,1)S(1)} %get-tuple-element.99), channel_id=1, source_target_pairs={{0,4},{1,5},{2,6},{3,7},{4,0},{5,1},{6,2},{7,3},{8,12},{9,13},{10,... | collective-permute-start | bytes 1966088 | tf_op jit(solution)/shard_map/ppermute | solution.py:1225
  182.1 488.5 %reduce-scatter.2.cloned.1.call-start = ((), (), s32[]{:S(2)}) async-start(), calls=%async_computation.4 | async-start | bytes 8847360 | tf_op jit(solution)/shard_map/reduce_scatter | solution.py:1395
  182.3 26.9 %collective-permute-start.7 = (bf16[640,512]{1,0:T(8,128)(2,1)S(1)}, bf16[640,512]{1,0:T(8,128)(2,1)S(1)}, u32[]{:S(2)}, u32[]{:S(2)}) collective-permute-start(bf16[640,512]{1,0:T(8,128)(2,1)S(1)} %get-tuple-element.99), channel_id=1, source_target_pairs={{0,6},{1,7},{2,4},{3,5},{4,2},{5,3},{6,0},{7,1},{8,14},{9,15},{10,... | collective-permute-start | bytes 1966088 | tf_op jit(solution)/shard_map/ppermute | solution.py:1225
  210.1 13.5 %collective-permute-start.8 = (bf16[1536,1152]{1,0:T(8,128)(2,1)}, bf16[1536,1152]{1,0:T(8,128)(2,1)}, u32[]{:S(2)}, u32[]{:S(2)}) collective-permute-start(bf16[1536,1152]{1,0:T(8,128)(2,1)} %all-gather.4.cloned.1.call-done.refs_2_), channel_id=1, source_target_pairs={{0,1},{1,0},{2,3},{3,2},{4,5},{5,4},{6,7},{7,6},{8,9},{9,8},{10,11... | collective-permute-start | bytes 10616840 | tf_op jit(solution)/shard_map/ppermute | solution.py:1225
  213.6 11.3 %collective-permute-start.9 = (bf16[1536,1152]{1,0:T(8,128)(2,1)}, bf16[1536,1152]{1,0:T(8,128)(2,1)}, u32[]{:S(2)}, u32[]{:S(2)}) collective-permute-start(bf16[1536,1152]{1,0:T(8,128)(2,1)} %all-gather.6.cloned.1.call-done.refs_3_), channel_id=1, source_target_pairs={{0,1},{1,0},{2,3},{3,2},{4,5},{5,4},{6,7},{7,6},{8,9},{9,8},{10,11... | collective-permute-start | bytes 10616840 | tf_op jit(solution)/shard_map/ppermute | solution.py:1225
  219.2 5.7 copy-start.6
  219.3 5.6 copy-start.5
  224.8 1.5 copy-start.9
  239.1 23.8 %copy-start.1 = (bf16[640,1536]{1,0:T(8,128)(2,1)}, bf16[640,1536]{1,0:T(8,128)(2,1)S(1)}, u32[]{:S(2)}) copy-start(bf16[640,1536]{1,0:T(8,128)(2,1)S(1)} %get-tuple-element.108.heads_ref.o_ref) | copy-start | bytes 5898244
  255.9 9.4 %collective-permute-start.10 = (bf16[1536,1152]{1,0:T(8,128)(2,1)}, bf16[1536,1152]{1,0:T(8,128)(2,1)}, u32[]{:S(2)}, u32[]{:S(2)}) collective-permute-start(bf16[1536,1152]{1,0:T(8,128)(2,1)} %all-gather.8.cloned.1.call-done.refs_4_), channel_id=1, source_target_pairs={{0,1},{1,0},{2,3},{3,2},{4,5},{5,4},{6,7},{7,6},{8,9},{9,8},{10,11... | collective-permute-start | bytes 10616840 | tf_op jit(solution)/shard_map/ppermute | solution.py:1225
  262.9 2.5 copy-start.11
  475.4 42.3 %copy-start.25 = (f32[32,48]{1,0:T(8,128)S(1)}, f32[32,48]{1,0:T(8,128)}, u32[]{:S(2)}) copy-start(f32[32,48]{1,0:T(8,128)} %copy-done.24) | copy-start | bytes 18436
  516.0 21.2 %collective-permute-start.11 = (bf16[4,1152,384]{2,1,0:T(8,128)(2,1)}, bf16[4,1152,384]{2,1,0:T(8,128)(2,1)S(1)}, u32[]{:S(2)}, u32[]{:S(2)}) collective-permute-start(bf16[4,1152,384]{2,1,0:T(8,128)(2,1)} %get-tuple-element.144), channel_id=1, source_target_pairs={{0,1},{1,0},{2,3},{3,2},{4,5},{5,4},{6,7},{7,6},{8,9},{9,8},{10,11... | collective-permute-start | bytes 10616840 | tf_op jit(solution)/shard_map/ppermute | solution.py:1225
  518.4 20.6 %copy-start = (bf16[4,1152,384]{2,1,0:T(8,128)(2,1)S(1)}, bf16[4,1152,384]{2,1,0:T(8,128)(2,1)}, u32[]{:S(2)}) copy-start(bf16[4,1152,384]{2,1,0:T(8,128)(2,1)} %get-tuple-element.140.first_mine) | copy-start | bytes 10616836
  537.2 1.8 copy-start.12
  546.6 1.3 copy-start.19
  546.6 119.3 %collective-permute-start.12 = (bf16[640,1536]{1,0:T(8,128)(2,1)}, bf16[640,1536]{1,0:T(8,128)(2,1)}, u32[]{:S(2)}, u32[]{:S(2)}) collective-permute-start(bf16[640,1536]{1,0:T(8,128)(2,1)} %get-tuple-element.167), channel_id=1, source_target_pairs={{0,2},{1,3},{2,0},{3,1},{4,6},{5,7},{6,4},{7,5},{8,10},{9,11},{10,... | collective-permute-start | bytes 5898248 | tf_op jit(solution)/shard_map/ppermute | solution.py:1225
  547.9 3.0 copy-start.28
  550.1 115.8 %collective-permute-start.13 = (bf16[640,1536]{1,0:T(8,128)(2,1)S(1)}, bf16[640,1536]{1,0:T(8,128)(2,1)}, u32[]{:S(2)}, u32[]{:S(2)}) collective-permute-start(bf16[640,1536]{1,0:T(8,128)(2,1)S(1)} %add_convert_fusion), channel_id=1, source_target_pairs={{0,4},{1,5},{2,6},{3,7},{4,0},{5,1},{6,2},{7,3},{8,12},{9,13},{10,... | collective-permute-start | bytes 5898248 | tf_op jit(solution)/shard_map/ppermute | solution.py:1225
  774.1 3.1 copy-start.14
  777.2 2.3 copy-start.17
  778.5 2.2 copy-start.16
  780.7 2.1 copy-start.15
  (3 other events, 3.2 us)
Sparse Core Ops, SparseCore 0:
  45.1 69.2 all-gather.3
  116.5 68.5 all-gather.5
  187.3 68.5 all-gather.7
  546.7 123.7 reduce-scatter.1

commit v9 on v8

--- a/solution.py
+++ b/solution.py
@@ -16,7 +16,7 @@
 KEY_TILE = 256
 ROW_TILE = 128
 BRANCH_CUTS = (4, 3)
-FFN_CHUNK = 768
+FFN_CHUNK = 256
 FFN_PARTS = 2
 WG_TILE = 384
 PACE = 1.0

time: 798 us -> 796 us (level)
  transfers between devices with their start and end apart: 18 -> 18, of which waited for: 7 -> 7; matrix products, arithmetic and copies ran while one was open for 6% -> 7% of each run, Pallas kernels for 33% -> 34%
where the time goes in v9:
time: 796 us; the launch traced here: 788 us
  Pallas kernels  618 us (78%)
  waiting for transfers between devices  58.3 us (7%)
  local copies, waits for them, and re-layouts  45.5 us (6%)
  other arithmetic  30 us (4%)
  starting transfers between devices  15.5 us (2%)
  between operations  14.6 us (2%)
    pallas_call x8, Pallas kernels, call_beside(): pl.pallas_call(whole_body, grid=grid, in_specs=list(in_specs) + [anywhere...  331 us
    pallas_call x1, Pallas kernels, spread(): pl.pallas_call(spread_body, in_specs=[anywhere] * 5, out_specs=[anywhere]...  115 us
    pallas_call x1, Pallas kernels, finish(): pl.pallas_call(finish_body, in_specs=[anywhere] * 10, out_specs=[inside]...  99.7 us
    pallas_call x1, Pallas kernels, attend_back_fast(): pl.pallas_call(attend_back_body, grid_spec=pltpu.PrefetchScalarGridSpec(n...  24.5 us
    unnamed x75, local copies, waits for them, and re-layouts  22.3 us
    ppermute x11, waiting for transfers between devices, swap(): return lax.ppermute(array, 'gy', [(i, i ^ bits) for i in range(8)])  22.1 us
    pallas_call x1, Pallas kernels, branch_back(): pl.pallas_call(branch_back_body, grid=(steps,), in_specs=[moving, first[0...  18.8 us
    ppermute x3, waiting for transfers between devices, on_core(): lax.ppermute(attn_own, 'gx', [(i, (i + k) % 4) for i in range(4)])  18.6 us
  transfers between devices with their start and end apart: 18, of which 7 were waited for; matrix products, arithmetic and copies ran while one was open for 7% of the time, Pallas kernels for 34%

profile of v9, /device:TPU:9, one launch (start us, length us, event | category | flops | bytes accessed | tf_op | source)
XLA Modules:
  0.0 787.7 jit_solution(13519765625260344430)
XLA Ops:
  7.3 2.7 dynamic-slice_bitcast_fusion.3
  12.3 2.5 collective-permute-start.2
  14.7 2.2 collective-permute-start.1
  16.9 1.6 copy.34
  19.5 3.4 maximum_select_fusion.x_ref.refs_8_
  22.9 3.4 maximum_select_fusion.1.refs_4_.refs_1_.cot_ref
  26.4 11.0 %collective-permute-done.2.refs_2_ = bf16[48,3712]{1,0:T(8,128)(2,1)} collective-permute-done((bf16[48,3712]{1,0:T(8,128)(2,1)S(1)}, bf16[48,3712]{1,0:T(8,128)(2,1)}, u32[]{:S(2)}, u32[]{:S(2)}) %collective-permute-start.2) | collective-permute-done | bytes 356384 | tf_op jit(solution)/shard_map/ppermute | solution.py:1280
  37.4 7.6 collective-permute-done.1.refs_1_
  45.1 1.5 copy.35
  47.7 1.5 copy.36
  52.5 114.6 %spread.1 = (bf16[4,8,48,3712]{3,2,1,0:T(8,128)(2,1)}, bf16[640,1536]{1,0:T(8,128)(2,1)}, bf16[640,1536]{1,0:T(8,128)(2,1)}, bf16[640,1536]{1,0:T(8,128)(2,1)}) custom-call(bf16[48,3712]{1,0:T(8,128)(2,1)} %copy-done.18, bf16[48,3712]{1,0:T(8,128)(2,1)} %collective-permute-done.1.refs_1_, bf16[48,3712]{1,0:T(8,128)(2,1)} %collective-permute-done.2.refs_2_, ...), custom_call_target="tpu_custom_call" | custom-call | bytes 314572800 | tf_op jit(solution)/shard_map/spread/pallas_call | solution.py:884
  169.0 8.9 %project.1 = (bf16[640,1536]{1,0:T(8,128)(2,1)S(1)}, bf16[640,1536]{1,0:T(8,128)(2,1)S(1)}, bf16[640,512]{1,0:T(8,128)(2,1)S(1)}) custom-call(bf16[640,1536]{1,0:T(8,128)(2,1)} %maximum_select_fusion.x_ref.refs_8_, f32[1,1536]{1,0:T(1,128)S(1)} %reshape.181.gain_ref.refs_9_, bf16[1536,3712]{1,0:T(8,128)(2,1)} %bitcast.48, f32[1,2048]{1,0:T(1,128)S(1)} %reshape.182.b_ref, ...), custom_call_target="tpu_custom_call" | custom-call | flops 4026531840 | bytes 14155776 | tf_op jit(solution)/shard_map/project/pallas_call | solution.py:795
  178.0 1.3 copy-done.7
  179.3 1.3 copy-done.8
  180.6 1.4 collective-permute-start.6
  183.8 1.7 broadcast_in_dim.158
  186.4 8.7 %collective-permute-done.5 = bf16[640,512]{1,0:T(8,128)(2,1)S(1)} collective-permute-done((bf16[640,512]{1,0:T(8,128)(2,1)S(1)}, bf16[640,512]{1,0:T(8,128)(2,1)S(1)}, u32[]{:S(2)}, u32[]{:S(2)}) %collective-permute-start.5) | collective-permute-done | bytes 655392 | tf_op jit(solution)/shard_map/ppermute | solution.py:1225
  197.0 12.2 %collective-permute-done.7 = bf16[640,512]{1,0:T(8,128)(2,1)S(1)} collective-permute-done((bf16[640,512]{1,0:T(8,128)(2,1)S(1)}, bf16[640,512]{1,0:T(8,128)(2,1)S(1)}, u32[]{:S(2)}, u32[]{:S(2)}) %collective-permute-start.7) | collective-permute-done | bytes 655392 | tf_op jit(solution)/shard_map/ppermute | solution.py:1225
  210.1 3.5 collective-permute-start.8
  213.8 5.1 or_reduce_fusion
  219.3 4.3 select_convert_fusion.bias_ref
  223.6 1.3 collective-permute-done.9.refs_6_
  224.9 1.5 copy-done.9
  226.4 12.0 %tree_attention.1 = (bf16[640,1536]{1,0:T(8,128)(2,1)S(1)}, f32[5,2,1,768]{3,2,1,0:T(1,128)S(1)}) custom-call(s32[5,10]{1,0:T(8,128)S(1)} %select_reduce_fusion.5.list_ref, s32[5]{0:T(128)S(1)} %convert_reduce_fusion.4.count_ref, bf16[640,1536]{1,0:T(8,128)(2,1)S(1)} %copy-done.9, bf16[2560,512]{1,0:T(8,128)(2,1)} %constant_dynamic-update-slice_fusion.kv_ref, ...), custom_call_target="tpu_custom_call" | custom-call | flops 10066329600 | bytes 6553600 | tf_op jit(solution)/shard_map/tree_attention/pallas_call | solution.py:647
  239.1 16.9 %all-gather.8.cloned.1.call-done.refs_4_ = bf16[1536,1152]{1,0:T(8,128)(2,1)} async-done(((bf16[384,1152]{1,0:T(8,128)(2,1)}), bf16[1536,1152]{1,0:T(8,128)(2,1)}) %all-gather.8.cloned.1.call-update) | async-done | bytes 3538960 | tf_op jit(solution)/shard_map/all_gather | solution.py:1301
  256.5 6.3 multiply_reduce_fusion
  262.9 1.9 multiply_convert_fusion.refs_0_.refs_8_.refs_9_.refs_4_
  265.4 51.7 %ffn_block.4 = (bf16[640,2304]{1,0:T(8,128)(2,1)}, bf16[640,2304]{1,0:T(8,128)(2,1)}, bf16[640,2304]{1,0:T(8,128)(2,1)}, bf16[640,1536]{1,0:T(8,128)(2,1)}, bf16...) custom-call(bf16[640,1536]{1,0:T(8,128)(2,1)} %multiply_convert_fusion.refs_0_.refs_8_.refs_9_.refs_4_, ...), custom_call_target="tpu_custom_call" | custom-call | flops 27179089920 | bytes 35979264 | tf_op jit(solution)/shard_map/ffn_block/pallas_call | solution.py:439
  317.0 38.4 %ffn_block.5 = (bf16[640,2304]{1,0:T(8,128)(2,1)}, bf16[640,2304]{1,0:T(8,128)(2,1)}, bf16[640,2304]{1,0:T(8,128)(2,1)}, bf16[640,1536]{1,0:T(8,128)(2,1)}, bf16...) custom-call(bf16[640,1536]{1,0:T(8,128)(2,1)} %get-tuple-element.112.refs_0_.refs_8_.refs_5_, ...), custom_call_target="tpu_custom_call" | custom-call | flops 27179089920 | bytes 35979264 | tf_op jit(solution)/shard_map/ffn_block/pallas_call | solution.py:439
  355.4 39.3 %ffn_block.6 = (bf16[640,2304]{1,0:T(8,128)(2,1)}, bf16[640,2304]{1,0:T(8,128)(2,1)}, bf16[640,2304]{1,0:T(8,128)(2,1)}, bf16[640,1536]{1,0:T(8,128)(2,1)}, bf16...) custom-call(bf16[640,1536]{1,0:T(8,128)(2,1)} %get-tuple-element.115.refs_0_.refs_7_, ...), custom_call_target="tpu_custom_call" | custom-call | flops 27179089920 | bytes 35979264 | tf_op jit(solution)/shard_map/ffn_block/pallas_call | solution.py:439
  394.8 38.3 %ffn_block.7 = (bf16[640,2304]{1,0:T(8,128)(2,1)}, bf16[640,2304]{1,0:T(8,128)(2,1)}, bf16[640,2304]{1,0:T(8,128)(2,1)}, bf16[640,1536]{1,0:T(8,128)(2,1)}, bf16...) custom-call(bf16[640,1536]{1,0:T(8,128)(2,1)} %get-tuple-element.122.refs_9_.refs_0_.refs_6_, ...), custom_call_target="tpu_custom_call" | custom-call | flops 27179089920 | bytes 35979264 | tf_op jit(solution)/shard_map/ffn_block/pallas_call | solution.py:439
  434.1 2.9 add_convert_fusion.1.refs_11_
  437.0 34.7 %ffn_wgrad.3 = (bf16[4,1152,384]{2,1,0:T(8,128)(2,1)}, bf16[4,1152,384]{2,1,0:T(8,128)(2,1)}, bf16[128,1536]{1,0:T(8,128)(2,1)}, bf16[128,1536]{1,0:T(8,128)(2,1...) custom-call(bf16[640,2304]{1,0:T(8,128)(2,1)} %get-tuple-element.119.refs_0_, ...), custom_call_target="tpu_custom_call" | custom-call | flops 18119393280 | bytes 19660800 | tf_op jit(solution)/shard_map/ffn_wgrad/pallas_call | solution.py:439
  471.8 2.3 add_convert_fusion.2.refs_10_
  474.1 40.9 %ffn_wgrad.4 = (bf16[4,1152,384]{2,1,0:T(8,128)(2,1)}, bf16[4,1152,384]{2,1,0:T(8,128)(2,1)}, bf16[4,1152,384]{2,1,0:T(8,128)(2,1)}, bf16[448,1536]{1,0:T(8,128)(2,1)}, bf16[256,1536]{1,0:T(8,128)(2,1)}) custom-call(bf16[640,2304]{1,0:T(8,128)(2,1)} %get-tuple-element.131.refs_0_, bf16[640,2304]{1,0:T(8,128)(2,1)} %get-tuple-element.132.refs_1_, ...), custom_call_target="tpu_custom_call" | custom-call | flops 18119393280 | bytes 19660800 | tf_op jit(solution)/shard_map/ffn_wgrad/pallas_call | solution.py:439
  515.0 1.4 collective-permute-start.11
  517.1 18.8 %branch_back.1 = (f32[640,1536]{1,0:T(8,128)}, bf16[640,1536]{1,0:T(8,128)(2,1)}, f32[1,1536]{1,0:T(1,128)}, bf16[1536,1536]{1,0:T(8,128)(2,1)}) custom-call(bf16[640,1536]{1,0:T(8,128)(2,1)} %get-tuple-element.111.own_ref, bf16[512,1536]{1,0:T(8,128)(2,1)} %get-tuple-element.118.xa_ref, bf16[128,1536]{1,0:T(8,128)(2,1)} %get-tuple-element.129.xb_ref, ...), custom_call_target="tpu_custom_call" | custom-call | flops 6039797760 | bytes 29097984 | tf_op jit(solution)/shard_map/branch_back/pallas_call | solution.py:943
  535.9 1.8 copy-done.12
  537.7 7.6 both_back.1
  546.6 2.2 add_convert_fusion
  549.5 24.5 %tree_attention_back.1 = (bf16[640,1536]{1,0:T(8,128)(2,1)}, bf16[2560,512]{1,0:T(8,128)(2,1)}) custom-call(s32[5,10]{1,0:T(8,128)} %copy-done.5, s32[5]{0:T(128)} %copy-done.6, bf16[640,1536]{1,0:T(8,128)(2,1)} %copy-done.8, bf16[2560,512]{1,0:T(8,128)(2,1)} %constant_dynamic-update-slice_fusion.kv_ref, bf16[2560,640]{1,0:T(8,128)(2,1)} %select_convert_fusion.bias_ref, ...), custom_call_target="tpu_custom_call" | custom-call | flops 25165824000 | bytes 13107200 | tf_op jit(solution)/shard_map/tree_attention_back/pallas_call | solution.py:738
  574.0 62.1 %ffn_wgrad.5 = (bf16[4,1152,384]{2,1,0:T(8,128)(2,1)}, bf16[4,1152,384]{2,1,0:T(8,128)(2,1)}, bf16[640,512]{1,0:T(8,128)(2,1)}, bf16[640,512]{1,0:T(8,128)(2,1)}, bf16[640,512]{1,0:T(8,128)(2,1)}) custom-call(bf16[640,2304]{1,0:T(8,128)(2,1)} %get-tuple-element.148.refs_0_, bf16[640,2304]{1,0:T(8,128)(2,1)} %get-tuple-element.149.refs_1_, ...), custom_call_target="tpu_custom_call" | custom-call | flops 18119393280 | bytes 19660800 | tf_op jit(solution)/shard_map/ffn_wgrad/pallas_call | solution.py:439
  636.0 2.0 constant_dynamic-slice_fusion.refs_1_
  638.0 26.0 %project_back.1 = (bf16[640,1536]{1,0:T(8,128)(2,1)}, f32[1,2048]{1,0:T(1,128)}, f32[1,1536]{1,0:T(1,128)}, bf16[1536,2176]{1,0:T(8,128)(2,1)}, bf16[4,1152,384]{2,1,0:T(8,128)(2,1)}) custom-call(bf16[640,1536]{1,0:T(8,128)(2,1)} %get-tuple-element.146.refs_0_, bf16[640,512]{1,0:T(8,128)(2,1)} %constant_dynamic-slice_fusion.refs_1_, ...), custom_call_target="tpu_custom_call" | custom-call | flops 8053063680 | bytes 32243712 | tf_op jit(solution)/shard_map/project_back/pallas_call | solution.py:439
  667.6 99.7 %finish.1 = (f32[48,2176]{1,0:T(8,128)}, f32[48,1536]{1,0:T(8,128)}, f32[1120,384]{1,0:T(8,128)}, f32[1120,384]{1,0:T(8,128)}, f32[1120,384]{1,0:T(8,128)}, /*in...) custom-call(bf16[4,2,2,2,48,2176]{5,4,3,2,1,0:T(8,128)(2,1)} %bitcast.54, ...), custom_call_target="tpu_custom_call" | custom-call | bytes 209715200 | tf_op jit(solution)/shard_map/finish/pallas_call | solution.py:1191
  768.1 1.8 slice.55
  771.1 3.1 copy.51
  774.2 1.3 copy.52
  (161 shorter events, 32.1 us)
Async XLA Ops:
  7.2 174.8 %all-gather.4.cloned.1.call-start = ((), (), s32[]{:S(2)}) async-start(), calls=%async_computation.1 | async-start | bytes 4423680 | tf_op jit(solution)/shard_map/all_gather | solution.py:1299
  7.2 3.5 copy-start.13
  10.0 1.9 copy-start.29
  10.0 1.9 copy-start.30
  10.0 1.9 copy-start.31
  10.0 2.2 copy-start.23
  10.0 2.2 copy-start.26
  10.0 9.5 %collective-permute-start = (bf16[320,1536]{1,0:T(8,128)(2,1)}, bf16[320,1536]{1,0:T(8,128)(2,1)}, u32[]{:S(2)}, u32[]{:S(2)}) collective-permute-start(bf16[320,1536]{1,0:T(8,128)(2,1)} %get-tuple-element.191), channel_id=1, source_target_pairs={{0,1},{1,0},{2,3},{3,2},{4,5},{5,4},{6,7},{7,6},{8,9},{9,8},{10,11... | collective-permute-start | bytes 2949128 | tf_op jit(solution)/shard_map/ppermute | solution.py:1225
  11.8 11.1 %collective-permute-start.4 = (bf16[320,1536]{1,0:T(8,128)(2,1)}, bf16[320,1536]{1,0:T(8,128)(2,1)}, u32[]{:S(2)}, u32[]{:S(2)}) collective-permute-start(bf16[320,1536]{1,0:T(8,128)(2,1)} %get-tuple-element.189), channel_id=1, source_target_pairs={{0,1},{1,0},{2,3},{3,2},{4,5},{5,4},{6,7},{7,6},{8,9},{9,8},{10,11... | collective-permute-start | bytes 2949128 | tf_op jit(solution)/shard_map/ppermute | solution.py:1225
  12.2 10.7 %copy-start.18 = (bf16[48,3712]{1,0:T(8,128)(2,1)}, bf16[48,3712]{1,0:T(8,128)(2,1)S(1)}, u32[]{:S(2)}) copy-start(bf16[48,3712]{1,0:T(8,128)(2,1)S(1)} %fusion.6.refs_0_) | copy-start | bytes 1069060
  12.2 14.2 %collective-permute-start.3 = (bf16[48,3712]{1,0:T(8,128)(2,1)S(1)}, bf16[48,3712]{1,0:T(8,128)(2,1)}, u32[]{:S(2)}, u32[]{:S(2)}) collective-permute-start(bf16[48,3712]{1,0:T(8,128)(2,1)S(1)} %fusion.6.refs_0_), channel_id=1, source_target_pairs={{0,24},{8,0},{16,8},{24,16},{1,25},{9,1},{17,9},{25,17},{2,26},{10... | collective-permute-start | bytes 1069064 | tf_op jit(solution)/shard_map/ppermute | solution.py:1280
  12.3 25.1 %collective-permute-start.2 = (bf16[48,3712]{1,0:T(8,128)(2,1)S(1)}, bf16[48,3712]{1,0:T(8,128)(2,1)}, u32[]{:S(2)}, u32[]{:S(2)}) collective-permute-start(bf16[48,3712]{1,0:T(8,128)(2,1)S(1)} %fusion.6.refs_0_), channel_id=1, source_target_pairs={{0,16},{8,24},{16,0},{24,8},{1,17},{9,25},{17,1},{25,9},{2,18},{10... | collective-permute-start | bytes 1069064 | tf_op jit(solution)/shard_map/ppermute | solution.py:1280
  14.7 30.2 %collective-permute-start.1 = (bf16[48,3712]{1,0:T(8,128)(2,1)S(1)}, bf16[48,3712]{1,0:T(8,128)(2,1)}, u32[]{:S(2)}, u32[]{:S(2)}) collective-permute-start(bf16[48,3712]{1,0:T(8,128)(2,1)S(1)} %fusion.6.refs_0_), channel_id=1, source_target_pairs={{0,8},{8,16},{16,24},{24,0},{1,9},{9,17},{17,25},{25,1},{2,10},{10... | collective-permute-start | bytes 1069064 | tf_op jit(solution)/shard_map/ppermute | solution.py:1280
  22.9 22.1 %copy-start.20 = (bf16[384,1120]{0,1:T(8,128)(2,1)S(1)}, bf16[384,1120]{0,1:T(8,128)(2,1)}, u32[]{:S(2)}) copy-start(bf16[384,1120]{0,1:T(8,128)(2,1)} %param.22) | copy-start | bytes 2580484
  45.0 2.6 copy-start.21
  45.0 165.0 %all-gather.6.cloned.1.call-start = ((), (), s32[]{:S(2)}) async-start(), calls=%async_computation.2 | async-start | bytes 4423680 | tf_op jit(solution)/shard_map/all_gather | solution.py:1299
  47.6 2.6 copy-start.27
  47.6 2.6 copy-start.32
  47.6 208.3 %all-gather.8.cloned.1.call-start = ((), (), s32[]{:S(2)}) async-start(), calls=%async_computation.3 | async-start | bytes 4423680 | tf_op jit(solution)/shard_map/all_gather | solution.py:1301
  52.5 116.4 %copy-start.2 = (f32[640,128]{1,0:T(8,128)}, f32[640,128]{1,0:T(8,128)S(1)}, u32[]{:S(2)}) copy-start(f32[640,128]{1,0:T(8,128)S(1)} %get-tuple-element.201.cos_ref.refs_5_) | copy-start | bytes 983044
  52.5 116.4 %copy-start.3 = (f32[640,128]{1,0:T(8,128)}, f32[640,128]{1,0:T(8,128)S(1)}, u32[]{:S(2)}) copy-start(f32[640,128]{1,0:T(8,128)S(1)} %get-tuple-element.202.sin_ref.refs_6_) | copy-start | bytes 983044
  168.9 87.6 %copy-start.24 = (f32[32,48]{1,0:T(8,128)}, f32[32,48]{1,0:T(8,128)S(1)}, u32[]{:S(2)}) copy-start(f32[32,48]{1,0:T(8,128)S(1)} %get-tuple-element.192) | copy-start | bytes 18436
  169.0 9.0 %copy-start.4 = (f32[1,1536]{1,0:T(1,128)}, f32[1,1536]{1,0:T(1,128)S(1)}, u32[]{:S(2)}) copy-start(f32[1,1536]{1,0:T(1,128)S(1)} %reshape.181.gain_ref.refs_9_) | copy-start | bytes 18436
  179.3 1.3 copy-start.8
  180.6 14.6 %collective-permute-start.5 = (bf16[640,512]{1,0:T(8,128)(2,1)S(1)}, bf16[640,512]{1,0:T(8,128)(2,1)S(1)}, u32[]{:S(2)}, u32[]{:S(2)}) collective-permute-start(bf16[640,512]{1,0:T(8,128)(2,1)S(1)} %get-tuple-element.99), channel_id=1, source_target_pairs={{0,2},{1,3},{2,0},{3,1},{4,6},{5,7},{6,4},{7,5},{8,10},{9,11},{10,... | collective-permute-start | bytes 1966088 | tf_op jit(solution)/shard_map/ppermute | solution.py:1225
  180.6 15.5 %collective-permute-start.6 = (bf16[640,512]{1,0:T(8,128)(2,1)S(1)}, bf16[640,512]{1,0:T(8,128)(2,1)S(1)}, u32[]{:S(2)}, u32[]{:S(2)}) collective-permute-start(bf16[640,512]{1,0:T(8,128)(2,1)S(1)} %get-tuple-element.99), channel_id=1, source_target_pairs={{0,4},{1,5},{2,6},{3,7},{4,0},{5,1},{6,2},{7,3},{8,12},{9,13},{10,... | collective-permute-start | bytes 1966088 | tf_op jit(solution)/shard_map/ppermute | solution.py:1225
  182.0 485.6 %reduce-scatter.2.cloned.1.call-start = ((), (), s32[]{:S(2)}) async-start(), calls=%async_computation.4 | async-start | bytes 8847360 | tf_op jit(solution)/shard_map/reduce_scatter | solution.py:1395
  182.6 26.6 %collective-permute-start.7 = (bf16[640,512]{1,0:T(8,128)(2,1)S(1)}, bf16[640,512]{1,0:T(8,128)(2,1)S(1)}, u32[]{:S(2)}, u32[]{:S(2)}) collective-permute-start(bf16[640,512]{1,0:T(8,128)(2,1)S(1)} %get-tuple-element.99), channel_id=1, source_target_pairs={{0,6},{1,7},{2,4},{3,5},{4,2},{5,3},{6,0},{7,1},{8,14},{9,15},{10,... | collective-permute-start | bytes 1966088 | tf_op jit(solution)/shard_map/ppermute | solution.py:1225
  210.1 13.5 %collective-permute-start.8 = (bf16[1536,1152]{1,0:T(8,128)(2,1)}, bf16[1536,1152]{1,0:T(8,128)(2,1)}, u32[]{:S(2)}, u32[]{:S(2)}) collective-permute-start(bf16[1536,1152]{1,0:T(8,128)(2,1)} %all-gather.4.cloned.1.call-done.refs_2_), channel_id=1, source_target_pairs={{0,1},{1,0},{2,3},{3,2},{4,5},{5,4},{6,7},{7,6},{8,9},{9,8},{10,11... | collective-permute-start | bytes 10616840 | tf_op jit(solution)/shard_map/ppermute | solution.py:1225
  213.6 11.3 %collective-permute-start.9 = (bf16[1536,1152]{1,0:T(8,128)(2,1)}, bf16[1536,1152]{1,0:T(8,128)(2,1)}, u32[]{:S(2)}, u32[]{:S(2)}) collective-permute-start(bf16[1536,1152]{1,0:T(8,128)(2,1)} %all-gather.6.cloned.1.call-done.refs_3_), channel_id=1, source_target_pairs={{0,1},{1,0},{2,3},{3,2},{4,5},{5,4},{6,7},{7,6},{8,9},{9,8},{10,11... | collective-permute-start | bytes 10616840 | tf_op jit(solution)/shard_map/ppermute | solution.py:1225
  219.2 5.7 copy-start.6
  219.3 5.6 copy-start.5
  224.9 1.5 copy-start.9
  239.1 23.8 %copy-start.1 = (bf16[640,1536]{1,0:T(8,128)(2,1)}, bf16[640,1536]{1,0:T(8,128)(2,1)S(1)}, u32[]{:S(2)}) copy-start(bf16[640,1536]{1,0:T(8,128)(2,1)S(1)} %get-tuple-element.108.heads_ref.o_ref) | copy-start | bytes 5898244
  255.9 9.4 %collective-permute-start.10 = (bf16[1536,1152]{1,0:T(8,128)(2,1)}, bf16[1536,1152]{1,0:T(8,128)(2,1)}, u32[]{:S(2)}, u32[]{:S(2)}) collective-permute-start(bf16[1536,1152]{1,0:T(8,128)(2,1)} %all-gather.8.cloned.1.call-done.refs_4_), channel_id=1, source_target_pairs={{0,1},{1,0},{2,3},{3,2},{4,5},{5,4},{6,7},{7,6},{8,9},{9,8},{10,11... | collective-permute-start | bytes 10616840 | tf_op jit(solution)/shard_map/ppermute | solution.py:1225
  262.9 2.5 copy-start.11
  474.1 42.3 %copy-start.25 = (f32[32,48]{1,0:T(8,128)S(1)}, f32[32,48]{1,0:T(8,128)}, u32[]{:S(2)}) copy-start(f32[32,48]{1,0:T(8,128)} %copy-done.24) | copy-start | bytes 18436
  515.0 20.9 %collective-permute-start.11 = (bf16[4,1152,384]{2,1,0:T(8,128)(2,1)}, bf16[4,1152,384]{2,1,0:T(8,128)(2,1)S(1)}, u32[]{:S(2)}, u32[]{:S(2)}) collective-permute-start(bf16[4,1152,384]{2,1,0:T(8,128)(2,1)} %get-tuple-element.144), channel_id=1, source_target_pairs={{0,1},{1,0},{2,3},{3,2},{4,5},{5,4},{6,7},{7,6},{8,9},{9,8},{10,11... | collective-permute-start | bytes 10616840 | tf_op jit(solution)/shard_map/ppermute | solution.py:1225
  517.1 20.6 %copy-start = (bf16[4,1152,384]{2,1,0:T(8,128)(2,1)S(1)}, bf16[4,1152,384]{2,1,0:T(8,128)(2,1)}, u32[]{:S(2)}) copy-start(bf16[4,1152,384]{2,1,0:T(8,128)(2,1)} %get-tuple-element.140.first_mine) | copy-start | bytes 10616836
  535.9 1.8 copy-start.12
  545.3 1.3 copy-start.19
  545.3 121.7 %collective-permute-start.12 = (bf16[640,1536]{1,0:T(8,128)(2,1)}, bf16[640,1536]{1,0:T(8,128)(2,1)}, u32[]{:S(2)}, u32[]{:S(2)}) collective-permute-start(bf16[640,1536]{1,0:T(8,128)(2,1)} %get-tuple-element.167), channel_id=1, source_target_pairs={{0,2},{1,3},{2,0},{3,1},{4,6},{5,7},{6,4},{7,5},{8,10},{9,11},{10,... | collective-permute-start | bytes 5898248 | tf_op jit(solution)/shard_map/ppermute | solution.py:1225
  546.6 2.7 copy-start.28
  548.8 118.2 %collective-permute-start.13 = (bf16[640,1536]{1,0:T(8,128)(2,1)S(1)}, bf16[640,1536]{1,0:T(8,128)(2,1)}, u32[]{:S(2)}, u32[]{:S(2)}) collective-permute-start(bf16[640,1536]{1,0:T(8,128)(2,1)S(1)} %add_convert_fusion), channel_id=1, source_target_pairs={{0,4},{1,5},{2,6},{3,7},{4,0},{5,1},{6,2},{7,3},{8,12},{9,13},{10,... | collective-permute-start | bytes 5898248 | tf_op jit(solution)/shard_map/ppermute | solution.py:1225
  771.1 3.1 copy-start.14
  774.2 2.3 copy-start.17
  775.5 2.2 copy-start.16
  777.7 2.1 copy-start.15
  (3 other events, 3.2 us)
Sparse Core Ops, SparseCore 0:
  45.1 69.2 all-gather.3
  116.5 68.5 all-gather.5
  187.3 68.5 all-gather.7
  545.4 122.1 reduce-scatter.1
